TPU v7x, 256 devices: a whole 4x4x8 slice. The times are simulated.
256 devices in a mesh: tm: 16 (over z, core), tile: 4 (over x), group: 4 (over y).
Axes of the slice: x: 4, y: 4, z: 8, core: 2. Of those that a mesh axis runs over, the one named last changes fastest.
Arguments:
- latents: bfloat16 [4, 32, 12, 64, 384], P('group', 'tm', 'tile'), may hold values from -6 to 6
- frame_counts: int32 [4, 4], P('group'), may hold values from 1 to 15, 32 in all within a row
- gain_one: float32 [384], replicated, may hold values from 0.1 to 1.9
- gain_two: float32 [384], replicated, may hold values from 0.1 to 1.9
- conv_one: bfloat16 [10368, 384], P(('tm', 'group')), may hold values from -0.0625 to 0.0625
- conv_two: bfloat16 [10368, 384], P(('tm', 'group')), may hold values from -0.0625 to 0.0625
Outputs:
- upsampled: bfloat16 [4, 32, 24, 128, 384], P('group', 'tm', 'tile')
Inputs may be any that keep to these rules, and one draw needn't show every extreme that they name: `frame_counts`: each group's counts sum to 32; in each group the largest count equals 15.
All inputs are finite; a program needn't handle non-finite values.
Results may differ from a plain program's by a relative error of at most 0.0041.
Values may be sent and summed in bfloat16 or wider, within the bound.
No kernel may reach another device: no remote copies, remote signals or barrier semaphores. Data moves between devices by JAX's collectives and lax.ppermute only.
A program may use at most 128 MiB of HBM per device.

v0:
```python
import jax
import jax.numpy as jnp
from jax import lax
from jax.sharding import PartitionSpec as P

EPS = 1e-06


def passed_along(x, axis, by):
    peers = lax.axis_size(axis)
    pairs = [(i, i + by) for i in range(peers) if 0 <= i + by < peers]
    return lax.ppermute(x, axis, pairs)


def with_halo(cells, sides, width):
    for axis, dim in sides:
        count = lax.axis_size(axis)
        ends = count - 1
        head = lax.slice_in_dim(cells, 0, width, axis=dim)
        tail = lax.slice_in_dim(cells, cells.shape[dim] - width, cells.shape[dim], axis=dim)
        cells = jnp.concatenate(
            [
                lax.ppermute(tail, axis, [(i, (i + 1) % count) for i in range(ends)]),
                cells,
                lax.ppermute(head, axis, [((i + 1) % count, i) for i in range(ends)]),
            ],
            axis=dim,
        )
    return cells


def norm_silu(values, gain):
    mean_sq = jnp.mean(values * values, axis=-1, keepdims=True)
    return jax.nn.silu(values * lax.rsqrt(mean_sq + EPS) * gain)


def video_start(slots, counts):
    starts = jnp.cumsum(counts) - counts
    hit = starts[None, :] <= slots[:, None]
    return jnp.max(jnp.where(hit, starts[None, :], 0), axis=1)


def causal_conv(padded, weight, out_slots, counts):
    channels = weight.shape[1]
    padded = jnp.pad(padded, ((0, 0), (0, 0), (1, 1), (0, 0)))
    frames = padded.shape[0] - 2
    height = padded.shape[1] - 2
    width = padded.shape[2] - 2
    begins = video_start(out_slots, counts)
    total = jnp.zeros((frames, height, width, channels), jnp.float32)
    for time_tap in range(3):
        partial_sum = jnp.zeros((frames * height * width, channels), jnp.float32)
        for row_tap in range(3):
            columns = jnp.concatenate(
                [
                    padded[
                        time_tap : time_tap + frames,
                        row_tap : row_tap + height,
                        col_tap : col_tap + width,
                    ]
                    for col_tap in range(3)
                ],
                axis=-1,
            )
            first_row = (time_tap * 3 + row_tap) * 3 * channels
            block_w = weight[first_row : first_row + 3 * channels]
            partial_sum = partial_sum + jnp.dot(
                columns.reshape(-1, 3 * channels), block_w, preferred_element_type=jnp.float32
            )
        valid = (out_slots - (2 - time_tap) >= begins).astype(jnp.float32)
        total = total + valid[:, None, None, None] * partial_sum.reshape(
            frames, height, width, channels
        )
    return total


def body(latents, frame_counts, gain_one, gain_two, conv_one, conv_two):
    counts = frame_counts.reshape(-1)
    source = latents[0].astype(jnp.float32)
    frames = source.shape[0]
    base_slot = lax.axis_index("tm") * frames
    weight_one, weight_two = (
        lax.all_gather(conv_one, ("tm", "group"), axis=0, tiled=True),
        lax.all_gather(conv_two, ("tm", "group"), axis=0, tiled=True),
    )
    hidden_one = norm_silu(source, gain_one).astype(jnp.bfloat16)
    earlier = passed_along(hidden_one, "tm", 1)
    extended = jnp.concatenate([earlier, hidden_one], axis=0)
    padded_one = with_halo(extended, (("tile", 1),), 1)
    out_count = extended.shape[0] - 2
    slots_one = base_slot - (out_count - frames) + jnp.arange(out_count, dtype=jnp.int32)
    first = causal_conv(padded_one, weight_one, slots_one, counts)
    hidden_two = norm_silu(first, gain_two).astype(jnp.bfloat16)
    hidden_prior = passed_along(hidden_two, "tm", 1)
    extended_two = jnp.concatenate([hidden_prior, hidden_two], axis=0)
    padded_two = with_halo(extended_two, (("tile", 1),), 1)
    slots_two = base_slot + jnp.arange(frames, dtype=jnp.int32)
    second = causal_conv(padded_two, weight_two, slots_two, counts)
    block = (source + second).astype(jnp.bfloat16)
    height, width, channels = (block.shape[1], block.shape[2], block.shape[3])
    result = jnp.broadcast_to(
        block[:, :, None, :, None, :], (frames, height, 2, width, 2, channels)
    ).reshape(frames, 2 * height, 2 * width, channels)
    return result[None]


def solution(mesh):
    in_specs = (
        P("group", "tm", "tile", None, None),
        P("group", None),
        P(),
        P(),
        P(("tm", "group"), None),
        P(("tm", "group"), None),
    )
    out_specs = P("group", "tm", "tile", None, None)
    return jax.shard_map(body, mesh=mesh, in_specs=in_specs, out_specs=out_specs, check_vma=False)
```

profile of v0, /device:TPU:32, one launch (start us, length us, event | category | flops | bytes accessed | tf_op | source)
XLA Modules:
  0.0 207.3 jit_solution(13909518443019649055)
XLA Ops:
  6.5 0.7 all-gather.5.cloned.1.call-update
  7.3 0.7 all-gather.7.cloned.1.call-update
  8.0 1.1 fusion.39
  9.1 1.2 fusion.46
  10.3 1.9 collective-permute-start
  12.3 0.8 reduce-window_clone.1
  13.1 0.7 subtract_bitcast_fusion
  13.8 0.2 fusion.52
  14.0 4.4 %collective-permute-done = bf16[2,3,64,384]{3,2,1,0:T(8,128)(2,1)S(1)} collective-permute-done((bf16[2,3,64,384]{3,2,1,0:T(8,128)(2,1)S(1)}, bf16[2,3,64,384]{3,2,1,0:T(8,128)(2,1)S(1)}, u32[]{:S(2)}, u32[]{:S(2)}) %collective-permute-start) | collective-permute-done | bytes 294944 | tf_op jit(solution)/shard_map/ppermute | solution.py:12
  18.4 1.3 collective-permute-start.2
  19.7 4.6 %collective-permute-start.1 = (bf16[4,1,64,384]{3,2,1,0:T(8,128)(2,1)S(1)}, bf16[4,1,64,384]{3,2,1,0:T(8,128)(2,1)S(1)}, u32[]{:S(2)}, u32[]{:S(2)}) collective-permute-start(bf16[4,1,64,384]{3,2,1,0:T(8,128)(2,1)S(1)} %get-tuple-element.59), channel_id=1, source_target_pairs={{0,4},{4,8},{8,12},{1,5},{5,9},{9,13},{2,6},{6,10},{10,14},{3,7},{... | collective-permute-start | bytes 589832 | tf_op jit(solution)/shard_map/ppermute | solution.py:23
  24.5 0.3 copy-done.10
  25.1 1.6 collective-permute-done.2
  26.7 1.2 collective-permute-done.1
  27.9 0.1 pad_maximum_fusion.18
  28.0 0.5 fusion.8
  28.5 0.1 fusion.58
  28.6 0.1 fusion.57
  28.8 1.0 fusion.54
  29.8 1.2 pad_maximum_fusion.5
  30.9 1.2 pad_maximum_fusion.2
  32.1 1.5 pad_maximum_fusion.7
  33.6 1.6 pad_maximum_fusion.3
  35.2 60.2 %all-gather.5.cloned.1.call-done = bf16[64,162,384]{2,1,0:T(8,128)(2,1)} async-done(((bf16[1,162,384]{2,1,0:T(8,128)(2,1)}), bf16[64,162,384]{2,1,0:T(8,128)(2,1)}) %all-gather.5.cloned.1.call-update) | async-done | bytes 7962640 | tf_op jit(solution)/shard_map/all_gather | solution.py:83
  95.4 9.4 %reshape.187 = bf16[10368,384]{1,0:T(8,128)(2,1)} reshape(bf16[64,162,384]{2,1,0:T(8,128)(2,1)} %all-gather.5.cloned.1.call-done) | data formatting | bytes 15925248
  104.8 2.0 fusion.33
  106.8 2.0 fusion.37
  108.8 2.4 %fusion.27 = f32[384,384]{1,0:T(8,128)S(1)} fusion(bf16[384,1152]{1,0:T(8,128)(2,1)S(1)} %bitcast.73, bf16[10368,384]{1,0:T(8,128)(2,1)} %reshape.187), kind=kOutput, calls=%fused_computation.44 | convolution fusion | flops 339738624 | bytes 2359296 | tf_op jit(solution)/shard_map/dot_general | solution.py:67
  111.2 1.8 convolution_add_fusion.9
  113.1 0.6 convolution_add_fusion.8
  113.7 0.5 copy-done.1
  114.2 0.6 convolution_add_fusion.11
  114.9 0.6 convolution_add_fusion.10
  115.5 0.6 convolution_add_fusion.7
  116.2 0.5 copy-done.3
  116.7 0.8 multiply_reduce_fusion
  117.6 0.3 multiply_convert_fusion
  117.9 2.1 %collective-permute-start.3 = (bf16[2,3,64,384]{3,2,1,0:T(8,128)(2,1)S(1)}, bf16[2,3,64,384]{3,2,1,0:T(8,128)(2,1)S(1)}, u32[]{:S(2)}, u32[]{:S(2)}) collective-permute-start(bf16[2,3,64,384]{3,2,1,0:T(8,128)(2,1)S(1)} %multiply_convert_fusion), channel_id=1, source_target_pairs={{0,16},{16,32},{32,48},{48,64},{64,80},{80,96},{96,112},{112,128},... | collective-permute-start | bytes 884744 | tf_op jit(solution)/shard_map/ppermute | solution.py:12
  120.1 6.8 %collective-permute-done.3 = bf16[2,3,64,384]{3,2,1,0:T(8,128)(2,1)S(1)} collective-permute-done((bf16[2,3,64,384]{3,2,1,0:T(8,128)(2,1)S(1)}, bf16[2,3,64,384]{3,2,1,0:T(8,128)(2,1)S(1)}, u32[]{:S(2)}, u32[]{:S(2)}) %collective-permute-start.3) | collective-permute-done | bytes 294944 | tf_op jit(solution)/shard_map/ppermute | solution.py:12
  126.9 1.3 collective-permute-start.5
  128.2 4.7 %collective-permute-start.4 = (bf16[4,1,64,384]{3,2,1,0:T(8,128)(2,1)S(1)}, bf16[4,1,64,384]{3,2,1,0:T(8,128)(2,1)S(1)}, u32[]{:S(2)}, u32[]{:S(2)}) collective-permute-start(bf16[4,1,64,384]{3,2,1,0:T(8,128)(2,1)S(1)} %get-tuple-element.55), channel_id=1, source_target_pairs={{0,4},{4,8},{8,12},{1,5},{5,9},{9,13},{2,6},{6,10},{10,14},{3,7},{... | collective-permute-start | bytes 589832 | tf_op jit(solution)/shard_map/ppermute | solution.py:23
  133.0 45.2 %all-gather.7.cloned.1.call-done = bf16[64,162,384]{2,1,0:T(8,128)(2,1)} async-done(((bf16[1,162,384]{2,1,0:T(8,128)(2,1)}), bf16[64,162,384]{2,1,0:T(8,128)(2,1)}) %all-gather.7.cloned.1.call-update) | async-done | bytes 7962640 | tf_op jit(solution)/shard_map/all_gather | solution.py:84
  178.2 9.5 %reshape.189 = bf16[10368,384]{1,0:T(8,128)(2,1)} reshape(bf16[64,162,384]{2,1,0:T(8,128)(2,1)} %all-gather.7.cloned.1.call-done) | data formatting | bytes 15925248
  187.7 0.5 select_maximum_fusion
  188.2 1.0 fusion.53
  189.2 0.1 pad_maximum_fusion.19
  189.3 0.1 fusion.56
  189.5 0.1 fusion.55
  189.7 0.2 slice-done
  189.9 1.3 slice-done.1
  191.1 0.6 fusion.13
  191.9 0.6 fusion.19
  192.7 0.6 fusion.23
  193.3 0.4 pad_maximum_fusion.11
  193.7 0.6 convolution_add_fusion.1
  194.5 0.6 convolution_add_fusion
  195.1 0.6 convolution_add_fusion.3
  195.9 0.6 convolution_add_fusion.2
  196.5 0.6 convolution_add_fusion.5
  197.3 0.6 convolution_add_fusion.4
  197.9 0.3 copy-done.4
  198.2 0.2 fusion.47
  198.5 0.7 broadcast_in_dim.17
  199.2 1.3 broadcast_in_dim_reshape.3
  (48 shorter events, 1.4 us)
Async XLA Ops:
  6.5 88.8 %all-gather.5.cloned.1.call-start = ((), (), s32[]{:S(2)}) async-start(), calls=%async_computation | async-start | bytes 8386560 | tf_op jit(solution)/shard_map/all_gather | solution.py:83
  7.3 170.9 %all-gather.7.cloned.1.call-start = ((), (), s32[]{:S(2)}) async-start(), calls=%async_computation.1 | async-start | bytes 8386560 | tf_op jit(solution)/shard_map/all_gather | solution.py:84
  10.3 8.0 %collective-permute-start = (bf16[2,3,64,384]{3,2,1,0:T(8,128)(2,1)S(1)}, bf16[2,3,64,384]{3,2,1,0:T(8,128)(2,1)S(1)}, u32[]{:S(2)}, u32[]{:S(2)}) collective-permute-start(bf16[2,3,64,384]{3,2,1,0:T(8,128)(2,1)S(1)} %fusion.46), channel_id=1, source_target_pairs={{0,16},{16,32},{32,48},{48,64},{64,80},{80,96},{96,112},{112,128},... | collective-permute-start | bytes 884744 | tf_op jit(solution)/shard_map/ppermute | solution.py:12
  18.4 8.3 %collective-permute-start.2 = (bf16[4,1,64,384]{3,2,1,0:T(8,128)(2,1)S(1)}, bf16[4,1,64,384]{3,2,1,0:T(8,128)(2,1)S(1)}, u32[]{:S(2)}, u32[]{:S(2)}) collective-permute-start(bf16[4,1,64,384]{3,2,1,0:T(8,128)(2,1)S(1)} %get-tuple-element.60), channel_id=1, source_target_pairs={{4,0},{8,4},{12,8},{5,1},{9,5},{13,9},{6,2},{10,6},{14,10},{7,3},{... | collective-permute-start | bytes 589832 | tf_op jit(solution)/shard_map/ppermute | solution.py:25
  19.7 8.1 %collective-permute-start.1 = (bf16[4,1,64,384]{3,2,1,0:T(8,128)(2,1)S(1)}, bf16[4,1,64,384]{3,2,1,0:T(8,128)(2,1)S(1)}, u32[]{:S(2)}, u32[]{:S(2)}) collective-permute-start(bf16[4,1,64,384]{3,2,1,0:T(8,128)(2,1)S(1)} %get-tuple-element.59), channel_id=1, source_target_pairs={{0,4},{4,8},{8,12},{1,5},{5,9},{9,13},{2,6},{6,10},{10,14},{3,7},{... | collective-permute-start | bytes 589832 | tf_op jit(solution)/shard_map/ppermute | solution.py:23
  24.3 0.5 copy-start.10
  24.3 4.2 %copy-start.8 = (f32[2]{0:T(128)}, f32[2]{0:T(128)S(1)}, u32[]{:S(2)}) copy-start(f32[2]{0:T(128)S(1)} %get-tuple-element.68) | copy-start | bytes 28
  35.2 69.6 %copy-start.5 = (bf16[2,3,64,1152]{3,2,1,0:T(8,128)(2,1)S(1)}, bf16[2,3,64,1152]{3,2,1,0:T(8,128)(2,1)}, u32[]{:S(2)}) copy-start(bf16[2,3,64,1152]{3,2,1,0:T(8,128)(2,1)} %get-tuple-element.74) | copy-start | bytes 2654212
  104.8 2.0 copy-start.6
  104.8 4.0 %copy-start.7 = (bf16[2,3,64,1152]{3,2,1,0:T(8,128)(2,1)S(1)}, bf16[2,3,64,1152]{3,2,1,0:T(8,128)(2,1)}, u32[]{:S(2)}) copy-start(bf16[2,3,64,1152]{3,2,1,0:T(8,128)(2,1)} %get-tuple-element.76) | copy-start | bytes 2654212
  104.8 6.4 %copy-start.2 = (bf16[2,3,64,1152]{3,2,1,0:T(8,128)(2,1)S(1)}, bf16[2,3,64,1152]{3,2,1,0:T(8,128)(2,1)}, u32[]{:S(2)}) copy-start(bf16[2,3,64,1152]{3,2,1,0:T(8,128)(2,1)} %get-tuple-element.65) | copy-start | bytes 2654212
  106.8 6.2 %copy-start = (bf16[10368,384]{1,0:T(8,128)(2,1)S(1)}, bf16[10368,384]{1,0:T(8,128)(2,1)}, u32[]{:S(2)}) copy-start(bf16[10368,384]{1,0:T(8,128)(2,1)} %reshape.187) | copy-start | bytes 23887876
  113.0 1.2 copy-start.1
  115.5 1.2 copy-start.3
  116.7 0.9 copy-start.9
  116.7 0.9 copy-start.11
  116.7 0.9 copy-start.12
  117.9 9.0 %collective-permute-start.3 = (bf16[2,3,64,384]{3,2,1,0:T(8,128)(2,1)S(1)}, bf16[2,3,64,384]{3,2,1,0:T(8,128)(2,1)S(1)}, u32[]{:S(2)}, u32[]{:S(2)}) collective-permute-start(bf16[2,3,64,384]{3,2,1,0:T(8,128)(2,1)S(1)} %multiply_convert_fusion), channel_id=1, source_target_pairs={{0,16},{16,32},{32,48},{48,64},{64,80},{80,96},{96,112},{112,128},... | collective-permute-start | bytes 884744 | tf_op jit(solution)/shard_map/ppermute | solution.py:12
  126.9 60.7 %collective-permute-start.5 = (bf16[4,1,64,384]{3,2,1,0:T(8,128)(2,1)S(1)}, bf16[4,1,64,384]{3,2,1,0:T(8,128)(2,1)S(1)}, u32[]{:S(2)}, u32[]{:S(2)}) collective-permute-start(bf16[4,1,64,384]{3,2,1,0:T(8,128)(2,1)S(1)} %get-tuple-element.56), channel_id=1, source_target_pairs={{4,0},{8,4},{12,8},{5,1},{9,5},{13,9},{6,2},{10,6},{14,10},{7,3},{... | collective-permute-start | bytes 589832 | tf_op jit(solution)/shard_map/ppermute | solution.py:25
  128.2 59.4 %collective-permute-start.4 = (bf16[4,1,64,384]{3,2,1,0:T(8,128)(2,1)S(1)}, bf16[4,1,64,384]{3,2,1,0:T(8,128)(2,1)S(1)}, u32[]{:S(2)}, u32[]{:S(2)}) collective-permute-start(bf16[4,1,64,384]{3,2,1,0:T(8,128)(2,1)S(1)} %get-tuple-element.55), channel_id=1, source_target_pairs={{0,4},{4,8},{8,12},{1,5},{5,9},{9,13},{2,6},{6,10},{10,14},{3,7},{... | collective-permute-start | bytes 589832 | tf_op jit(solution)/shard_map/ppermute | solution.py:23
  187.7 2.2 %slice-start = ((s8[7962624]{0:T(1024)(128)(4,1)}), s8[4194304]{0:T(1024)(128)(4,1)S(1)}, s32[]{:S(2)}) async-start(s8[7962624]{0:T(1024)(128)(4,1)} %bitcast.51), calls=%async_computation.2 | async-start | bytes 8388608
  188.1 3.0 %slice-start.1 = ((s8[7962624]{0:T(1024)(128)(4,1)}), s8[3768320]{0:T(1024)(128)(4,1)S(1)}, s32[]{:S(2)}) async-start(s8[7962624]{0:T(1024)(128)(4,1)} %bitcast.51), calls=%async_computation.3 | async-start | bytes 7536640
  197.3 1.0 copy-start.4
Sparse Core Ops, SparseCore 0:
  10.1 85.1 all-gather.4
  98.2 79.9 all-gather.6
where the time goes:
time: 210 us; the launch traced here: 207 us
  waiting for transfers between devices  121 us (58%)
  local copies, waits for them, and re-layouts  27.1 us (13%)
  matrix products  17.2 us (8%)
  starting transfers between devices  16 us (8%)
  between operations  13.9 us (7%)
  other arithmetic  12.4 us (6%)
    all_gather x1, waiting for transfers between devices, body(): lax.all_gather(conv_one, ('tm', 'group'), axis=0, tiled=True)  60.2 us
    all_gather x1, waiting for transfers between devices, body(): lax.all_gather(conv_two, ('tm', 'group'), axis=0, tiled=True)  45.2 us
    unnamed x32, local copies, waits for them, and re-layouts  22 us
    dot_general x18, matrix products, causal_conv(): jnp.dot(columns.reshape(-1, 3 * channels), block_w, preferred_element_typ...  17.2 us
    ppermute x2, waiting for transfers between devices, passed_along(): return lax.ppermute(x, axis, pairs)  11.3 us
    ppermute x2, starting transfers between devices, with_halo(): lax.ppermute(tail, axis, [(i, (i + 1) % count) for i in range(ends)])  9.3 us
    concatenate x11, other arithmetic, causal_conv(): jnp.concatenate([padded[time_tap:time_tap + frames, row_tap:row_tap + hei...  6.47 us
  transfers between devices with their start and end apart: 8, of which 6 were waited for; matrix products, arithmetic and copies ran while one was open for 21% of the time, Pallas kernels for 0%

commit v1 on v0

v1 whole, which is shorter than its diff:
```python
import functools
import jax
import jax.numpy as jnp
from jax import lax
from jax.experimental import pallas as pl
from jax.experimental.pallas import tpu as pltpu
from jax.sharding import Mesh, PartitionSpec as P

EPS = 1e-06
SLOT = ("z", "core")
LANE = 128


def video_start(slots, counts):
    starts = jnp.cumsum(counts) - counts
    hit = starts[None, :] <= slots[:, None]
    return jnp.max(jnp.where(hit, starts[None, :], 0), axis=1)


def spread(x, axis):
    n = lax.axis_size(axis)
    return lax.all_to_all(jnp.broadcast_to(x[None], (n,) + x.shape), axis, 0, 0)


def earlier(x):
    n = lax.axis_size(SLOT)
    return lax.ppermute(x, SLOT, [(i, i + 1) for i in range(n - 1)])


def fill_shifted(taps, slot, row, frame_row):
    width, channels = frame_row.shape
    wide = frame_row.astype(jnp.float32)
    col = lax.broadcasted_iota(jnp.int32, (width, channels), 0)
    left = jnp.where(col == 0, 0.0, pltpu.roll(wide, 1, 0))
    right = jnp.where(col == width - 1, 0.0, pltpu.roll(wide, width - 1, 0))
    taps[0, slot, row] = left.astype(frame_row.dtype)
    taps[1, slot, row] = frame_row
    taps[2, slot, row] = right.astype(frame_row.dtype)


def clear_border(taps):
    _, slots, rows, width, channels = taps.shape
    blank = jnp.zeros((width, channels), taps.dtype)
    for e in range(3):
        for slot in range(slots):
            taps[e, slot, 0] = blank
            taps[e, slot, rows - 1] = blank


def conv_one_kernel(valid, halo, own, weight, out, taps):
    parts, frames, each, width, channels = own.shape
    rows = parts * each
    clear_border(taps)
    for slot in range(2 * frames):
        source = halo if slot < frames else own
        for row in range(rows):
            fill_shifted(taps, slot, row + 1, source[row // each, slot % frames, row % each])
    for slot in range(2 * frames):
        pairs = [(s, slot - s) for s in range(frames) if 0 <= slot - s < 3]
        total = None
        for b in range(3):
            columns = jnp.concatenate(
                [taps[e, slot, b : b + rows].reshape(rows * width, channels) for e in range(3)], axis=1
            )
            blocks = []
            for _, a in pairs:
                first = (a * 3 + b) * 3 * channels
                blocks.append(weight[first : first + 3 * channels, :])
            packed = blocks[0] if len(blocks) == 1 else jnp.concatenate(blocks, axis=1)
            term = jnp.dot(columns, packed, preferred_element_type=jnp.float32)
            total = term if total is None else total + term
        for i, (s, a) in enumerate(pairs):
            piece = valid[s, a] * total[:, i * LANE : (i + 1) * LANE]
            piece = piece.reshape(rows, width, LANE)
            if a == 0:
                out[s] = piece
            else:
                out[s] = out[s] + piece


def conv_two_kernel(valid, halo, own, weight, out, taps, acc):
    frames, rows, width, lanes = own.shape
    parts = out.shape[0]
    each = rows // parts
    channels = weight.shape[1]
    clear_border(taps)
    for slot in range(2 * frames):
        source = halo if slot < frames else own
        for row in range(rows):
            fill_shifted(taps, slot, row + 1, source[slot % frames, row])
    for s in range(frames):
        for a in range(3):
            slot = s + a
            columns = jnp.concatenate(
                [
                    taps[e, slot, b : b + rows].reshape(rows * width, lanes)
                    for b in range(3)
                    for e in range(3)
                ],
                axis=1,
            )
            block = weight[a * 9 * lanes : (a + 1) * 9 * lanes, :]
            term = valid[s, a] * jnp.dot(columns, block, preferred_element_type=jnp.float32)
            if a == 0:
                acc[...] = term
            else:
                acc[...] = acc[...] + term
        done = acc[...].astype(out.dtype).reshape(parts, each, width, channels)
        for part in range(parts):
            out[part, s] = done[part]


VMEM = pl.BlockSpec(memory_space=pltpu.VMEM)
SMEM = pl.BlockSpec(memory_space=pltpu.SMEM)
PARAMS = pltpu.CompilerParams(vmem_limit_bytes=52 * 1024 * 1024)


def conv_one_call(valid, halo, own, weight):
    parts, frames, each, width, channels = own.shape
    rows = parts * each
    flops = 2 * 6 * rows * width * 9 * channels * LANE
    return pl.pallas_call(
        conv_one_kernel,
        out_shape=jax.ShapeDtypeStruct((frames, rows, width, LANE), jnp.float32),
        in_specs=[SMEM, VMEM, VMEM, VMEM],
        out_specs=VMEM,
        scratch_shapes=[pltpu.VMEM((3, 2 * frames, rows + 2, width, channels), jnp.bfloat16)],
        compiler_params=PARAMS,
        cost_estimate=pl.CostEstimate(flops=flops, bytes_accessed=6_000_000, transcendentals=0),
        name="conv_one",
    )(valid, halo, own, weight)


def conv_two_call(valid, halo, own, weight, parts):
    frames, rows, width, lanes = own.shape
    channels = weight.shape[1]
    flops = 2 * 6 * rows * width * 9 * lanes * channels
    return pl.pallas_call(
        conv_two_kernel,
        out_shape=jax.ShapeDtypeStruct((parts, frames, rows // parts, width, channels), jnp.bfloat16),
        in_specs=[SMEM, VMEM, VMEM, VMEM],
        out_specs=VMEM,
        scratch_shapes=[
            pltpu.VMEM((3, 2 * frames, rows + 2, width, lanes), jnp.bfloat16),
            pltpu.VMEM((rows * width, channels), jnp.float32),
        ],
        compiler_params=PARAMS,
        cost_estimate=pl.CostEstimate(flops=flops, bytes_accessed=6_000_000, transcendentals=0),
        name="conv_two",
    )(valid, halo, own, weight)


def pick(rows, columns, transposed, part, step):
    big = lax.broadcasted_iota(jnp.int32, (rows, columns), 1 if transposed else 0)
    small = lax.broadcasted_iota(jnp.int32, (rows, columns), 0 if transposed else 1)
    return (big == step * small + part).astype(jnp.bfloat16)


def body(latents, frame_counts, gain_one, gain_two, conv_one, conv_two):
    part = lax.axis_index("tile")
    parts = lax.axis_size("tile")
    side = lax.axis_index("group") % 2
    counts = frame_counts.reshape(-1)
    source = latents[0].astype(jnp.float32)
    frames, each, width, channels = source.shape
    share = channels // parts
    shard = conv_one.shape[0]
    rows = parts * each

    with jax.named_scope("weights"):
        take = pick(channels, share, False, part, parts)
        mine_one = jnp.dot(conv_one, take, preferred_element_type=jnp.float32).astype(jnp.bfloat16)
        pairs = [(i, i ^ 1) for i in range(lax.axis_size("group"))]
        other = lax.ppermute(conv_two, "group", pairs)
        couple = jnp.concatenate(
            [jnp.where(side == 0, conv_two, other), jnp.where(side == 0, other, conv_two)], axis=0
        )
        half = shard // 2
        rows_take = pick(half, 2 * shard, True, part, parts)
        mine_two = jnp.dot(rows_take, couple, preferred_element_type=jnp.float32).astype(jnp.bfloat16)
        mine_two = lax.dynamic_slice_in_dim(mine_two, side * (channels // 2), channels // 2, axis=1)
        mine = jnp.concatenate([mine_one[:half], mine_one[half:], mine_two], axis=1)
        everything = lax.all_gather(mine, SLOT + ("group",), axis=0)
        weight_one = jnp.stack([everything[:, :, :share], everything[:, :, share : 2 * share]], axis=1)
        weight_one = weight_one.reshape(-1, share)
        weight_one = jnp.pad(weight_one, ((0, 0), (0, LANE - share)))
        weight_two = everything[:, :, 2 * share :].reshape(-1, 2, half, channels // 2)
        weight_two = jnp.swapaxes(weight_two, 1, 2).reshape(-1, share, channels)
        weight_two = jnp.pad(weight_two, ((0, 0), (0, LANE - share), (0, 0))).reshape(-1, channels)

    base = lax.axis_index(SLOT) * frames
    slots = base + jnp.arange(frames, dtype=jnp.int32)
    begins = video_start(slots, counts)
    before = 2 - jnp.arange(3, dtype=jnp.int32)
    valid = (slots[:, None] - before[None, :] >= begins[:, None]).astype(jnp.float32)

    with jax.named_scope("first"):
        mean_sq = jnp.mean(source * source, axis=-1, keepdims=True)
        hidden_one = jax.nn.silu(source * lax.rsqrt(mean_sq + EPS) * gain_one).astype(jnp.bfloat16)
        prior = earlier(hidden_one)
        own_all = spread(hidden_one, "tile")
        prior_all = spread(prior, "tile")
        first = conv_one_call(valid, prior_all, own_all, weight_one)

    with jax.named_scope("second"):
        squares = jnp.sum(first * first, axis=-1)
        squares = jnp.sum(spread(squares, "tile"), axis=0)
        gain_mine = lax.dynamic_index_in_dim(gain_two.reshape(share, parts), part, 1, keepdims=False)
        gain_mine = jnp.pad(gain_mine, (0, LANE - share))
        scale = lax.rsqrt(squares / channels + EPS)
        hidden_two = jax.nn.silu(first * scale[..., None] * gain_mine).astype(jnp.bfloat16)
        prior_two = earlier(hidden_two)
        partial_sums = conv_two_call(valid, prior_two, hidden_two, weight_two, parts)
        arrived = lax.all_to_all(partial_sums, "tile", 0, 0)
        second = jnp.sum(arrived.astype(jnp.float32), axis=0)

    block = (source + second).astype(jnp.bfloat16)
    result = jnp.broadcast_to(
        block[:, :, None, :, None, :], (frames, each, 2, width, 2, channels)
    ).reshape(frames, 2 * each, 2 * width, channels)
    return result[None]


def solution(mesh):
    sizes = mesh.devices.shape
    fine = Mesh(mesh.devices.reshape((sizes[0] // 2, 2) + sizes[1:]), ("z", "core", "tile", "group"))
    in_specs = (
        P("group", SLOT, "tile", None, None),
        P("group", None),
        P(),
        P(),
        P(SLOT + ("group",), None),
        P(SLOT + ("group",), None),
    )
    out_specs = P("group", SLOT, "tile", None, None)
    return jax.shard_map(body, mesh=fine, in_specs=in_specs, out_specs=out_specs, check_vma=False)
```

time: 210 us -> 186 us (0.89)
  waiting for transfers between devices: 121 us -> 75.9 us
  blocking collectives: 0 us -> 19.4 us
  matrix products: 17.2 us -> 0.47 us
  Pallas kernels: 0 us -> 16.2 us
  other arithmetic: 12.4 us -> 4.98 us
  local copies, waits for them, and re-layouts: 27.1 us -> 33.9 us
    all_gather x2 -> x1, waiting for transfers between devices: 105 us -> 54 us  [body(): everything = lax.all_gather(mine, SLOT + ('group',), axis=0)]
    unnamed x32 -> x17, local copies, waits for them, and re-layouts: 22 us -> 1.75 us
    all_to_all x0 -> x1, blocking collectives: none -> 19.4 us  [body(): arrived = lax.all_to_all(partial_sums, 'tile', 0, 0)]
    dot_general x18 -> x2, matrix products: 17.2 us -> 0.47 us  [the longest x1 0.26 us: body(): jnp.dot(rows_take, couple, preferred_element_type=jnp.float32)]
    pallas_call x0 -> x2, Pallas kernels: none -> 16.2 us  [the longest x1 8.32 us: conv_one_call(): pl.pallas_call(conv_one_kernel, out_shape=jax.ShapeDtypeStruct((frames, r...]
    all_to_all x0 -> x3, waiting for transfers between devices: none -> 12.4 us  [spread(): return lax.all_to_all(jnp.broadcast_to(x[None], (n,) + x.shape), axis, 0, 0)]
    all_to_all x0 -> x3, starting transfers between devices: none -> 12.2 us  [spread(): return lax.all_to_all(jnp.broadcast_to(x[None], (n,) + x.shape), axis, 0, 0)]
    reshape x0 -> x4, local copies, waits for them, and re-layouts: none -> 11.9 us  [the longest x2 6.31 us: body(): weight_one = weight_one.reshape(-1, share)]
  transfers between devices with their start and end apart: 8 -> 7, of which waited for: 6 -> 5; matrix products, arithmetic and copies ran while one was open for 21% -> 17% of each run, Pallas kernels for 0% -> 0%
where the time goes in v1:
time: 186 us; the launch traced here: 182 us
  waiting for transfers between devices  75.9 us (41%)
  local copies, waits for them, and re-layouts  33.9 us (18%)
  blocking collectives  19.4 us (10%)
  starting transfers between devices  17.9 us (10%)
  Pallas kernels  16.2 us (9%)
  between operations  13.7 us (7%)
  other arithmetic  4.98 us (3%)
    all_gather x1, waiting for transfers between devices, body(): everything = lax.all_gather(mine, SLOT + ('group',), axis=0)  54 us
    all_to_all x1, blocking collectives, body(): arrived = lax.all_to_all(partial_sums, 'tile', 0, 0)  19.4 us
    all_to_all x3, waiting for transfers between devices, spread(): return lax.all_to_all(jnp.broadcast_to(x[None], (n,) + x.shape), axis, 0, 0)  12.4 us
    all_to_all x3, starting transfers between devices, spread(): return lax.all_to_all(jnp.broadcast_to(x[None], (n,) + x.shape), axis, 0, 0)  12.2 us
    pallas_call x1, Pallas kernels, conv_one_call(): pl.pallas_call(conv_one_kernel, out_shape=jax.ShapeDtypeStruct((frames, r...  8.32 us
    pallas_call x1, Pallas kernels, conv_two_call(): pl.pallas_call(conv_two_kernel, out_shape=jax.ShapeDtypeStruct((parts, fr...  7.86 us
    reshape x2, local copies, waits for them, and re-layouts, body(): weight_one = weight_one.reshape(-1, share)  6.31 us
    ppermute x2, waiting for transfers between devices, earlier(): return lax.ppermute(x, SLOT, [(i, i + 1) for i in range(n - 1)])  5.91 us
  transfers between devices with their start and end apart: 7, of which 5 were waited for; matrix products, arithmetic and copies ran while one was open for 17% of the time, Pallas kernels for 0%

profile of v1, /device:TPU:32, one launch (start us, length us, event | category | flops | bytes accessed | tf_op | source)
XLA Modules:
  0.0 182.4 jit_solution(6158229797105808533)
XLA Ops:
  6.5 0.0 copy-start
  6.5 0.0 copy-start.1
  6.5 0.0 copy-start.4
  6.5 0.0 all-gather.4.cloned.1.call-start
  6.5 1.7 collective-permute-start.1
  8.2 0.0 copy-done
  8.2 0.2 fusion
  8.5 3.6 %collective-permute-done.1 = bf16[162,384]{1,0:T(8,128)(2,1)S(1)} collective-permute-done((bf16[162,384]{1,0:T(8,128)(2,1)}, bf16[162,384]{1,0:T(8,128)(2,1)S(1)}, u32[]{:S(2)}, u32[]{:S(2)}) %collective-permute-start.1) | collective-permute-done | bytes 124448 | tf_op jit(solution)/shard_map/weights/ppermute | solution.py:174
  12.0 0.9 broadcast_select_fusion.1
  13.0 0.3 fusion.21
  13.2 0.1 dynamic-slice_convert_fusion
  13.3 0.7 maximum_bitcast_fusion
  14.0 0.0 all-gather.4.cloned.1.call-update
  14.1 0.0 copy-done.1
  14.1 0.1 fusion.4
  14.2 0.0 copy-done.4
  14.2 0.3 fusion.20
  14.5 1.2 broadcast_in_dim.23
  15.7 0.0 copy-start.6
  15.7 4.4 %all-to-all-start.1 = ((bf16[4,2,3,64,384]{4,3,2,1,0:T(8,128)(2,1)}), bf16[4,2,3,64,384]{4,3,2,1,0:T(8,128)(2,1)S(1)}, u32[]{:S(2)}, u32[]{:S(2)}) async-start(bf16[4,2,3,64,384]{4,3,2,1,0:T(8,128)(2,1)} %broadcast_in_dim.23), calls=%async_computation.1 | async-start | bytes 2359296 | tf_op jit(solution)/shard_map/first/all_to_all | solution.py:22
  20.1 0.3 fusion.11
  20.4 1.9 %collective-permute-start = (bf16[2,3,64,384]{3,2,1,0:T(8,128)(2,1)S(1)}, bf16[2,3,64,384]{3,2,1,0:T(8,128)(2,1)S(1)}, u32[]{:S(2)}, u32[]{:S(2)}) collective-permute-start(bf16[2,3,64,384]{3,2,1,0:T(8,128)(2,1)S(1)} %fusion.11), channel_id=1, source_target_pairs={{0,16},{16,32},{32,48},{48,64},{64,80},{80,96},{96,112},{112,128},... | collective-permute-start | bytes 884744 | tf_op jit(solution)/shard_map/first/ppermute | solution.py:27
  22.3 0.0 copy-done.6
  22.3 0.2 reduce-window_clone.1
  22.5 5.9 %collective-permute-done = bf16[2,3,64,384]{3,2,1,0:T(8,128)(2,1)S(1)} collective-permute-done((bf16[2,3,64,384]{3,2,1,0:T(8,128)(2,1)S(1)}, bf16[2,3,64,384]{3,2,1,0:T(8,128)(2,1)S(1)}, u32[]{:S(2)}, u32[]{:S(2)}) %collective-permute-start) | collective-permute-done | bytes 294944 | tf_op jit(solution)/shard_map/first/ppermute | solution.py:27
  28.4 7.3 %all-to-all-done.1.own = bf16[4,2,3,64,384]{4,3,2,1,0:T(8,128)(2,1)S(1)} async-done(((bf16[4,2,3,64,384]{4,3,2,1,0:T(8,128)(2,1)}), bf16[4,2,3,64,384]{4,3,2,1,0:T(8,128)(2,1)S(1)}, u32[]{:S(2)}, u32[]{:S(2)}) %all-to-all-start.1) | async-done | bytes 1179680 | tf_op jit(solution)/shard_map/first/all_to_all | solution.py:22
  35.7 0.0 copy-start.3
  35.7 1.4 broadcast_in_dim.21
  37.1 0.1 copy-done.3
  37.2 3.5 %all-to-all-start = ((bf16[4,2,3,64,384]{4,3,2,1,0:T(8,128)(2,1)}), bf16[4,2,3,64,384]{4,3,2,1,0:T(8,128)(2,1)S(1)}, u32[]{:S(2)}, u32[]{:S(2)}) async-start(bf16[4,2,3,64,384]{4,3,2,1,0:T(8,128)(2,1)} %broadcast_in_dim.21), calls=%async_computation | async-start | bytes 2359296 | tf_op jit(solution)/shard_map/first/all_to_all | solution.py:22
  40.8 0.2 fusion.27
  41.0 0.1 compare_convert_fusion.valid
  41.0 54.0 %all-gather.4.cloned.1.call-done = bf16[64,81,384]{2,1,0:T(8,128)(2,1)} async-done(((bf16[1,81,384]{2,1,0:T(8,128)(2,1)}), bf16[64,81,384]{2,1,0:T(8,128)(2,1)}) %all-gather.4.cloned.1.call-update) | async-done | bytes 3981328 | tf_op jit(solution)/shard_map/weights/all_gather | solution.py:183
  95.0 2.9 %slice_bitcast_fusion.1 = (bf16[64,1,81,96]{3,2,0,1:T(8,128)(2,1)S(1)}, bf16[64,1,81,96]{3,2,0,1:T(8,128)(2,1)S(1)}) fusion(bf16[64,81,384]{2,1,0:T(8,128)(2,1)} %all-gather.4.cloned.1.call-done), kind=kLoop, calls=%fused_computation.3 | loop fusion | bytes 3981312 | tf_op jit(solution)/shard_map/weights/stack | solution.py:184
  97.9 0.7 pad_maximum_fusion
  98.6 1.8 copy.28
  100.4 4.5 %reshape.69 = bf16[10368,96]{1,0:T(8,128)(2,1)} reshape(bf16[64,2,81,96]{3,2,1,0:T(8,128)(2,1)} %copy.28) | data formatting | bytes 3981312 | tf_op jit(solution)/shard_map/weights/reshape | solution.py:185
  104.9 3.1 %pad.12.weight = bf16[10368,128]{1,0:T(8,128)(2,1)} pad(bf16[10368,96]{1,0:T(8,128)(2,1)} %reshape.69, bf16[]{:T(256)} %constant.67.clone.1), padding=0_0x0_32 | pad | bytes 4644866 | tf_op jit(solution)/shard_map/weights/jit(_pad)/pad | solution.py:186
  108.0 0.0 all-to-all-done.halo
  108.0 8.3 %conv_one.1 = f32[2,12,64,128]{3,2,1,0:T(8,128)S(1)} custom-call(f32[2,3]{1,0:T(2,128)S(1)} %compare_convert_fusion.valid, bf16[4,2,3,64,384]{4,3,2,1,0:T(8,128)(2,1)S(1)} %all-to-all-done.halo, bf16[4,2,3,64,384]{4,3,2,1,0:T(8,128)(2,1)} %copy-done.3, bf16[10368,128]{1,0:T(8,128)(2,1)} %pad.12.weight), custom_call_target="tpu_custom_call" | custom-call | flops 4076863488 | bytes 6000000 | tf_op jit(solution)/shard_map/first/conv_one/pallas_call | solution.py:122
  116.3 0.3 multiply_reduce_fusion
  116.7 0.7 reshape.71
  117.4 4.2 %all-to-all-start.2 = ((f32[4,1,1536]{2,1,0:T(1,128)}), f32[4,1,1536]{2,1,0:T(1,128)S(1)}, u32[]{:S(2)}, u32[]{:S(2)}) async-start(f32[4,1,1536]{2,1,0:T(1,128)} %reshape.71), calls=%async_computation.2 | async-start | bytes 49152 | tf_op jit(solution)/shard_map/second/all_to_all | solution.py:22
  121.6 0.0 copy-done.5
  121.6 0.1 reshape.60
  121.7 0.2 dynamic-slice_reduce_fusion
  121.9 5.1 %all-to-all-done.2 = f32[4,1,1536]{2,1,0:T(1,128)S(1)} async-done(((f32[4,1,1536]{2,1,0:T(1,128)}), f32[4,1,1536]{2,1,0:T(1,128)S(1)}, u32[]{:S(2)}, u32[]{:S(2)}) %all-to-all-start.2) | async-done | bytes 24608 | tf_op jit(solution)/shard_map/second/all_to_all | solution.py:22
  127.0 0.5 broadcast.62
  127.5 0.7 reduce.2
  128.3 0.1 reshape.72
  128.4 0.3 multiply_convert_fusion.own
  128.7 2.1 %collective-permute-start.2 = (bf16[2,12,64,128]{3,2,1,0:T(8,128)(2,1)S(1)}, bf16[2,12,64,128]{3,2,1,0:T(8,128)(2,1)S(1)}, u32[]{:S(2)}, u32[]{:S(2)}) collective-permute-start(bf16[2,12,64,128]{3,2,1,0:T(8,128)(2,1)S(1)} %multiply_convert_fusion.own), channel_id=1, source_target_pairs={{0,16},{16,32},{32,48},{48,64},{64,80},{80,96},{96,112},{112,128},... | collective-permute-start | bytes 1179656 | tf_op jit(solution)/shard_map/second/ppermute | solution.py:27
  130.8 3.4 %slice.24 = bf16[64,81,192]{2,1,0:T(8,128)(2,1)S(1)} slice(bf16[64,81,384]{2,1,0:T(8,128)(2,1)} %all-gather.4.cloned.1.call-done), slice={[0:64], [0:81], [192:384]} | slice | bytes 3981312 | tf_op jit(solution)/shard_map/weights/slice | solution.py:187
  134.2 3.6 %copy.27 = bf16[32,81,2,192]{3,2,1,0:T(2,128)(2,1)} copy(bf16[32,81,2,192]{3,1,2,0:T(8,128)(2,1)S(1)} %bitcast.49) | data formatting | bytes 3981312 | tf_op jit(solution)/shard_map/weights/transpose | solution.py:188
  137.8 5.5 %reshape.62 = bf16[27,96,384]{2,1,0:T(8,128)(2,1)S(1)} reshape(bf16[32,81,2,192]{3,2,1,0:T(2,128)(2,1)} %copy.27) | data formatting | bytes 3981312 | tf_op jit(solution)/shard_map/weights/reshape | solution.py:188
  143.3 2.0 %pad.14 = bf16[27,128,384]{2,1,0:T(8,128)(2,1)} pad(bf16[27,96,384]{2,1,0:T(8,128)(2,1)S(1)} %reshape.62, bf16[]{:T(256)} %constant.67.clone.1), padding=0_0x0_32x0_0 | pad | bytes 4644866 | tf_op jit(solution)/shard_map/weights/jit(_pad)/pad | solution.py:189
  145.3 0.0 collective-permute-done.2.halo
  145.3 7.9 %conv_two.1 = bf16[4,2,3,64,384]{4,3,2,1,0:T(8,128)(2,1)S(1)} custom-call(f32[2,3]{1,0:T(2,128)S(1)} %compare_convert_fusion.valid, bf16[2,12,64,128]{3,2,1,0:T(8,128)(2,1)S(1)} %collective-permute-done.2.halo, bf16[2,12,64,128]{3,2,1,0:T(8,128)(2,1)S(1)} %multiply_convert_fusion.own, bf16[3456,384]{1,0:T(8,128)(2,1)} %bitcast.50), custom_call_target="tpu_custom_call" | custom-call | flops 4076863488 | bytes 6000000 | tf_op jit(solution)/shard_map/second/conv_two/pallas_call | solution.py:138
  153.1 19.4 %all_to_all.20 = bf16[4,2,3,64,384]{4,3,2,1,0:T(8,128)(2,1)S(1)} all-to-all(bf16[4,2,3,64,384]{4,3,2,1,0:T(8,128)(2,1)S(1)} %conv_two.1), channel_id=1, replica_groups=mesh['z'=8,'core'=2,'tile'=4,'group'=4] {'tile'}, dimensions={0} | all-to-all | bytes 2359296 | tf_op jit(solution)/shard_map/second/all_to_all | solution.py:214
  172.6 0.2 convert_reduce_fusion
  172.7 0.8 copy-done.2
  173.5 0.1 fusion.12
  173.6 0.7 broadcast_in_dim.25
  174.3 1.3 broadcast_in_dim_reshape.3
  (15 shorter events, 0.1 us)
Async XLA Ops:
  6.5 1.7 copy-start
  6.5 7.5 %copy-start.1 = (bf16[1,2,3,64,384]{4,3,2,1,0:T(8,128)(2,1)S(1)}, bf16[1,2,3,64,384]{4,3,2,1,0:T(8,128)(2,1)}, u32[]{:S(2)}) copy-start(bf16[1,2,3,64,384]{4,3,2,1,0:T(8,128)(2,1)} %param.6) | copy-start | bytes 884740
  6.5 7.7 %copy-start.4 = (f32[384]{0:T(512)S(1)}, f32[384]{0:T(512)}, u32[]{:S(2)}) copy-start(f32[384]{0:T(512)} %param.8) | copy-start | bytes 4612
  6.5 88.5 %all-gather.4.cloned.1.call-start = ((), (), s32[]{:S(2)}) async-start(), calls=%async_computation.4 | async-start | bytes 4392960 | tf_op jit(solution)/shard_map/weights/all_gather | solution.py:183
  6.5 5.5 %collective-permute-start.1 = (bf16[162,384]{1,0:T(8,128)(2,1)}, bf16[162,384]{1,0:T(8,128)(2,1)S(1)}, u32[]{:S(2)}, u32[]{:S(2)}) collective-permute-start(bf16[162,384]{1,0:T(8,128)(2,1)} %param.11), channel_id=1, source_target_pairs={{0,1},{1,0},{2,3},{3,2},{4,5},{5,4},{6,7},{7,6},{8,9},{9,8},{10,11... | collective-permute-start | bytes 373256 | tf_op jit(solution)/shard_map/weights/ppermute | solution.py:174
  15.7 6.6 %copy-start.6 = (s32[1,4]{1,0:T(1,128)S(1)}, s32[1,4]{1,0:T(1,128)}, u32[]{:S(2)}) copy-start(s32[1,4]{1,0:T(1,128)} %param.7) | copy-start | bytes 52
  15.7 20.1 %all-to-all-start.1 = ((bf16[4,2,3,64,384]{4,3,2,1,0:T(8,128)(2,1)}), bf16[4,2,3,64,384]{4,3,2,1,0:T(8,128)(2,1)S(1)}, u32[]{:S(2)}, u32[]{:S(2)}) async-start(bf16[4,2,3,64,384]{4,3,2,1,0:T(8,128)(2,1)} %broadcast_in_dim.23), calls=%async_computation.1 | async-start | bytes 2359296 | tf_op jit(solution)/shard_map/first/all_to_all | solution.py:22
  20.4 8.0 %collective-permute-start = (bf16[2,3,64,384]{3,2,1,0:T(8,128)(2,1)S(1)}, bf16[2,3,64,384]{3,2,1,0:T(8,128)(2,1)S(1)}, u32[]{:S(2)}, u32[]{:S(2)}) collective-permute-start(bf16[2,3,64,384]{3,2,1,0:T(8,128)(2,1)S(1)} %fusion.11), channel_id=1, source_target_pairs={{0,16},{16,32},{32,48},{48,64},{64,80},{80,96},{96,112},{112,128},... | collective-permute-start | bytes 884744 | tf_op jit(solution)/shard_map/first/ppermute | solution.py:27
  35.7 1.5 copy-start.3
  37.2 70.8 %all-to-all-start = ((bf16[4,2,3,64,384]{4,3,2,1,0:T(8,128)(2,1)}), bf16[4,2,3,64,384]{4,3,2,1,0:T(8,128)(2,1)S(1)}, u32[]{:S(2)}, u32[]{:S(2)}) async-start(bf16[4,2,3,64,384]{4,3,2,1,0:T(8,128)(2,1)} %broadcast_in_dim.21), calls=%async_computation | async-start | bytes 2359296 | tf_op jit(solution)/shard_map/first/all_to_all | solution.py:22
  108.0 13.6 %copy-start.5 = (f32[384]{0:T(512)S(1)}, f32[384]{0:T(512)}, u32[]{:S(2)}) copy-start(f32[384]{0:T(512)} %param.9) | copy-start | bytes 4612
  117.4 9.7 %all-to-all-start.2 = ((f32[4,1,1536]{2,1,0:T(1,128)}), f32[4,1,1536]{2,1,0:T(1,128)S(1)}, u32[]{:S(2)}, u32[]{:S(2)}) async-start(f32[4,1,1536]{2,1,0:T(1,128)} %reshape.71), calls=%async_computation.2 | async-start | bytes 49152 | tf_op jit(solution)/shard_map/second/all_to_all | solution.py:22
  128.7 16.5 %collective-permute-start.2 = (bf16[2,12,64,128]{3,2,1,0:T(8,128)(2,1)S(1)}, bf16[2,12,64,128]{3,2,1,0:T(8,128)(2,1)S(1)}, u32[]{:S(2)}, u32[]{:S(2)}) collective-permute-start(bf16[2,12,64,128]{3,2,1,0:T(8,128)(2,1)S(1)} %multiply_convert_fusion.own), channel_id=1, source_target_pairs={{0,16},{16,32},{32,48},{48,64},{64,80},{80,96},{96,112},{112,128},... | collective-permute-start | bytes 1179656 | tf_op jit(solution)/shard_map/second/ppermute | solution.py:27
  172.6 1.0 copy-start.2
Sparse Core Ops, SparseCore 0:
  14.2 80.7 all-gather.3

commit v2 on v1

--- a/solution.py
+++ b/solution.py
@@ -47,7 +47,7 @@
             taps[e, slot, rows - 1] = blank
 
 
-def conv_one_kernel(valid, halo, own, weight, out, taps):
+def conv_one_kernel(share, valid, halo, own, weight, out, taps):
     parts, frames, each, width, channels = own.shape
     rows = parts * each
     clear_border(taps)
@@ -71,7 +71,8 @@
             total = term if total is None else total + term
         for i, (s, a) in enumerate(pairs):
             piece = valid[s, a] * total[:, i * LANE : (i + 1) * LANE]
-            piece = piece.reshape(rows, width, LANE)
+            lane = lax.broadcasted_iota(jnp.int32, piece.shape, 1)
+            piece = jnp.where(lane < share, piece, 0.0).reshape(rows, width, LANE)
             if a == 0:
                 out[s] = piece
             else:
@@ -120,7 +121,7 @@
     rows = parts * each
     flops = 2 * 6 * rows * width * 9 * channels * LANE
     return pl.pallas_call(
-        conv_one_kernel,
+        functools.partial(conv_one_kernel, channels // parts),
         out_shape=jax.ShapeDtypeStruct((frames, rows, width, LANE), jnp.float32),
         in_specs=[SMEM, VMEM, VMEM, VMEM],
         out_specs=VMEM,
@@ -150,6 +151,70 @@
     )(valid, halo, own, weight)
 
 
+def gathered(core, mine, other, k, c):
+    left, right = mine[k].astype(jnp.float32), other[k].astype(jnp.float32)
+    return jnp.where(core[0] == c, left, right)
+
+
+def assemble_one_kernel(core, mine, other, out, wide):
+    chips, piece_rows, lanes = mine.shape
+    shard = out.shape[0] // (2 * chips)
+    share = lanes // 4
+    for k in range(chips):
+        z, y = k // 4, k % 4
+        for c in range(2):
+            piece = gathered(core, mine, other, k, c)
+            start = shard * (8 * z + 4 * c + y)
+            for j in range(4):
+                rows = min(piece_rows, shard - j * piece_rows)
+                low = (j * share) // LANE * LANE
+                window = piece[:, low : min(low + 2 * LANE, lanes)]
+                shift = j * share - low
+                if shift:
+                    window = pltpu.roll(window, window.shape[1] - shift, 1)
+                first = start + j * piece_rows
+                wide[first : first + rows, :] = window[:rows, :LANE]
+    out[...] = wide[...].astype(out.dtype)
+
+
+def assemble_two_kernel(core, mine, other, out, wide, piece_buf):
+    chips, piece_rows, channels = mine.shape
+    share = piece_rows * 2 - 1
+    taps = out.shape[0] // LANE
+    width = share * chips // taps
+    for t in range(taps):
+        wide[t * LANE + width : (t + 1) * LANE, :] = jnp.zeros((LANE - width, channels), jnp.float32)
+    for k in range(chips):
+        z, y = k // 4, k % 4
+        for c in range(2):
+            i = 8 * z + 4 * c + y
+            first = share * (i // 2) + (piece_rows - 1) * (i % 2)
+            piece = gathered(core, mine, other, k, c)
+            split = min(piece_rows, (first // width + 1) * width - first)
+            at = first // width * LANE + first % width
+            if split == piece_rows:
+                wide[at : at + piece_rows, :] = piece
+            else:
+                piece_buf[0:piece_rows, :] = piece
+                wide[at : at + split, :] = piece_buf[0:split, :]
+                at = (first // width + 1) * LANE
+                wide[at : at + piece_rows - split, :] = piece_buf[split:piece_rows, :]
+    out[...] = wide[...].astype(out.dtype)
+
+
+def assemble_call(kernel, core, mine, other, shape, extra, name):
+    return pl.pallas_call(
+        kernel,
+        out_shape=jax.ShapeDtypeStruct(shape, jnp.bfloat16),
+        in_specs=[SMEM, VMEM, VMEM],
+        out_specs=VMEM,
+        scratch_shapes=[pltpu.VMEM(shape, jnp.float32)] + extra,
+        compiler_params=PARAMS,
+        cost_estimate=pl.CostEstimate(flops=4_000_000, bytes_accessed=5_000_000, transcendentals=0),
+        name=name,
+    )(core, mine, other)
+
+
 def pick(rows, columns, transposed, part, step):
     big = lax.broadcasted_iota(jnp.int32, (rows, columns), 1 if transposed else 0)
     small = lax.broadcasted_iota(jnp.int32, (rows, columns), 0 if transposed else 1)
@@ -160,33 +225,45 @@
     part = lax.axis_index("tile")
     parts = lax.axis_size("tile")
     side = lax.axis_index("group") % 2
+    core = lax.axis_index("core")
     counts = frame_counts.reshape(-1)
     source = latents[0].astype(jnp.float32)
     frames, each, width, channels = source.shape
     share = channels // parts
     shard = conv_one.shape[0]
-    rows = parts * each
-
-    with jax.named_scope("weights"):
+    piece_rows = shard // 4 + 1
+    chips = lax.axis_size("z") * lax.axis_size("group")
+    flag = core.astype(jnp.int32).reshape(1)
+
+    def from_all_chips(piece):
+        mine = spread(piece, ("z", "group"))
+        return mine, lax.ppermute(mine, "core", [(0, 1), (1, 0)])
+
+    with jax.named_scope("weight_one"):
         take = pick(channels, share, False, part, parts)
-        mine_one = jnp.dot(conv_one, take, preferred_element_type=jnp.float32).astype(jnp.bfloat16)
+        piece = jnp.dot(conv_one, take, preferred_element_type=jnp.float32).astype(jnp.bfloat16)
+        piece = jnp.pad(piece, ((0, 4 * piece_rows - shard), (0, 0)))
+        piece = jnp.concatenate([piece[j * piece_rows : (j + 1) * piece_rows] for j in range(4)], axis=1)
+        mine_one, other_one = from_all_chips(piece)
+        weight_one = assemble_call(
+            assemble_one_kernel, flag, mine_one, other_one, (2 * chips * shard, LANE), [], "assemble_one"
+        )
+
+    with jax.named_scope("weight_two"):
+        conv_two, mine_one = lax.optimization_barrier((conv_two, mine_one))
         pairs = [(i, i ^ 1) for i in range(lax.axis_size("group"))]
         other = lax.ppermute(conv_two, "group", pairs)
         couple = jnp.concatenate(
             [jnp.where(side == 0, conv_two, other), jnp.where(side == 0, other, conv_two)], axis=0
         )
-        half = shard // 2
-        rows_take = pick(half, 2 * shard, True, part, parts)
-        mine_two = jnp.dot(rows_take, couple, preferred_element_type=jnp.float32).astype(jnp.bfloat16)
-        mine_two = lax.dynamic_slice_in_dim(mine_two, side * (channels // 2), channels // 2, axis=1)
-        mine = jnp.concatenate([mine_one[:half], mine_one[half:], mine_two], axis=1)
-        everything = lax.all_gather(mine, SLOT + ("group",), axis=0)
-        weight_one = jnp.stack([everything[:, :, :share], everything[:, :, share : 2 * share]], axis=1)
-        weight_one = weight_one.reshape(-1, share)
-        weight_one = jnp.pad(weight_one, ((0, 0), (0, LANE - share)))
-        weight_two = everything[:, :, 2 * share :].reshape(-1, 2, half, channels // 2)
-        weight_two = jnp.swapaxes(weight_two, 1, 2).reshape(-1, share, channels)
-        weight_two = jnp.pad(weight_two, ((0, 0), (0, LANE - share), (0, 0))).reshape(-1, channels)
+        rows_take = pick(piece_rows, 2 * shard, True, part + parts * (piece_rows - 1) * side, parts)
+        piece = jnp.dot(rows_take, couple, preferred_element_type=jnp.float32).astype(jnp.bfloat16)
+        mine_two, other_two = from_all_chips(piece)
+        taps = 2 * chips * shard // channels
+        weight_two = assemble_call(
+            assemble_two_kernel, flag, mine_two, other_two, (taps * LANE, channels),
+            [pltpu.VMEM((48, channels), jnp.float32)], "assemble_two"
+        )
 
     base = lax.axis_index(SLOT) * frames
     slots = base + jnp.arange(frames, dtype=jnp.int32)

time: 186 us -> 178 us (0.957); the launches traced: 182 us -> 177 us
  starting transfers between devices: 17.9 us -> 38.3 us
  local copies, waits for them, and re-layouts: 33.9 us -> 16.5 us
  between operations: 13.7 us -> 0.28 us
  Pallas kernels: 16.2 us -> 24.2 us
  waiting for transfers between devices: 75.9 us -> 72.6 us
    all_gather x1 -> x0, waiting for transfers between devices: 54 us -> none  [body(): everything = lax.all_gather(mine, SLOT + ('group',), axis=0)]
    all_to_all x3 -> x5, waiting for transfers between devices: 12.4 us -> 40.5 us  [spread(): return lax.all_to_all(jnp.broadcast_to(x[None], (n,) + x.shape), axis, 0, 0)]
    all_to_all x3 -> x5, starting transfers between devices: 12.2 us -> 32.9 us  [spread(): return lax.all_to_all(jnp.broadcast_to(x[None], (n,) + x.shape), axis, 0, 0)]
    ppermute x2, waiting for transfers between devices: 5.91 us -> 26.1 us  [earlier(): return lax.ppermute(x, SLOT, [(i, i + 1) for i in range(n - 1)])]
    reshape x3 -> x0, local copies, waits for them, and re-layouts: 11.8 us -> none  [the longest x2 6.31 us: body(): weight_one = weight_one.reshape(-1, share)]
    pallas_call x1 -> x3, Pallas kernels: 8.32 us -> 16.4 us  [the longest x1 8.28 us: conv_one_call(): pl.pallas_call(functools.partial(conv_one_kernel, channels // parts), out...]
    ppermute x0 -> x2, local copies, waits for them, and re-layouts: none -> 5.21 us  [from_all_chips(): return (mine, lax.ppermute(mine, 'core', [(0, 1), (1, 0)]))]
    pad x2 -> x0, local copies, waits for them, and re-layouts: 5.09 us -> none  [the longest x1 3.13 us: body(): weight_one = jnp.pad(weight_one, ((0, 0), (0, LANE - share)))]
  transfers between devices with their start and end apart: 7 -> 10, of which waited for: 5 -> 9; matrix products, arithmetic and copies ran while one was open for 17% -> 6% of each run, Pallas kernels for 0% -> 9%
where the time goes in v2:
time: 178 us; the launch traced here: 177 us
  waiting for transfers between devices  72.6 us (41%)
  starting transfers between devices  38.3 us (22%)
  Pallas kernels  24.2 us (14%)
  blocking collectives  19.8 us (11%)
  local copies, waits for them, and re-layouts  16.5 us (9%)
  other arithmetic  4.67 us (3%)
    all_to_all x5, waiting for transfers between devices, spread(): return lax.all_to_all(jnp.broadcast_to(x[None], (n,) + x.shape), axis, 0, 0)  40.5 us
    all_to_all x5, starting transfers between devices, spread(): return lax.all_to_all(jnp.broadcast_to(x[None], (n,) + x.shape), axis, 0, 0)  32.9 us
    ppermute x2, waiting for transfers between devices, earlier(): return lax.ppermute(x, SLOT, [(i, i + 1) for i in range(n - 1)])  26.1 us
    all_to_all x1, blocking collectives, body(): arrived = lax.all_to_all(partial_sums, 'tile', 0, 0)  19.8 us
    pallas_call x1, Pallas kernels, conv_one_call(): pl.pallas_call(functools.partial(conv_one_kernel, channels // parts), out...  8.28 us
    pallas_call x2, Pallas kernels, assemble_call(): pl.pallas_call(kernel, out_shape=jax.ShapeDtypeStruct(shape, jnp.bfloat16...  8.08 us
    pallas_call x1, Pallas kernels, conv_two_call(): pl.pallas_call(conv_two_kernel, out_shape=jax.ShapeDtypeStruct((parts, fr...  7.83 us
    ppermute x2, local copies, waits for them, and re-layouts, from_all_chips(): return (mine, lax.ppermute(mine, 'core', [(0, 1), (1, 0)]))  5.21 us
  transfers between devices with their start and end apart: 10, of which 9 were waited for; matrix products, arithmetic and copies ran while one was open for 6% of the time, Pallas kernels for 9%

profile of v2, /device:TPU:32, one launch (start us, length us, event | category | flops | bytes accessed | tf_op | source)
XLA Modules:
  0.0 176.7 jit_solution(11947921196578602898)
XLA Ops:
  0.0 0.0 copy-start
  0.0 1.1 fusion.4
  1.1 1.2 fusion.20
  2.4 1.2 broadcast_in_dim.27
  3.6 4.3 %all-to-all-start.1 = ((bf16[4,2,3,64,384]{4,3,2,1,0:T(8,128)(2,1)}), bf16[4,2,3,64,384]{4,3,2,1,0:T(8,128)(2,1)S(1)}, u32[]{:S(2)}, u32[]{:S(2)}) async-start(bf16[4,2,3,64,384]{4,3,2,1,0:T(8,128)(2,1)} %broadcast_in_dim.27), calls=%async_computation.1 | async-start | bytes 2359296 | tf_op jit(solution)/shard_map/first/all_to_all | solution.py:22
  7.9 0.0 copy-done
  7.9 0.2 fusion
  8.1 0.1 pad_maximum_fusion
  8.2 16.2 %all-to-all-done.1.own = bf16[4,2,3,64,384]{4,3,2,1,0:T(8,128)(2,1)S(1)} async-done(((bf16[4,2,3,64,384]{4,3,2,1,0:T(8,128)(2,1)}), bf16[4,2,3,64,384]{4,3,2,1,0:T(8,128)(2,1)S(1)}, u32[]{:S(2)}, u32[]{:S(2)}) %all-to-all-start.1) | async-done | bytes 1179680 | tf_op jit(solution)/shard_map/first/all_to_all | solution.py:22
  24.4 1.2 broadcast_in_dim.28
  25.6 0.2 copy-done.4
  25.8 11.4 %all-to-all-start.2 = ((bf16[32,41,384]{2,1,0:T(8,128)(2,1)}), bf16[32,41,384]{2,1,0:T(8,128)(2,1)S(1)}, u32[]{:S(2)}, u32[]{:S(2)}) async-start(bf16[32,41,384]{2,1,0:T(8,128)(2,1)} %broadcast_in_dim.28), calls=%async_computation.2 | async-start | bytes 2359296 | tf_op jit(solution)/shard_map/weight_one/all_to_all | solution.py:22
  37.2 0.0 copy-done.3
  37.2 0.0 copy-done.6
  37.2 0.3 fusion.11
  37.4 1.9 %collective-permute-start = (bf16[2,3,64,384]{3,2,1,0:T(8,128)(2,1)S(1)}, bf16[2,3,64,384]{3,2,1,0:T(8,128)(2,1)S(1)}, u32[]{:S(2)}, u32[]{:S(2)}) collective-permute-start(bf16[2,3,64,384]{3,2,1,0:T(8,128)(2,1)S(1)} %fusion.11), channel_id=1, source_target_pairs={{0,16},{16,32},{32,48},{48,64},{64,80},{80,96},{96,112},{112,128},... | collective-permute-start | bytes 884744 | tf_op jit(solution)/shard_map/first/ppermute | solution.py:27
  39.4 25.3 %collective-permute-done = bf16[2,3,64,384]{3,2,1,0:T(8,128)(2,1)S(1)} collective-permute-done((bf16[2,3,64,384]{3,2,1,0:T(8,128)(2,1)S(1)}, bf16[2,3,64,384]{3,2,1,0:T(8,128)(2,1)S(1)}, u32[]{:S(2)}, u32[]{:S(2)}) %collective-permute-start) | collective-permute-done | bytes 294944 | tf_op jit(solution)/shard_map/first/ppermute | solution.py:27
  64.6 1.4 all-to-all-done.2.mine
  66.0 1.2 broadcast_in_dim.25
  67.2 3.7 %all-to-all-start = ((bf16[4,2,3,64,384]{4,3,2,1,0:T(8,128)(2,1)}), bf16[4,2,3,64,384]{4,3,2,1,0:T(8,128)(2,1)S(1)}, u32[]{:S(2)}, u32[]{:S(2)}) async-start(bf16[4,2,3,64,384]{4,3,2,1,0:T(8,128)(2,1)} %broadcast_in_dim.25), calls=%async_computation | async-start | bytes 2359296 | tf_op jit(solution)/shard_map/first/all_to_all | solution.py:22
  70.9 0.0 copy-done.5
  70.9 1.5 collective-permute-start.3
  72.4 3.5 %collective-permute-done.3 = bf16[162,384]{1,0:T(8,128)(2,1)S(1)} collective-permute-done((bf16[162,384]{1,0:T(8,128)(2,1)S(1)}, bf16[162,384]{1,0:T(8,128)(2,1)S(1)}, u32[]{:S(2)}, u32[]{:S(2)}) %collective-permute-start.3) | collective-permute-done | bytes 124448 | tf_op jit(solution)/shard_map/weight_two/ppermute | solution.py:255
  75.9 0.2 convolution_convert_fusion.1
  76.2 9.3 %all-to-all-done.halo = bf16[4,2,3,64,384]{4,3,2,1,0:T(8,128)(2,1)S(1)} async-done(((bf16[4,2,3,64,384]{4,3,2,1,0:T(8,128)(2,1)}), bf16[4,2,3,64,384]{4,3,2,1,0:T(8,128)(2,1)S(1)}, u32[]{:S(2)}, u32[]{:S(2)}) %all-to-all-start) | async-done | bytes 1179680 | tf_op jit(solution)/shard_map/first/all_to_all | solution.py:22
  85.5 1.3 broadcast_in_dim.30
  86.8 0.1 copy-done.1
  86.9 10.3 %all-to-all-start.4 = ((bf16[32,41,384]{2,1,0:T(8,128)(2,1)}), bf16[32,41,384]{2,1,0:T(8,128)(2,1)S(1)}, u32[]{:S(2)}, u32[]{:S(2)}) async-start(bf16[32,41,384]{2,1,0:T(8,128)(2,1)} %broadcast_in_dim.30), calls=%async_computation.4 | async-start | bytes 2359296 | tf_op jit(solution)/shard_map/weight_two/all_to_all | solution.py:22
  97.2 0.0 copy-start.8
  97.3 1.2 copy.17
  98.5 0.0 collective-permute-start.1
  98.5 0.0 copy-done.8
  98.5 0.2 reduce-window_clone.1
  98.7 0.2 fusion.26
  98.9 0.1 compare_convert_fusion.valid
  98.9 2.5 %collective-permute-done.1 = bf16[32,41,384]{2,0,1:T(8,128)(2,1)} collective-permute-done((bf16[32,41,384]{2,0,1:T(8,128)(2,1)}, bf16[32,41,384]{2,0,1:T(8,128)(2,1)}, u32[]{:S(2)}, u32[]{:S(2)}) %collective-permute-start.1) | collective-permute-done | bytes 1007648 | tf_op jit(solution)/shard_map/weight_one/ppermute | solution.py:240
  101.4 2.6 %copy.18.other = bf16[32,41,384]{2,1,0:T(8,128)(2,1)} copy(bf16[32,41,384]{2,0,1:T(8,128)(2,1)} %collective-permute-done.1) | data formatting | bytes 2015232 | tf_op jit(solution)/shard_map/weight_one/ppermute | solution.py:240
  104.1 4.4 %assemble_one.1.weight = bf16[10368,128]{1,0:T(8,128)(2,1)} custom-call(s32[1]{0:T(128)} %bitcast.3.core, bf16[32,41,384]{2,1,0:T(8,128)(2,1)S(1)} %all-to-all-done.2.mine, bf16[32,41,384]{2,1,0:T(8,128)(2,1)} %copy.18.other), custom_call_target="tpu_custom_call" | custom-call | flops 4000000 | bytes 5000000 | tf_op jit(solution)/shard_map/weight_one/assemble_one/pallas_call | solution.py:206
  108.4 8.3 %conv_one.1 = f32[2,12,64,128]{3,2,1,0:T(8,128)S(1)} custom-call(f32[2,3]{1,0:T(2,128)S(1)} %compare_convert_fusion.valid, bf16[4,2,3,64,384]{4,3,2,1,0:T(8,128)(2,1)S(1)} %copy-done.2, bf16[4,2,3,64,384]{4,3,2,1,0:T(8,128)(2,1)} %copy-done.4, bf16[10368,128]{1,0:T(8,128)(2,1)} %assemble_one.1.weight), custom_call_target="tpu_custom_call" | custom-call | flops 4076863488 | bytes 6000000 | tf_op jit(solution)/shard_map/first/conv_one/pallas_call | solution.py:123
  116.7 0.3 multiply_reduce_fusion
  117.0 0.0 copy-start.7
  117.0 8.6 %all-to-all-done.4.mine = bf16[32,41,384]{2,1,0:T(8,128)(2,1)S(1)} async-done(((bf16[32,41,384]{2,1,0:T(8,128)(2,1)}), bf16[32,41,384]{2,1,0:T(8,128)(2,1)S(1)}, u32[]{:S(2)}, u32[]{:S(2)}) %all-to-all-start.4) | async-done | bytes 1007648 | tf_op jit(solution)/shard_map/weight_two/all_to_all | solution.py:22
  125.6 1.2 copy.21
  126.8 0.0 collective-permute-start.4
  126.8 0.7 reshape.56
  127.5 3.3 %all-to-all-start.3 = ((f32[4,1,1536]{2,1,0:T(1,128)}), f32[4,1,1536]{2,1,0:T(1,128)S(1)}, u32[]{:S(2)}, u32[]{:S(2)}) async-start(f32[4,1,1536]{2,1,0:T(1,128)} %reshape.56), calls=%async_computation.3 | async-start | bytes 49152 | tf_op jit(solution)/shard_map/second/all_to_all | solution.py:22
  130.8 0.1 reshape.53
  130.9 0.2 dynamic-slice_reduce_fusion
  131.1 5.1 %all-to-all-done.3 = f32[4,1,1536]{2,1,0:T(1,128)S(1)} async-done(((f32[4,1,1536]{2,1,0:T(1,128)}), f32[4,1,1536]{2,1,0:T(1,128)S(1)}, u32[]{:S(2)}, u32[]{:S(2)}) %all-to-all-start.3) | async-done | bytes 24608 | tf_op jit(solution)/shard_map/second/all_to_all | solution.py:22
  136.2 0.5 broadcast.62
  136.7 0.6 reduce.2
  137.3 0.1 reshape.57
  137.5 0.3 multiply_convert_fusion.own
  137.8 1.9 %collective-permute-start.2 = (bf16[2,12,64,128]{3,2,1,0:T(8,128)(2,1)S(1)}, bf16[2,12,64,128]{3,2,1,0:T(8,128)(2,1)S(1)}, u32[]{:S(2)}, u32[]{:S(2)}) collective-permute-start(bf16[2,12,64,128]{3,2,1,0:T(8,128)(2,1)S(1)} %multiply_convert_fusion.own), channel_id=1, source_target_pairs={{0,16},{16,32},{32,48},{48,64},{64,80},{80,96},{96,112},{112,128},... | collective-permute-start | bytes 1179656 | tf_op jit(solution)/shard_map/second/ppermute | solution.py:27
  139.7 0.0 collective-permute-done.4
  139.7 2.6 %copy.22.other = bf16[32,41,384]{2,1,0:T(8,128)(2,1)} copy(bf16[32,41,384]{2,0,1:T(8,128)(2,1)} %collective-permute-done.4) | data formatting | bytes 2015232 | tf_op jit(solution)/shard_map/weight_two/ppermute | solution.py:240
  142.3 3.7 %assemble_two.1.weight = bf16[3456,384]{1,0:T(8,128)(2,1)} custom-call(s32[1]{0:T(128)} %bitcast.3.core, bf16[32,41,384]{2,1,0:T(8,128)(2,1)S(1)} %all-to-all-done.4.mine, bf16[32,41,384]{2,1,0:T(8,128)(2,1)} %copy.22.other), custom_call_target="tpu_custom_call" | custom-call | flops 4000000 | bytes 5000000 | tf_op jit(solution)/shard_map/weight_two/assemble_two/pallas_call | solution.py:206
  146.0 0.8 collective-permute-done.2.halo
  146.9 7.8 %conv_two.1 = bf16[4,2,3,64,384]{4,3,2,1,0:T(8,128)(2,1)S(1)} custom-call(f32[2,3]{1,0:T(2,128)S(1)} %compare_convert_fusion.valid, bf16[2,12,64,128]{3,2,1,0:T(8,128)(2,1)S(1)} %collective-permute-done.2.halo, bf16[2,12,64,128]{3,2,1,0:T(8,128)(2,1)S(1)} %multiply_convert_fusion.own, bf16[3456,384]{1,0:T(8,128)(2,1)} %assemble_two.1.weight), custom_call_target="tpu_custom_call" | custom-call | flops 4076863488 | bytes 6000000 | tf_op jit(solution)/shard_map/second/conv_two/pallas_call | solution.py:139
  154.7 19.8 %all_to_all.30 = bf16[4,2,3,64,384]{4,3,2,1,0:T(8,128)(2,1)S(1)} all-to-all(bf16[4,2,3,64,384]{4,3,2,1,0:T(8,128)(2,1)S(1)} %conv_two.1), channel_id=1, replica_groups=mesh['z'=8,'core'=2,'tile'=4,'group'=4] {'tile'}, dimensions={0} | all-to-all | bytes 2359296 | tf_op jit(solution)/shard_map/second/all_to_all | solution.py:291
  174.5 0.2 convert_reduce_fusion
  174.6 0.1 fusion.12
  174.7 0.7 broadcast_in_dim.31
  175.4 1.3 broadcast_in_dim_reshape.3
  (22 shorter events, 0.2 us)
Async XLA Ops:
  0.0 7.9 %copy-start = (bf16[162,384]{1,0:T(8,128)(2,1)S(1)}, bf16[162,384]{1,0:T(8,128)(2,1)}, u32[]{:S(2)}) copy-start(bf16[162,384]{1,0:T(8,128)(2,1)} %param.10) | copy-start | bytes 373252
  3.6 20.8 %all-to-all-start.1 = ((bf16[4,2,3,64,384]{4,3,2,1,0:T(8,128)(2,1)}), bf16[4,2,3,64,384]{4,3,2,1,0:T(8,128)(2,1)S(1)}, u32[]{:S(2)}, u32[]{:S(2)}) async-start(bf16[4,2,3,64,384]{4,3,2,1,0:T(8,128)(2,1)} %broadcast_in_dim.27), calls=%async_computation.1 | async-start | bytes 2359296 | tf_op jit(solution)/shard_map/first/all_to_all | solution.py:22
  24.4 1.4 copy-start.4
  25.6 11.6 %copy-start.3 = (bf16[1,2,3,64,384]{4,3,2,1,0:T(8,128)(2,1)S(1)}, bf16[1,2,3,64,384]{4,3,2,1,0:T(8,128)(2,1)}, u32[]{:S(2)}) copy-start(bf16[1,2,3,64,384]{4,3,2,1,0:T(8,128)(2,1)} %param.6) | copy-start | bytes 884740
  25.6 11.6 %copy-start.6 = (f32[384]{0:T(512)S(1)}, f32[384]{0:T(512)}, u32[]{:S(2)}) copy-start(f32[384]{0:T(512)} %param.8) | copy-start | bytes 4612
  25.8 40.2 %all-to-all-start.2 = ((bf16[32,41,384]{2,1,0:T(8,128)(2,1)}), bf16[32,41,384]{2,1,0:T(8,128)(2,1)S(1)}, u32[]{:S(2)}, u32[]{:S(2)}) async-start(bf16[32,41,384]{2,1,0:T(8,128)(2,1)} %broadcast_in_dim.28), calls=%async_computation.2 | async-start | bytes 2359296 | tf_op jit(solution)/shard_map/weight_one/all_to_all | solution.py:22
  37.4 27.2 %collective-permute-start = (bf16[2,3,64,384]{3,2,1,0:T(8,128)(2,1)S(1)}, bf16[2,3,64,384]{3,2,1,0:T(8,128)(2,1)S(1)}, u32[]{:S(2)}, u32[]{:S(2)}) collective-permute-start(bf16[2,3,64,384]{3,2,1,0:T(8,128)(2,1)S(1)} %fusion.11), channel_id=1, source_target_pairs={{0,16},{16,32},{32,48},{48,64},{64,80},{80,96},{96,112},{112,128},... | collective-permute-start | bytes 884744 | tf_op jit(solution)/shard_map/first/ppermute | solution.py:27
  67.2 3.7 %copy-start.5 = (bf16[162,384]{1,0:T(8,128)(2,1)S(1)}, bf16[162,384]{1,0:T(8,128)(2,1)}, u32[]{:S(2)}) copy-start(bf16[162,384]{1,0:T(8,128)(2,1)} %param.11) | copy-start | bytes 373252
  67.2 18.3 %all-to-all-start = ((bf16[4,2,3,64,384]{4,3,2,1,0:T(8,128)(2,1)}), bf16[4,2,3,64,384]{4,3,2,1,0:T(8,128)(2,1)S(1)}, u32[]{:S(2)}, u32[]{:S(2)}) async-start(bf16[4,2,3,64,384]{4,3,2,1,0:T(8,128)(2,1)} %broadcast_in_dim.25), calls=%async_computation | async-start | bytes 2359296 | tf_op jit(solution)/shard_map/first/all_to_all | solution.py:22
  70.9 5.0 %collective-permute-start.3 = (bf16[162,384]{1,0:T(8,128)(2,1)S(1)}, bf16[162,384]{1,0:T(8,128)(2,1)S(1)}, u32[]{:S(2)}, u32[]{:S(2)}) collective-permute-start(bf16[162,384]{1,0:T(8,128)(2,1)S(1)} %copy-done.5), channel_id=1, source_target_pairs={{0,1},{1,0},{2,3},{3,2},{4,5},{5,4},{6,7},{7,6},{8,9},{9,8},{10,11... | collective-permute-start | bytes 373256 | tf_op jit(solution)/shard_map/weight_two/ppermute | solution.py:255
  85.5 1.4 copy-start.1
  86.9 38.7 %all-to-all-start.4 = ((bf16[32,41,384]{2,1,0:T(8,128)(2,1)}), bf16[32,41,384]{2,1,0:T(8,128)(2,1)S(1)}, u32[]{:S(2)}, u32[]{:S(2)}) async-start(bf16[32,41,384]{2,1,0:T(8,128)(2,1)} %broadcast_in_dim.30), calls=%async_computation.4 | async-start | bytes 2359296 | tf_op jit(solution)/shard_map/weight_two/all_to_all | solution.py:22
  97.2 1.2 copy-start.8
  98.5 2.9 %collective-permute-start.1 = (bf16[32,41,384]{2,0,1:T(8,128)(2,1)}, bf16[32,41,384]{2,0,1:T(8,128)(2,1)}, u32[]{:S(2)}, u32[]{:S(2)}) collective-permute-start(bf16[32,41,384]{2,0,1:T(8,128)(2,1)} %copy.17), channel_id=1, source_target_pairs={{0,16},{16,0},{1,17},{17,1},{2,18},{18,2},{3,19},{19,3},{4,20},{20... | collective-permute-start | bytes 3022856 | tf_op jit(solution)/shard_map/weight_one/ppermute | solution.py:240
  104.1 4.4 %copy-start.2 = (bf16[4,2,3,64,384]{4,3,2,1,0:T(8,128)(2,1)S(1)}, bf16[4,2,3,64,384]{4,3,2,1,0:T(8,128)(2,1)}, u32[]{:S(2)}) copy-start(bf16[4,2,3,64,384]{4,3,2,1,0:T(8,128)(2,1)} %copy-done.1) | copy-start | bytes 3538948
  117.0 13.8 %copy-start.7 = (f32[384]{0:T(512)S(1)}, f32[384]{0:T(512)}, u32[]{:S(2)}) copy-start(f32[384]{0:T(512)} %param.9) | copy-start | bytes 4612
  126.8 12.9 %collective-permute-start.4 = (bf16[32,41,384]{2,0,1:T(8,128)(2,1)}, bf16[32,41,384]{2,0,1:T(8,128)(2,1)}, u32[]{:S(2)}, u32[]{:S(2)}) collective-permute-start(bf16[32,41,384]{2,0,1:T(8,128)(2,1)} %copy.21), channel_id=1, source_target_pairs={{0,16},{16,0},{1,17},{17,1},{2,18},{18,2},{3,19},{19,3},{4,20},{20... | collective-permute-start | bytes 3022856 | tf_op jit(solution)/shard_map/weight_two/ppermute | solution.py:240
  127.5 8.6 %all-to-all-start.3 = ((f32[4,1,1536]{2,1,0:T(1,128)}), f32[4,1,1536]{2,1,0:T(1,128)S(1)}, u32[]{:S(2)}, u32[]{:S(2)}) async-start(f32[4,1,1536]{2,1,0:T(1,128)} %reshape.56), calls=%async_computation.3 | async-start | bytes 49152 | tf_op jit(solution)/shard_map/second/all_to_all | solution.py:22
  137.8 9.1 %collective-permute-start.2 = (bf16[2,12,64,128]{3,2,1,0:T(8,128)(2,1)S(1)}, bf16[2,12,64,128]{3,2,1,0:T(8,128)(2,1)S(1)}, u32[]{:S(2)}, u32[]{:S(2)}) collective-permute-start(bf16[2,12,64,128]{3,2,1,0:T(8,128)(2,1)S(1)} %multiply_convert_fusion.own), channel_id=1, source_target_pairs={{0,16},{16,32},{32,48},{48,64},{64,80},{80,96},{96,112},{112,128},... | collective-permute-start | bytes 1179656 | tf_op jit(solution)/shard_map/second/ppermute | solution.py:27

commit v3 on v2

--- a/solution.py
+++ b/solution.py
@@ -9,6 +9,7 @@
 EPS = 1e-06
 SLOT = ("z", "core")
 LANE = 128
+TILE_ROWS = 48
 
 
 def video_start(slots, counts):
@@ -25,6 +26,11 @@
 def earlier(x):
     n = lax.axis_size(SLOT)
     return lax.ppermute(x, SLOT, [(i, i + 1) for i in range(n - 1)])
+
+
+def onward(x, by):
+    n = lax.axis_size("tile")
+    return lax.ppermute(x, "tile", [(i, (i + by) % n) for i in range(n)])
 
 
 def fill_shifted(taps, slot, row, frame_row):
@@ -47,14 +53,16 @@
             taps[e, slot, rows - 1] = blank
 
 
-def conv_one_kernel(share, valid, halo, own, weight, out, taps):
+def conv_one_kernel(share, valid, part, halo, own, weight, out, taps):
     parts, frames, each, width, channels = own.shape
     rows = parts * each
     clear_border(taps)
-    for slot in range(2 * frames):
-        source = halo if slot < frames else own
-        for row in range(rows):
-            fill_shifted(taps, slot, row + 1, source[row // each, slot % frames, row % each])
+    for back in range(parts):
+        top = lax.rem(part[0] + parts - back, parts) * each + 1
+        for slot in range(2 * frames):
+            source = halo if slot < frames else own
+            for j in range(each):
+                fill_shifted(taps, slot, top + j, source[back, slot % frames, j])
     for slot in range(2 * frames):
         pairs = [(s, slot - s) for s in range(frames) if 0 <= slot - s < 3]
         total = None
@@ -79,36 +87,35 @@
                 out[s] = out[s] + piece
 
 
-def conv_two_kernel(valid, halo, own, weight, out, taps, acc):
+def conv_two_kernel(s, valid, part, halo, own, weight, *rest):
+    *outs, taps, acc = rest
     frames, rows, width, lanes = own.shape
-    parts = out.shape[0]
+    parts = len(outs)
     each = rows // parts
     channels = weight.shape[1]
     clear_border(taps)
-    for slot in range(2 * frames):
-        source = halo if slot < frames else own
+    for a in range(3):
+        source = halo if s + a < frames else own
         for row in range(rows):
-            fill_shifted(taps, slot, row + 1, source[slot % frames, row])
-    for s in range(frames):
-        for a in range(3):
-            slot = s + a
-            columns = jnp.concatenate(
-                [
-                    taps[e, slot, b : b + rows].reshape(rows * width, lanes)
-                    for b in range(3)
-                    for e in range(3)
-                ],
-                axis=1,
-            )
-            block = weight[a * 9 * lanes : (a + 1) * 9 * lanes, :]
-            term = valid[s, a] * jnp.dot(columns, block, preferred_element_type=jnp.float32)
-            if a == 0:
-                acc[...] = term
-            else:
-                acc[...] = acc[...] + term
-        done = acc[...].astype(out.dtype).reshape(parts, each, width, channels)
-        for part in range(parts):
-            out[part, s] = done[part]
+            fill_shifted(taps, a, row + 1, source[(s + a) % frames, row])
+    for a in range(3):
+        columns = jnp.concatenate(
+            [
+                taps[e, a, b : b + rows].reshape(rows * width, lanes)
+                for b in range(3)
+                for e in range(3)
+            ],
+            axis=1,
+        )
+        block = weight[a * 9 * lanes : (a + 1) * 9 * lanes, :]
+        term = valid[s, a] * jnp.dot(columns, block, preferred_element_type=jnp.float32)
+        if a == 0:
+            acc[...] = term
+        else:
+            acc[...] = acc[...] + term
+    for d in range(parts):
+        top = pl.multiple_of(lax.rem(part[0] + d, parts) * (each * width), 64)
+        outs[d][...] = acc[pl.ds(top, each * width), :].astype(outs[d].dtype).reshape(each, width, channels)
 
 
 VMEM = pl.BlockSpec(memory_space=pltpu.VMEM)
@@ -116,39 +123,39 @@
 PARAMS = pltpu.CompilerParams(vmem_limit_bytes=52 * 1024 * 1024)
 
 
-def conv_one_call(valid, halo, own, weight):
+def conv_one_call(valid, part, halo, own, weight):
     parts, frames, each, width, channels = own.shape
     rows = parts * each
     flops = 2 * 6 * rows * width * 9 * channels * LANE
     return pl.pallas_call(
         functools.partial(conv_one_kernel, channels // parts),
         out_shape=jax.ShapeDtypeStruct((frames, rows, width, LANE), jnp.float32),
-        in_specs=[SMEM, VMEM, VMEM, VMEM],
+        in_specs=[SMEM, SMEM, VMEM, VMEM, VMEM],
         out_specs=VMEM,
         scratch_shapes=[pltpu.VMEM((3, 2 * frames, rows + 2, width, channels), jnp.bfloat16)],
         compiler_params=PARAMS,
         cost_estimate=pl.CostEstimate(flops=flops, bytes_accessed=6_000_000, transcendentals=0),
         name="conv_one",
-    )(valid, halo, own, weight)
-
-
-def conv_two_call(valid, halo, own, weight, parts):
+    )(valid, part, halo, own, weight)
+
+
+def conv_two_call(slot, valid, part, halo, own, weight, parts):
     frames, rows, width, lanes = own.shape
     channels = weight.shape[1]
-    flops = 2 * 6 * rows * width * 9 * lanes * channels
+    flops = 2 * 3 * rows * width * 9 * lanes * channels
     return pl.pallas_call(
-        conv_two_kernel,
-        out_shape=jax.ShapeDtypeStruct((parts, frames, rows // parts, width, channels), jnp.bfloat16),
-        in_specs=[SMEM, VMEM, VMEM, VMEM],
-        out_specs=VMEM,
+        functools.partial(conv_two_kernel, slot),
+        out_shape=[jax.ShapeDtypeStruct((rows // parts, width, channels), jnp.bfloat16)] * parts,
+        in_specs=[SMEM, SMEM, VMEM, VMEM, VMEM],
+        out_specs=[VMEM] * parts,
         scratch_shapes=[
-            pltpu.VMEM((3, 2 * frames, rows + 2, width, lanes), jnp.bfloat16),
+            pltpu.VMEM((3, 3, rows + 2, width, lanes), jnp.bfloat16),
             pltpu.VMEM((rows * width, channels), jnp.float32),
         ],
         compiler_params=PARAMS,
         cost_estimate=pl.CostEstimate(flops=flops, bytes_accessed=6_000_000, transcendentals=0),
         name="conv_two",
-    )(valid, halo, own, weight)
+    )(valid, part, halo, own, weight)
 
 
 def gathered(core, mine, other, k, c):
@@ -157,11 +164,12 @@
 
 
 def assemble_one_kernel(core, mine, other, out, wide):
-    chips, piece_rows, lanes = mine.shape
+    chips, _, lanes = mine.shape
     shard = out.shape[0] // (2 * chips)
     share = lanes // 4
+    piece_rows = shard // 4 + 1
     for k in range(chips):
-        z, y = k // 4, k % 4
+        y, z = k // 8, k % 8
         for c in range(2):
             piece = gathered(core, mine, other, k, c)
             start = shard * (8 * z + 4 * c + y)
@@ -178,18 +186,19 @@
 
 
 def assemble_two_kernel(core, mine, other, out, wide, piece_buf):
-    chips, piece_rows, channels = mine.shape
-    share = piece_rows * 2 - 1
+    chips, _, channels = mine.shape
     taps = out.shape[0] // LANE
-    width = share * chips // taps
+    width = channels // 4
+    share = taps * width // chips
+    piece_rows = (share + 1) // 2
     for t in range(taps):
         wide[t * LANE + width : (t + 1) * LANE, :] = jnp.zeros((LANE - width, channels), jnp.float32)
     for k in range(chips):
-        z, y = k // 4, k % 4
+        y, z = k // 8, k % 8
         for c in range(2):
             i = 8 * z + 4 * c + y
             first = share * (i // 2) + (piece_rows - 1) * (i % 2)
-            piece = gathered(core, mine, other, k, c)
+            piece = gathered(core, mine, other, k, c)[:piece_rows]
             split = min(piece_rows, (first // width + 1) * width - first)
             at = first // width * LANE + first % width
             if split == piece_rows:
@@ -236,7 +245,7 @@
     flag = core.astype(jnp.int32).reshape(1)
 
     def from_all_chips(piece):
-        mine = spread(piece, ("z", "group"))
+        mine = spread(spread(piece, "z"), "group").reshape(chips, TILE_ROWS, channels)
         return mine, lax.ppermute(mine, "core", [(0, 1), (1, 0)])
 
     with jax.named_scope("weight_one"):
@@ -244,6 +253,7 @@
         piece = jnp.dot(conv_one, take, preferred_element_type=jnp.float32).astype(jnp.bfloat16)
         piece = jnp.pad(piece, ((0, 4 * piece_rows - shard), (0, 0)))
         piece = jnp.concatenate([piece[j * piece_rows : (j + 1) * piece_rows] for j in range(4)], axis=1)
+        piece = jnp.pad(piece, ((0, TILE_ROWS - piece_rows), (0, 0)))
         mine_one, other_one = from_all_chips(piece)
         weight_one = assemble_call(
             assemble_one_kernel, flag, mine_one, other_one, (2 * chips * shard, LANE), [], "assemble_one"
@@ -256,13 +266,13 @@
         couple = jnp.concatenate(
             [jnp.where(side == 0, conv_two, other), jnp.where(side == 0, other, conv_two)], axis=0
         )
-        rows_take = pick(piece_rows, 2 * shard, True, part + parts * (piece_rows - 1) * side, parts)
+        rows_take = pick(TILE_ROWS, 2 * shard, True, part + parts * (piece_rows - 1) * side, parts)
         piece = jnp.dot(rows_take, couple, preferred_element_type=jnp.float32).astype(jnp.bfloat16)
         mine_two, other_two = from_all_chips(piece)
         taps = 2 * chips * shard // channels
         weight_two = assemble_call(
             assemble_two_kernel, flag, mine_two, other_two, (taps * LANE, channels),
-            [pltpu.VMEM((48, channels), jnp.float32)], "assemble_two"
+            [pltpu.VMEM((TILE_ROWS, channels), jnp.float32)], "assemble_two"
         )
 
     base = lax.axis_index(SLOT) * frames
@@ -274,22 +284,25 @@
     with jax.named_scope("first"):
         mean_sq = jnp.mean(source * source, axis=-1, keepdims=True)
         hidden_one = jax.nn.silu(source * lax.rsqrt(mean_sq + EPS) * gain_one).astype(jnp.bfloat16)
-        prior = earlier(hidden_one)
-        own_all = spread(hidden_one, "tile")
-        prior_all = spread(prior, "tile")
-        first = conv_one_call(valid, prior_all, own_all, weight_one)
+        own_all = jnp.stack([hidden_one] + [onward(hidden_one, d) for d in range(1, parts)])
+        prior_all = earlier(own_all)
+        part_ref = part.astype(jnp.int32).reshape(1)
+        first = conv_one_call(valid, part_ref, prior_all, own_all, weight_one)
 
     with jax.named_scope("second"):
         squares = jnp.sum(first * first, axis=-1)
-        squares = jnp.sum(spread(squares, "tile"), axis=0)
+        squares = squares + sum(onward(squares, d) for d in range(1, parts))
         gain_mine = lax.dynamic_index_in_dim(gain_two.reshape(share, parts), part, 1, keepdims=False)
         gain_mine = jnp.pad(gain_mine, (0, LANE - share))
         scale = lax.rsqrt(squares / channels + EPS)
         hidden_two = jax.nn.silu(first * scale[..., None] * gain_mine).astype(jnp.bfloat16)
         prior_two = earlier(hidden_two)
-        partial_sums = conv_two_call(valid, prior_two, hidden_two, weight_two, parts)
-        arrived = lax.all_to_all(partial_sums, "tile", 0, 0)
-        second = jnp.sum(arrived.astype(jnp.float32), axis=0)
+        sums = []
+        for slot in reversed(range(frames)):
+            mine, *rest = conv_two_call(slot, valid, part_ref, prior_two, hidden_two, weight_two, parts)
+            arrived = [onward(r, d) for d, r in enumerate(rest, 1)]
+            sums.append(sum((r.astype(jnp.float32) for r in arrived), mine.astype(jnp.float32)))
+        second = jnp.stack(sums[::-1])
 
     block = (source + second).astype(jnp.bfloat16)
     result = jnp.broadcast_to(

time: 178 us -> 138 us (0.78)
  waiting for transfers between devices: 72.6 us -> 46.2 us
  local copies, waits for them, and re-layouts: 16.5 us -> 6.23 us
  starting transfers between devices: 38.3 us -> 33.4 us
  Pallas kernels: 24.2 us -> 27.9 us
    ppermute x2, waiting for transfers between devices: 26.1 us -> 3.45 us  [earlier(): return lax.ppermute(x, SLOT, [(i, i + 1) for i in range(n - 1)])]
    all_to_all x5 -> x3, starting transfers between devices: 32.9 us -> 13.8 us  [spread(): return lax.all_to_all(jnp.broadcast_to(x[None], (n,) + x.shape), axis, 0, 0)]
    ppermute x0 -> x12, starting transfers between devices: none -> 14.9 us  [onward(): return lax.ppermute(x, 'tile', [(i, (i + by) % n) for i in range(n)])]
    ppermute x0 -> x12, waiting for transfers between devices: none -> 14.7 us  [onward(): return lax.ppermute(x, 'tile', [(i, (i + by) % n) for i in range(n)])]
    all_to_all x5 -> x3, waiting for transfers between devices: 40.5 us -> 28 us  [spread(): return lax.all_to_all(jnp.broadcast_to(x[None], (n,) + x.shape), axis, 0, 0)]
    ppermute x2 -> x0, local copies, waits for them, and re-layouts: 5.21 us -> none  [from_all_chips(): return (mine, lax.ppermute(mine, 'core', [(0, 1), (1, 0)]))]
    ppermute x1, waiting for transfers between devices: 3.51 us -> 0.01 us  [body(): other = lax.ppermute(conv_two, 'group', pairs)]
    all_to_all x3 -> x0, local copies, waits for them, and re-layouts: 2.9 us -> none  [spread(): return lax.all_to_all(jnp.broadcast_to(x[None], (n,) + x.shape), axis, 0, 0)]
  transfers between devices with their start and end apart: 10 -> 20, of which waited for: 9 -> 11; matrix products, arithmetic and copies ran while one was open for 6% -> 4% of each run, Pallas kernels for 9% -> 17%
where the time goes in v3:
time: 138 us; the launch traced here: 137 us
  waiting for transfers between devices  46.2 us (33%)
  starting transfers between devices  33.4 us (24%)
  Pallas kernels  27.9 us (20%)
  blocking collectives  19.5 us (14%)
  local copies, waits for them, and re-layouts  6.23 us (5%)
  other arithmetic  3.22 us (2%)
    all_to_all x3, waiting for transfers between devices, spread(): return lax.all_to_all(jnp.broadcast_to(x[None], (n,) + x.shape), axis, 0, 0)  28 us
    all_to_all x1, blocking collectives, spread(): return lax.all_to_all(jnp.broadcast_to(x[None], (n,) + x.shape), axis, 0, 0)  19.5 us
    ppermute x12, starting transfers between devices, onward(): return lax.ppermute(x, 'tile', [(i, (i + by) % n) for i in range(n)])  14.9 us
    ppermute x12, waiting for transfers between devices, onward(): return lax.ppermute(x, 'tile', [(i, (i + by) % n) for i in range(n)])  14.7 us
    all_to_all x3, starting transfers between devices, spread(): return lax.all_to_all(jnp.broadcast_to(x[None], (n,) + x.shape), axis, 0, 0)  13.8 us
    pallas_call x2, Pallas kernels, conv_two_call(): pl.pallas_call(functools.partial(conv_two_kernel, slot), out_shape=[jax.S...  10.1 us
    pallas_call x1, Pallas kernels, conv_one_call(): pl.pallas_call(functools.partial(conv_one_kernel, channels // parts), out...  9.91 us
    pallas_call x2, Pallas kernels, assemble_call(): pl.pallas_call(kernel, out_shape=jax.ShapeDtypeStruct(shape, jnp.bfloat16...  7.92 us
  transfers between devices with their start and end apart: 20, of which 11 were waited for; matrix products, arithmetic and copies ran while one was open for 4% of the time, Pallas kernels for 17%

profile of v3, /device:TPU:32, one launch (start us, length us, event | category | flops | bytes accessed | tf_op | source)
XLA Modules:
  0.0 137.1 jit_solution(14950077549734290617)
XLA Ops:
  0.0 0.9 copy-done
  0.9 0.2 fusion
  1.1 0.1 fusion.30
  1.3 19.5 %all_to_all.20 = bf16[8,48,384]{2,1,0:T(8,128)(2,1)S(1)} all-to-all(bf16[8,48,384]{2,1,0:T(8,128)(2,1)S(1)} %broadcast_in_dim.17), channel_id=1, replica_groups=mesh['z'=8,'core'=2,'tile'=4,'group'=4] {'z'}, dimensions={0} | all-to-all | bytes 589824 | tf_op jit(solution)/shard_map/weight_one/all_to_all | solution.py:23
  20.8 1.1 broadcast_in_dim.18
  21.9 4.6 %all-to-all-start.1 = ((bf16[4,8,48,384]{3,2,1,0:T(8,128)(2,1)}), bf16[4,8,48,384]{3,2,1,0:T(8,128)(2,1)S(1)}, u32[]{:S(2)}, u32[]{:S(2)}) async-start(bf16[4,8,48,384]{3,2,1,0:T(8,128)(2,1)} %broadcast_in_dim.18), calls=%async_computation.1 | async-start | bytes 2359296 | tf_op jit(solution)/shard_map/weight_one/all_to_all | solution.py:23
  26.5 0.1 fusion.4
  26.6 14.6 %all-to-all-done.1 = bf16[4,8,48,384]{3,2,1,0:T(8,128)(2,1)S(1)} async-done(((bf16[4,8,48,384]{3,2,1,0:T(8,128)(2,1)}), bf16[4,8,48,384]{3,2,1,0:T(8,128)(2,1)S(1)}, u32[]{:S(2)}, u32[]{:S(2)}) %all-to-all-start.1) | async-done | bytes 1179680 | tf_op jit(solution)/shard_map/weight_one/all_to_all | solution.py:23
  41.3 0.8 collective-permute-start.9
  42.1 0.3 fusion.11
  42.3 2.8 %collective-permute-start.2 = (bf16[2,3,64,384]{3,2,1,0:T(8,128)(2,1)S(1)}, bf16[2,3,64,384]{3,2,1,0:T(8,128)(2,1)S(1)}, u32[]{:S(2)}, u32[]{:S(2)}) collective-permute-start(bf16[2,3,64,384]{3,2,1,0:T(8,128)(2,1)S(1)} %fusion.11), channel_id=1, source_target_pairs={{0,12},{4,0},{8,4},{12,8},{1,13},{5,1},{9,5},{13,9},{2,14},{6,2},{... | collective-permute-start | bytes 884744 | tf_op jit(solution)/shard_map/first/ppermute | solution.py:33
  45.2 0.8 collective-permute-start.1
  46.0 0.9 collective-permute-start
  46.9 0.2 convolution_convert_fusion.1
  47.2 0.7 broadcast_in_dim.19
  47.9 5.5 %all-to-all-start.2 = ((bf16[8,48,384]{2,1,0:T(8,128)(2,1)}), bf16[8,48,384]{2,1,0:T(8,128)(2,1)S(1)}, u32[]{:S(2)}, u32[]{:S(2)}) async-start(bf16[8,48,384]{2,1,0:T(8,128)(2,1)} %broadcast_in_dim.19), calls=%async_computation.2 | async-start | bytes 589824 | tf_op jit(solution)/shard_map/weight_two/all_to_all | solution.py:23
  53.4 0.3 fusion.19
  53.7 0.1 collective-permute-start.4
  53.8 2.8 %collective-permute-done = bf16[2,3,64,384]{3,2,1,0:T(8,128)(2,1)S(1)} collective-permute-done((bf16[2,3,64,384]{3,2,1,0:T(8,128)(2,1)S(1)}, bf16[2,3,64,384]{3,2,1,0:T(8,128)(2,1)S(1)}, u32[]{:S(2)}, u32[]{:S(2)}) %collective-permute-start) | collective-permute-done | bytes 294944 | tf_op jit(solution)/shard_map/first/ppermute | solution.py:33
  56.6 1.2 pad_maximum_fusion.own
  57.8 1.9 %collective-permute-start.3 = (bf16[4,2,3,64,384]{4,3,2,1,0:T(8,128)(2,1)}, bf16[4,2,3,64,384]{4,3,2,1,0:T(8,128)(2,1)}, u32[]{:S(2)}, u32[]{:S(2)}) collective-permute-start(bf16[4,2,3,64,384]{4,3,2,1,0:T(8,128)(2,1)} %pad_maximum_fusion.own), channel_id=1, source_target_pairs={{0,16},{16,32},{32,48},{48,64},{64,80},{80,96},{96,112},{112,128},... | collective-permute-start | bytes 3538952 | tf_op jit(solution)/shard_map/first/ppermute | solution.py:28
  59.7 2.6 %all-to-all-done.2 = bf16[8,48,384]{2,1,0:T(8,128)(2,1)S(1)} async-done(((bf16[8,48,384]{2,1,0:T(8,128)(2,1)}), bf16[8,48,384]{2,1,0:T(8,128)(2,1)S(1)}, u32[]{:S(2)}, u32[]{:S(2)}) %all-to-all-start.2) | async-done | bytes 294944 | tf_op jit(solution)/shard_map/weight_two/all_to_all | solution.py:23
  62.3 1.1 broadcast_in_dim.20
  63.4 3.7 %all-to-all-start.3 = ((bf16[4,8,48,384]{3,2,1,0:T(8,128)(2,1)}), bf16[4,8,48,384]{3,2,1,0:T(8,128)(2,1)S(1)}, u32[]{:S(2)}, u32[]{:S(2)}) async-start(bf16[4,8,48,384]{3,2,1,0:T(8,128)(2,1)} %broadcast_in_dim.20), calls=%async_computation.3 | async-start | bytes 2359296 | tf_op jit(solution)/shard_map/weight_two/all_to_all | solution.py:23
  67.1 0.2 reduce-window_clone.1
  67.3 0.2 fusion.32
  67.5 0.1 compare_convert_fusion.valid
  67.5 0.0 collective-permute-done.4.other
  67.5 4.2 %assemble_one.1.weight = bf16[10368,128]{1,0:T(8,128)(2,1)} custom-call(s32[1]{0:T(128)} %bitcast.6.core, bf16[32,48,384]{2,1,0:T(8,128)(2,1)S(1)} %bitcast.45, bf16[32,48,384]{2,1,0:T(8,128)(2,1)} %collective-permute-done.4.other), custom_call_target="tpu_custom_call" | custom-call | flops 4000000 | bytes 5000000 | tf_op jit(solution)/shard_map/weight_one/assemble_one/pallas_call | solution.py:215
  71.7 10.8 %all-to-all-done.3 = bf16[4,8,48,384]{3,2,1,0:T(8,128)(2,1)S(1)} async-done(((bf16[4,8,48,384]{3,2,1,0:T(8,128)(2,1)}), bf16[4,8,48,384]{3,2,1,0:T(8,128)(2,1)S(1)}, u32[]{:S(2)}, u32[]{:S(2)}) %all-to-all-start.3) | async-done | bytes 1179680 | tf_op jit(solution)/shard_map/weight_two/all_to_all | solution.py:23
  82.5 0.0 collective-permute-start.10
  82.5 0.0 collective-permute-done.3.halo
  82.5 9.9 %conv_one.1 = f32[2,12,64,128]{3,2,1,0:T(8,128)S(1)} custom-call(f32[2,3]{1,0:T(2,128)S(1)} %compare_convert_fusion.valid, s32[1]{0:T(128)} %bitcast.2.part, bf16[4,2,3,64,384]{4,3,2,1,0:T(8,128)(2,1)} %collective-permute-done.3.halo, bf16[4,2,3,64,384]{4,3,2,1,0:T(8,128)(2,1)} %pad_maximum_fusion.own, bf16[10368,128]{1,0:T(8,128)(2,1)} %assemble_one.1.weight), custom_call_target="tpu_custom_call" | custom-call | flops 4076863488 | bytes 6000000 | tf_op jit(solution)/shard_map/first/conv_one/pallas_call | solution.py:130
  92.4 0.3 multiply_reduce_fusion
  92.7 0.7 collective-permute-start.7
  93.4 1.4 %collective-permute-start.5 = (f32[2,12,64]{2,1,0:T(8,128)S(1)}, f32[2,12,64]{2,1,0:T(8,128)S(1)}, u32[]{:S(2)}, u32[]{:S(2)}) collective-permute-start(f32[2,12,64]{2,1,0:T(8,128)S(1)} %multiply_reduce_fusion), channel_id=1, source_target_pairs={{0,4},{4,8},{8,12},{12,0},{1,5},{5,9},{9,13},{13,1},{2,6},{6,10},{... | collective-permute-start | bytes 18440 | tf_op jit(solution)/shard_map/second/ppermute | solution.py:33
  94.8 0.3 collective-permute-start.6
  95.1 0.1 reshape.74
  95.2 0.2 dynamic-slice_reduce_fusion
  95.4 1.1 collective-permute-done.7
  96.5 1.9 %collective-permute-done.5 = f32[2,12,64]{2,1,0:T(8,128)S(1)} collective-permute-done((f32[2,12,64]{2,1,0:T(8,128)S(1)}, f32[2,12,64]{2,1,0:T(8,128)S(1)}, u32[]{:S(2)}, u32[]{:S(2)}) %collective-permute-start.5) | collective-permute-done | bytes 6176 | tf_op jit(solution)/shard_map/second/ppermute | solution.py:33
  98.4 1.7 %collective-permute-done.6 = f32[2,12,64]{2,1,0:T(8,128)S(1)} collective-permute-done((f32[2,12,64]{2,1,0:T(8,128)S(1)}, f32[2,12,64]{2,1,0:T(8,128)S(1)}, u32[]{:S(2)}, u32[]{:S(2)}) %collective-permute-start.6) | collective-permute-done | bytes 6176 | tf_op jit(solution)/shard_map/second/ppermute | solution.py:33
  100.1 0.3 multiply_convert_fusion.own
  100.4 1.9 %collective-permute-start.8 = (bf16[2,12,64,128]{3,2,1,0:T(8,128)(2,1)S(1)}, bf16[2,12,64,128]{3,2,1,0:T(8,128)(2,1)S(1)}, u32[]{:S(2)}, u32[]{:S(2)}) collective-permute-start(bf16[2,12,64,128]{3,2,1,0:T(8,128)(2,1)S(1)} %multiply_convert_fusion.own), channel_id=1, source_target_pairs={{0,16},{16,32},{32,48},{48,64},{64,80},{80,96},{96,112},{112,128},... | collective-permute-start | bytes 1179656 | tf_op jit(solution)/shard_map/second/ppermute | solution.py:28
  102.3 3.7 %assemble_two.1.weight = bf16[3456,384]{1,0:T(8,128)(2,1)} custom-call(s32[1]{0:T(128)} %bitcast.6.core, bf16[32,48,384]{2,1,0:T(8,128)(2,1)S(1)} %bitcast.47, bf16[32,48,384]{2,1,0:T(8,128)(2,1)} %collective-permute-done.10.other), custom_call_target="tpu_custom_call" | custom-call | flops 4000000 | bytes 5000000 | tf_op jit(solution)/shard_map/weight_two/assemble_two/pallas_call | solution.py:215
  106.0 3.4 %collective-permute-done.8.halo = bf16[2,12,64,128]{3,2,1,0:T(8,128)(2,1)S(1)} collective-permute-done((bf16[2,12,64,128]{3,2,1,0:T(8,128)(2,1)S(1)}, bf16[2,12,64,128]{3,2,1,0:T(8,128)(2,1)S(1)}, u32[]{:S(2)}, u32[]{:S(2)}) %collective-permute-start.8) | collective-permute-done | bytes 393248 | tf_op jit(solution)/shard_map/second/ppermute | solution.py:28
  109.5 5.1 %conv_two.3 = (bf16[3,64,384]{2,1,0:T(8,128)(2,1)S(1)}, bf16[3,64,384]{2,1,0:T(8,128)(2,1)S(1)}, bf16[3,64,384]{2,1,0:T(8,128)(2,1)S(1)}, bf16[3,64,384]{2,1,0:T(8,128)(2,1)S(1)}) custom-call(f32[2,3]{1,0:T(2,128)S(1)} %compare_convert_fusion.valid, s32[1]{0:T(128)} %bitcast.2.part, bf16[2,12,64,128]{3,2,1,0:T(8,128)(2,1)S(1)} %collective-permute-done.8.halo, ...), custom_call_target="tpu_custom_call" | custom-call | flops 2038431744 | bytes 6000000 | tf_op jit(solution)/shard_map/second/conv_two/pallas_call | solution.py:146
  114.5 2.2 %collective-permute-start.16 = (bf16[3,64,384]{2,1,0:T(8,128)(2,1)S(1)}, bf16[3,64,384]{2,1,0:T(8,128)(2,1)S(1)}, u32[]{:S(2)}, u32[]{:S(2)}) collective-permute-start(bf16[3,64,384]{2,1,0:T(8,128)(2,1)S(1)} %get-tuple-element.22), channel_id=1, source_target_pairs={{0,12},{4,0},{8,4},{12,8},{1,13},{5,1},{9,5},{13,9},{2,14},{6,2},{... | collective-permute-start | bytes 442376 | tf_op jit(solution)/shard_map/second/ppermute | solution.py:33
  116.7 0.2 collective-permute-start.15
  116.9 0.7 collective-permute-start.14
  117.6 5.1 %conv_two.2 = (bf16[3,64,384]{2,1,0:T(8,128)(2,1)S(1)}, bf16[3,64,384]{2,1,0:T(8,128)(2,1)S(1)}, bf16[3,64,384]{2,1,0:T(8,128)(2,1)S(1)}, bf16[3,64,384]{2,1,0:T(8,128)(2,1)S(1)}) custom-call(f32[2,3]{1,0:T(2,128)S(1)} %compare_convert_fusion.valid, s32[1]{0:T(128)} %bitcast.2.part, bf16[2,12,64,128]{3,2,1,0:T(8,128)(2,1)S(1)} %collective-permute-done.8.halo, ...), custom_call_target="tpu_custom_call" | custom-call | flops 2038431744 | bytes 6000000 | tf_op jit(solution)/shard_map/second/conv_two/pallas_call | solution.py:146
  122.7 2.6 %collective-permute-start.13 = (bf16[3,64,384]{2,1,0:T(8,128)(2,1)S(1)}, bf16[3,64,384]{2,1,0:T(8,128)(2,1)S(1)}, u32[]{:S(2)}, u32[]{:S(2)}) collective-permute-start(bf16[3,64,384]{2,1,0:T(8,128)(2,1)S(1)} %get-tuple-element.18), channel_id=1, source_target_pairs={{0,12},{4,0},{8,4},{12,8},{1,13},{5,1},{9,5},{13,9},{2,14},{6,2},{... | collective-permute-start | bytes 442376 | tf_op jit(solution)/shard_map/second/ppermute | solution.py:33
  125.3 2.1 %collective-permute-start.12 = (bf16[3,64,384]{2,1,0:T(8,128)(2,1)S(1)}, bf16[3,64,384]{2,1,0:T(8,128)(2,1)S(1)}, u32[]{:S(2)}, u32[]{:S(2)}) collective-permute-start(bf16[3,64,384]{2,1,0:T(8,128)(2,1)S(1)} %get-tuple-element.17), channel_id=1, source_target_pairs={{0,8},{4,12},{8,0},{12,4},{1,9},{5,13},{9,1},{13,5},{2,10},{6,14},... | collective-permute-start | bytes 442376 | tf_op jit(solution)/shard_map/second/ppermute | solution.py:33
  127.4 0.0 collective-permute-done.16
  127.4 0.2 collective-permute-start.11
  127.6 0.0 collective-permute-done.15
  127.6 0.1 add_bitcast_fusion
  127.6 3.6 %collective-permute-done.13 = bf16[3,64,384]{2,1,0:T(8,128)(2,1)S(1)} collective-permute-done((bf16[3,64,384]{2,1,0:T(8,128)(2,1)S(1)}, bf16[3,64,384]{2,1,0:T(8,128)(2,1)S(1)}, u32[]{:S(2)}, u32[]{:S(2)}) %collective-permute-start.13) | collective-permute-done | bytes 147488 | tf_op jit(solution)/shard_map/second/ppermute | solution.py:33
  131.3 2.1 %collective-permute-done.12 = bf16[3,64,384]{2,1,0:T(8,128)(2,1)S(1)} collective-permute-done((bf16[3,64,384]{2,1,0:T(8,128)(2,1)S(1)}, bf16[3,64,384]{2,1,0:T(8,128)(2,1)S(1)}, u32[]{:S(2)}, u32[]{:S(2)}) %collective-permute-start.12) | collective-permute-done | bytes 147488 | tf_op jit(solution)/shard_map/second/ppermute | solution.py:33
  133.4 1.6 %collective-permute-done.11 = bf16[3,64,384]{2,1,0:T(8,128)(2,1)S(1)} collective-permute-done((bf16[3,64,384]{2,1,0:T(8,128)(2,1)S(1)}, bf16[3,64,384]{2,1,0:T(8,128)(2,1)S(1)}, u32[]{:S(2)}, u32[]{:S(2)}) %collective-permute-start.11) | collective-permute-done | bytes 147488 | tf_op jit(solution)/shard_map/second/ppermute | solution.py:33
  134.9 0.1 add_bitcast_fusion.1
  135.0 0.1 fusion.12
  135.1 0.7 broadcast_in_dim.21
  135.8 1.3 broadcast_in_dim_reshape.3
  (27 shorter events, 0.1 us)
Async XLA Ops:
  0.0 0.9 copy-start
  21.9 4.6 %copy-start.1 = (bf16[1,2,3,64,384]{4,3,2,1,0:T(8,128)(2,1)S(1)}, bf16[1,2,3,64,384]{4,3,2,1,0:T(8,128)(2,1)}, u32[]{:S(2)}) copy-start(bf16[1,2,3,64,384]{4,3,2,1,0:T(8,128)(2,1)} %param.6) | copy-start | bytes 884740
  21.9 19.4 %copy-start.2 = (bf16[162,384]{1,0:T(8,128)(2,1)S(1)}, bf16[162,384]{1,0:T(8,128)(2,1)}, u32[]{:S(2)}) copy-start(bf16[162,384]{1,0:T(8,128)(2,1)} %param.11) | copy-start | bytes 373252
  21.9 20.2 %copy-start.3 = (f32[384]{0:T(512)S(1)}, f32[384]{0:T(512)}, u32[]{:S(2)}) copy-start(f32[384]{0:T(512)} %param.8) | copy-start | bytes 4612
  21.9 19.4 %all-to-all-start.1 = ((bf16[4,8,48,384]{3,2,1,0:T(8,128)(2,1)}), bf16[4,8,48,384]{3,2,1,0:T(8,128)(2,1)S(1)}, u32[]{:S(2)}, u32[]{:S(2)}) async-start(bf16[4,8,48,384]{3,2,1,0:T(8,128)(2,1)} %broadcast_in_dim.18), calls=%async_computation.1 | async-start | bytes 2359296 | tf_op jit(solution)/shard_map/weight_one/all_to_all | solution.py:23
  41.3 5.6 %collective-permute-start.9 = (bf16[162,384]{1,0:T(8,128)(2,1)S(1)}, bf16[162,384]{1,0:T(8,128)(2,1)S(1)}, u32[]{:S(2)}, u32[]{:S(2)}) collective-permute-start(bf16[162,384]{1,0:T(8,128)(2,1)S(1)} %copy-done.2), channel_id=1, source_target_pairs={{0,1},{1,0},{2,3},{3,2},{4,5},{5,4},{6,7},{7,6},{8,9},{9,8},{10,11... | collective-permute-start | bytes 373256 | tf_op jit(solution)/shard_map/weight_two/ppermute | solution.py:265
  42.3 11.4 %collective-permute-start.2 = (bf16[2,3,64,384]{3,2,1,0:T(8,128)(2,1)S(1)}, bf16[2,3,64,384]{3,2,1,0:T(8,128)(2,1)S(1)}, u32[]{:S(2)}, u32[]{:S(2)}) collective-permute-start(bf16[2,3,64,384]{3,2,1,0:T(8,128)(2,1)S(1)} %fusion.11), channel_id=1, source_target_pairs={{0,12},{4,0},{8,4},{12,8},{1,13},{5,1},{9,5},{13,9},{2,14},{6,2},{... | collective-permute-start | bytes 884744 | tf_op jit(solution)/shard_map/first/ppermute | solution.py:33
  45.2 8.6 %collective-permute-start.1 = (bf16[2,3,64,384]{3,2,1,0:T(8,128)(2,1)S(1)}, bf16[2,3,64,384]{3,2,1,0:T(8,128)(2,1)S(1)}, u32[]{:S(2)}, u32[]{:S(2)}) collective-permute-start(bf16[2,3,64,384]{3,2,1,0:T(8,128)(2,1)S(1)} %fusion.11), channel_id=1, source_target_pairs={{0,8},{4,12},{8,0},{12,4},{1,9},{5,13},{9,1},{13,5},{2,10},{6,14},... | collective-permute-start | bytes 884744 | tf_op jit(solution)/shard_map/first/ppermute | solution.py:33
  46.0 10.6 %collective-permute-start = (bf16[2,3,64,384]{3,2,1,0:T(8,128)(2,1)S(1)}, bf16[2,3,64,384]{3,2,1,0:T(8,128)(2,1)S(1)}, u32[]{:S(2)}, u32[]{:S(2)}) collective-permute-start(bf16[2,3,64,384]{3,2,1,0:T(8,128)(2,1)S(1)} %fusion.11), channel_id=1, source_target_pairs={{0,4},{4,8},{8,12},{12,0},{1,5},{5,9},{9,13},{13,1},{2,6},{6,10},{... | collective-permute-start | bytes 884744 | tf_op jit(solution)/shard_map/first/ppermute | solution.py:33
  47.9 14.4 %all-to-all-start.2 = ((bf16[8,48,384]{2,1,0:T(8,128)(2,1)}), bf16[8,48,384]{2,1,0:T(8,128)(2,1)S(1)}, u32[]{:S(2)}, u32[]{:S(2)}) async-start(bf16[8,48,384]{2,1,0:T(8,128)(2,1)} %broadcast_in_dim.19), calls=%async_computation.2 | async-start | bytes 589824 | tf_op jit(solution)/shard_map/weight_two/all_to_all | solution.py:23
  53.7 13.9 %collective-permute-start.4 = (bf16[32,48,384]{2,1,0:T(8,128)(2,1)S(1)}, bf16[32,48,384]{2,1,0:T(8,128)(2,1)}, u32[]{:S(2)}, u32[]{:S(2)}) collective-permute-start(bf16[32,48,384]{2,1,0:T(8,128)(2,1)S(1)} %bitcast.44), channel_id=1, source_target_pairs={{0,16},{16,0},{1,17},{17,1},{2,18},{18,2},{3,19},{19,3},{4,20},{20... | collective-permute-start | bytes 3538952 | tf_op jit(solution)/shard_map/weight_one/ppermute | solution.py:249
  57.8 24.7 %collective-permute-start.3 = (bf16[4,2,3,64,384]{4,3,2,1,0:T(8,128)(2,1)}, bf16[4,2,3,64,384]{4,3,2,1,0:T(8,128)(2,1)}, u32[]{:S(2)}, u32[]{:S(2)}) collective-permute-start(bf16[4,2,3,64,384]{4,3,2,1,0:T(8,128)(2,1)} %pad_maximum_fusion.own), channel_id=1, source_target_pairs={{0,16},{16,32},{32,48},{48,64},{64,80},{80,96},{96,112},{112,128},... | collective-permute-start | bytes 3538952 | tf_op jit(solution)/shard_map/first/ppermute | solution.py:28
  63.4 3.7 %copy-start.5 = (s32[1,4]{1,0:T(1,128)S(1)}, s32[1,4]{1,0:T(1,128)}, u32[]{:S(2)}) copy-start(s32[1,4]{1,0:T(1,128)} %param.7) | copy-start | bytes 52
  63.4 19.1 %all-to-all-start.3 = ((bf16[4,8,48,384]{3,2,1,0:T(8,128)(2,1)}), bf16[4,8,48,384]{3,2,1,0:T(8,128)(2,1)S(1)}, u32[]{:S(2)}, u32[]{:S(2)}) async-start(bf16[4,8,48,384]{3,2,1,0:T(8,128)(2,1)} %broadcast_in_dim.20), calls=%async_computation.3 | async-start | bytes 2359296 | tf_op jit(solution)/shard_map/weight_two/all_to_all | solution.py:23
  82.5 19.8 %collective-permute-start.10 = (bf16[32,48,384]{2,1,0:T(8,128)(2,1)S(1)}, bf16[32,48,384]{2,1,0:T(8,128)(2,1)}, u32[]{:S(2)}, u32[]{:S(2)}) collective-permute-start(bf16[32,48,384]{2,1,0:T(8,128)(2,1)S(1)} %bitcast.46), channel_id=1, source_target_pairs={{0,16},{16,0},{1,17},{17,1},{2,18},{18,2},{3,19},{19,3},{4,20},{20... | collective-permute-start | bytes 3538952 | tf_op jit(solution)/shard_map/weight_two/ppermute | solution.py:249
  82.5 12.6 %copy-start.4 = (f32[384]{0:T(512)S(1)}, f32[384]{0:T(512)}, u32[]{:S(2)}) copy-start(f32[384]{0:T(512)} %param.9) | copy-start | bytes 4612
  92.7 3.8 %collective-permute-start.7 = (f32[2,12,64]{2,1,0:T(8,128)S(1)}, f32[2,12,64]{2,1,0:T(8,128)S(1)}, u32[]{:S(2)}, u32[]{:S(2)}) collective-permute-start(f32[2,12,64]{2,1,0:T(8,128)S(1)} %multiply_reduce_fusion), channel_id=1, source_target_pairs={{0,12},{4,0},{8,4},{12,8},{1,13},{5,1},{9,5},{13,9},{2,14},{6,2},{... | collective-permute-start | bytes 18440 | tf_op jit(solution)/shard_map/second/ppermute | solution.py:33
  93.4 4.9 %collective-permute-start.5 = (f32[2,12,64]{2,1,0:T(8,128)S(1)}, f32[2,12,64]{2,1,0:T(8,128)S(1)}, u32[]{:S(2)}, u32[]{:S(2)}) collective-permute-start(f32[2,12,64]{2,1,0:T(8,128)S(1)} %multiply_reduce_fusion), channel_id=1, source_target_pairs={{0,4},{4,8},{8,12},{12,0},{1,5},{5,9},{9,13},{13,1},{2,6},{6,10},{... | collective-permute-start | bytes 18440 | tf_op jit(solution)/shard_map/second/ppermute | solution.py:33
  94.8 5.2 %collective-permute-start.6 = (f32[2,12,64]{2,1,0:T(8,128)S(1)}, f32[2,12,64]{2,1,0:T(8,128)S(1)}, u32[]{:S(2)}, u32[]{:S(2)}) collective-permute-start(f32[2,12,64]{2,1,0:T(8,128)S(1)} %multiply_reduce_fusion), channel_id=1, source_target_pairs={{0,8},{4,12},{8,0},{12,4},{1,9},{5,13},{9,1},{13,5},{2,10},{6,14},... | collective-permute-start | bytes 18440 | tf_op jit(solution)/shard_map/second/ppermute | solution.py:33
  100.4 9.1 %collective-permute-start.8 = (bf16[2,12,64,128]{3,2,1,0:T(8,128)(2,1)S(1)}, bf16[2,12,64,128]{3,2,1,0:T(8,128)(2,1)S(1)}, u32[]{:S(2)}, u32[]{:S(2)}) collective-permute-start(bf16[2,12,64,128]{3,2,1,0:T(8,128)(2,1)S(1)} %multiply_convert_fusion.own), channel_id=1, source_target_pairs={{0,16},{16,32},{32,48},{48,64},{64,80},{80,96},{96,112},{112,128},... | collective-permute-start | bytes 1179656 | tf_op jit(solution)/shard_map/second/ppermute | solution.py:28
  114.5 12.9 %collective-permute-start.16 = (bf16[3,64,384]{2,1,0:T(8,128)(2,1)S(1)}, bf16[3,64,384]{2,1,0:T(8,128)(2,1)S(1)}, u32[]{:S(2)}, u32[]{:S(2)}) collective-permute-start(bf16[3,64,384]{2,1,0:T(8,128)(2,1)S(1)} %get-tuple-element.22), channel_id=1, source_target_pairs={{0,12},{4,0},{8,4},{12,8},{1,13},{5,1},{9,5},{13,9},{2,14},{6,2},{... | collective-permute-start | bytes 442376 | tf_op jit(solution)/shard_map/second/ppermute | solution.py:33
  116.7 10.9 %collective-permute-start.15 = (bf16[3,64,384]{2,1,0:T(8,128)(2,1)S(1)}, bf16[3,64,384]{2,1,0:T(8,128)(2,1)S(1)}, u32[]{:S(2)}, u32[]{:S(2)}) collective-permute-start(bf16[3,64,384]{2,1,0:T(8,128)(2,1)S(1)} %get-tuple-element.21), channel_id=1, source_target_pairs={{0,8},{4,12},{8,0},{12,4},{1,9},{5,13},{9,1},{13,5},{2,10},{6,14},... | collective-permute-start | bytes 442376 | tf_op jit(solution)/shard_map/second/ppermute | solution.py:33
  116.9 10.7 %collective-permute-start.14 = (bf16[3,64,384]{2,1,0:T(8,128)(2,1)S(1)}, bf16[3,64,384]{2,1,0:T(8,128)(2,1)S(1)}, u32[]{:S(2)}, u32[]{:S(2)}) collective-permute-start(bf16[3,64,384]{2,1,0:T(8,128)(2,1)S(1)} %get-tuple-element.20), channel_id=1, source_target_pairs={{0,4},{4,8},{8,12},{12,0},{1,5},{5,9},{9,13},{13,1},{2,6},{6,10},{... | collective-permute-start | bytes 442376 | tf_op jit(solution)/shard_map/second/ppermute | solution.py:33
  122.7 8.6 %collective-permute-start.13 = (bf16[3,64,384]{2,1,0:T(8,128)(2,1)S(1)}, bf16[3,64,384]{2,1,0:T(8,128)(2,1)S(1)}, u32[]{:S(2)}, u32[]{:S(2)}) collective-permute-start(bf16[3,64,384]{2,1,0:T(8,128)(2,1)S(1)} %get-tuple-element.18), channel_id=1, source_target_pairs={{0,12},{4,0},{8,4},{12,8},{1,13},{5,1},{9,5},{13,9},{2,14},{6,2},{... | collective-permute-start | bytes 442376 | tf_op jit(solution)/shard_map/second/ppermute | solution.py:33
  125.3 8.1 %collective-permute-start.12 = (bf16[3,64,384]{2,1,0:T(8,128)(2,1)S(1)}, bf16[3,64,384]{2,1,0:T(8,128)(2,1)S(1)}, u32[]{:S(2)}, u32[]{:S(2)}) collective-permute-start(bf16[3,64,384]{2,1,0:T(8,128)(2,1)S(1)} %get-tuple-element.17), channel_id=1, source_target_pairs={{0,8},{4,12},{8,0},{12,4},{1,9},{5,13},{9,1},{13,5},{2,10},{6,14},... | collective-permute-start | bytes 442376 | tf_op jit(solution)/shard_map/second/ppermute | solution.py:33
  127.4 7.5 %collective-permute-start.11 = (bf16[3,64,384]{2,1,0:T(8,128)(2,1)S(1)}, bf16[3,64,384]{2,1,0:T(8,128)(2,1)S(1)}, u32[]{:S(2)}, u32[]{:S(2)}) collective-permute-start(bf16[3,64,384]{2,1,0:T(8,128)(2,1)S(1)} %get-tuple-element.16), channel_id=1, source_target_pairs={{0,4},{4,8},{8,12},{12,0},{1,5},{5,9},{9,13},{13,1},{2,6},{6,10},{... | collective-permute-start | bytes 442376 | tf_op jit(solution)/shard_map/second/ppermute | solution.py:33

commit v4 on v3

--- a/solution.py
+++ b/solution.py
@@ -18,19 +18,18 @@
     return jnp.max(jnp.where(hit, starts[None, :], 0), axis=1)
 
 
-def spread(x, axis):
-    n = lax.axis_size(axis)
-    return lax.all_to_all(jnp.broadcast_to(x[None], (n,) + x.shape), axis, 0, 0)
-
-
 def earlier(x):
     n = lax.axis_size(SLOT)
     return lax.ppermute(x, SLOT, [(i, i + 1) for i in range(n - 1)])
 
 
-def onward(x, by):
-    n = lax.axis_size("tile")
-    return lax.ppermute(x, "tile", [(i, (i + by) % n) for i in range(n)])
+def onward(x, by, axis="tile"):
+    n = lax.axis_size(axis)
+    return lax.ppermute(x, axis, [(i, (i + by) % n) for i in range(n)])
+
+
+def from_all(x, axis):
+    return jnp.stack([x] + [onward(x, d, axis) for d in range(1, lax.axis_size(axis))])
 
 
 def fill_shifted(taps, slot, row, frame_row):
@@ -158,60 +157,59 @@
     )(valid, part, halo, own, weight)
 
 
-def gathered(core, mine, other, k, c):
-    left, right = mine[k].astype(jnp.float32), other[k].astype(jnp.float32)
-    return jnp.where(core[0] == c, left, right)
-
-
-def assemble_one_kernel(core, mine, other, out, wide):
-    chips, _, lanes = mine.shape
-    shard = out.shape[0] // (2 * chips)
+def gathered(place, mine, other, i):
+    ys, zs = mine.shape[:2]
+    z, c, y = i // (2 * ys), i // ys % 2, i % ys
+    back_y = lax.rem(place[1] + ys - y, ys)
+    left, right = mine[back_y, z].astype(jnp.float32), other[back_y, z].astype(jnp.float32)
+    return jnp.where(place[0] == c, left, right)
+
+
+def assemble_one_kernel(place, mine, other, out, wide):
+    shards = 2 * mine.shape[0] * mine.shape[1]
+    lanes = mine.shape[3]
+    shard = out.shape[0] // shards
     share = lanes // 4
     piece_rows = shard // 4 + 1
-    for k in range(chips):
-        y, z = k // 8, k % 8
-        for c in range(2):
-            piece = gathered(core, mine, other, k, c)
-            start = shard * (8 * z + 4 * c + y)
-            for j in range(4):
-                rows = min(piece_rows, shard - j * piece_rows)
-                low = (j * share) // LANE * LANE
-                window = piece[:, low : min(low + 2 * LANE, lanes)]
-                shift = j * share - low
-                if shift:
-                    window = pltpu.roll(window, window.shape[1] - shift, 1)
-                first = start + j * piece_rows
-                wide[first : first + rows, :] = window[:rows, :LANE]
+    for i in range(shards):
+        piece = gathered(place, mine, other, i)
+        for j in range(4):
+            rows = min(piece_rows, shard - j * piece_rows)
+            low = (j * share) // LANE * LANE
+            window = piece[:, low : min(low + 2 * LANE, lanes)]
+            shift = j * share - low
+            if shift:
+                window = pltpu.roll(window, window.shape[1] - shift, 1)
+            first = shard * i + j * piece_rows
+            wide[first : first + rows, :] = window[:rows, :LANE]
     out[...] = wide[...].astype(out.dtype)
 
 
-def assemble_two_kernel(core, mine, other, out, wide, piece_buf):
-    chips, _, channels = mine.shape
+def assemble_two_kernel(place, mine, other, out, wide, piece_buf):
+    shards = 2 * mine.shape[0] * mine.shape[1]
+    channels = mine.shape[3]
     taps = out.shape[0] // LANE
     width = channels // 4
-    share = taps * width // chips
+    share = 2 * taps * width // shards
     piece_rows = (share + 1) // 2
     for t in range(taps):
         wide[t * LANE + width : (t + 1) * LANE, :] = jnp.zeros((LANE - width, channels), jnp.float32)
-    for k in range(chips):
-        y, z = k // 8, k % 8
-        for c in range(2):
-            i = 8 * z + 4 * c + y
-            first = share * (i // 2) + (piece_rows - 1) * (i % 2)
-            piece = gathered(core, mine, other, k, c)[:piece_rows]
-            split = min(piece_rows, (first // width + 1) * width - first)
-            at = first // width * LANE + first % width
-            if split == piece_rows:
-                wide[at : at + piece_rows, :] = piece
-            else:
-                piece_buf[0:piece_rows, :] = piece
-                wide[at : at + split, :] = piece_buf[0:split, :]
-                at = (first // width + 1) * LANE
-                wide[at : at + piece_rows - split, :] = piece_buf[split:piece_rows, :]
+    for i in range(shards):
+        first = share * (i // 2) + (piece_rows - 1) * (i % 2)
+        piece = gathered(place, mine, other, i)[:piece_rows]
+        split = min(piece_rows, (first // width + 1) * width - first)
+        at = first // width * LANE + first % width
+        if split == piece_rows:
+            wide[at : at + piece_rows, :] = piece
+        else:
+            piece_buf[0:piece_rows, :] = piece
+            wide[at : at + split, :] = piece_buf[0:split, :]
+            at = (first // width + 1) * LANE
+            wide[at : at + piece_rows - split, :] = piece_buf[split:piece_rows, :]
     out[...] = wide[...].astype(out.dtype)
 
 
-def assemble_call(kernel, core, mine, other, shape, extra, name):
+def assemble_call(kernel, place, mine, other, shape, extra, name):
     return pl.pallas_call(
         kernel,
         out_shape=jax.ShapeDtypeStruct(shape, jnp.bfloat16),
@@ -221,7 +219,7 @@
         compiler_params=PARAMS,
         cost_estimate=pl.CostEstimate(flops=4_000_000, bytes_accessed=5_000_000, transcendentals=0),
         name=name,
-    )(core, mine, other)
+    )(place, mine, other)
 
 
 def pick(rows, columns, transposed, part, step):
@@ -241,39 +239,44 @@
     share = channels // parts
     shard = conv_one.shape[0]
     piece_rows = shard // 4 + 1
-    chips = lax.axis_size("z") * lax.axis_size("group")
-    flag = core.astype(jnp.int32).reshape(1)
-
-    def from_all_chips(piece):
-        mine = spread(spread(piece, "z"), "group").reshape(chips, TILE_ROWS, channels)
-        return mine, lax.ppermute(mine, "core", [(0, 1), (1, 0)])
-
-    with jax.named_scope("weight_one"):
-        take = pick(channels, share, False, part, parts)
-        piece = jnp.dot(conv_one, take, preferred_element_type=jnp.float32).astype(jnp.bfloat16)
-        piece = jnp.pad(piece, ((0, 4 * piece_rows - shard), (0, 0)))
-        piece = jnp.concatenate([piece[j * piece_rows : (j + 1) * piece_rows] for j in range(4)], axis=1)
-        piece = jnp.pad(piece, ((0, TILE_ROWS - piece_rows), (0, 0)))
-        mine_one, other_one = from_all_chips(piece)
-        weight_one = assemble_call(
-            assemble_one_kernel, flag, mine_one, other_one, (2 * chips * shard, LANE), [], "assemble_one"
-        )
-
-    with jax.named_scope("weight_two"):
-        conv_two, mine_one = lax.optimization_barrier((conv_two, mine_one))
+    shards = lax.axis_size(SLOT) * lax.axis_size("group")
+    place = jnp.stack([core, lax.axis_index("group")]).astype(jnp.int32)
+
+    with jax.named_scope("pixels"):
+        mean_sq = jnp.mean(source * source, axis=-1, keepdims=True)
+        hidden_one = jax.nn.silu(source * lax.rsqrt(mean_sq + EPS) * gain_one).astype(jnp.bfloat16)
+        own_all = from_all(hidden_one, "tile")
+
+    with jax.named_scope("pieces"):
         pairs = [(i, i ^ 1) for i in range(lax.axis_size("group"))]
         other = lax.ppermute(conv_two, "group", pairs)
         couple = jnp.concatenate(
             [jnp.where(side == 0, conv_two, other), jnp.where(side == 0, other, conv_two)], axis=0
         )
         rows_take = pick(TILE_ROWS, 2 * shard, True, part + parts * (piece_rows - 1) * side, parts)
-        piece = jnp.dot(rows_take, couple, preferred_element_type=jnp.float32).astype(jnp.bfloat16)
-        mine_two, other_two = from_all_chips(piece)
-        taps = 2 * chips * shard // channels
-        weight_two = assemble_call(
-            assemble_two_kernel, flag, mine_two, other_two, (taps * LANE, channels),
-            [pltpu.VMEM((TILE_ROWS, channels), jnp.float32)], "assemble_two"
+        piece_two = jnp.dot(rows_take, couple, preferred_element_type=jnp.float32).astype(jnp.bfloat16)
+        take = pick(channels, share, False, part, parts)
+        piece = jnp.dot(conv_one, take, preferred_element_type=jnp.float32).astype(jnp.bfloat16)
+        piece = jnp.pad(piece, ((0, 4 * piece_rows - shard), (0, 0)))
+        piece = jnp.concatenate([piece[j * piece_rows : (j + 1) * piece_rows] for j in range(4)], axis=1)
+        piece = jnp.pad(piece, ((0, TILE_ROWS - piece_rows), (0, 0)))
+        pieces = jnp.concatenate([piece, piece_two], axis=0)
+        column = lax.all_to_all(jnp.broadcast_to(pieces, (lax.axis_size("z"),) + pieces.shape), "z", 0, 0)
+
+    column, own_all = lax.optimization_barrier((column, own_all))
+    with jax.named_scope("weight_one"):
+        mine = from_all(column[:, :TILE_ROWS], "group")
+        prior_all = earlier(own_all)
+        mine, prior_all = lax.optimization_barrier((mine, prior_all))
+        swapped = lax.ppermute(mine, "core", [(0, 1), (1, 0)])
+        weight_one = assemble_call(
+            assemble_one_kernel, place, mine, swapped, (shards * shard, LANE), [], "assemble_one"
         )
+
+    with jax.named_scope("weight_two"):
+        column, _ = lax.optimization_barrier((column, mine))
+        later = column[:, TILE_ROWS:]
+        later = [later] + [onward(later, d, "group") for d in range(1, lax.axis_size("group"))]
 
     base = lax.axis_index(SLOT) * frames
     slots = base + jnp.arange(frames, dtype=jnp.int32)
@@ -282,15 +285,21 @@
     valid = (slots[:, None] - before[None, :] >= begins[:, None]).astype(jnp.float32)
 
     with jax.named_scope("first"):
-        mean_sq = jnp.mean(source * source, axis=-1, keepdims=True)
-        hidden_one = jax.nn.silu(source * lax.rsqrt(mean_sq + EPS) * gain_one).astype(jnp.bfloat16)
-        own_all = jnp.stack([hidden_one] + [onward(hidden_one, d) for d in range(1, parts)])
-        prior_all = earlier(own_all)
         part_ref = part.astype(jnp.int32).reshape(1)
         first = conv_one_call(valid, part_ref, prior_all, own_all, weight_one)
 
+    with jax.named_scope("weight_two"):
+        squares = jnp.sum(first * first, axis=-1)
+        squares, later = lax.optimization_barrier((squares, later))
+        mine = jnp.stack(later)
+        swapped = lax.ppermute(mine, "core", [(0, 1), (1, 0)])
+        taps = shards * shard // channels
+        weight_two = assemble_call(
+            assemble_two_kernel, place, mine, swapped, (taps * LANE, channels),
+            [pltpu.VMEM((TILE_ROWS, channels), jnp.float32)], "assemble_two"
+        )
+
     with jax.named_scope("second"):
-        squares = jnp.sum(first * first, axis=-1)
         squares = squares + sum(onward(squares, d) for d in range(1, parts))
         gain_mine = lax.dynamic_index_in_dim(gain_two.reshape(share, parts), part, 1, keepdims=False)
         gain_mine = jnp.pad(gain_mine, (0, LANE - share))

time: 138 us -> 121 us (0.88)
  blocking collectives: 19.5 us -> 0 us
  starting transfers between devices: 33.4 us -> 37.7 us
  local copies, waits for them, and re-layouts: 6.23 us -> 3.54 us
    all_to_all x3 -> x1, waiting for transfers between devices: 28 us -> 0.01 us  [body(): lax.all_to_all(jnp.broadcast_to(pieces, (lax.axis_size('z'),) + pieces.sh...]
    ppermute x14 -> x20, waiting for transfers between devices: 14.7 us -> 39.2 us  [the longest x18 39.2 us: onward(): return lax.ppermute(x, axis, [(i, (i + by) % n) for i in range(n)])]
    all_to_all x1 -> x0, blocking collectives: 19.5 us -> none  [spread(): return lax.all_to_all(jnp.broadcast_to(x[None], (n,) + x.shape), axis, 0, 0)]
    ppermute x14 -> x20, starting transfers between devices: 15 us -> 23.5 us  [the longest x18 23.2 us: onward(): return lax.ppermute(x, axis, [(i, (i + by) % n) for i in range(n)])]
    all_to_all x3 -> x1, starting transfers between devices: 13.8 us -> 8.57 us  [body(): lax.all_to_all(jnp.broadcast_to(pieces, (lax.axis_size('z'),) + pieces.sh...]
    ppermute x1, waiting for transfers between devices: 0.01 us -> 3.47 us  [body(): other = lax.ppermute(conv_two, 'group', pairs)]
    broadcast_in_dim x4 -> x1, local copies, waits for them, and re-layouts: 3.01 us -> 0.87 us  [body(): jnp.broadcast_to(pieces, (lax.axis_size('z'),) + pieces.shape)]
  transfers between devices with their start and end apart: 20 -> 24, of which waited for: 11 -> 13; matrix products, arithmetic and copies ran while one was open for 4% -> 3% of each run, Pallas kernels for 17% -> 19%
where the time goes in v4:
time: 121 us; the launch traced here: 120 us
  waiting for transfers between devices  45.8 us (38%)
  starting transfers between devices  37.7 us (31%)
  Pallas kernels  27.8 us (23%)
  other arithmetic  4.57 us (4%)
  local copies, waits for them, and re-layouts  3.54 us (3%)
    ppermute x18, waiting for transfers between devices, onward(): return lax.ppermute(x, axis, [(i, (i + by) % n) for i in range(n)])  39.2 us
    ppermute x18, starting transfers between devices, onward(): return lax.ppermute(x, axis, [(i, (i + by) % n) for i in range(n)])  23.2 us
    pallas_call x2, Pallas kernels, conv_two_call(): pl.pallas_call(functools.partial(conv_two_kernel, slot), out_shape=[jax.S...  10.1 us
    pallas_call x1, Pallas kernels, conv_one_call(): pl.pallas_call(functools.partial(conv_one_kernel, channels // parts), out...  9.57 us
    all_to_all x1, starting transfers between devices, body(): lax.all_to_all(jnp.broadcast_to(pieces, (lax.axis_size('z'),) + pieces.sh...  8.57 us
    pallas_call x2, Pallas kernels, assemble_call(): pl.pallas_call(kernel, out_shape=jax.ShapeDtypeStruct(shape, jnp.bfloat16...  8.15 us
    ppermute x2, starting transfers between devices, earlier(): return lax.ppermute(x, SLOT, [(i, i + 1) for i in range(n - 1)])  4.05 us
    ppermute x1, waiting for transfers between devices, body(): other = lax.ppermute(conv_two, 'group', pairs)  3.47 us
  transfers between devices with their start and end apart: 24, of which 13 were waited for; matrix products, arithmetic and copies ran while one was open for 3% of the time, Pallas kernels for 19%

profile of v4, /device:TPU:32, one launch (start us, length us, event | category | flops | bytes accessed | tf_op | source)
XLA Modules:
  0.0 120.2 jit_solution(5245373497585089599)
XLA Ops:
  0.0 1.6 %collective-permute-start = (bf16[162,384]{1,0:T(8,128)(2,1)}, bf16[162,384]{1,0:T(8,128)(2,1)S(1)}, u32[]{:S(2)}, u32[]{:S(2)}) collective-permute-start(bf16[162,384]{1,0:T(8,128)(2,1)} %param.11), channel_id=1, source_target_pairs={{0,1},{1,0},{2,3},{3,2},{4,5},{5,4},{6,7},{7,6},{8,9},{9,8},{10,11... | collective-permute-start | bytes 373256 | tf_op jit(solution)/shard_map/pieces/ppermute | solution.py:252
  1.6 0.2 fusion
  1.8 0.1 fusion.30
  1.9 3.5 %collective-permute-done = bf16[162,384]{1,0:T(8,128)(2,1)S(1)} collective-permute-done((bf16[162,384]{1,0:T(8,128)(2,1)}, bf16[162,384]{1,0:T(8,128)(2,1)S(1)}, u32[]{:S(2)}, u32[]{:S(2)}) %collective-permute-start) | collective-permute-done | bytes 124448 | tf_op jit(solution)/shard_map/pieces/ppermute | solution.py:252
  5.4 0.9 broadcast_select_fusion.1
  6.4 0.2 convolution_convert_fusion.1
  6.6 0.9 broadcast_in_dim.15
  7.5 8.6 %all-to-all-start = ((bf16[8,96,384]{2,1,0:T(8,128)(2,1)}), bf16[8,96,384]{2,1,0:T(8,128)(2,1)S(1)}, u32[]{:S(2)}, u32[]{:S(2)}) async-start(bf16[8,96,384]{2,1,0:T(8,128)(2,1)} %broadcast_in_dim.15), calls=%async_computation | async-start | bytes 1179648 | tf_op jit(solution)/shard_map/pieces/all_to_all | solution.py:264
  16.1 0.1 fusion.4
  16.2 0.3 fusion.11
  16.5 2.8 %collective-permute-start.3 = (bf16[2,3,64,384]{3,2,1,0:T(8,128)(2,1)S(1)}, bf16[2,3,64,384]{3,2,1,0:T(8,128)(2,1)S(1)}, u32[]{:S(2)}, u32[]{:S(2)}) collective-permute-start(bf16[2,3,64,384]{3,2,1,0:T(8,128)(2,1)S(1)} %fusion.11), channel_id=1, source_target_pairs={{0,12},{4,0},{8,4},{12,8},{1,13},{5,1},{9,5},{13,9},{2,14},{6,2},{... | collective-permute-start | bytes 884744 | tf_op jit(solution)/shard_map/pixels/ppermute | solution.py:28
  19.3 0.8 collective-permute-start.2
  20.1 0.9 collective-permute-start.1
  21.0 0.3 fusion.19
  21.3 9.2 %collective-permute-done.3 = bf16[2,3,64,384]{3,2,1,0:T(8,128)(2,1)S(1)} collective-permute-done((bf16[2,3,64,384]{3,2,1,0:T(8,128)(2,1)S(1)}, bf16[2,3,64,384]{3,2,1,0:T(8,128)(2,1)S(1)}, u32[]{:S(2)}, u32[]{:S(2)}) %collective-permute-start.3) | collective-permute-done | bytes 294944 | tf_op jit(solution)/shard_map/pixels/ppermute | solution.py:28
  30.5 0.3 collective-permute-done.2
  30.8 3.4 %collective-permute-done.1 = bf16[2,3,64,384]{3,2,1,0:T(8,128)(2,1)S(1)} collective-permute-done((bf16[2,3,64,384]{3,2,1,0:T(8,128)(2,1)S(1)}, bf16[2,3,64,384]{3,2,1,0:T(8,128)(2,1)S(1)}, u32[]{:S(2)}, u32[]{:S(2)}) %collective-permute-start.1) | collective-permute-done | bytes 294944 | tf_op jit(solution)/shard_map/pixels/ppermute | solution.py:28
  34.2 1.2 pad_maximum_fusion.own
  35.4 1.9 %collective-permute-start.7 = (bf16[4,2,3,64,384]{4,3,2,1,0:T(8,128)(2,1)}, bf16[4,2,3,64,384]{4,3,2,1,0:T(8,128)(2,1)S(1)}, u32[]{:S(2)}, u32[]{:S(2)}) collective-permute-start(bf16[4,2,3,64,384]{4,3,2,1,0:T(8,128)(2,1)} %pad_maximum_fusion.own), channel_id=1, source_target_pairs={{0,16},{16,32},{32,48},{48,64},{64,80},{80,96},{96,112},{112,128},... | collective-permute-start | bytes 3538952 | tf_op jit(solution)/shard_map/weight_one/ppermute | solution.py:23
  37.4 3.1 %collective-permute-start.6 = (bf16[8,48,384]{2,1,0:T(8,128)(2,1)S(1)}, bf16[8,48,384]{2,1,0:T(8,128)(2,1)S(1)}, u32[]{:S(2)}, u32[]{:S(2)}) collective-permute-start(bf16[8,48,384]{2,1,0:T(8,128)(2,1)S(1)} %get-tuple-element.42), channel_id=1, source_target_pairs={{0,3},{1,0},{2,1},{3,2},{4,7},{5,4},{6,5},{7,6},{8,11},{9,8},{10,9... | collective-permute-start | bytes 884744 | tf_op jit(solution)/shard_map/weight_one/ppermute | solution.py:28
  40.5 0.6 collective-permute-start.5
  41.1 1.0 collective-permute-start.4
  42.1 11.4 %collective-permute-done.6 = bf16[8,48,384]{2,1,0:T(8,128)(2,1)S(1)} collective-permute-done((bf16[8,48,384]{2,1,0:T(8,128)(2,1)S(1)}, bf16[8,48,384]{2,1,0:T(8,128)(2,1)S(1)}, u32[]{:S(2)}, u32[]{:S(2)}) %collective-permute-start.6) | collective-permute-done | bytes 294944 | tf_op jit(solution)/shard_map/weight_one/ppermute | solution.py:28
  53.5 4.7 %collective-permute-done.4 = bf16[8,48,384]{2,1,0:T(8,128)(2,1)S(1)} collective-permute-done((bf16[8,48,384]{2,1,0:T(8,128)(2,1)S(1)}, bf16[8,48,384]{2,1,0:T(8,128)(2,1)S(1)}, u32[]{:S(2)}, u32[]{:S(2)}) %collective-permute-start.4) | collective-permute-done | bytes 294944 | tf_op jit(solution)/shard_map/weight_one/ppermute | solution.py:28
  58.2 0.2 pad_maximum_fusion.1.mine
  58.4 0.2 collective-permute-start.8
  58.6 0.3 copy-done.5
  58.8 0.2 reduce-window_clone.1
  59.0 0.1 pad_add_fusion.place
  59.1 0.2 fusion.32
  59.4 0.1 collective-permute-start.9
  59.5 1.7 %collective-permute-start.10 = (bf16[8,48,384]{2,1,0:T(8,128)(2,1)S(1)}, bf16[8,48,384]{2,1,0:T(8,128)(2,1)S(1)}, u32[]{:S(2)}, u32[]{:S(2)}) collective-permute-start(bf16[8,48,384]{2,1,0:T(8,128)(2,1)S(1)} %slice.26), channel_id=1, source_target_pairs={{0,2},{1,3},{2,0},{3,1},{4,6},{5,7},{6,4},{7,5},{8,10},{9,11},{10,... | collective-permute-start | bytes 884744 | tf_op jit(solution)/shard_map/weight_two/ppermute | solution.py:28
  61.2 1.5 %collective-permute-start.11 = (bf16[8,48,384]{2,1,0:T(8,128)(2,1)S(1)}, bf16[8,48,384]{2,1,0:T(8,128)(2,1)S(1)}, u32[]{:S(2)}, u32[]{:S(2)}) collective-permute-start(bf16[8,48,384]{2,1,0:T(8,128)(2,1)S(1)} %slice.26), channel_id=1, source_target_pairs={{0,3},{1,0},{2,1},{3,2},{4,7},{5,4},{6,5},{7,6},{8,11},{9,8},{10,9... | collective-permute-start | bytes 884744 | tf_op jit(solution)/shard_map/weight_two/ppermute | solution.py:28
  62.7 4.3 %assemble_one.1.weight = bf16[10368,128]{1,0:T(8,128)(2,1)} custom-call(s32[2]{0:T(128)S(1)} %pad_add_fusion.place, bf16[4,8,48,384]{3,2,1,0:T(8,128)(2,1)S(1)} %pad_maximum_fusion.1.mine, bf16[4,8,48,384]{3,2,1,0:T(8,128)(2,1)} %collective-permute-done.8.other), custom_call_target="tpu_custom_call" | custom-call | flops 4000000 | bytes 5000000 | tf_op jit(solution)/shard_map/weight_one/assemble_one/pallas_call | solution.py:213
  67.0 9.6 %conv_one.1 = f32[2,12,64,128]{3,2,1,0:T(8,128)S(1)} custom-call(f32[2,3]{1,0:T(2,128)S(1)} %compare_convert_fusion.valid, s32[1]{0:T(128)} %bitcast.2.part, bf16[4,2,3,64,384]{4,3,2,1,0:T(8,128)(2,1)S(1)} %collective-permute-done.7.halo, bf16[4,2,3,64,384]{4,3,2,1,0:T(8,128)(2,1)} %pad_maximum_fusion.own, bf16[10368,128]{1,0:T(8,128)(2,1)} %assemble_one.1.weight), custom_call_target="tpu_custom_call" | custom-call | flops 4076863488 | bytes 6000000 | tf_op jit(solution)/shard_map/first/conv_one/pallas_call | solution.py:129
  76.6 0.3 multiply_reduce_fusion
  76.9 0.2 pad_maximum_fusion.2.mine
  77.1 0.1 collective-permute-start.16
  77.2 0.7 collective-permute-start.14
  77.9 1.4 %collective-permute-start.12 = (f32[2,12,64]{2,1,0:T(8,128)S(1)}, f32[2,12,64]{2,1,0:T(8,128)S(1)}, u32[]{:S(2)}, u32[]{:S(2)}) collective-permute-start(f32[2,12,64]{2,1,0:T(8,128)S(1)} %multiply_reduce_fusion), channel_id=1, source_target_pairs={{0,4},{4,8},{8,12},{12,0},{1,5},{5,9},{9,13},{13,1},{2,6},{6,10},{... | collective-permute-start | bytes 18440 | tf_op jit(solution)/shard_map/second/ppermute | solution.py:28
  79.3 0.8 collective-permute-start.13
  80.1 0.1 reshape.59
  80.2 0.2 dynamic-slice_reduce_fusion
  80.4 0.6 collective-permute-done.14
  81.0 1.8 %collective-permute-done.12 = f32[2,12,64]{2,1,0:T(8,128)S(1)} collective-permute-done((f32[2,12,64]{2,1,0:T(8,128)S(1)}, f32[2,12,64]{2,1,0:T(8,128)S(1)}, u32[]{:S(2)}, u32[]{:S(2)}) %collective-permute-start.12) | collective-permute-done | bytes 6176 | tf_op jit(solution)/shard_map/second/ppermute | solution.py:28
  82.9 1.7 %collective-permute-done.13 = f32[2,12,64]{2,1,0:T(8,128)S(1)} collective-permute-done((f32[2,12,64]{2,1,0:T(8,128)S(1)}, f32[2,12,64]{2,1,0:T(8,128)S(1)}, u32[]{:S(2)}, u32[]{:S(2)}) %collective-permute-start.13) | collective-permute-done | bytes 6176 | tf_op jit(solution)/shard_map/second/ppermute | solution.py:28
  84.6 0.3 multiply_convert_fusion.own
  84.9 2.1 %collective-permute-start.15 = (bf16[2,12,64,128]{3,2,1,0:T(8,128)(2,1)S(1)}, bf16[2,12,64,128]{3,2,1,0:T(8,128)(2,1)S(1)}, u32[]{:S(2)}, u32[]{:S(2)}) collective-permute-start(bf16[2,12,64,128]{3,2,1,0:T(8,128)(2,1)S(1)} %multiply_convert_fusion.own), channel_id=1, source_target_pairs={{0,16},{16,32},{32,48},{48,64},{64,80},{80,96},{96,112},{112,128},... | collective-permute-start | bytes 1179656 | tf_op jit(solution)/shard_map/second/ppermute | solution.py:23
  87.0 3.8 %assemble_two.1.weight = bf16[3456,384]{1,0:T(8,128)(2,1)} custom-call(s32[2]{0:T(128)S(1)} %pad_add_fusion.place, bf16[4,8,48,384]{3,2,1,0:T(8,128)(2,1)S(1)} %pad_maximum_fusion.2.mine, bf16[4,8,48,384]{3,2,1,0:T(8,128)(2,1)} %collective-permute-done.16.other), custom_call_target="tpu_custom_call" | custom-call | flops 4000000 | bytes 5000000 | tf_op jit(solution)/shard_map/weight_two/assemble_two/pallas_call | solution.py:213
  90.9 3.1 %collective-permute-done.15.halo = bf16[2,12,64,128]{3,2,1,0:T(8,128)(2,1)S(1)} collective-permute-done((bf16[2,12,64,128]{3,2,1,0:T(8,128)(2,1)S(1)}, bf16[2,12,64,128]{3,2,1,0:T(8,128)(2,1)S(1)}, u32[]{:S(2)}, u32[]{:S(2)}) %collective-permute-start.15) | collective-permute-done | bytes 393248 | tf_op jit(solution)/shard_map/second/ppermute | solution.py:23
  94.0 5.1 %conv_two.3 = (bf16[3,64,384]{2,1,0:T(8,128)(2,1)S(1)}, bf16[3,64,384]{2,1,0:T(8,128)(2,1)S(1)}, bf16[3,64,384]{2,1,0:T(8,128)(2,1)S(1)}, bf16[3,64,384]{2,1,0:T(8,128)(2,1)S(1)}) custom-call(f32[2,3]{1,0:T(2,128)S(1)} %compare_convert_fusion.valid, s32[1]{0:T(128)} %bitcast.2.part, bf16[2,12,64,128]{3,2,1,0:T(8,128)(2,1)S(1)} %collective-permute-done.15.halo, ...), custom_call_target="tpu_custom_call" | custom-call | flops 2038431744 | bytes 6000000 | tf_op jit(solution)/shard_map/second/conv_two/pallas_call | solution.py:145
  99.1 1.9 %collective-permute-start.22 = (bf16[3,64,384]{2,1,0:T(8,128)(2,1)S(1)}, bf16[3,64,384]{2,1,0:T(8,128)(2,1)S(1)}, u32[]{:S(2)}, u32[]{:S(2)}) collective-permute-start(bf16[3,64,384]{2,1,0:T(8,128)(2,1)S(1)} %get-tuple-element.40), channel_id=1, source_target_pairs={{0,12},{4,0},{8,4},{12,8},{1,13},{5,1},{9,5},{13,9},{2,14},{6,2},{... | collective-permute-start | bytes 442376 | tf_op jit(solution)/shard_map/second/ppermute | solution.py:28
  100.9 0.3 collective-permute-start.21
  101.2 0.7 collective-permute-start.20
  101.9 5.1 %conv_two.2 = (bf16[3,64,384]{2,1,0:T(8,128)(2,1)S(1)}, bf16[3,64,384]{2,1,0:T(8,128)(2,1)S(1)}, bf16[3,64,384]{2,1,0:T(8,128)(2,1)S(1)}, bf16[3,64,384]{2,1,0:T(8,128)(2,1)S(1)}) custom-call(f32[2,3]{1,0:T(2,128)S(1)} %compare_convert_fusion.valid, s32[1]{0:T(128)} %bitcast.2.part, bf16[2,12,64,128]{3,2,1,0:T(8,128)(2,1)S(1)} %collective-permute-done.15.halo, ...), custom_call_target="tpu_custom_call" | custom-call | flops 2038431744 | bytes 6000000 | tf_op jit(solution)/shard_map/second/conv_two/pallas_call | solution.py:145
  107.0 2.6 %collective-permute-start.19 = (bf16[3,64,384]{2,1,0:T(8,128)(2,1)S(1)}, bf16[3,64,384]{2,1,0:T(8,128)(2,1)S(1)}, u32[]{:S(2)}, u32[]{:S(2)}) collective-permute-start(bf16[3,64,384]{2,1,0:T(8,128)(2,1)S(1)} %get-tuple-element.36), channel_id=1, source_target_pairs={{0,12},{4,0},{8,4},{12,8},{1,13},{5,1},{9,5},{13,9},{2,14},{6,2},{... | collective-permute-start | bytes 442376 | tf_op jit(solution)/shard_map/second/ppermute | solution.py:28
  109.6 2.1 %collective-permute-start.18 = (bf16[3,64,384]{2,1,0:T(8,128)(2,1)S(1)}, bf16[3,64,384]{2,1,0:T(8,128)(2,1)S(1)}, u32[]{:S(2)}, u32[]{:S(2)}) collective-permute-start(bf16[3,64,384]{2,1,0:T(8,128)(2,1)S(1)} %get-tuple-element.35), channel_id=1, source_target_pairs={{0,8},{4,12},{8,0},{12,4},{1,9},{5,13},{9,1},{13,5},{2,10},{6,14},... | collective-permute-start | bytes 442376 | tf_op jit(solution)/shard_map/second/ppermute | solution.py:28
  111.7 0.2 collective-permute-start.17
  112.0 2.5 %collective-permute-done.19 = bf16[3,64,384]{2,1,0:T(8,128)(2,1)S(1)} collective-permute-done((bf16[3,64,384]{2,1,0:T(8,128)(2,1)S(1)}, bf16[3,64,384]{2,1,0:T(8,128)(2,1)S(1)}, u32[]{:S(2)}, u32[]{:S(2)}) %collective-permute-start.19) | collective-permute-done | bytes 147488 | tf_op jit(solution)/shard_map/second/ppermute | solution.py:28
  114.5 2.0 %collective-permute-done.18 = bf16[3,64,384]{2,1,0:T(8,128)(2,1)S(1)} collective-permute-done((bf16[3,64,384]{2,1,0:T(8,128)(2,1)S(1)}, bf16[3,64,384]{2,1,0:T(8,128)(2,1)S(1)}, u32[]{:S(2)}, u32[]{:S(2)}) %collective-permute-start.18) | collective-permute-done | bytes 147488 | tf_op jit(solution)/shard_map/second/ppermute | solution.py:28
  116.4 1.6 %collective-permute-done.17 = bf16[3,64,384]{2,1,0:T(8,128)(2,1)S(1)} collective-permute-done((bf16[3,64,384]{2,1,0:T(8,128)(2,1)S(1)}, bf16[3,64,384]{2,1,0:T(8,128)(2,1)S(1)}, u32[]{:S(2)}, u32[]{:S(2)}) %collective-permute-start.17) | collective-permute-done | bytes 147488 | tf_op jit(solution)/shard_map/second/ppermute | solution.py:28
  118.1 0.1 fusion.12
  118.2 0.7 broadcast_in_dim.16
  118.9 1.3 %broadcast_in_dim_reshape.3 = bf16[1,2,6,128,384]{4,3,2,1,0:T(8,128)(2,1)} reshape(bf16[2,3,2,64,2,384]{5,4,3,2,1,0:T(2,128)(2,1)S(1)} %broadcast_in_dim.16) | data formatting | bytes 2359296 | tf_op jit(solution)/shard_map/broadcast_in_dim;reshape | solution.py:320
  (37 shorter events, 0.4 us)
Async XLA Ops:
  0.0 1.6 %copy-start = (bf16[162,384]{1,0:T(8,128)(2,1)S(1)}, bf16[162,384]{1,0:T(8,128)(2,1)}, u32[]{:S(2)}) copy-start(bf16[162,384]{1,0:T(8,128)(2,1)} %param.10) | copy-start | bytes 373252
  0.0 5.4 %collective-permute-start = (bf16[162,384]{1,0:T(8,128)(2,1)}, bf16[162,384]{1,0:T(8,128)(2,1)S(1)}, u32[]{:S(2)}, u32[]{:S(2)}) collective-permute-start(bf16[162,384]{1,0:T(8,128)(2,1)} %param.11), channel_id=1, source_target_pairs={{0,1},{1,0},{2,3},{3,2},{4,5},{5,4},{6,7},{7,6},{8,9},{9,8},{10,11... | collective-permute-start | bytes 373256 | tf_op jit(solution)/shard_map/pieces/ppermute | solution.py:252
  6.3 9.7 %copy-start.1 = (bf16[1,2,3,64,384]{4,3,2,1,0:T(8,128)(2,1)S(1)}, bf16[1,2,3,64,384]{4,3,2,1,0:T(8,128)(2,1)}, u32[]{:S(2)}) copy-start(bf16[1,2,3,64,384]{4,3,2,1,0:T(8,128)(2,1)} %param.6) | copy-start | bytes 884740
  6.6 9.6 %copy-start.3 = (f32[384]{0:T(512)S(1)}, f32[384]{0:T(512)}, u32[]{:S(2)}) copy-start(f32[384]{0:T(512)} %param.8) | copy-start | bytes 4612
  7.5 27.9 %all-to-all-start = ((bf16[8,96,384]{2,1,0:T(8,128)(2,1)}), bf16[8,96,384]{2,1,0:T(8,128)(2,1)S(1)}, u32[]{:S(2)}, u32[]{:S(2)}) async-start(bf16[8,96,384]{2,1,0:T(8,128)(2,1)} %broadcast_in_dim.15), calls=%async_computation | async-start | bytes 1179648 | tf_op jit(solution)/shard_map/pieces/all_to_all | solution.py:264
  16.5 14.0 %collective-permute-start.3 = (bf16[2,3,64,384]{3,2,1,0:T(8,128)(2,1)S(1)}, bf16[2,3,64,384]{3,2,1,0:T(8,128)(2,1)S(1)}, u32[]{:S(2)}, u32[]{:S(2)}) collective-permute-start(bf16[2,3,64,384]{3,2,1,0:T(8,128)(2,1)S(1)} %fusion.11), channel_id=1, source_target_pairs={{0,12},{4,0},{8,4},{12,8},{1,13},{5,1},{9,5},{13,9},{2,14},{6,2},{... | collective-permute-start | bytes 884744 | tf_op jit(solution)/shard_map/pixels/ppermute | solution.py:28
  19.3 11.5 %collective-permute-start.2 = (bf16[2,3,64,384]{3,2,1,0:T(8,128)(2,1)S(1)}, bf16[2,3,64,384]{3,2,1,0:T(8,128)(2,1)S(1)}, u32[]{:S(2)}, u32[]{:S(2)}) collective-permute-start(bf16[2,3,64,384]{3,2,1,0:T(8,128)(2,1)S(1)} %fusion.11), channel_id=1, source_target_pairs={{0,8},{4,12},{8,0},{12,4},{1,9},{5,13},{9,1},{13,5},{2,10},{6,14},... | collective-permute-start | bytes 884744 | tf_op jit(solution)/shard_map/pixels/ppermute | solution.py:28
  20.1 14.1 %collective-permute-start.1 = (bf16[2,3,64,384]{3,2,1,0:T(8,128)(2,1)S(1)}, bf16[2,3,64,384]{3,2,1,0:T(8,128)(2,1)S(1)}, u32[]{:S(2)}, u32[]{:S(2)}) collective-permute-start(bf16[2,3,64,384]{3,2,1,0:T(8,128)(2,1)S(1)} %fusion.11), channel_id=1, source_target_pairs={{0,4},{4,8},{8,12},{12,0},{1,5},{5,9},{9,13},{13,1},{2,6},{6,10},{... | collective-permute-start | bytes 884744 | tf_op jit(solution)/shard_map/pixels/ppermute | solution.py:28
  35.4 23.0 %collective-permute-start.7 = (bf16[4,2,3,64,384]{4,3,2,1,0:T(8,128)(2,1)}, bf16[4,2,3,64,384]{4,3,2,1,0:T(8,128)(2,1)S(1)}, u32[]{:S(2)}, u32[]{:S(2)}) collective-permute-start(bf16[4,2,3,64,384]{4,3,2,1,0:T(8,128)(2,1)} %pad_maximum_fusion.own), channel_id=1, source_target_pairs={{0,16},{16,32},{32,48},{48,64},{64,80},{80,96},{96,112},{112,128},... | collective-permute-start | bytes 3538952 | tf_op jit(solution)/shard_map/weight_one/ppermute | solution.py:23
  37.4 16.1 %collective-permute-start.6 = (bf16[8,48,384]{2,1,0:T(8,128)(2,1)S(1)}, bf16[8,48,384]{2,1,0:T(8,128)(2,1)S(1)}, u32[]{:S(2)}, u32[]{:S(2)}) collective-permute-start(bf16[8,48,384]{2,1,0:T(8,128)(2,1)S(1)} %get-tuple-element.42), channel_id=1, source_target_pairs={{0,3},{1,0},{2,1},{3,2},{4,7},{5,4},{6,5},{7,6},{8,11},{9,8},{10,9... | collective-permute-start | bytes 884744 | tf_op jit(solution)/shard_map/weight_one/ppermute | solution.py:28
  40.5 13.1 %collective-permute-start.5 = (bf16[8,48,384]{2,1,0:T(8,128)(2,1)S(1)}, bf16[8,48,384]{2,1,0:T(8,128)(2,1)S(1)}, u32[]{:S(2)}, u32[]{:S(2)}) collective-permute-start(bf16[8,48,384]{2,1,0:T(8,128)(2,1)S(1)} %get-tuple-element.42), channel_id=1, source_target_pairs={{0,2},{1,3},{2,0},{3,1},{4,6},{5,7},{6,4},{7,5},{8,10},{9,11},{10,... | collective-permute-start | bytes 884744 | tf_op jit(solution)/shard_map/weight_one/ppermute | solution.py:28
  41.1 17.1 %collective-permute-start.4 = (bf16[8,48,384]{2,1,0:T(8,128)(2,1)S(1)}, bf16[8,48,384]{2,1,0:T(8,128)(2,1)S(1)}, u32[]{:S(2)}, u32[]{:S(2)}) collective-permute-start(bf16[8,48,384]{2,1,0:T(8,128)(2,1)S(1)} %get-tuple-element.42), channel_id=1, source_target_pairs={{0,1},{1,2},{2,3},{3,0},{4,5},{5,6},{6,7},{7,4},{8,9},{9,10},{10,1... | collective-permute-start | bytes 884744 | tf_op jit(solution)/shard_map/weight_one/ppermute | solution.py:28
  58.2 0.7 copy-start.5
  58.4 4.4 %collective-permute-start.8 = (bf16[4,8,48,384]{3,2,1,0:T(8,128)(2,1)S(1)}, bf16[4,8,48,384]{3,2,1,0:T(8,128)(2,1)}, u32[]{:S(2)}, u32[]{:S(2)}) collective-permute-start(bf16[4,8,48,384]{3,2,1,0:T(8,128)(2,1)S(1)} %pad_maximum_fusion.1.mine), channel_id=1, source_target_pairs={{0,16},{16,0},{1,17},{17,1},{2,18},{18,2},{3,19},{19,3},{4,20},{20... | collective-permute-start | bytes 3538952 | tf_op jit(solution)/shard_map/weight_one/ppermute | solution.py:271
  59.4 17.5 %collective-permute-start.9 = (bf16[8,48,384]{2,1,0:T(8,128)(2,1)S(1)}, bf16[8,48,384]{2,1,0:T(8,128)(2,1)S(1)}, u32[]{:S(2)}, u32[]{:S(2)}) collective-permute-start(bf16[8,48,384]{2,1,0:T(8,128)(2,1)S(1)} %slice.26), channel_id=1, source_target_pairs={{0,1},{1,2},{2,3},{3,0},{4,5},{5,6},{6,7},{7,4},{8,9},{9,10},{10,1... | collective-permute-start | bytes 884744 | tf_op jit(solution)/shard_map/weight_two/ppermute | solution.py:28
  59.5 17.4 %collective-permute-start.10 = (bf16[8,48,384]{2,1,0:T(8,128)(2,1)S(1)}, bf16[8,48,384]{2,1,0:T(8,128)(2,1)S(1)}, u32[]{:S(2)}, u32[]{:S(2)}) collective-permute-start(bf16[8,48,384]{2,1,0:T(8,128)(2,1)S(1)} %slice.26), channel_id=1, source_target_pairs={{0,2},{1,3},{2,0},{3,1},{4,6},{5,7},{6,4},{7,5},{8,10},{9,11},{10,... | collective-permute-start | bytes 884744 | tf_op jit(solution)/shard_map/weight_two/ppermute | solution.py:28
  61.2 15.7 %collective-permute-start.11 = (bf16[8,48,384]{2,1,0:T(8,128)(2,1)S(1)}, bf16[8,48,384]{2,1,0:T(8,128)(2,1)S(1)}, u32[]{:S(2)}, u32[]{:S(2)}) collective-permute-start(bf16[8,48,384]{2,1,0:T(8,128)(2,1)S(1)} %slice.26), channel_id=1, source_target_pairs={{0,3},{1,0},{2,1},{3,2},{4,7},{5,4},{6,5},{7,6},{8,11},{9,8},{10,9... | collective-permute-start | bytes 884744 | tf_op jit(solution)/shard_map/weight_two/ppermute | solution.py:28
  76.9 3.2 %copy-start.4 = (f32[384]{0:T(512)S(1)}, f32[384]{0:T(512)}, u32[]{:S(2)}) copy-start(f32[384]{0:T(512)} %param.9) | copy-start | bytes 4612
  77.1 9.9 %collective-permute-start.16 = (bf16[4,8,48,384]{3,2,1,0:T(8,128)(2,1)S(1)}, bf16[4,8,48,384]{3,2,1,0:T(8,128)(2,1)}, u32[]{:S(2)}, u32[]{:S(2)}) collective-permute-start(bf16[4,8,48,384]{3,2,1,0:T(8,128)(2,1)S(1)} %pad_maximum_fusion.2.mine), channel_id=1, source_target_pairs={{0,16},{16,0},{1,17},{17,1},{2,18},{18,2},{3,19},{19,3},{4,20},{20... | collective-permute-start | bytes 3538952 | tf_op jit(solution)/shard_map/weight_two/ppermute | solution.py:295
  77.2 3.8 %collective-permute-start.14 = (f32[2,12,64]{2,1,0:T(8,128)S(1)}, f32[2,12,64]{2,1,0:T(8,128)S(1)}, u32[]{:S(2)}, u32[]{:S(2)}) collective-permute-start(f32[2,12,64]{2,1,0:T(8,128)S(1)} %multiply_reduce_fusion), channel_id=1, source_target_pairs={{0,12},{4,0},{8,4},{12,8},{1,13},{5,1},{9,5},{13,9},{2,14},{6,2},{... | collective-permute-start | bytes 18440 | tf_op jit(solution)/shard_map/second/ppermute | solution.py:28
  77.9 4.9 %collective-permute-start.12 = (f32[2,12,64]{2,1,0:T(8,128)S(1)}, f32[2,12,64]{2,1,0:T(8,128)S(1)}, u32[]{:S(2)}, u32[]{:S(2)}) collective-permute-start(f32[2,12,64]{2,1,0:T(8,128)S(1)} %multiply_reduce_fusion), channel_id=1, source_target_pairs={{0,4},{4,8},{8,12},{12,0},{1,5},{5,9},{9,13},{13,1},{2,6},{6,10},{... | collective-permute-start | bytes 18440 | tf_op jit(solution)/shard_map/second/ppermute | solution.py:28
  79.3 5.2 %collective-permute-start.13 = (f32[2,12,64]{2,1,0:T(8,128)S(1)}, f32[2,12,64]{2,1,0:T(8,128)S(1)}, u32[]{:S(2)}, u32[]{:S(2)}) collective-permute-start(f32[2,12,64]{2,1,0:T(8,128)S(1)} %multiply_reduce_fusion), channel_id=1, source_target_pairs={{0,8},{4,12},{8,0},{12,4},{1,9},{5,13},{9,1},{13,5},{2,10},{6,14},... | collective-permute-start | bytes 18440 | tf_op jit(solution)/shard_map/second/ppermute | solution.py:28
  84.9 9.1 %collective-permute-start.15 = (bf16[2,12,64,128]{3,2,1,0:T(8,128)(2,1)S(1)}, bf16[2,12,64,128]{3,2,1,0:T(8,128)(2,1)S(1)}, u32[]{:S(2)}, u32[]{:S(2)}) collective-permute-start(bf16[2,12,64,128]{3,2,1,0:T(8,128)(2,1)S(1)} %multiply_convert_fusion.own), channel_id=1, source_target_pairs={{0,16},{16,32},{32,48},{48,64},{64,80},{80,96},{96,112},{112,128},... | collective-permute-start | bytes 1179656 | tf_op jit(solution)/shard_map/second/ppermute | solution.py:23
  99.1 12.6 %collective-permute-start.22 = (bf16[3,64,384]{2,1,0:T(8,128)(2,1)S(1)}, bf16[3,64,384]{2,1,0:T(8,128)(2,1)S(1)}, u32[]{:S(2)}, u32[]{:S(2)}) collective-permute-start(bf16[3,64,384]{2,1,0:T(8,128)(2,1)S(1)} %get-tuple-element.40), channel_id=1, source_target_pairs={{0,12},{4,0},{8,4},{12,8},{1,13},{5,1},{9,5},{13,9},{2,14},{6,2},{... | collective-permute-start | bytes 442376 | tf_op jit(solution)/shard_map/second/ppermute | solution.py:28
  100.9 10.9 %collective-permute-start.21 = (bf16[3,64,384]{2,1,0:T(8,128)(2,1)S(1)}, bf16[3,64,384]{2,1,0:T(8,128)(2,1)S(1)}, u32[]{:S(2)}, u32[]{:S(2)}) collective-permute-start(bf16[3,64,384]{2,1,0:T(8,128)(2,1)S(1)} %get-tuple-element.39), channel_id=1, source_target_pairs={{0,8},{4,12},{8,0},{12,4},{1,9},{5,13},{9,1},{13,5},{2,10},{6,14},... | collective-permute-start | bytes 442376 | tf_op jit(solution)/shard_map/second/ppermute | solution.py:28
  101.2 10.7 %collective-permute-start.20 = (bf16[3,64,384]{2,1,0:T(8,128)(2,1)S(1)}, bf16[3,64,384]{2,1,0:T(8,128)(2,1)S(1)}, u32[]{:S(2)}, u32[]{:S(2)}) collective-permute-start(bf16[3,64,384]{2,1,0:T(8,128)(2,1)S(1)} %get-tuple-element.38), channel_id=1, source_target_pairs={{0,4},{4,8},{8,12},{12,0},{1,5},{5,9},{9,13},{13,1},{2,6},{6,10},{... | collective-permute-start | bytes 442376 | tf_op jit(solution)/shard_map/second/ppermute | solution.py:28
  107.0 11.1 %copy-start.2 = (bf16[1,2,3,64,384]{4,3,2,1,0:T(8,128)(2,1)S(1)}, bf16[1,2,3,64,384]{4,3,2,1,0:T(8,128)(2,1)}, u32[]{:S(2)}) copy-start(bf16[1,2,3,64,384]{4,3,2,1,0:T(8,128)(2,1)} %param.6) | copy-start | bytes 884740
  107.0 7.5 %collective-permute-start.19 = (bf16[3,64,384]{2,1,0:T(8,128)(2,1)S(1)}, bf16[3,64,384]{2,1,0:T(8,128)(2,1)S(1)}, u32[]{:S(2)}, u32[]{:S(2)}) collective-permute-start(bf16[3,64,384]{2,1,0:T(8,128)(2,1)S(1)} %get-tuple-element.36), channel_id=1, source_target_pairs={{0,12},{4,0},{8,4},{12,8},{1,13},{5,1},{9,5},{13,9},{2,14},{6,2},{... | collective-permute-start | bytes 442376 | tf_op jit(solution)/shard_map/second/ppermute | solution.py:28
  109.6 6.8 %collective-permute-start.18 = (bf16[3,64,384]{2,1,0:T(8,128)(2,1)S(1)}, bf16[3,64,384]{2,1,0:T(8,128)(2,1)S(1)}, u32[]{:S(2)}, u32[]{:S(2)}) collective-permute-start(bf16[3,64,384]{2,1,0:T(8,128)(2,1)S(1)} %get-tuple-element.35), channel_id=1, source_target_pairs={{0,8},{4,12},{8,0},{12,4},{1,9},{5,13},{9,1},{13,5},{2,10},{6,14},... | collective-permute-start | bytes 442376 | tf_op jit(solution)/shard_map/second/ppermute | solution.py:28
  111.7 6.4 %collective-permute-start.17 = (bf16[3,64,384]{2,1,0:T(8,128)(2,1)S(1)}, bf16[3,64,384]{2,1,0:T(8,128)(2,1)S(1)}, u32[]{:S(2)}, u32[]{:S(2)}) collective-permute-start(bf16[3,64,384]{2,1,0:T(8,128)(2,1)S(1)} %get-tuple-element.34), channel_id=1, source_target_pairs={{0,4},{4,8},{8,12},{12,0},{1,5},{5,9},{9,13},{13,1},{2,6},{6,10},{... | collective-permute-start | bytes 442376 | tf_op jit(solution)/shard_map/second/ppermute | solution.py:28

commit v5 on v4

--- a/solution.py
+++ b/solution.py
@@ -52,38 +52,42 @@
             taps[e, slot, rows - 1] = blank
 
 
-def conv_one_kernel(share, valid, part, halo, own, weight, out, taps):
+def conv_one_kernel(share, valid, halo, own, weight, out, frame_buf, acc):
     parts, frames, each, width, channels = own.shape
     rows = parts * each
-    clear_border(taps)
-    for back in range(parts):
-        top = lax.rem(part[0] + parts - back, parts) * each + 1
-        for slot in range(2 * frames):
-            source = halo if slot < frames else own
-            for j in range(each):
-                fill_shifted(taps, slot, top + j, source[back, slot % frames, j])
+    blank = jnp.zeros((width, channels), own.dtype)
+    for slot in range(2 * frames):
+        frame_buf[slot, 0] = blank
+        frame_buf[slot, rows + 1] = blank
+        source = halo if slot < frames else own
+        for row in range(rows):
+            frame_buf[slot, row + 1] = source[row // each, slot % frames, row % each]
     for slot in range(2 * frames):
         pairs = [(s, slot - s) for s in range(frames) if 0 <= slot - s < 3]
-        total = None
-        for b in range(3):
-            columns = jnp.concatenate(
-                [taps[e, slot, b : b + rows].reshape(rows * width, channels) for e in range(3)], axis=1
-            )
+        columns = jnp.concatenate(
+            [frame_buf[slot, b : b + rows].reshape(rows * width, channels) for b in range(3)], axis=1
+        )
+        for e in range(3):
             blocks = []
             for _, a in pairs:
-                first = (a * 3 + b) * 3 * channels
-                blocks.append(weight[first : first + 3 * channels, :])
+                taps = [(a * 3 + b) * 3 + e for b in range(3)]
+                blocks.append(jnp.concatenate([weight[t * channels : (t + 1) * channels, :] for t in taps], axis=0))
             packed = blocks[0] if len(blocks) == 1 else jnp.concatenate(blocks, axis=1)
             term = jnp.dot(columns, packed, preferred_element_type=jnp.float32)
-            total = term if total is None else total + term
-        for i, (s, a) in enumerate(pairs):
-            piece = valid[s, a] * total[:, i * LANE : (i + 1) * LANE]
-            lane = lax.broadcasted_iota(jnp.int32, piece.shape, 1)
-            piece = jnp.where(lane < share, piece, 0.0).reshape(rows, width, LANE)
-            if a == 0:
-                out[s] = piece
-            else:
-                out[s] = out[s] + piece
+            for i, (s, a) in enumerate(pairs):
+                piece = valid[s, a] * term[:, i * LANE : (i + 1) * LANE]
+                if a == 0:
+                    acc[s, e] = piece
+                else:
+                    acc[s, e] = acc[s, e] + piece
+    pixels = rows * width
+    lane = lax.broadcasted_iota(jnp.int32, (pixels, LANE), 1)
+    col = lax.rem(lax.broadcasted_iota(jnp.int32, (pixels, LANE), 0), width)
+    for s in range(frames):
+        left = jnp.where(col == 0, 0.0, pltpu.roll(acc[s, 0], 1, 0))
+        right = jnp.where(col == width - 1, 0.0, pltpu.roll(acc[s, 2], pixels - 1, 0))
+        done = jnp.where(lane < share, acc[s, 1] + left + right, 0.0)
+        out[s] = done.reshape(rows, width, LANE)
 
 
 def conv_two_kernel(s, valid, part, halo, own, weight, *rest):
@@ -122,20 +126,23 @@
 PARAMS = pltpu.CompilerParams(vmem_limit_bytes=52 * 1024 * 1024)
 
 
-def conv_one_call(valid, part, halo, own, weight):
+def conv_one_call(valid, halo, own, weight):
     parts, frames, each, width, channels = own.shape
     rows = parts * each
     flops = 2 * 6 * rows * width * 9 * channels * LANE
     return pl.pallas_call(
         functools.partial(conv_one_kernel, channels // parts),
         out_shape=jax.ShapeDtypeStruct((frames, rows, width, LANE), jnp.float32),
-        in_specs=[SMEM, SMEM, VMEM, VMEM, VMEM],
+        in_specs=[SMEM, VMEM, VMEM, VMEM],
         out_specs=VMEM,
-        scratch_shapes=[pltpu.VMEM((3, 2 * frames, rows + 2, width, channels), jnp.bfloat16)],
+        scratch_shapes=[
+            pltpu.VMEM((2 * frames, rows + 2, width, channels), jnp.bfloat16),
+            pltpu.VMEM((frames, 3, rows * width, LANE), jnp.float32),
+        ],
         compiler_params=PARAMS,
         cost_estimate=pl.CostEstimate(flops=flops, bytes_accessed=6_000_000, transcendentals=0),
         name="conv_one",
-    )(valid, part, halo, own, weight)
+    )(valid, halo, own, weight)
 
 
 def conv_two_call(slot, valid, part, halo, own, weight, parts):
@@ -160,28 +167,30 @@
 def gathered(place, mine, other, i):
     ys, zs = mine.shape[:2]
     z, c, y = i // (2 * ys), i // ys % 2, i % ys
-    back_y = lax.rem(place[1] + ys - y, ys)
-    left, right = mine[back_y, z].astype(jnp.float32), other[back_y, z].astype(jnp.float32)
-    return jnp.where(place[0] == c, left, right)
+    at = lax.rem(place[2] + ys - y, ys), lax.rem(place[1] + zs - z, zs)
+    return jnp.where(place[0] == c, mine[at].astype(jnp.float32), other[at].astype(jnp.float32))
 
 
 def assemble_one_kernel(place, mine, other, out, wide):
-    shards = 2 * mine.shape[0] * mine.shape[1]
-    lanes = mine.shape[3]
-    shard = out.shape[0] // shards
+    ys, zs, _, lanes = mine.shape
+    shard = out.shape[0] // (2 * ys * zs)
     share = lanes // 4
     piece_rows = shard // 4 + 1
-    for i in range(shards):
-        piece = gathered(place, mine, other, i)
-        for j in range(4):
-            rows = min(piece_rows, shard - j * piece_rows)
-            low = (j * share) // LANE * LANE
-            window = piece[:, low : min(low + 2 * LANE, lanes)]
-            shift = j * share - low
-            if shift:
-                window = pltpu.roll(window, window.shape[1] - shift, 1)
-            first = shard * i + j * piece_rows
-            wide[first : first + rows, :] = window[:rows, :LANE]
+    for pieces, core in ((mine, place[0]), (other, 1 - place[0])):
+        for z in range(zs):
+            top = pl.multiple_of((2 * z + core) * (ys * shard), 8)
+            view = wide.at[pl.ds(top, ys * shard), :]
+            for y in range(ys):
+                piece = pieces[lax.rem(place[2] + ys - y, ys), lax.rem(place[1] + zs - z, zs)].astype(jnp.float32)
+                for j in range(4):
+                    rows = min(piece_rows, shard - j * piece_rows)
+                    low = (j * share) // LANE * LANE
+                    window = piece[:, low : min(low + 2 * LANE, lanes)]
+                    shift = j * share - low
+                    if shift:
+                        window = pltpu.roll(window, window.shape[1] - shift, 1)
+                    first = shard * y + j * piece_rows
+                    view[first : first + rows, :] = window[:rows, :LANE]
     out[...] = wide[...].astype(out.dtype)
 
 
@@ -240,28 +249,29 @@
     shard = conv_one.shape[0]
     piece_rows = shard // 4 + 1
     shards = lax.axis_size(SLOT) * lax.axis_size("group")
-    place = jnp.stack([core, lax.axis_index("group")]).astype(jnp.int32)
+    place = jnp.stack([core, lax.axis_index("z"), lax.axis_index("group")]).astype(jnp.int32)
 
     with jax.named_scope("pixels"):
         mean_sq = jnp.mean(source * source, axis=-1, keepdims=True)
         hidden_one = jax.nn.silu(source * lax.rsqrt(mean_sq + EPS) * gain_one).astype(jnp.bfloat16)
-        own_all = from_all(hidden_one, "tile")
+        own_all = lax.all_to_all(jnp.broadcast_to(hidden_one, (parts,) + hidden_one.shape), "tile", 0, 0)
 
     with jax.named_scope("pieces"):
+        conv_one, conv_two, hidden_one = lax.optimization_barrier((conv_one, conv_two, hidden_one))
         pairs = [(i, i ^ 1) for i in range(lax.axis_size("group"))]
         other = lax.ppermute(conv_two, "group", pairs)
-        couple = jnp.concatenate(
-            [jnp.where(side == 0, conv_two, other), jnp.where(side == 0, other, conv_two)], axis=0
-        )
-        rows_take = pick(TILE_ROWS, 2 * shard, True, part + parts * (piece_rows - 1) * side, parts)
-        piece_two = jnp.dot(rows_take, couple, preferred_element_type=jnp.float32).astype(jnp.bfloat16)
         take = pick(channels, share, False, part, parts)
         piece = jnp.dot(conv_one, take, preferred_element_type=jnp.float32).astype(jnp.bfloat16)
         piece = jnp.pad(piece, ((0, 4 * piece_rows - shard), (0, 0)))
         piece = jnp.concatenate([piece[j * piece_rows : (j + 1) * piece_rows] for j in range(4)], axis=1)
         piece = jnp.pad(piece, ((0, TILE_ROWS - piece_rows), (0, 0)))
+        couple = jnp.concatenate(
+            [jnp.where(side == 0, conv_two, other), jnp.where(side == 0, other, conv_two)], axis=0
+        )
+        rows_take = pick(TILE_ROWS, 2 * shard, True, part + parts * (piece_rows - 1) * side, parts)
+        piece_two = jnp.dot(rows_take, couple, preferred_element_type=jnp.float32).astype(jnp.bfloat16)
         pieces = jnp.concatenate([piece, piece_two], axis=0)
-        column = lax.all_to_all(jnp.broadcast_to(pieces, (lax.axis_size("z"),) + pieces.shape), "z", 0, 0)
+        column = from_all(pieces, "z")
 
     column, own_all = lax.optimization_barrier((column, own_all))
     with jax.named_scope("weight_one"):
@@ -286,7 +296,7 @@
 
     with jax.named_scope("first"):
         part_ref = part.astype(jnp.int32).reshape(1)
-        first = conv_one_call(valid, part_ref, prior_all, own_all, weight_one)
+        first = conv_one_call(valid, prior_all, own_all, weight_one)
 
     with jax.named_scope("weight_two"):
         squares = jnp.sum(first * first, axis=-1)

time: 121 us -> 123 us (1.017)
  starting transfers between devices: 37.7 us -> 50.6 us
  waiting for transfers between devices: 45.8 us -> 34.5 us
  Pallas kernels: 27.8 us -> 26.2 us
  local copies, waits for them, and re-layouts: 3.54 us -> 5.01 us
    ppermute x18 -> x22, starting transfers between devices: 23.2 us -> 40.2 us  [onward(): return lax.ppermute(x, axis, [(i, (i + by) % n) for i in range(n)])]
    ppermute x18 -> x22, waiting for transfers between devices: 39.2 us -> 32.4 us  [onward(): return lax.ppermute(x, axis, [(i, (i + by) % n) for i in range(n)])]
    all_to_all x1, starting transfers between devices: 8.57 us -> 4.43 us  [body(): lax.all_to_all(jnp.broadcast_to(hidden_one, (parts,) + hidden_one.shape),...]
    ppermute x1, waiting for transfers between devices: 3.47 us -> 0.01 us  [body(): other = lax.ppermute(conv_two, 'group', pairs)]
    pallas_call x1, Pallas kernels: 9.57 us -> 8.11 us  [conv_one_call(): pl.pallas_call(functools.partial(conv_one_kernel, channels // parts), out...]
  transfers between devices with their start and end apart: 24 -> 28, of which waited for: 13 -> 15; matrix products, arithmetic and copies ran while one was open for 3% -> 3% of each run, Pallas kernels for 19% -> 17%
where the time goes in v5:
time: 123 us; the launch traced here: 121 us
  starting transfers between devices  50.6 us (41%)
  waiting for transfers between devices  34.5 us (28%)
  Pallas kernels  26.2 us (21%)
  local copies, waits for them, and re-layouts  5.01 us (4%)
  other arithmetic  4.2 us (3%)
    ppermute x22, starting transfers between devices, onward(): return lax.ppermute(x, axis, [(i, (i + by) % n) for i in range(n)])  40.2 us
    ppermute x22, waiting for transfers between devices, onward(): return lax.ppermute(x, axis, [(i, (i + by) % n) for i in range(n)])  32.4 us
    pallas_call x2, Pallas kernels, conv_two_call(): pl.pallas_call(functools.partial(conv_two_kernel, slot), out_shape=[jax.S...  10.1 us
    pallas_call x1, Pallas kernels, conv_one_call(): pl.pallas_call(functools.partial(conv_one_kernel, channels // parts), out...  8.11 us
    pallas_call x2, Pallas kernels, assemble_call(): pl.pallas_call(kernel, out_shape=jax.ShapeDtypeStruct(shape, jnp.bfloat16...  7.97 us
    all_to_all x1, starting transfers between devices, body(): lax.all_to_all(jnp.broadcast_to(hidden_one, (parts,) + hidden_one.shape),...  4.43 us
    ppermute x2, starting transfers between devices, earlier(): return lax.ppermute(x, SLOT, [(i, i + 1) for i in range(n - 1)])  4.07 us
  transfers between devices with their start and end apart: 28, of which 15 were waited for; matrix products, arithmetic and copies ran while one was open for 3% of the time, Pallas kernels for 17%

profile of v5, /device:TPU:32, one launch (start us, length us, event | category | flops | bytes accessed | tf_op | source)
XLA Modules:
  0.0 121.3 jit_solution(8440799910748547184)
XLA Ops:
  0.0 1.1 fusion
  1.1 1.2 %fusion.7 = bf16[2,3,64,384]{3,2,1,0:T(8,128)(2,1)S(1)} fusion(bf16[1,2,3,64,384]{4,3,2,1,0:T(8,128)(2,1)} %param.6, f32[384]{0:T(512)} %param.8, f32[2,3,64]{2,1,0:T(4,128)S(1)} %add_rsqrt_fusion.1), kind=kLoop, calls=%fused_computation.16 | loop fusion | flops 1179648 | bytes 592896 | tf_op jit(solution)/shard_map/pixels/convert_element_type | solution.py:256
  2.4 1.7 %collective-permute-start = (bf16[162,384]{1,0:T(8,128)(2,1)}, bf16[162,384]{1,0:T(8,128)(2,1)S(1)}, u32[]{:S(2)}, u32[]{:S(2)}) collective-permute-start(bf16[162,384]{1,0:T(8,128)(2,1)} %param.11), channel_id=1, source_target_pairs={{0,1},{1,0},{2,3},{3,2},{4,5},{5,4},{6,7},{7,6},{8,9},{9,8},{10,11... | collective-permute-start | bytes 373256 | tf_op jit(solution)/shard_map/pieces/ppermute | solution.py:262
  4.0 1.2 broadcast_in_dim.15
  5.2 4.4 %all-to-all-start = ((bf16[4,2,3,64,384]{4,3,2,1,0:T(8,128)(2,1)}), bf16[4,2,3,64,384]{4,3,2,1,0:T(8,128)(2,1)}, u32[]{:S(2)}, u32[]{:S(2)}) async-start(bf16[4,2,3,64,384]{4,3,2,1,0:T(8,128)(2,1)} %broadcast_in_dim.15), calls=%async_computation | async-start | bytes 2359296 | tf_op jit(solution)/shard_map/pixels/all_to_all | solution.py:257
  9.7 0.2 convolution_convert_fusion
  10.0 0.1 fusion.19
  10.1 0.2 convolution_convert_fusion.1
  10.4 2.0 %collective-permute-start.1 = (bf16[96,384]{1,0:T(8,128)(2,1)S(1)}, bf16[96,384]{1,0:T(8,128)(2,1)S(1)}, u32[]{:S(2)}, u32[]{:S(2)}) collective-permute-start(bf16[96,384]{1,0:T(8,128)(2,1)S(1)} %pad_maximum_fusion.2), channel_id=1, source_target_pairs={{0,32},{32,64},{64,96},{96,128},{128,160},{160,192},{192,224},{224... | collective-permute-start | bytes 221192 | tf_op jit(solution)/shard_map/pieces/ppermute | solution.py:28
  12.4 4.5 %collective-permute-start.2 = (bf16[96,384]{1,0:T(8,128)(2,1)S(1)}, bf16[96,384]{1,0:T(8,128)(2,1)S(1)}, u32[]{:S(2)}, u32[]{:S(2)}) collective-permute-start(bf16[96,384]{1,0:T(8,128)(2,1)S(1)} %pad_maximum_fusion.2), channel_id=1, source_target_pairs={{0,64},{32,96},{64,128},{96,160},{128,192},{160,224},{192,0},{224,... | collective-permute-start | bytes 221192 | tf_op jit(solution)/shard_map/pieces/ppermute | solution.py:28
  16.9 1.9 %collective-permute-start.3 = (bf16[96,384]{1,0:T(8,128)(2,1)S(1)}, bf16[96,384]{1,0:T(8,128)(2,1)S(1)}, u32[]{:S(2)}, u32[]{:S(2)}) collective-permute-start(bf16[96,384]{1,0:T(8,128)(2,1)S(1)} %pad_maximum_fusion.2), channel_id=1, source_target_pairs={{0,96},{32,128},{64,160},{96,192},{128,224},{160,0},{192,32},{224,... | collective-permute-start | bytes 221192 | tf_op jit(solution)/shard_map/pieces/ppermute | solution.py:28
  18.8 1.4 %collective-permute-start.4 = (bf16[96,384]{1,0:T(8,128)(2,1)S(1)}, bf16[96,384]{1,0:T(8,128)(2,1)S(1)}, u32[]{:S(2)}, u32[]{:S(2)}) collective-permute-start(bf16[96,384]{1,0:T(8,128)(2,1)S(1)} %pad_maximum_fusion.2), channel_id=1, source_target_pairs={{0,128},{32,160},{64,192},{96,224},{128,0},{160,32},{192,64},{224,... | collective-permute-start | bytes 221192 | tf_op jit(solution)/shard_map/pieces/ppermute | solution.py:28
  20.2 3.1 %collective-permute-start.5 = (bf16[96,384]{1,0:T(8,128)(2,1)S(1)}, bf16[96,384]{1,0:T(8,128)(2,1)S(1)}, u32[]{:S(2)}, u32[]{:S(2)}) collective-permute-start(bf16[96,384]{1,0:T(8,128)(2,1)S(1)} %pad_maximum_fusion.2), channel_id=1, source_target_pairs={{0,160},{32,192},{64,224},{96,0},{128,32},{160,64},{192,96},{224,1... | collective-permute-start | bytes 221192 | tf_op jit(solution)/shard_map/pieces/ppermute | solution.py:28
  23.4 2.5 %collective-permute-start.6 = (bf16[96,384]{1,0:T(8,128)(2,1)S(1)}, bf16[96,384]{1,0:T(8,128)(2,1)S(1)}, u32[]{:S(2)}, u32[]{:S(2)}) collective-permute-start(bf16[96,384]{1,0:T(8,128)(2,1)S(1)} %pad_maximum_fusion.2), channel_id=1, source_target_pairs={{0,192},{32,224},{64,0},{96,32},{128,64},{160,96},{192,128},{224,1... | collective-permute-start | bytes 221192 | tf_op jit(solution)/shard_map/pieces/ppermute | solution.py:28
  25.8 2.3 %collective-permute-start.7 = (bf16[96,384]{1,0:T(8,128)(2,1)S(1)}, bf16[96,384]{1,0:T(8,128)(2,1)S(1)}, u32[]{:S(2)}, u32[]{:S(2)}) collective-permute-start(bf16[96,384]{1,0:T(8,128)(2,1)S(1)} %pad_maximum_fusion.2), channel_id=1, source_target_pairs={{0,224},{32,0},{64,32},{96,64},{128,96},{160,128},{192,160},{224,1... | collective-permute-start | bytes 221192 | tf_op jit(solution)/shard_map/pieces/ppermute | solution.py:28
  28.2 0.8 collective-permute-done.3
  29.0 0.6 collective-permute-done.4
  29.6 2.0 %collective-permute-done.5 = bf16[96,384]{1,0:T(8,128)(2,1)S(1)} collective-permute-done((bf16[96,384]{1,0:T(8,128)(2,1)S(1)}, bf16[96,384]{1,0:T(8,128)(2,1)S(1)}, u32[]{:S(2)}, u32[]{:S(2)}) %collective-permute-start.5) | collective-permute-done | bytes 73760 | tf_op jit(solution)/shard_map/pieces/ppermute | solution.py:28
  31.6 3.2 %collective-permute-done.6 = bf16[96,384]{1,0:T(8,128)(2,1)S(1)} collective-permute-done((bf16[96,384]{1,0:T(8,128)(2,1)S(1)}, bf16[96,384]{1,0:T(8,128)(2,1)S(1)}, u32[]{:S(2)}, u32[]{:S(2)}) %collective-permute-start.6) | collective-permute-done | bytes 73760 | tf_op jit(solution)/shard_map/pieces/ppermute | solution.py:28
  34.8 0.9 collective-permute-done.7
  35.7 1.9 %collective-permute-start.11 = (bf16[4,2,3,64,384]{4,3,2,1,0:T(8,128)(2,1)}, bf16[4,2,3,64,384]{4,3,2,1,0:T(8,128)(2,1)S(1)}, u32[]{:S(2)}, u32[]{:S(2)}) collective-permute-start(bf16[4,2,3,64,384]{4,3,2,1,0:T(8,128)(2,1)} %all-to-all-done.own), channel_id=1, source_target_pairs={{0,16},{16,32},{32,48},{48,64},{64,80},{80,96},{96,112},{112,128},... | collective-permute-start | bytes 3538952 | tf_op jit(solution)/shard_map/weight_one/ppermute | solution.py:23
  37.7 2.3 %collective-permute-start.10 = (bf16[8,48,384]{2,1,0:T(8,128)(2,1)S(1)}, bf16[8,48,384]{2,1,0:T(8,128)(2,1)S(1)}, u32[]{:S(2)}, u32[]{:S(2)}) collective-permute-start(bf16[8,48,384]{2,1,0:T(8,128)(2,1)S(1)} %get-tuple-element.46), channel_id=1, source_target_pairs={{0,3},{1,0},{2,1},{3,2},{4,7},{5,4},{6,5},{7,6},{8,11},{9,8},{10,9... | collective-permute-start | bytes 884744 | tf_op jit(solution)/shard_map/weight_one/ppermute | solution.py:28
  40.0 0.8 collective-permute-start.9
  40.8 1.3 %collective-permute-start.8 = (bf16[8,48,384]{2,1,0:T(8,128)(2,1)S(1)}, bf16[8,48,384]{2,1,0:T(8,128)(2,1)S(1)}, u32[]{:S(2)}, u32[]{:S(2)}) collective-permute-start(bf16[8,48,384]{2,1,0:T(8,128)(2,1)S(1)} %get-tuple-element.46), channel_id=1, source_target_pairs={{0,1},{1,2},{2,3},{3,0},{4,5},{5,6},{6,7},{7,4},{8,9},{9,10},{10,1... | collective-permute-start | bytes 884744 | tf_op jit(solution)/shard_map/weight_one/ppermute | solution.py:28
  42.1 11.3 %collective-permute-done.10 = bf16[8,48,384]{2,1,0:T(8,128)(2,1)S(1)} collective-permute-done((bf16[8,48,384]{2,1,0:T(8,128)(2,1)S(1)}, bf16[8,48,384]{2,1,0:T(8,128)(2,1)S(1)}, u32[]{:S(2)}, u32[]{:S(2)}) %collective-permute-start.10) | collective-permute-done | bytes 294944 | tf_op jit(solution)/shard_map/weight_one/ppermute | solution.py:28
  53.5 3.7 %collective-permute-done.8 = bf16[8,48,384]{2,1,0:T(8,128)(2,1)S(1)} collective-permute-done((bf16[8,48,384]{2,1,0:T(8,128)(2,1)S(1)}, bf16[8,48,384]{2,1,0:T(8,128)(2,1)S(1)}, u32[]{:S(2)}, u32[]{:S(2)}) %collective-permute-start.8) | collective-permute-done | bytes 294944 | tf_op jit(solution)/shard_map/weight_one/ppermute | solution.py:28
  57.2 0.2 pad_maximum_fusion.mine
  57.4 0.2 collective-permute-start.12
  57.5 0.3 copy-done.5
  57.8 0.2 reduce-window_clone.1
  58.1 0.2 fusion.21
  58.4 0.1 collective-permute-start.13
  58.5 2.1 %collective-permute-start.14 = (bf16[8,48,384]{2,1,0:T(8,128)(2,1)S(1)}, bf16[8,48,384]{2,1,0:T(8,128)(2,1)S(1)}, u32[]{:S(2)}, u32[]{:S(2)}) collective-permute-start(bf16[8,48,384]{2,1,0:T(8,128)(2,1)S(1)} %slice.26), channel_id=1, source_target_pairs={{0,2},{1,3},{2,0},{3,1},{4,6},{5,7},{6,4},{7,5},{8,10},{9,11},{10,... | collective-permute-start | bytes 884744 | tf_op jit(solution)/shard_map/weight_two/ppermute | solution.py:28
  60.5 1.6 %collective-permute-start.15 = (bf16[8,48,384]{2,1,0:T(8,128)(2,1)S(1)}, bf16[8,48,384]{2,1,0:T(8,128)(2,1)S(1)}, u32[]{:S(2)}, u32[]{:S(2)}) collective-permute-start(bf16[8,48,384]{2,1,0:T(8,128)(2,1)S(1)} %slice.26), channel_id=1, source_target_pairs={{0,3},{1,0},{2,1},{3,2},{4,7},{5,4},{6,5},{7,6},{8,11},{9,8},{10,9... | collective-permute-start | bytes 884744 | tf_op jit(solution)/shard_map/weight_two/ppermute | solution.py:28
  62.2 4.1 %assemble_one.1.weight = bf16[10368,128]{1,0:T(8,128)(2,1)} custom-call(s32[3]{0:T(128)S(1)} %pad_add_fusion.place, bf16[4,8,48,384]{3,2,1,0:T(8,128)(2,1)S(1)} %pad_maximum_fusion.mine, bf16[4,8,48,384]{3,2,1,0:T(8,128)(2,1)} %collective-permute-done.12.other), custom_call_target="tpu_custom_call" | custom-call | flops 4000000 | bytes 5000000 | tf_op jit(solution)/shard_map/weight_one/assemble_one/pallas_call | solution.py:222
  66.3 8.1 %conv_one.1 = f32[2,12,64,128]{3,2,1,0:T(8,128)S(1)} custom-call(f32[2,3]{1,0:T(2,128)S(1)} %compare_convert_fusion.valid, bf16[4,2,3,64,384]{4,3,2,1,0:T(8,128)(2,1)S(1)} %collective-permute-done.11.halo, bf16[4,2,3,64,384]{4,3,2,1,0:T(8,128)(2,1)} %all-to-all-done.own, bf16[10368,128]{1,0:T(8,128)(2,1)} %assemble_one.1.weight), custom_call_target="tpu_custom_call" | custom-call | flops 4076863488 | bytes 6000000 | tf_op jit(solution)/shard_map/first/conv_one/pallas_call | solution.py:133
  74.4 0.3 multiply_reduce_fusion
  74.7 0.4 collective-permute-done.13
  75.1 0.6 collective-permute-done.15
  75.7 0.2 pad_maximum_fusion.1.mine
  75.9 0.1 collective-permute-start.20
  76.0 3.0 %collective-permute-start.18 = (f32[2,12,64]{2,1,0:T(8,128)S(1)}, f32[2,12,64]{2,1,0:T(8,128)S(1)}, u32[]{:S(2)}, u32[]{:S(2)}) collective-permute-start(f32[2,12,64]{2,1,0:T(8,128)S(1)} %multiply_reduce_fusion), channel_id=1, source_target_pairs={{0,12},{4,0},{8,4},{12,8},{1,13},{5,1},{9,5},{13,9},{2,14},{6,2},{... | collective-permute-start | bytes 18440 | tf_op jit(solution)/shard_map/second/ppermute | solution.py:28
  79.0 2.3 %collective-permute-start.17 = (f32[2,12,64]{2,1,0:T(8,128)S(1)}, f32[2,12,64]{2,1,0:T(8,128)S(1)}, u32[]{:S(2)}, u32[]{:S(2)}) collective-permute-start(f32[2,12,64]{2,1,0:T(8,128)S(1)} %multiply_reduce_fusion), channel_id=1, source_target_pairs={{0,8},{4,12},{8,0},{12,4},{1,9},{5,13},{9,1},{13,5},{2,10},{6,14},... | collective-permute-start | bytes 18440 | tf_op jit(solution)/shard_map/second/ppermute | solution.py:28
  81.3 0.1 reshape.59
  81.4 0.2 dynamic-slice_reduce_fusion
  81.6 2.3 %collective-permute-done.16 = f32[2,12,64]{2,1,0:T(8,128)S(1)} collective-permute-done((f32[2,12,64]{2,1,0:T(8,128)S(1)}, f32[2,12,64]{2,1,0:T(8,128)S(1)}, u32[]{:S(2)}, u32[]{:S(2)}) %collective-permute-start.16) | collective-permute-done | bytes 6176 | tf_op jit(solution)/shard_map/second/ppermute | solution.py:28
  83.9 0.3 collective-permute-done.17
  84.2 0.3 multiply_convert_fusion.own
  84.5 2.1 %collective-permute-start.19 = (bf16[2,12,64,128]{3,2,1,0:T(8,128)(2,1)S(1)}, bf16[2,12,64,128]{3,2,1,0:T(8,128)(2,1)S(1)}, u32[]{:S(2)}, u32[]{:S(2)}) collective-permute-start(bf16[2,12,64,128]{3,2,1,0:T(8,128)(2,1)S(1)} %multiply_convert_fusion.own), channel_id=1, source_target_pairs={{0,16},{16,32},{32,48},{48,64},{64,80},{80,96},{96,112},{112,128},... | collective-permute-start | bytes 1179656 | tf_op jit(solution)/shard_map/second/ppermute | solution.py:23
  86.7 1.0 copy-done.2
  87.7 3.8 %assemble_two.1.weight = bf16[3456,384]{1,0:T(8,128)(2,1)} custom-call(s32[3]{0:T(128)S(1)} %pad_add_fusion.place, bf16[4,8,48,384]{3,2,1,0:T(8,128)(2,1)S(1)} %pad_maximum_fusion.1.mine, bf16[4,8,48,384]{3,2,1,0:T(8,128)(2,1)} %copy-done.2), custom_call_target="tpu_custom_call" | custom-call | flops 4000000 | bytes 5000000 | tf_op jit(solution)/shard_map/weight_two/assemble_two/pallas_call | solution.py:222
  91.5 2.1 %collective-permute-done.19.halo = bf16[2,12,64,128]{3,2,1,0:T(8,128)(2,1)S(1)} collective-permute-done((bf16[2,12,64,128]{3,2,1,0:T(8,128)(2,1)S(1)}, bf16[2,12,64,128]{3,2,1,0:T(8,128)(2,1)S(1)}, u32[]{:S(2)}, u32[]{:S(2)}) %collective-permute-start.19) | collective-permute-done | bytes 393248 | tf_op jit(solution)/shard_map/second/ppermute | solution.py:23
  93.6 5.1 %conv_two.3 = (bf16[3,64,384]{2,1,0:T(8,128)(2,1)S(1)}, bf16[3,64,384]{2,1,0:T(8,128)(2,1)S(1)}, bf16[3,64,384]{2,1,0:T(8,128)(2,1)S(1)}, bf16[3,64,384]{2,1,0:T(8,128)(2,1)S(1)}) custom-call(f32[2,3]{1,0:T(2,128)S(1)} %compare_convert_fusion.valid, s32[1]{0:T(128)} %bitcast.2.part, bf16[2,12,64,128]{3,2,1,0:T(8,128)(2,1)S(1)} %collective-permute-done.19.halo, ...), custom_call_target="tpu_custom_call" | custom-call | flops 2038431744 | bytes 6000000 | tf_op jit(solution)/shard_map/second/conv_two/pallas_call | solution.py:152
  98.7 3.3 %collective-permute-start.26 = (bf16[3,64,384]{2,1,0:T(8,128)(2,1)S(1)}, bf16[3,64,384]{2,1,0:T(8,128)(2,1)S(1)}, u32[]{:S(2)}, u32[]{:S(2)}) collective-permute-start(bf16[3,64,384]{2,1,0:T(8,128)(2,1)S(1)} %get-tuple-element.44), channel_id=1, source_target_pairs={{0,12},{4,0},{8,4},{12,8},{1,13},{5,1},{9,5},{13,9},{2,14},{6,2},{... | collective-permute-start | bytes 442376 | tf_op jit(solution)/shard_map/second/ppermute | solution.py:28
  102.0 1.0 collective-permute-start.24
  103.0 5.1 %conv_two.2 = (bf16[3,64,384]{2,1,0:T(8,128)(2,1)S(1)}, bf16[3,64,384]{2,1,0:T(8,128)(2,1)S(1)}, bf16[3,64,384]{2,1,0:T(8,128)(2,1)S(1)}, bf16[3,64,384]{2,1,0:T(8,128)(2,1)S(1)}) custom-call(f32[2,3]{1,0:T(2,128)S(1)} %compare_convert_fusion.valid, s32[1]{0:T(128)} %bitcast.2.part, bf16[2,12,64,128]{3,2,1,0:T(8,128)(2,1)S(1)} %collective-permute-done.19.halo, ...), custom_call_target="tpu_custom_call" | custom-call | flops 2038431744 | bytes 6000000 | tf_op jit(solution)/shard_map/second/conv_two/pallas_call | solution.py:152
  108.0 2.4 %collective-permute-start.23 = (bf16[3,64,384]{2,1,0:T(8,128)(2,1)S(1)}, bf16[3,64,384]{2,1,0:T(8,128)(2,1)S(1)}, u32[]{:S(2)}, u32[]{:S(2)}) collective-permute-start(bf16[3,64,384]{2,1,0:T(8,128)(2,1)S(1)} %get-tuple-element.40), channel_id=1, source_target_pairs={{0,12},{4,0},{8,4},{12,8},{1,13},{5,1},{9,5},{13,9},{2,14},{6,2},{... | collective-permute-start | bytes 442376 | tf_op jit(solution)/shard_map/second/ppermute | solution.py:28
  110.4 2.3 %collective-permute-start.22 = (bf16[3,64,384]{2,1,0:T(8,128)(2,1)S(1)}, bf16[3,64,384]{2,1,0:T(8,128)(2,1)S(1)}, u32[]{:S(2)}, u32[]{:S(2)}) collective-permute-start(bf16[3,64,384]{2,1,0:T(8,128)(2,1)S(1)} %get-tuple-element.39), channel_id=1, source_target_pairs={{0,8},{4,12},{8,0},{12,4},{1,9},{5,13},{9,1},{13,5},{2,10},{6,14},... | collective-permute-start | bytes 442376 | tf_op jit(solution)/shard_map/second/ppermute | solution.py:28
  112.8 2.6 %collective-permute-done.23 = bf16[3,64,384]{2,1,0:T(8,128)(2,1)S(1)} collective-permute-done((bf16[3,64,384]{2,1,0:T(8,128)(2,1)S(1)}, bf16[3,64,384]{2,1,0:T(8,128)(2,1)S(1)}, u32[]{:S(2)}, u32[]{:S(2)}) %collective-permute-start.23) | collective-permute-done | bytes 147488 | tf_op jit(solution)/shard_map/second/ppermute | solution.py:28
  115.4 2.1 %collective-permute-done.22 = bf16[3,64,384]{2,1,0:T(8,128)(2,1)S(1)} collective-permute-done((bf16[3,64,384]{2,1,0:T(8,128)(2,1)S(1)}, bf16[3,64,384]{2,1,0:T(8,128)(2,1)S(1)}, u32[]{:S(2)}, u32[]{:S(2)}) %collective-permute-start.22) | collective-permute-done | bytes 147488 | tf_op jit(solution)/shard_map/second/ppermute | solution.py:28
  117.5 1.6 %collective-permute-done.21 = bf16[3,64,384]{2,1,0:T(8,128)(2,1)S(1)} collective-permute-done((bf16[3,64,384]{2,1,0:T(8,128)(2,1)S(1)}, bf16[3,64,384]{2,1,0:T(8,128)(2,1)S(1)}, u32[]{:S(2)}, u32[]{:S(2)}) %collective-permute-start.21) | collective-permute-done | bytes 147488 | tf_op jit(solution)/shard_map/second/ppermute | solution.py:28
  119.2 0.1 fusion.8
  119.3 0.7 broadcast_in_dim.16
  120.0 1.3 %broadcast_in_dim_reshape.3 = bf16[1,2,6,128,384]{4,3,2,1,0:T(8,128)(2,1)} reshape(bf16[2,3,2,64,2,384]{5,4,3,2,1,0:T(2,128)(2,1)S(1)} %broadcast_in_dim.16) | data formatting | bytes 2359296 | tf_op jit(solution)/shard_map/broadcast_in_dim;reshape | solution.py:330
  (51 shorter events, 0.7 us)
Async XLA Ops:
  0.0 9.7 %copy-start = (bf16[162,384]{1,0:T(8,128)(2,1)S(1)}, bf16[162,384]{1,0:T(8,128)(2,1)}, u32[]{:S(2)}) copy-start(bf16[162,384]{1,0:T(8,128)(2,1)} %param.10) | copy-start | bytes 373252
  2.4 7.7 %collective-permute-start = (bf16[162,384]{1,0:T(8,128)(2,1)}, bf16[162,384]{1,0:T(8,128)(2,1)S(1)}, u32[]{:S(2)}, u32[]{:S(2)}) collective-permute-start(bf16[162,384]{1,0:T(8,128)(2,1)} %param.11), channel_id=1, source_target_pairs={{0,1},{1,0},{2,3},{3,2},{4,5},{5,4},{6,7},{7,6},{8,9},{9,8},{10,11... | collective-permute-start | bytes 373256 | tf_op jit(solution)/shard_map/pieces/ppermute | solution.py:262
  5.2 4.8 %copy-start.3 = (bf16[162,384]{1,0:T(8,128)(2,1)S(1)}, bf16[162,384]{1,0:T(8,128)(2,1)}, u32[]{:S(2)}) copy-start(bf16[162,384]{1,0:T(8,128)(2,1)} %param.11) | copy-start | bytes 373252
  5.2 30.5 %all-to-all-start = ((bf16[4,2,3,64,384]{4,3,2,1,0:T(8,128)(2,1)}), bf16[4,2,3,64,384]{4,3,2,1,0:T(8,128)(2,1)}, u32[]{:S(2)}, u32[]{:S(2)}) async-start(bf16[4,2,3,64,384]{4,3,2,1,0:T(8,128)(2,1)} %broadcast_in_dim.15), calls=%async_computation | async-start | bytes 2359296 | tf_op jit(solution)/shard_map/pixels/all_to_all | solution.py:257
  10.4 13.0 %collective-permute-start.1 = (bf16[96,384]{1,0:T(8,128)(2,1)S(1)}, bf16[96,384]{1,0:T(8,128)(2,1)S(1)}, u32[]{:S(2)}, u32[]{:S(2)}) collective-permute-start(bf16[96,384]{1,0:T(8,128)(2,1)S(1)} %pad_maximum_fusion.2), channel_id=1, source_target_pairs={{0,32},{32,64},{64,96},{96,128},{128,160},{160,192},{192,224},{224... | collective-permute-start | bytes 221192 | tf_op jit(solution)/shard_map/pieces/ppermute | solution.py:28
  12.4 13.5 %collective-permute-start.2 = (bf16[96,384]{1,0:T(8,128)(2,1)S(1)}, bf16[96,384]{1,0:T(8,128)(2,1)S(1)}, u32[]{:S(2)}, u32[]{:S(2)}) collective-permute-start(bf16[96,384]{1,0:T(8,128)(2,1)S(1)} %pad_maximum_fusion.2), channel_id=1, source_target_pairs={{0,64},{32,96},{64,128},{96,160},{128,192},{160,224},{192,0},{224,... | collective-permute-start | bytes 221192 | tf_op jit(solution)/shard_map/pieces/ppermute | solution.py:28
  16.9 12.1 %collective-permute-start.3 = (bf16[96,384]{1,0:T(8,128)(2,1)S(1)}, bf16[96,384]{1,0:T(8,128)(2,1)S(1)}, u32[]{:S(2)}, u32[]{:S(2)}) collective-permute-start(bf16[96,384]{1,0:T(8,128)(2,1)S(1)} %pad_maximum_fusion.2), channel_id=1, source_target_pairs={{0,96},{32,128},{64,160},{96,192},{128,224},{160,0},{192,32},{224,... | collective-permute-start | bytes 221192 | tf_op jit(solution)/shard_map/pieces/ppermute | solution.py:28
  18.8 10.8 %collective-permute-start.4 = (bf16[96,384]{1,0:T(8,128)(2,1)S(1)}, bf16[96,384]{1,0:T(8,128)(2,1)S(1)}, u32[]{:S(2)}, u32[]{:S(2)}) collective-permute-start(bf16[96,384]{1,0:T(8,128)(2,1)S(1)} %pad_maximum_fusion.2), channel_id=1, source_target_pairs={{0,128},{32,160},{64,192},{96,224},{128,0},{160,32},{192,64},{224,... | collective-permute-start | bytes 221192 | tf_op jit(solution)/shard_map/pieces/ppermute | solution.py:28
  20.2 11.4 %collective-permute-start.5 = (bf16[96,384]{1,0:T(8,128)(2,1)S(1)}, bf16[96,384]{1,0:T(8,128)(2,1)S(1)}, u32[]{:S(2)}, u32[]{:S(2)}) collective-permute-start(bf16[96,384]{1,0:T(8,128)(2,1)S(1)} %pad_maximum_fusion.2), channel_id=1, source_target_pairs={{0,160},{32,192},{64,224},{96,0},{128,32},{160,64},{192,96},{224,1... | collective-permute-start | bytes 221192 | tf_op jit(solution)/shard_map/pieces/ppermute | solution.py:28
  23.4 11.4 %collective-permute-start.6 = (bf16[96,384]{1,0:T(8,128)(2,1)S(1)}, bf16[96,384]{1,0:T(8,128)(2,1)S(1)}, u32[]{:S(2)}, u32[]{:S(2)}) collective-permute-start(bf16[96,384]{1,0:T(8,128)(2,1)S(1)} %pad_maximum_fusion.2), channel_id=1, source_target_pairs={{0,192},{32,224},{64,0},{96,32},{128,64},{160,96},{192,128},{224,1... | collective-permute-start | bytes 221192 | tf_op jit(solution)/shard_map/pieces/ppermute | solution.py:28
  25.8 9.9 %collective-permute-start.7 = (bf16[96,384]{1,0:T(8,128)(2,1)S(1)}, bf16[96,384]{1,0:T(8,128)(2,1)S(1)}, u32[]{:S(2)}, u32[]{:S(2)}) collective-permute-start(bf16[96,384]{1,0:T(8,128)(2,1)S(1)} %pad_maximum_fusion.2), channel_id=1, source_target_pairs={{0,224},{32,0},{64,32},{96,64},{128,96},{160,128},{192,160},{224,1... | collective-permute-start | bytes 221192 | tf_op jit(solution)/shard_map/pieces/ppermute | solution.py:28
  35.7 21.6 %collective-permute-start.11 = (bf16[4,2,3,64,384]{4,3,2,1,0:T(8,128)(2,1)}, bf16[4,2,3,64,384]{4,3,2,1,0:T(8,128)(2,1)S(1)}, u32[]{:S(2)}, u32[]{:S(2)}) collective-permute-start(bf16[4,2,3,64,384]{4,3,2,1,0:T(8,128)(2,1)} %all-to-all-done.own), channel_id=1, source_target_pairs={{0,16},{16,32},{32,48},{48,64},{64,80},{80,96},{96,112},{112,128},... | collective-permute-start | bytes 3538952 | tf_op jit(solution)/shard_map/weight_one/ppermute | solution.py:23
  37.7 15.7 %collective-permute-start.10 = (bf16[8,48,384]{2,1,0:T(8,128)(2,1)S(1)}, bf16[8,48,384]{2,1,0:T(8,128)(2,1)S(1)}, u32[]{:S(2)}, u32[]{:S(2)}) collective-permute-start(bf16[8,48,384]{2,1,0:T(8,128)(2,1)S(1)} %get-tuple-element.46), channel_id=1, source_target_pairs={{0,3},{1,0},{2,1},{3,2},{4,7},{5,4},{6,5},{7,6},{8,11},{9,8},{10,9... | collective-permute-start | bytes 884744 | tf_op jit(solution)/shard_map/weight_one/ppermute | solution.py:28
  40.0 13.5 %collective-permute-start.9 = (bf16[8,48,384]{2,1,0:T(8,128)(2,1)S(1)}, bf16[8,48,384]{2,1,0:T(8,128)(2,1)S(1)}, u32[]{:S(2)}, u32[]{:S(2)}) collective-permute-start(bf16[8,48,384]{2,1,0:T(8,128)(2,1)S(1)} %get-tuple-element.46), channel_id=1, source_target_pairs={{0,2},{1,3},{2,0},{3,1},{4,6},{5,7},{6,4},{7,5},{8,10},{9,11},{10,... | collective-permute-start | bytes 884744 | tf_op jit(solution)/shard_map/weight_one/ppermute | solution.py:28
  40.8 16.3 %collective-permute-start.8 = (bf16[8,48,384]{2,1,0:T(8,128)(2,1)S(1)}, bf16[8,48,384]{2,1,0:T(8,128)(2,1)S(1)}, u32[]{:S(2)}, u32[]{:S(2)}) collective-permute-start(bf16[8,48,384]{2,1,0:T(8,128)(2,1)S(1)} %get-tuple-element.46), channel_id=1, source_target_pairs={{0,1},{1,2},{2,3},{3,0},{4,5},{5,6},{6,7},{7,4},{8,9},{9,10},{10,1... | collective-permute-start | bytes 884744 | tf_op jit(solution)/shard_map/weight_one/ppermute | solution.py:28
  57.2 0.7 copy-start.5
  57.4 4.8 %collective-permute-start.12 = (bf16[4,8,48,384]{3,2,1,0:T(8,128)(2,1)S(1)}, bf16[4,8,48,384]{3,2,1,0:T(8,128)(2,1)}, u32[]{:S(2)}, u32[]{:S(2)}) collective-permute-start(bf16[4,8,48,384]{3,2,1,0:T(8,128)(2,1)S(1)} %pad_maximum_fusion.mine), channel_id=1, source_target_pairs={{0,16},{16,0},{1,17},{17,1},{2,18},{18,2},{3,19},{19,3},{4,20},{20... | collective-permute-start | bytes 3538952 | tf_op jit(solution)/shard_map/weight_one/ppermute | solution.py:281
  58.4 16.7 %collective-permute-start.13 = (bf16[8,48,384]{2,1,0:T(8,128)(2,1)S(1)}, bf16[8,48,384]{2,1,0:T(8,128)(2,1)S(1)}, u32[]{:S(2)}, u32[]{:S(2)}) collective-permute-start(bf16[8,48,384]{2,1,0:T(8,128)(2,1)S(1)} %slice.26), channel_id=1, source_target_pairs={{0,1},{1,2},{2,3},{3,0},{4,5},{5,6},{6,7},{7,4},{8,9},{9,10},{10,1... | collective-permute-start | bytes 884744 | tf_op jit(solution)/shard_map/weight_two/ppermute | solution.py:28
  58.5 16.6 %collective-permute-start.14 = (bf16[8,48,384]{2,1,0:T(8,128)(2,1)S(1)}, bf16[8,48,384]{2,1,0:T(8,128)(2,1)S(1)}, u32[]{:S(2)}, u32[]{:S(2)}) collective-permute-start(bf16[8,48,384]{2,1,0:T(8,128)(2,1)S(1)} %slice.26), channel_id=1, source_target_pairs={{0,2},{1,3},{2,0},{3,1},{4,6},{5,7},{6,4},{7,5},{8,10},{9,11},{10,... | collective-permute-start | bytes 884744 | tf_op jit(solution)/shard_map/weight_two/ppermute | solution.py:28
  60.5 15.1 %collective-permute-start.15 = (bf16[8,48,384]{2,1,0:T(8,128)(2,1)S(1)}, bf16[8,48,384]{2,1,0:T(8,128)(2,1)S(1)}, u32[]{:S(2)}, u32[]{:S(2)}) collective-permute-start(bf16[8,48,384]{2,1,0:T(8,128)(2,1)S(1)} %slice.26), channel_id=1, source_target_pairs={{0,3},{1,0},{2,1},{3,2},{4,7},{5,4},{6,5},{7,6},{8,11},{9,8},{10,9... | collective-permute-start | bytes 884744 | tf_op jit(solution)/shard_map/weight_two/ppermute | solution.py:28
  75.7 5.6 %copy-start.4 = (f32[384]{0:T(512)S(1)}, f32[384]{0:T(512)}, u32[]{:S(2)}) copy-start(f32[384]{0:T(512)} %param.9) | copy-start | bytes 4612
  75.9 10.8 %collective-permute-start.20 = (bf16[4,8,48,384]{3,2,1,0:T(8,128)(2,1)S(1)}, bf16[4,8,48,384]{3,2,1,0:T(8,128)(2,1)S(1)}, u32[]{:S(2)}, u32[]{:S(2)}) collective-permute-start(bf16[4,8,48,384]{3,2,1,0:T(8,128)(2,1)S(1)} %pad_maximum_fusion.1.mine), channel_id=1, source_target_pairs={{0,16},{16,0},{1,17},{17,1},{2,18},{18,2},{3,19},{19,3},{4,20},{20... | collective-permute-start | bytes 3538952 | tf_op jit(solution)/shard_map/weight_two/ppermute | solution.py:305
  76.0 5.6 %collective-permute-start.18 = (f32[2,12,64]{2,1,0:T(8,128)S(1)}, f32[2,12,64]{2,1,0:T(8,128)S(1)}, u32[]{:S(2)}, u32[]{:S(2)}) collective-permute-start(f32[2,12,64]{2,1,0:T(8,128)S(1)} %multiply_reduce_fusion), channel_id=1, source_target_pairs={{0,12},{4,0},{8,4},{12,8},{1,13},{5,1},{9,5},{13,9},{2,14},{6,2},{... | collective-permute-start | bytes 18440 | tf_op jit(solution)/shard_map/second/ppermute | solution.py:28
  79.0 4.9 %collective-permute-start.16 = (f32[2,12,64]{2,1,0:T(8,128)S(1)}, f32[2,12,64]{2,1,0:T(8,128)S(1)}, u32[]{:S(2)}, u32[]{:S(2)}) collective-permute-start(f32[2,12,64]{2,1,0:T(8,128)S(1)} %multiply_reduce_fusion), channel_id=1, source_target_pairs={{0,4},{4,8},{8,12},{12,0},{1,5},{5,9},{9,13},{13,1},{2,6},{6,10},{... | collective-permute-start | bytes 18440 | tf_op jit(solution)/shard_map/second/ppermute | solution.py:28
  79.0 5.2 %collective-permute-start.17 = (f32[2,12,64]{2,1,0:T(8,128)S(1)}, f32[2,12,64]{2,1,0:T(8,128)S(1)}, u32[]{:S(2)}, u32[]{:S(2)}) collective-permute-start(f32[2,12,64]{2,1,0:T(8,128)S(1)} %multiply_reduce_fusion), channel_id=1, source_target_pairs={{0,8},{4,12},{8,0},{12,4},{1,9},{5,13},{9,1},{13,5},{2,10},{6,14},... | collective-permute-start | bytes 18440 | tf_op jit(solution)/shard_map/second/ppermute | solution.py:28
  84.5 9.1 %collective-permute-start.19 = (bf16[2,12,64,128]{3,2,1,0:T(8,128)(2,1)S(1)}, bf16[2,12,64,128]{3,2,1,0:T(8,128)(2,1)S(1)}, u32[]{:S(2)}, u32[]{:S(2)}) collective-permute-start(bf16[2,12,64,128]{3,2,1,0:T(8,128)(2,1)S(1)} %multiply_convert_fusion.own), channel_id=1, source_target_pairs={{0,16},{16,32},{32,48},{48,64},{64,80},{80,96},{96,112},{112,128},... | collective-permute-start | bytes 1179656 | tf_op jit(solution)/shard_map/second/ppermute | solution.py:23
  86.7 1.0 copy-start.2
  98.7 14.0 %collective-permute-start.26 = (bf16[3,64,384]{2,1,0:T(8,128)(2,1)S(1)}, bf16[3,64,384]{2,1,0:T(8,128)(2,1)S(1)}, u32[]{:S(2)}, u32[]{:S(2)}) collective-permute-start(bf16[3,64,384]{2,1,0:T(8,128)(2,1)S(1)} %get-tuple-element.44), channel_id=1, source_target_pairs={{0,12},{4,0},{8,4},{12,8},{1,13},{5,1},{9,5},{13,9},{2,14},{6,2},{... | collective-permute-start | bytes 442376 | tf_op jit(solution)/shard_map/second/ppermute | solution.py:28
  102.0 10.7 %collective-permute-start.25 = (bf16[3,64,384]{2,1,0:T(8,128)(2,1)S(1)}, bf16[3,64,384]{2,1,0:T(8,128)(2,1)S(1)}, u32[]{:S(2)}, u32[]{:S(2)}) collective-permute-start(bf16[3,64,384]{2,1,0:T(8,128)(2,1)S(1)} %get-tuple-element.43), channel_id=1, source_target_pairs={{0,8},{4,12},{8,0},{12,4},{1,9},{5,13},{9,1},{13,5},{2,10},{6,14},... | collective-permute-start | bytes 442376 | tf_op jit(solution)/shard_map/second/ppermute | solution.py:28
  102.0 10.7 %collective-permute-start.24 = (bf16[3,64,384]{2,1,0:T(8,128)(2,1)S(1)}, bf16[3,64,384]{2,1,0:T(8,128)(2,1)S(1)}, u32[]{:S(2)}, u32[]{:S(2)}) collective-permute-start(bf16[3,64,384]{2,1,0:T(8,128)(2,1)S(1)} %get-tuple-element.42), channel_id=1, source_target_pairs={{0,4},{4,8},{8,12},{12,0},{1,5},{5,9},{9,13},{13,1},{2,6},{6,10},{... | collective-permute-start | bytes 442376 | tf_op jit(solution)/shard_map/second/ppermute | solution.py:28
  108.0 11.2 %copy-start.1 = (bf16[1,2,3,64,384]{4,3,2,1,0:T(8,128)(2,1)S(1)}, bf16[1,2,3,64,384]{4,3,2,1,0:T(8,128)(2,1)}, u32[]{:S(2)}) copy-start(bf16[1,2,3,64,384]{4,3,2,1,0:T(8,128)(2,1)} %param.6) | copy-start | bytes 884740
  108.0 7.4 %collective-permute-start.23 = (bf16[3,64,384]{2,1,0:T(8,128)(2,1)S(1)}, bf16[3,64,384]{2,1,0:T(8,128)(2,1)S(1)}, u32[]{:S(2)}, u32[]{:S(2)}) collective-permute-start(bf16[3,64,384]{2,1,0:T(8,128)(2,1)S(1)} %get-tuple-element.40), channel_id=1, source_target_pairs={{0,12},{4,0},{8,4},{12,8},{1,13},{5,1},{9,5},{13,9},{2,14},{6,2},{... | collective-permute-start | bytes 442376 | tf_op jit(solution)/shard_map/second/ppermute | solution.py:28
  110.4 7.1 %collective-permute-start.22 = (bf16[3,64,384]{2,1,0:T(8,128)(2,1)S(1)}, bf16[3,64,384]{2,1,0:T(8,128)(2,1)S(1)}, u32[]{:S(2)}, u32[]{:S(2)}) collective-permute-start(bf16[3,64,384]{2,1,0:T(8,128)(2,1)S(1)} %get-tuple-element.39), channel_id=1, source_target_pairs={{0,8},{4,12},{8,0},{12,4},{1,9},{5,13},{9,1},{13,5},{2,10},{6,14},... | collective-permute-start | bytes 442376 | tf_op jit(solution)/shard_map/second/ppermute | solution.py:28
  112.7 6.4 %collective-permute-start.21 = (bf16[3,64,384]{2,1,0:T(8,128)(2,1)S(1)}, bf16[3,64,384]{2,1,0:T(8,128)(2,1)S(1)}, u32[]{:S(2)}, u32[]{:S(2)}) collective-permute-start(bf16[3,64,384]{2,1,0:T(8,128)(2,1)S(1)} %get-tuple-element.38), channel_id=1, source_target_pairs={{0,4},{4,8},{8,12},{12,0},{1,5},{5,9},{9,13},{13,1},{2,6},{6,10},{... | collective-permute-start | bytes 442376 | tf_op jit(solution)/shard_map/second/ppermute | solution.py:28

commit v6 on v5

v6 whole, which is shorter than its diff:
```python
import functools
import jax
import jax.numpy as jnp
from jax import lax
from jax.experimental import pallas as pl
from jax.experimental.pallas import tpu as pltpu
from jax.sharding import Mesh, PartitionSpec as P

EPS = 1e-06
SLOT = ("z", "core")
LANE = 128
TILE_ROWS = 48


def video_start(slots, counts):
    starts = jnp.cumsum(counts) - counts
    hit = starts[None, :] <= slots[:, None]
    return jnp.max(jnp.where(hit, starts[None, :], 0), axis=1)


def earlier(x):
    n = lax.axis_size(SLOT)
    return lax.ppermute(x, SLOT, [(i, i + 1) for i in range(n - 1)])


def onward(x, by, axis="tile"):
    n = lax.axis_size(axis)
    return lax.ppermute(x, axis, [(i, (i + by) % n) for i in range(n)])


def across(x, bit):
    return lax.ppermute(x, "tile", [(i, i ^ bit) for i in range(lax.axis_size("tile"))])


def from_all(x, axis):
    return jnp.stack([x] + [onward(x, d, axis) for d in range(1, lax.axis_size(axis))])


def fill_shifted(taps, slot, row, frame_row):
    width, channels = frame_row.shape
    wide = frame_row.astype(jnp.float32)
    col = lax.broadcasted_iota(jnp.int32, (width, channels), 0)
    left = jnp.where(col == 0, 0.0, pltpu.roll(wide, 1, 0))
    right = jnp.where(col == width - 1, 0.0, pltpu.roll(wide, width - 1, 0))
    taps[0, slot, row] = left.astype(frame_row.dtype)
    taps[1, slot, row] = frame_row
    taps[2, slot, row] = right.astype(frame_row.dtype)


def clear_border(taps):
    _, slots, rows, width, channels = taps.shape
    blank = jnp.zeros((width, channels), taps.dtype)
    for e in range(3):
        for slot in range(slots):
            taps[e, slot, 0] = blank
            taps[e, slot, rows - 1] = blank


def assemble_one(place, mine, other, out, wide):
    ys, zs, _, lanes = mine.shape
    shard = out.shape[0] // (2 * ys * zs)
    share = lanes // 4
    piece_rows = shard // 4 + 1
    for pieces, core in ((mine, place[0]), (other, 1 - place[0])):
        for z in range(zs):
            top = pl.multiple_of((2 * z + core) * (ys * shard), 8)
            view = wide.at[pl.ds(top, ys * shard), :]
            for y in range(ys):
                piece = pieces[lax.rem(place[1] + ys - y, ys), z].astype(jnp.float32)
                for j in range(4):
                    rows = min(piece_rows, shard - j * piece_rows)
                    low = (j * share) // LANE * LANE
                    window = piece[:, low : min(low + 2 * LANE, lanes)]
                    shift = j * share - low
                    if shift:
                        window = pltpu.roll(window, window.shape[1] - shift, 1)
                    first = shard * y + j * piece_rows
                    view[first : first + rows, :] = window[:rows, :LANE]
    out[...] = wide[...].astype(out.dtype)


def conv_one_kernel(share, valid, place, halo, own, mine, other, out, frame_buf, acc, weight, wide):
    parts, frames, each, width, channels = own.shape
    rows = parts * each
    blank = jnp.zeros((width, channels), own.dtype)
    for slot in range(2 * frames):
        frame_buf[slot, 0] = blank
        frame_buf[slot, rows + 1] = blank
        source = halo if slot < frames else own
        for back in range(parts):
            top = lax.rem(place[2] + parts - back, parts) * each + 1
            for j in range(each):
                frame_buf[slot, top + j] = source[back, slot % frames, j]
    assemble_one(place, mine, other, weight, wide)
    for slot in range(2 * frames):
        pairs = [(s, slot - s) for s in range(frames) if 0 <= slot - s < 3]
        columns = jnp.concatenate(
            [frame_buf[slot, b : b + rows].reshape(rows * width, channels) for b in range(3)], axis=1
        )
        for e in range(3):
            blocks = []
            for _, a in pairs:
                taps = [(a * 3 + b) * 3 + e for b in range(3)]
                blocks.append(jnp.concatenate([weight[t * channels : (t + 1) * channels, :] for t in taps], axis=0))
            packed = blocks[0] if len(blocks) == 1 else jnp.concatenate(blocks, axis=1)
            term = jnp.dot(columns, packed, preferred_element_type=jnp.float32)
            for i, (s, a) in enumerate(pairs):
                piece = valid[s, a] * term[:, i * LANE : (i + 1) * LANE]
                if a == 0:
                    acc[s, e] = piece
                else:
                    acc[s, e] = acc[s, e] + piece
    pixels = rows * width
    lane = lax.broadcasted_iota(jnp.int32, (pixels, LANE), 1)
    col = lax.rem(lax.broadcasted_iota(jnp.int32, (pixels, LANE), 0), width)
    for s in range(frames):
        left = jnp.where(col == 0, 0.0, pltpu.roll(acc[s, 0], 1, 0))
        right = jnp.where(col == width - 1, 0.0, pltpu.roll(acc[s, 2], pixels - 1, 0))
        done = jnp.where(lane < share, acc[s, 1] + left + right, 0.0)
        out[s] = done.reshape(rows, width, LANE)


def conv_two_kernel(valid, place, halo, own, weight, *rest):
    *outs, taps, acc = rest
    frames, rows, width, lanes = own.shape
    parts = len(outs)
    each = rows // parts
    channels = weight.shape[1]
    clear_border(taps)
    for slot in range(2 * frames):
        source = halo if slot < frames else own
        for row in range(rows):
            fill_shifted(taps, slot, row + 1, source[slot % frames, row])
    for slot in range(2 * frames):
        pairs = [(s, slot - s) for s in range(frames) if 0 <= slot - s < 3]
        columns = jnp.concatenate(
            [
                taps[e, slot, b : b + rows].reshape(rows * width, lanes)
                for b in range(3)
                for e in range(3)
            ],
            axis=1,
        )
        blocks = [weight[a * 9 * lanes : (a + 1) * 9 * lanes, :] for _, a in pairs]
        packed = blocks[0] if len(blocks) == 1 else jnp.concatenate(blocks, axis=1)
        term = jnp.dot(columns, packed, preferred_element_type=jnp.float32)
        for i, (s, a) in enumerate(pairs):
            piece = valid[s, a] * term[:, i * channels : (i + 1) * channels]
            if a == 0:
                acc[s] = piece
            else:
                acc[s] = acc[s] + piece
    for d in range(parts):
        top = pl.multiple_of(lax.rem(place[2] + d, parts) * (each * width), 64)
        for s in range(frames):
            done = acc[s, pl.ds(top, each * width), :].astype(outs[d].dtype)
            outs[d][s] = done.reshape(each, width, channels)


VMEM = pl.BlockSpec(memory_space=pltpu.VMEM)
SMEM = pl.BlockSpec(memory_space=pltpu.SMEM)
PARAMS = pltpu.CompilerParams(vmem_limit_bytes=52 * 1024 * 1024)


def conv_one_call(valid, place, halo, own, mine, other):
    parts, frames, each, width, channels = own.shape
    rows = parts * each
    flops = 2 * 6 * rows * width * 9 * channels * LANE
    return pl.pallas_call(
        functools.partial(conv_one_kernel, channels // parts),
        out_shape=jax.ShapeDtypeStruct((frames, rows, width, LANE), jnp.float32),
        in_specs=[SMEM, SMEM, VMEM, VMEM, VMEM, VMEM],
        out_specs=VMEM,
        scratch_shapes=[
            pltpu.VMEM((2 * frames, rows + 2, width, channels), jnp.bfloat16),
            pltpu.VMEM((frames, 3, rows * width, LANE), jnp.float32),
            pltpu.VMEM((27 * channels, LANE), jnp.bfloat16),
            pltpu.VMEM((27 * channels, LANE), jnp.float32),
        ],
        compiler_params=PARAMS,
        cost_estimate=pl.CostEstimate(flops=flops, bytes_accessed=6_000_000, transcendentals=0),
        name="conv_one",
    )(valid, place, halo, own, mine, other)


def conv_two_call(valid, place, halo, own, weight, parts):
    frames, rows, width, lanes = own.shape
    channels = weight.shape[1]
    flops = 2 * 6 * rows * width * 9 * lanes * channels
    return pl.pallas_call(
        conv_two_kernel,
        out_shape=[jax.ShapeDtypeStruct((frames, rows // parts, width, channels), jnp.bfloat16)] * parts,
        in_specs=[SMEM, SMEM, VMEM, VMEM, VMEM],
        out_specs=[VMEM] * parts,
        scratch_shapes=[
            pltpu.VMEM((3, 2 * frames, rows + 2, width, lanes), jnp.bfloat16),
            pltpu.VMEM((frames, rows * width, channels), jnp.float32),
        ],
        compiler_params=PARAMS,
        cost_estimate=pl.CostEstimate(flops=flops, bytes_accessed=6_000_000, transcendentals=0),
        name="conv_two",
    )(valid, place, halo, own, weight)


def gathered(place, mine, other, i):
    ys, zs = mine.shape[:2]
    z, c, y = i // (2 * ys), i // ys % 2, i % ys
    at = lax.rem(place[1] + ys - y, ys), z
    return jnp.where(place[0] == c, mine[at].astype(jnp.float32), other[at].astype(jnp.float32))


def assemble_two_kernel(place, mine, other, out, wide, piece_buf):
    shards = 2 * mine.shape[0] * mine.shape[1]
    channels = mine.shape[3]
    taps = out.shape[0] // LANE
    width = channels // 4
    share = 2 * taps * width // shards
    piece_rows = (share + 1) // 2
    for t in range(taps):
        wide[t * LANE + width : (t + 1) * LANE, :] = jnp.zeros((LANE - width, channels), jnp.float32)
    for m in range(shards // 2):
        even, odd = gathered(place, mine, other, 2 * m), gathered(place, mine, other, 2 * m + 1)
        half = piece_rows - 1
        piece_buf[0:TILE_ROWS, :] = even
        piece_buf[TILE_ROWS : 2 * TILE_ROWS, :] = odd
        piece_buf[half : half + 1, :] = even[half : half + 1] + odd[0:1]
        done = 0
        while done < share:
            first = share * m + done
            source = done if done <= half else done - half + TILE_ROWS
            count = min((first // width + 1) * width - first, (piece_rows if done <= half else share) - done)
            at = first // width * LANE + first % width
            wide[at : at + count, :] = piece_buf[source : source + count, :]
            done += count
    out[...] = wide[...].astype(out.dtype)


def assemble_call(kernel, place, mine, other, shape, extra, name):
    return pl.pallas_call(
        kernel,
        out_shape=jax.ShapeDtypeStruct(shape, jnp.bfloat16),
        in_specs=[SMEM, VMEM, VMEM],
        out_specs=VMEM,
        scratch_shapes=[pltpu.VMEM(shape, jnp.float32)] + extra,
        compiler_params=PARAMS,
        cost_estimate=pl.CostEstimate(flops=4_000_000, bytes_accessed=5_000_000, transcendentals=0),
        name=name,
    )(place, mine, other)


def pick(rows, columns, transposed, part, step):
    big = lax.broadcasted_iota(jnp.int32, (rows, columns), 1 if transposed else 0)
    small = lax.broadcasted_iota(jnp.int32, (rows, columns), 0 if transposed else 1)
    return (big == step * small + part).astype(jnp.bfloat16)


def body(latents, frame_counts, gain_one, gain_two, conv_one, conv_two):
    part = lax.axis_index("tile")
    parts = lax.axis_size("tile")
    side = lax.axis_index("group") % 2
    core = lax.axis_index("core")
    counts = frame_counts.reshape(-1)
    source = latents[0].astype(jnp.float32)
    frames, each, width, channels = source.shape
    share = channels // parts
    shard = conv_one.shape[0]
    piece_rows = shard // 4 + 1
    shards = lax.axis_size(SLOT) * lax.axis_size("group")
    place = jnp.stack([core, lax.axis_index("group"), part]).astype(jnp.int32)

    with jax.named_scope("pixels"):
        mean_sq = jnp.mean(source * source, axis=-1, keepdims=True)
        hidden_one = jax.nn.silu(source * lax.rsqrt(mean_sq + EPS) * gain_one).astype(jnp.bfloat16)
        own_all = from_all(hidden_one, "tile")

    with jax.named_scope("pieces"):
        take = pick(channels, share, False, part, parts)
        piece = jnp.dot(conv_one, take, preferred_element_type=jnp.float32).astype(jnp.bfloat16)
        piece = jnp.pad(piece, ((0, 4 * piece_rows - shard), (0, 0)))
        piece = jnp.concatenate([piece[j * piece_rows : (j + 1) * piece_rows] for j in range(4)], axis=1)
        piece = jnp.pad(piece, ((0, TILE_ROWS - piece_rows), (0, 0)))
        rows_take = pick(TILE_ROWS, shard, True, part - 2 * side, parts)
        piece_two = jnp.dot(rows_take, conv_two, preferred_element_type=jnp.float32).astype(jnp.bfloat16)
        pieces = jnp.concatenate([piece, piece_two], axis=0)
        column = lax.all_to_all(jnp.broadcast_to(pieces, (lax.axis_size("z"),) + pieces.shape), "z", 0, 0)

    column, own_all = lax.optimization_barrier((column, own_all))
    with jax.named_scope("weight_one"):
        mine = from_all(column[:, :TILE_ROWS], "group")
        prior_all = earlier(own_all)
        mine, prior_all = lax.optimization_barrier((mine, prior_all))
        swapped = lax.ppermute(mine, "core", [(0, 1), (1, 0)])
        one_mine, one_swapped = mine, swapped

    with jax.named_scope("weight_two"):
        column, _ = lax.optimization_barrier((column, mine))
        later = column[:, TILE_ROWS:]
        later = [later] + [onward(later, d, "group") for d in range(1, lax.axis_size("group"))]

    base = lax.axis_index(SLOT) * frames
    slots = base + jnp.arange(frames, dtype=jnp.int32)
    begins = video_start(slots, counts)
    before = 2 - jnp.arange(3, dtype=jnp.int32)
    valid = (slots[:, None] - before[None, :] >= begins[:, None]).astype(jnp.float32)

    with jax.named_scope("first"):
        first = conv_one_call(valid, place, prior_all, own_all, one_mine, one_swapped)

    with jax.named_scope("weight_two"):
        squares = jnp.sum(first * first, axis=-1)
        squares = squares + across(squares, 1)
        squares, later = lax.optimization_barrier((squares, later))
        mine = jnp.stack(later)
        swapped = lax.ppermute(mine, "core", [(0, 1), (1, 0)])
        taps = shards * shard // channels
        weight_two = assemble_call(
            assemble_two_kernel, place, mine, swapped, (taps * LANE, channels),
            [pltpu.VMEM((2 * TILE_ROWS, channels), jnp.float32)], "assemble_two"
        )

    with jax.named_scope("second"):
        squares = squares + across(squares, 2)
        gain_mine = lax.dynamic_index_in_dim(gain_two.reshape(share, parts), part, 1, keepdims=False)
        gain_mine = jnp.pad(gain_mine, (0, LANE - share))
        scale = lax.rsqrt(squares / channels + EPS)
        hidden_two = jax.nn.silu(first * scale[..., None] * gain_mine).astype(jnp.bfloat16)
        prior_two = earlier(hidden_two)
        sums, *rest = conv_two_call(valid, place, prior_two, hidden_two, weight_two, parts)
        arrived = [onward(r, d) for d, r in enumerate(rest, 1)]
        second = sum((r.astype(jnp.float32) for r in arrived), sums.astype(jnp.float32))

    block = (source + second).astype(jnp.bfloat16)
    result = jnp.broadcast_to(
        block[:, :, None, :, None, :], (frames, each, 2, width, 2, channels)
    ).reshape(frames, 2 * each, 2 * width, channels)
    return result[None]


def solution(mesh):
    sizes = mesh.devices.shape
    fine = Mesh(mesh.devices.reshape((sizes[0] // 2, 2) + sizes[1:]), ("z", "core", "tile", "group"))
    in_specs = (
        P("group", SLOT, "tile", None, None),
        P("group", None),
        P(),
        P(),
        P(SLOT + ("group",), None),
        P(SLOT + ("group",), None),
    )
    out_specs = P("group", SLOT, "tile", None, None)
    return jax.shard_map(body, mesh=fine, in_specs=in_specs, out_specs=out_specs, check_vma=False)
```

time: 123 us -> 114 us (0.927)
  starting transfers between devices: 50.6 us -> 29.4 us
  waiting for transfers between devices: 34.5 us -> 54.9 us
  Pallas kernels: 26.2 us -> 20.4 us
  local copies, waits for them, and re-layouts: 5.01 us -> 3.29 us
    ppermute x22 -> x12, starting transfers between devices: 40.2 us -> 15.2 us  [onward(): return lax.ppermute(x, axis, [(i, (i + by) % n) for i in range(n)])]
    ppermute x22 -> x12, waiting for transfers between devices: 32.4 us -> 44.3 us  [onward(): return lax.ppermute(x, axis, [(i, (i + by) % n) for i in range(n)])]
    ppermute x1 -> x2, waiting for transfers between devices: 0.01 us -> 7.53 us  [across(): lax.ppermute(x, 'tile', [(i, i ^ bit) for i in range(lax.axis_size('tile'...]
    all_to_all x1, starting transfers between devices: 4.43 us -> 8.57 us  [body(): lax.all_to_all(jnp.broadcast_to(pieces, (lax.axis_size('z'),) + pieces.sh...]
    pallas_call x2 -> x1, Pallas kernels: 7.97 us -> 3.93 us  [assemble_call(): pl.pallas_call(kernel, out_shape=jax.ShapeDtypeStruct(shape, jnp.bfloat16...]
    pallas_call x2 -> x1, Pallas kernels: 10.1 us -> 7.31 us  [conv_two_call(): pl.pallas_call(conv_two_kernel, out_shape=[jax.ShapeDtypeStruct((frames,...]
    unnamed x18 -> x12, local copies, waits for them, and re-layouts: 1.43 us -> 0.03 us
  transfers between devices with their start and end apart: 28 -> 19, of which waited for: 15 -> 12; matrix products, arithmetic and copies ran while one was open for 3% -> 3% of each run, Pallas kernels for 17% -> 12%
where the time goes in v6:
time: 114 us; the launch traced here: 113 us
  waiting for transfers between devices  54.9 us (48%)
  starting transfers between devices  29.4 us (26%)
  Pallas kernels  20.4 us (18%)
  other arithmetic  3.64 us (3%)
  local copies, waits for them, and re-layouts  3.29 us (3%)
  matrix products  1.35 us (1%)
    ppermute x12, waiting for transfers between devices, onward(): return lax.ppermute(x, axis, [(i, (i + by) % n) for i in range(n)])  44.3 us
    ppermute x12, starting transfers between devices, onward(): return lax.ppermute(x, axis, [(i, (i + by) % n) for i in range(n)])  15.2 us
    pallas_call x1, Pallas kernels, conv_one_call(): pl.pallas_call(functools.partial(conv_one_kernel, channels // parts), out...  9.19 us
    all_to_all x1, starting transfers between devices, body(): lax.all_to_all(jnp.broadcast_to(pieces, (lax.axis_size('z'),) + pieces.sh...  8.57 us
    ppermute x2, waiting for transfers between devices, across(): lax.ppermute(x, 'tile', [(i, i ^ bit) for i in range(lax.axis_size('tile'...  7.53 us
    pallas_call x1, Pallas kernels, conv_two_call(): pl.pallas_call(conv_two_kernel, out_shape=[jax.ShapeDtypeStruct((frames,...  7.31 us
    ppermute x2, starting transfers between devices, earlier(): return lax.ppermute(x, SLOT, [(i, i + 1) for i in range(n - 1)])  4.07 us
    pallas_call x1, Pallas kernels, assemble_call(): pl.pallas_call(kernel, out_shape=jax.ShapeDtypeStruct(shape, jnp.bfloat16...  3.93 us
  transfers between devices with their start and end apart: 19, of which 12 were waited for; matrix products, arithmetic and copies ran while one was open for 3% of the time, Pallas kernels for 12%

profile of v6, /device:TPU:32, one launch (start us, length us, event | category | flops | bytes accessed | tf_op | source)
XLA Modules:
  0.0 113.2 jit_solution(6623352936338064303)
XLA Ops:
  0.0 1.2 %fusion = bf16[162,96]{1,0:T(8,128)(2,1)S(1)} fusion(bf16[162,384]{1,0:T(8,128)(2,1)} %param.10, s32[96]{0:T(128)S(1)} %multiply_add_fusion.1), kind=kOutput, calls=%fused_computation.5 | convolution fusion | flops 11996352 | bytes 155904 | tf_op jit(solution)/shard_map/pieces/dot_general | solution.py:278
  1.2 0.0 copy-start.1
  1.2 0.2 convolution_convert_fusion.1
  1.4 0.0 copy-start.3
  1.4 0.1 fusion.27
  1.6 0.9 broadcast_in_dim.15
  2.4 8.6 %all-to-all-start = ((bf16[8,96,384]{2,1,0:T(8,128)(2,1)}), bf16[8,96,384]{2,1,0:T(8,128)(2,1)S(1)}, u32[]{:S(2)}, u32[]{:S(2)}) async-start(bf16[8,96,384]{2,1,0:T(8,128)(2,1)} %broadcast_in_dim.15), calls=%async_computation | async-start | bytes 1179648 | tf_op jit(solution)/shard_map/pieces/all_to_all | solution.py:285
  11.0 0.1 fusion.4
  11.2 0.3 fusion.11
  11.4 2.8 %collective-permute-start.2 = (bf16[2,3,64,384]{3,2,1,0:T(8,128)(2,1)S(1)}, bf16[2,3,64,384]{3,2,1,0:T(8,128)(2,1)S(1)}, u32[]{:S(2)}, u32[]{:S(2)}) collective-permute-start(bf16[2,3,64,384]{3,2,1,0:T(8,128)(2,1)S(1)} %fusion.11), channel_id=1, source_target_pairs={{0,12},{4,0},{8,4},{12,8},{1,13},{5,1},{9,5},{13,9},{2,14},{6,2},{... | collective-permute-start | bytes 884744 | tf_op jit(solution)/shard_map/pixels/ppermute | solution.py:28
  14.3 0.8 collective-permute-start.1
  15.1 0.9 collective-permute-start
  15.9 0.3 fusion.19
  16.2 10.1 %collective-permute-done.2 = bf16[2,3,64,384]{3,2,1,0:T(8,128)(2,1)S(1)} collective-permute-done((bf16[2,3,64,384]{3,2,1,0:T(8,128)(2,1)S(1)}, bf16[2,3,64,384]{3,2,1,0:T(8,128)(2,1)S(1)}, u32[]{:S(2)}, u32[]{:S(2)}) %collective-permute-start.2) | collective-permute-done | bytes 294944 | tf_op jit(solution)/shard_map/pixels/ppermute | solution.py:28
  26.3 0.0 collective-permute-done.1
  26.3 3.7 %collective-permute-done = bf16[2,3,64,384]{3,2,1,0:T(8,128)(2,1)S(1)} collective-permute-done((bf16[2,3,64,384]{3,2,1,0:T(8,128)(2,1)S(1)}, bf16[2,3,64,384]{3,2,1,0:T(8,128)(2,1)S(1)}, u32[]{:S(2)}, u32[]{:S(2)}) %collective-permute-start) | collective-permute-done | bytes 294944 | tf_op jit(solution)/shard_map/pixels/ppermute | solution.py:28
  30.0 0.2 pad_maximum_fusion.own
  30.2 0.0 copy-start.2
  30.2 0.0 all-to-all-done
  30.2 1.9 %collective-permute-start.6 = (bf16[4,2,3,64,384]{4,3,2,1,0:T(8,128)(2,1)S(1)}, bf16[4,2,3,64,384]{4,3,2,1,0:T(8,128)(2,1)S(1)}, u32[]{:S(2)}, u32[]{:S(2)}) collective-permute-start(bf16[4,2,3,64,384]{4,3,2,1,0:T(8,128)(2,1)S(1)} %pad_maximum_fusion.own), channel_id=1, source_target_pairs={{0,16},{16,32},{32,48},{48,64},{64,80},{80,96},{96,112},{112,128},... | collective-permute-start | bytes 3538952 | tf_op jit(solution)/shard_map/weight_one/ppermute | solution.py:23
  32.1 0.1 slice_bitcast_fusion
  32.2 3.1 %collective-permute-start.5 = (bf16[8,48,384]{2,1,0:T(8,128)(2,1)S(1)}, bf16[8,48,384]{2,1,0:T(8,128)(2,1)S(1)}, u32[]{:S(2)}, u32[]{:S(2)}) collective-permute-start(bf16[8,48,384]{2,1,0:T(8,128)(2,1)S(1)} %get-tuple-element.34), channel_id=1, source_target_pairs={{0,3},{1,0},{2,1},{3,2},{4,7},{5,4},{6,5},{7,6},{8,11},{9,8},{10,9... | collective-permute-start | bytes 884744 | tf_op jit(solution)/shard_map/weight_one/ppermute | solution.py:28
  35.3 0.6 collective-permute-start.4
  35.9 1.0 collective-permute-start.3
  36.9 11.4 %collective-permute-done.5 = bf16[8,48,384]{2,1,0:T(8,128)(2,1)S(1)} collective-permute-done((bf16[8,48,384]{2,1,0:T(8,128)(2,1)S(1)}, bf16[8,48,384]{2,1,0:T(8,128)(2,1)S(1)}, u32[]{:S(2)}, u32[]{:S(2)}) %collective-permute-start.5) | collective-permute-done | bytes 294944 | tf_op jit(solution)/shard_map/weight_one/ppermute | solution.py:28
  48.3 0.0 collective-permute-done.4
  48.3 4.7 %collective-permute-done.3 = bf16[8,48,384]{2,1,0:T(8,128)(2,1)S(1)} collective-permute-done((bf16[8,48,384]{2,1,0:T(8,128)(2,1)S(1)}, bf16[8,48,384]{2,1,0:T(8,128)(2,1)S(1)}, u32[]{:S(2)}, u32[]{:S(2)}) %collective-permute-start.3) | collective-permute-done | bytes 294944 | tf_op jit(solution)/shard_map/weight_one/ppermute | solution.py:28
  53.0 1.2 %pad_maximum_fusion.1.mine = bf16[4,8,48,384]{3,2,1,0:T(8,128)(2,1)} fusion(bf16[1,8,48,384]{3,2,1,0:T(8,128)(2,1)S(1)} %bitcast.54, bf16[1,8,48,384]{3,2,1,0:T(8,128)(2,1)S(1)} %bitcast.56, bf16[1,8,48,384]{3,2,1,0:T(8,128)(2,1)S(1)} %bitcast.58, bf16[1,8,48,384]{3,2,1,0:T(8,128)(2,1)S(1)} %get-tuple-element.33), kind=kLoop, calls=%fused_computation.1 | loop fusion | flops 1769472 | bytes 2359296 | tf_op jit(solution)/shard_map/weight_one/stack | solution.py:36
  54.2 0.1 collective-permute-start.7
  54.3 0.2 reduce-window_clone.1
  54.5 0.1 pad_add_fusion.place
  54.6 0.2 fusion.29
  54.8 0.1 compare_convert_fusion.valid
  54.9 0.1 collective-permute-start.9
  55.0 1.8 %collective-permute-start.10 = (bf16[8,48,384]{2,1,0:T(8,128)(2,1)S(1)}, bf16[8,48,384]{2,1,0:T(8,128)(2,1)S(1)}, u32[]{:S(2)}, u32[]{:S(2)}) collective-permute-start(bf16[8,48,384]{2,1,0:T(8,128)(2,1)S(1)} %slice.26), channel_id=1, source_target_pairs={{0,2},{1,3},{2,0},{3,1},{4,6},{5,7},{6,4},{7,5},{8,10},{9,11},{10,... | collective-permute-start | bytes 884744 | tf_op jit(solution)/shard_map/weight_two/ppermute | solution.py:28
  56.8 1.5 %collective-permute-start.11 = (bf16[8,48,384]{2,1,0:T(8,128)(2,1)S(1)}, bf16[8,48,384]{2,1,0:T(8,128)(2,1)S(1)}, u32[]{:S(2)}, u32[]{:S(2)}) collective-permute-start(bf16[8,48,384]{2,1,0:T(8,128)(2,1)S(1)} %slice.26), channel_id=1, source_target_pairs={{0,3},{1,0},{2,1},{3,2},{4,7},{5,4},{6,5},{7,6},{8,11},{9,8},{10,9... | collective-permute-start | bytes 884744 | tf_op jit(solution)/shard_map/weight_two/ppermute | solution.py:28
  58.3 0.0 collective-permute-done.7.other
  58.3 9.2 %conv_one.1 = f32[2,12,64,128]{3,2,1,0:T(8,128)S(1)} custom-call(f32[2,3]{1,0:T(2,128)S(1)} %compare_convert_fusion.valid, s32[3]{0:T(128)S(1)} %pad_add_fusion.place, bf16[4,2,3,64,384]{4,3,2,1,0:T(8,128)(2,1)S(1)} %collective-permute-done.6.halo, bf16[4,2,3,64,384]{4,3,2,1,0:T(8,128)(2,1)} %copy-done.2, bf16[4,8,48,384]{3,2,1,0:T(8,128)(2,1)} %pad_maximum_fusion.1.mine, ...), custom_call_target="tpu_custom_call" | custom-call | flops 4076863488 | bytes 6000000 | tf_op jit(solution)/shard_map/first/conv_one/pallas_call | solution.py:169
  67.5 0.3 multiply_reduce_fusion
  67.8 0.1 collective-permute-start.8
  67.9 3.7 %collective-permute-done.8 = f32[2,12,64]{2,1,0:T(8,128)S(1)} collective-permute-done((f32[2,12,64]{2,1,0:T(8,128)S(1)}, f32[2,12,64]{2,1,0:T(8,128)S(1)}, u32[]{:S(2)}, u32[]{:S(2)}) %collective-permute-start.8) | collective-permute-done | bytes 6176 | tf_op jit(solution)/shard_map/weight_two/ppermute | solution.py:32
  71.6 0.2 collective-permute-done.9
  71.8 0.0 collective-permute-done.10
  71.8 0.6 collective-permute-done.11
  72.4 0.2 pad_maximum_fusion.2.mine
  72.6 0.1 collective-permute-start.14
  72.7 1.2 %collective-permute-start.12 = (f32[2,12,64]{2,1,0:T(8,128)S(1)}, f32[2,12,64]{2,1,0:T(8,128)S(1)}, u32[]{:S(2)}, u32[]{:S(2)}) collective-permute-start(f32[2,12,64]{2,1,0:T(8,128)S(1)} %add.99), channel_id=1, source_target_pairs={{0,8},{4,12},{8,0},{12,4},{1,9},{5,13},{9,1},{13,5},{2,10},{6,14},... | collective-permute-start | bytes 18440 | tf_op jit(solution)/shard_map/second/ppermute | solution.py:32
  74.0 0.1 reshape.33
  74.1 0.2 dynamic-slice_reduce_fusion
  74.3 3.8 %collective-permute-done.12 = f32[2,12,64]{2,1,0:T(8,128)S(1)} collective-permute-done((f32[2,12,64]{2,1,0:T(8,128)S(1)}, f32[2,12,64]{2,1,0:T(8,128)S(1)}, u32[]{:S(2)}, u32[]{:S(2)}) %collective-permute-start.12) | collective-permute-done | bytes 6176 | tf_op jit(solution)/shard_map/second/ppermute | solution.py:32
  78.1 0.3 multiply_convert_fusion.own
  78.4 2.1 %collective-permute-start.13 = (bf16[2,12,64,128]{3,2,1,0:T(8,128)(2,1)S(1)}, bf16[2,12,64,128]{3,2,1,0:T(8,128)(2,1)S(1)}, u32[]{:S(2)}, u32[]{:S(2)}) collective-permute-start(bf16[2,12,64,128]{3,2,1,0:T(8,128)(2,1)S(1)} %multiply_convert_fusion.own), channel_id=1, source_target_pairs={{0,16},{16,32},{32,48},{48,64},{64,80},{80,96},{96,112},{112,128},... | collective-permute-start | bytes 1179656 | tf_op jit(solution)/shard_map/second/ppermute | solution.py:23
  80.5 3.9 %assemble_two.1.weight = bf16[3456,384]{1,0:T(8,128)(2,1)} custom-call(s32[3]{0:T(128)S(1)} %pad_add_fusion.place, bf16[4,8,48,384]{3,2,1,0:T(8,128)(2,1)S(1)} %pad_maximum_fusion.2.mine, bf16[4,8,48,384]{3,2,1,0:T(8,128)(2,1)} %collective-permute-done.14.other), custom_call_target="tpu_custom_call" | custom-call | flops 4000000 | bytes 5000000 | tf_op jit(solution)/shard_map/weight_two/assemble_two/pallas_call | solution.py:239
  84.5 3.0 %collective-permute-done.13.halo = bf16[2,12,64,128]{3,2,1,0:T(8,128)(2,1)S(1)} collective-permute-done((bf16[2,12,64,128]{3,2,1,0:T(8,128)(2,1)S(1)}, bf16[2,12,64,128]{3,2,1,0:T(8,128)(2,1)S(1)}, u32[]{:S(2)}, u32[]{:S(2)}) %collective-permute-start.13) | collective-permute-done | bytes 393248 | tf_op jit(solution)/shard_map/second/ppermute | solution.py:23
  87.5 7.3 %conv_two.1 = (bf16[2,3,64,384]{3,2,1,0:T(8,128)(2,1)S(1)}, bf16[2,3,64,384]{3,2,1,0:T(8,128)(2,1)S(1)}, bf16[2,3,64,384]{3,2,1,0:T(8,128)(2,1)S(1)}, bf16[2,3,64,384]{3,2,1,0:T(8,128)(2,1)S(1)}) custom-call(f32[2,3]{1,0:T(2,128)S(1)} %compare_convert_fusion.valid, s32[3]{0:T(128)S(1)} %pad_add_fusion.place, ...), custom_call_target="tpu_custom_call" | custom-call | flops 4076863488 | bytes 6000000 | tf_op jit(solution)/shard_map/second/conv_two/pallas_call | solution.py:190
  94.8 1.0 collective-permute-start.17
  95.8 0.8 collective-permute-start.16
  96.6 0.8 collective-permute-start.15
  97.4 7.4 %collective-permute-done.17 = bf16[2,3,64,384]{3,2,1,0:T(8,128)(2,1)S(1)} collective-permute-done((bf16[2,3,64,384]{3,2,1,0:T(8,128)(2,1)S(1)}, bf16[2,3,64,384]{3,2,1,0:T(8,128)(2,1)S(1)}, u32[]{:S(2)}, u32[]{:S(2)}) %collective-permute-start.17) | collective-permute-done | bytes 294944 | tf_op jit(solution)/shard_map/second/ppermute | solution.py:28
  104.8 2.5 %collective-permute-done.16 = bf16[2,3,64,384]{3,2,1,0:T(8,128)(2,1)S(1)} collective-permute-done((bf16[2,3,64,384]{3,2,1,0:T(8,128)(2,1)S(1)}, bf16[2,3,64,384]{3,2,1,0:T(8,128)(2,1)S(1)}, u32[]{:S(2)}, u32[]{:S(2)}) %collective-permute-start.16) | collective-permute-done | bytes 294944 | tf_op jit(solution)/shard_map/second/ppermute | solution.py:28
  107.3 3.8 %collective-permute-done.15 = bf16[2,3,64,384]{3,2,1,0:T(8,128)(2,1)S(1)} collective-permute-done((bf16[2,3,64,384]{3,2,1,0:T(8,128)(2,1)S(1)}, bf16[2,3,64,384]{3,2,1,0:T(8,128)(2,1)S(1)}, u32[]{:S(2)}, u32[]{:S(2)}) %collective-permute-start.15) | collective-permute-done | bytes 294944 | tf_op jit(solution)/shard_map/second/ppermute | solution.py:28
  111.0 0.2 fusion.12
  111.2 0.7 broadcast_in_dim.16
  111.9 1.3 %broadcast_in_dim_reshape.3 = bf16[1,2,6,128,384]{4,3,2,1,0:T(8,128)(2,1)} reshape(bf16[2,3,2,64,2,384]{5,4,3,2,1,0:T(2,128)(2,1)S(1)} %broadcast_in_dim.16) | data formatting | bytes 2359296 | tf_op jit(solution)/shard_map/broadcast_in_dim;reshape | solution.py:336
  (23 shorter events, 0.1 us)
Async XLA Ops:
  0.0 1.2 %copy-start = (bf16[162,384]{1,0:T(8,128)(2,1)S(1)}, bf16[162,384]{1,0:T(8,128)(2,1)}, u32[]{:S(2)}) copy-start(bf16[162,384]{1,0:T(8,128)(2,1)} %param.11) | copy-start | bytes 373252
  1.2 9.8 %copy-start.1 = (bf16[1,2,3,64,384]{4,3,2,1,0:T(8,128)(2,1)S(1)}, bf16[1,2,3,64,384]{4,3,2,1,0:T(8,128)(2,1)}, u32[]{:S(2)}) copy-start(bf16[1,2,3,64,384]{4,3,2,1,0:T(8,128)(2,1)} %param.6) | copy-start | bytes 884740
  1.4 9.7 %copy-start.3 = (f32[384]{0:T(512)S(1)}, f32[384]{0:T(512)}, u32[]{:S(2)}) copy-start(f32[384]{0:T(512)} %param.8) | copy-start | bytes 4612
  2.4 27.8 %all-to-all-start = ((bf16[8,96,384]{2,1,0:T(8,128)(2,1)}), bf16[8,96,384]{2,1,0:T(8,128)(2,1)S(1)}, u32[]{:S(2)}, u32[]{:S(2)}) async-start(bf16[8,96,384]{2,1,0:T(8,128)(2,1)} %broadcast_in_dim.15), calls=%async_computation | async-start | bytes 1179648 | tf_op jit(solution)/shard_map/pieces/all_to_all | solution.py:285
  11.4 14.9 %collective-permute-start.2 = (bf16[2,3,64,384]{3,2,1,0:T(8,128)(2,1)S(1)}, bf16[2,3,64,384]{3,2,1,0:T(8,128)(2,1)S(1)}, u32[]{:S(2)}, u32[]{:S(2)}) collective-permute-start(bf16[2,3,64,384]{3,2,1,0:T(8,128)(2,1)S(1)} %fusion.11), channel_id=1, source_target_pairs={{0,12},{4,0},{8,4},{12,8},{1,13},{5,1},{9,5},{13,9},{2,14},{6,2},{... | collective-permute-start | bytes 884744 | tf_op jit(solution)/shard_map/pixels/ppermute | solution.py:28
  14.3 12.1 %collective-permute-start.1 = (bf16[2,3,64,384]{3,2,1,0:T(8,128)(2,1)S(1)}, bf16[2,3,64,384]{3,2,1,0:T(8,128)(2,1)S(1)}, u32[]{:S(2)}, u32[]{:S(2)}) collective-permute-start(bf16[2,3,64,384]{3,2,1,0:T(8,128)(2,1)S(1)} %fusion.11), channel_id=1, source_target_pairs={{0,8},{4,12},{8,0},{12,4},{1,9},{5,13},{9,1},{13,5},{2,10},{6,14},... | collective-permute-start | bytes 884744 | tf_op jit(solution)/shard_map/pixels/ppermute | solution.py:28
  15.1 14.9 %collective-permute-start = (bf16[2,3,64,384]{3,2,1,0:T(8,128)(2,1)S(1)}, bf16[2,3,64,384]{3,2,1,0:T(8,128)(2,1)S(1)}, u32[]{:S(2)}, u32[]{:S(2)}) collective-permute-start(bf16[2,3,64,384]{3,2,1,0:T(8,128)(2,1)S(1)} %fusion.11), channel_id=1, source_target_pairs={{0,4},{4,8},{8,12},{12,0},{1,5},{5,9},{9,13},{13,1},{2,6},{6,10},{... | collective-permute-start | bytes 884744 | tf_op jit(solution)/shard_map/pixels/ppermute | solution.py:28
  30.2 24.0 %copy-start.2 = (bf16[4,2,3,64,384]{4,3,2,1,0:T(8,128)(2,1)}, bf16[4,2,3,64,384]{4,3,2,1,0:T(8,128)(2,1)S(1)}, u32[]{:S(2)}) copy-start(bf16[4,2,3,64,384]{4,3,2,1,0:T(8,128)(2,1)S(1)} %pad_maximum_fusion.own) | copy-start | bytes 3538948
  30.2 24.0 %collective-permute-start.6 = (bf16[4,2,3,64,384]{4,3,2,1,0:T(8,128)(2,1)S(1)}, bf16[4,2,3,64,384]{4,3,2,1,0:T(8,128)(2,1)S(1)}, u32[]{:S(2)}, u32[]{:S(2)}) collective-permute-start(bf16[4,2,3,64,384]{4,3,2,1,0:T(8,128)(2,1)S(1)} %pad_maximum_fusion.own), channel_id=1, source_target_pairs={{0,16},{16,32},{32,48},{48,64},{64,80},{80,96},{96,112},{112,128},... | collective-permute-start | bytes 3538952 | tf_op jit(solution)/shard_map/weight_one/ppermute | solution.py:23
  32.2 16.1 %collective-permute-start.5 = (bf16[8,48,384]{2,1,0:T(8,128)(2,1)S(1)}, bf16[8,48,384]{2,1,0:T(8,128)(2,1)S(1)}, u32[]{:S(2)}, u32[]{:S(2)}) collective-permute-start(bf16[8,48,384]{2,1,0:T(8,128)(2,1)S(1)} %get-tuple-element.34), channel_id=1, source_target_pairs={{0,3},{1,0},{2,1},{3,2},{4,7},{5,4},{6,5},{7,6},{8,11},{9,8},{10,9... | collective-permute-start | bytes 884744 | tf_op jit(solution)/shard_map/weight_one/ppermute | solution.py:28
  35.3 13.1 %collective-permute-start.4 = (bf16[8,48,384]{2,1,0:T(8,128)(2,1)S(1)}, bf16[8,48,384]{2,1,0:T(8,128)(2,1)S(1)}, u32[]{:S(2)}, u32[]{:S(2)}) collective-permute-start(bf16[8,48,384]{2,1,0:T(8,128)(2,1)S(1)} %get-tuple-element.34), channel_id=1, source_target_pairs={{0,2},{1,3},{2,0},{3,1},{4,6},{5,7},{6,4},{7,5},{8,10},{9,11},{10,... | collective-permute-start | bytes 884744 | tf_op jit(solution)/shard_map/weight_one/ppermute | solution.py:28
  35.9 17.1 %collective-permute-start.3 = (bf16[8,48,384]{2,1,0:T(8,128)(2,1)S(1)}, bf16[8,48,384]{2,1,0:T(8,128)(2,1)S(1)}, u32[]{:S(2)}, u32[]{:S(2)}) collective-permute-start(bf16[8,48,384]{2,1,0:T(8,128)(2,1)S(1)} %get-tuple-element.34), channel_id=1, source_target_pairs={{0,1},{1,2},{2,3},{3,0},{4,5},{5,6},{6,7},{7,4},{8,9},{9,10},{10,1... | collective-permute-start | bytes 884744 | tf_op jit(solution)/shard_map/weight_one/ppermute | solution.py:28
  53.0 1.4 %copy-start.5 = (s32[1,4]{1,0:T(1,128)S(1)}, s32[1,4]{1,0:T(1,128)}, u32[]{:S(2)}) copy-start(s32[1,4]{1,0:T(1,128)} %param.7) | copy-start | bytes 52
  54.2 4.1 %collective-permute-start.7 = (bf16[4,8,48,384]{3,2,1,0:T(8,128)(2,1)}, bf16[4,8,48,384]{3,2,1,0:T(8,128)(2,1)}, u32[]{:S(2)}, u32[]{:S(2)}) collective-permute-start(bf16[4,8,48,384]{3,2,1,0:T(8,128)(2,1)} %pad_maximum_fusion.1.mine), channel_id=1, source_target_pairs={{0,16},{16,0},{1,17},{17,1},{2,18},{18,2},{3,19},{19,3},{4,20},{20... | collective-permute-start | bytes 3538952 | tf_op jit(solution)/shard_map/weight_one/ppermute | solution.py:292
  54.9 16.9 %collective-permute-start.9 = (bf16[8,48,384]{2,1,0:T(8,128)(2,1)S(1)}, bf16[8,48,384]{2,1,0:T(8,128)(2,1)S(1)}, u32[]{:S(2)}, u32[]{:S(2)}) collective-permute-start(bf16[8,48,384]{2,1,0:T(8,128)(2,1)S(1)} %slice.26), channel_id=1, source_target_pairs={{0,1},{1,2},{2,3},{3,0},{4,5},{5,6},{6,7},{7,4},{8,9},{9,10},{10,1... | collective-permute-start | bytes 884744 | tf_op jit(solution)/shard_map/weight_two/ppermute | solution.py:28
  55.0 16.8 %collective-permute-start.10 = (bf16[8,48,384]{2,1,0:T(8,128)(2,1)S(1)}, bf16[8,48,384]{2,1,0:T(8,128)(2,1)S(1)}, u32[]{:S(2)}, u32[]{:S(2)}) collective-permute-start(bf16[8,48,384]{2,1,0:T(8,128)(2,1)S(1)} %slice.26), channel_id=1, source_target_pairs={{0,2},{1,3},{2,0},{3,1},{4,6},{5,7},{6,4},{7,5},{8,10},{9,11},{10,... | collective-permute-start | bytes 884744 | tf_op jit(solution)/shard_map/weight_two/ppermute | solution.py:28
  56.8 15.7 %collective-permute-start.11 = (bf16[8,48,384]{2,1,0:T(8,128)(2,1)S(1)}, bf16[8,48,384]{2,1,0:T(8,128)(2,1)S(1)}, u32[]{:S(2)}, u32[]{:S(2)}) collective-permute-start(bf16[8,48,384]{2,1,0:T(8,128)(2,1)S(1)} %slice.26), channel_id=1, source_target_pairs={{0,3},{1,0},{2,1},{3,2},{4,7},{5,4},{6,5},{7,6},{8,11},{9,8},{10,9... | collective-permute-start | bytes 884744 | tf_op jit(solution)/shard_map/weight_two/ppermute | solution.py:28
  67.8 3.8 %collective-permute-start.8 = (f32[2,12,64]{2,1,0:T(8,128)S(1)}, f32[2,12,64]{2,1,0:T(8,128)S(1)}, u32[]{:S(2)}, u32[]{:S(2)}) collective-permute-start(f32[2,12,64]{2,1,0:T(8,128)S(1)} %multiply_reduce_fusion), channel_id=1, source_target_pairs={{0,4},{4,0},{8,12},{12,8},{1,5},{5,1},{9,13},{13,9},{2,6},{6,2},{1... | collective-permute-start | bytes 18440 | tf_op jit(solution)/shard_map/weight_two/ppermute | solution.py:32
  72.4 1.5 %copy-start.4 = (f32[384]{0:T(512)S(1)}, f32[384]{0:T(512)}, u32[]{:S(2)}) copy-start(f32[384]{0:T(512)} %param.9) | copy-start | bytes 4612
  72.6 7.9 %collective-permute-start.14 = (bf16[4,8,48,384]{3,2,1,0:T(8,128)(2,1)S(1)}, bf16[4,8,48,384]{3,2,1,0:T(8,128)(2,1)}, u32[]{:S(2)}, u32[]{:S(2)}) collective-permute-start(bf16[4,8,48,384]{3,2,1,0:T(8,128)(2,1)S(1)} %pad_maximum_fusion.2.mine), channel_id=1, source_target_pairs={{0,16},{16,0},{1,17},{17,1},{2,18},{18,2},{3,19},{19,3},{4,20},{20... | collective-permute-start | bytes 3538952 | tf_op jit(solution)/shard_map/weight_two/ppermute | solution.py:314
  72.7 5.3 %collective-permute-start.12 = (f32[2,12,64]{2,1,0:T(8,128)S(1)}, f32[2,12,64]{2,1,0:T(8,128)S(1)}, u32[]{:S(2)}, u32[]{:S(2)}) collective-permute-start(f32[2,12,64]{2,1,0:T(8,128)S(1)} %add.99), channel_id=1, source_target_pairs={{0,8},{4,12},{8,0},{12,4},{1,9},{5,13},{9,1},{13,5},{2,10},{6,14},... | collective-permute-start | bytes 18440 | tf_op jit(solution)/shard_map/second/ppermute | solution.py:32
  78.4 9.1 %collective-permute-start.13 = (bf16[2,12,64,128]{3,2,1,0:T(8,128)(2,1)S(1)}, bf16[2,12,64,128]{3,2,1,0:T(8,128)(2,1)S(1)}, u32[]{:S(2)}, u32[]{:S(2)}) collective-permute-start(bf16[2,12,64,128]{3,2,1,0:T(8,128)(2,1)S(1)} %multiply_convert_fusion.own), channel_id=1, source_target_pairs={{0,16},{16,32},{32,48},{48,64},{64,80},{80,96},{96,112},{112,128},... | collective-permute-start | bytes 1179656 | tf_op jit(solution)/shard_map/second/ppermute | solution.py:23
  94.8 10.0 %collective-permute-start.17 = (bf16[2,3,64,384]{3,2,1,0:T(8,128)(2,1)S(1)}, bf16[2,3,64,384]{3,2,1,0:T(8,128)(2,1)S(1)}, u32[]{:S(2)}, u32[]{:S(2)}) collective-permute-start(bf16[2,3,64,384]{3,2,1,0:T(8,128)(2,1)S(1)} %get-tuple-element.32), channel_id=1, source_target_pairs={{0,12},{4,0},{8,4},{12,8},{1,13},{5,1},{9,5},{13,9},{2,14},{6,2},{... | collective-permute-start | bytes 884744 | tf_op jit(solution)/shard_map/second/ppermute | solution.py:28
  95.8 11.5 %collective-permute-start.16 = (bf16[2,3,64,384]{3,2,1,0:T(8,128)(2,1)S(1)}, bf16[2,3,64,384]{3,2,1,0:T(8,128)(2,1)S(1)}, u32[]{:S(2)}, u32[]{:S(2)}) collective-permute-start(bf16[2,3,64,384]{3,2,1,0:T(8,128)(2,1)S(1)} %get-tuple-element.31), channel_id=1, source_target_pairs={{0,8},{4,12},{8,0},{12,4},{1,9},{5,13},{9,1},{13,5},{2,10},{6,14},... | collective-permute-start | bytes 884744 | tf_op jit(solution)/shard_map/second/ppermute | solution.py:28
  96.6 14.4 %collective-permute-start.15 = (bf16[2,3,64,384]{3,2,1,0:T(8,128)(2,1)S(1)}, bf16[2,3,64,384]{3,2,1,0:T(8,128)(2,1)S(1)}, u32[]{:S(2)}, u32[]{:S(2)}) collective-permute-start(bf16[2,3,64,384]{3,2,1,0:T(8,128)(2,1)S(1)} %get-tuple-element.30), channel_id=1, source_target_pairs={{0,4},{4,8},{8,12},{12,0},{1,5},{5,9},{9,13},{13,1},{2,6},{6,10},{... | collective-permute-start | bytes 884744 | tf_op jit(solution)/shard_map/second/ppermute | solution.py:28

commit v7 on v6

--- a/solution.py
+++ b/solution.py
@@ -30,6 +30,12 @@
 
 def across(x, bit):
     return lax.ppermute(x, "tile", [(i, i ^ bit) for i in range(lax.axis_size("tile"))])
+
+
+def ring(x, axis):
+    low, high = onward(x, 1, axis), onward(x, -1, axis)
+    half = x.shape[0] // 2
+    return [x, low, high, onward(low[:half], 1, axis), onward(high[half:], -1, axis)]
 
 
 def from_all(x, axis):
@@ -56,17 +62,15 @@
             taps[e, slot, rows - 1] = blank
 
 
-def assemble_one(place, mine, other, out, wide):
-    ys, zs, _, lanes = mine.shape
-    shard = out.shape[0] // (2 * ys * zs)
+def assemble_one(pieces, out, wide):
+    cores, ys, zs, _, lanes = pieces.shape
+    shard = out.shape[0] // (cores * ys * zs)
     share = lanes // 4
     piece_rows = shard // 4 + 1
-    for pieces, core in ((mine, place[0]), (other, 1 - place[0])):
-        for z in range(zs):
-            top = pl.multiple_of((2 * z + core) * (ys * shard), 8)
-            view = wide.at[pl.ds(top, ys * shard), :]
+    for z in range(zs):
+        for c in range(cores):
             for y in range(ys):
-                piece = pieces[lax.rem(place[1] + ys - y, ys), z].astype(jnp.float32)
+                piece = pieces[c, y, z].astype(jnp.float32)
                 for j in range(4):
                     rows = min(piece_rows, shard - j * piece_rows)
                     low = (j * share) // LANE * LANE
@@ -74,24 +78,48 @@
                     shift = j * share - low
                     if shift:
                         window = pltpu.roll(window, window.shape[1] - shift, 1)
-                    first = shard * y + j * piece_rows
-                    view[first : first + rows, :] = window[:rows, :LANE]
+                    first = shard * (z * cores * ys + c * ys + y) + j * piece_rows
+                    wide[first : first + rows, :] = window[:rows, :LANE]
     out[...] = wide[...].astype(out.dtype)
 
 
-def conv_one_kernel(share, valid, place, halo, own, mine, other, out, frame_buf, acc, weight, wide):
-    parts, frames, each, width, channels = own.shape
-    rows = parts * each
-    blank = jnp.zeros((width, channels), own.dtype)
+def conv_one_kernel(share, valid, place, *refs):
+    own_refs, halo_refs, mine_refs, other_refs = refs[:5], refs[5:8], refs[8:13], refs[13:15]
+    out, frame_buf, acc, weight, wide, pieces = refs[15:]
+    frames, each, width, channels = own_refs[0].shape
+    rows = out.shape[1]
+    parts = rows // each
+    cores, ys, zs = pieces.shape[:3]
+    blank = jnp.zeros((width, channels), frame_buf.dtype)
     for slot in range(2 * frames):
         frame_buf[slot, 0] = blank
         frame_buf[slot, rows + 1] = blank
-        source = halo if slot < frames else own
-        for back in range(parts):
-            top = lax.rem(place[2] + parts - back, parts) * each + 1
-            for j in range(each):
-                frame_buf[slot, top + j] = source[back, slot % frames, j]
-    assemble_one(place, mine, other, weight, wide)
+
+    def put(slot, back, block):
+        top = lax.rem(place[2] + parts - back, parts) * each + 1
+        for j in range(each):
+            frame_buf[slot, top + j] = block[j]
+
+    for s in range(frames):
+        for back, ref in zip((0, 1, 3), own_refs):
+            put(frames + s, back, ref[s])
+        put(frames + s, 2, own_refs[3 + s][0])
+        put(s, 0, halo_refs[0][s])
+        put(s, 1, halo_refs[1][0, s])
+        put(s, 3, halo_refs[1][1, s])
+        put(s, 2, halo_refs[2][s])
+    half = zs // 2
+    for c, third in ((place[0], lambda i: mine_refs[i]), (1 - place[0], lambda i: other_refs[0].at[i])):
+        for i, back in enumerate((0, 1, 3)):
+            source = third(i)
+            y = lax.rem(place[1] + ys - back, ys)
+            for z in range(zs):
+                pieces[c, y, z] = source[z]
+    y = lax.rem(place[1] + ys - 2, ys)
+    for z in range(zs):
+        pieces[place[0], y, z] = mine_refs[3 + z // half][z % half]
+        pieces[1 - place[0], y, z] = other_refs[1][z]
+    assemble_one(pieces, weight, wide)
     for slot in range(2 * frames):
         pairs = [(s, slot - s) for s in range(frames) if 0 <= slot - s < 3]
         columns = jnp.concatenate(
@@ -120,11 +148,10 @@
         out[s] = done.reshape(rows, width, LANE)
 
 
-def conv_two_kernel(valid, place, halo, own, weight, *rest):
-    *outs, taps, acc = rest
+def conv_two_kernel(valid, place, halo, own, weight, own_sum, up, down, up_last, down_last, taps, acc):
     frames, rows, width, lanes = own.shape
-    parts = len(outs)
-    each = rows // parts
+    each = own_sum.shape[1]
+    parts = rows // each
     channels = weight.shape[1]
     clear_border(taps)
     for slot in range(2 * frames):
@@ -150,11 +177,11 @@
                 acc[s] = piece
             else:
                 acc[s] = acc[s] + piece
-    for d in range(parts):
+    for ref, d, s, at in ((own_sum, 0, 0, 0), (own_sum, 0, 1, 1), (up, 2, 0, 0), (up, 1, 1, 1),
+                          (down, 3, 0, 0), (down, 2, 1, 1), (up_last, 1, 0, 0), (down_last, 3, 1, 0)):
         top = pl.multiple_of(lax.rem(place[2] + d, parts) * (each * width), 64)
-        for s in range(frames):
-            done = acc[s, pl.ds(top, each * width), :].astype(outs[d].dtype)
-            outs[d][s] = done.reshape(each, width, channels)
+        done = acc[s, pl.ds(top, each * width), :].astype(ref.dtype)
+        ref[at] = done.reshape(each, width, channels)
 
 
 VMEM = pl.BlockSpec(memory_space=pltpu.VMEM)
@@ -162,36 +189,40 @@
 PARAMS = pltpu.CompilerParams(vmem_limit_bytes=52 * 1024 * 1024)
 
 
-def conv_one_call(valid, place, halo, own, mine, other):
-    parts, frames, each, width, channels = own.shape
-    rows = parts * each
+def conv_one_call(valid, place, own, halo, mine, other):
+    frames, each, width, channels = own[0].shape
+    rows = each * lax.axis_size("tile")
+    zs, piece_rows, lanes = mine[0].shape
     flops = 2 * 6 * rows * width * 9 * channels * LANE
+    arrays = [*own, *halo, *mine, *other]
     return pl.pallas_call(
-        functools.partial(conv_one_kernel, channels // parts),
+        functools.partial(conv_one_kernel, channels * each // rows),
         out_shape=jax.ShapeDtypeStruct((frames, rows, width, LANE), jnp.float32),
-        in_specs=[SMEM, SMEM, VMEM, VMEM, VMEM, VMEM],
+        in_specs=[SMEM, SMEM] + [VMEM] * len(arrays),
         out_specs=VMEM,
         scratch_shapes=[
             pltpu.VMEM((2 * frames, rows + 2, width, channels), jnp.bfloat16),
             pltpu.VMEM((frames, 3, rows * width, LANE), jnp.float32),
             pltpu.VMEM((27 * channels, LANE), jnp.bfloat16),
             pltpu.VMEM((27 * channels, LANE), jnp.float32),
+            pltpu.VMEM((2, lax.axis_size("group"), zs, piece_rows, lanes), jnp.bfloat16),
         ],
         compiler_params=PARAMS,
         cost_estimate=pl.CostEstimate(flops=flops, bytes_accessed=6_000_000, transcendentals=0),
         name="conv_one",
-    )(valid, place, halo, own, mine, other)
+    )(valid, place, *arrays)
 
 
 def conv_two_call(valid, place, halo, own, weight, parts):
     frames, rows, width, lanes = own.shape
     channels = weight.shape[1]
     flops = 2 * 6 * rows * width * 9 * lanes * channels
+    shapes = [(n, rows // parts, width, channels) for n in (frames, frames, frames, 1, 1)]
     return pl.pallas_call(
         conv_two_kernel,
-        out_shape=[jax.ShapeDtypeStruct((frames, rows // parts, width, channels), jnp.bfloat16)] * parts,
+        out_shape=[jax.ShapeDtypeStruct(shape, jnp.bfloat16) for shape in shapes],
         in_specs=[SMEM, SMEM, VMEM, VMEM, VMEM],
-        out_specs=[VMEM] * parts,
+        out_specs=[VMEM] * len(shapes),
         scratch_shapes=[
             pltpu.VMEM((3, 2 * frames, rows + 2, width, lanes), jnp.bfloat16),
             pltpu.VMEM((frames, rows * width, channels), jnp.float32),
@@ -271,7 +302,8 @@
     with jax.named_scope("pixels"):
         mean_sq = jnp.mean(source * source, axis=-1, keepdims=True)
         hidden_one = jax.nn.silu(source * lax.rsqrt(mean_sq + EPS) * gain_one).astype(jnp.bfloat16)
-        own_all = from_all(hidden_one, "tile")
+        own = ring(hidden_one, "tile")
+        halo = [earlier(own[0]), earlier(jnp.stack(own[1:3])), earlier(jnp.concatenate(own[3:]))]
 
     with jax.named_scope("pieces"):
         take = pick(channels, share, False, part, parts)
@@ -284,13 +316,12 @@
         pieces = jnp.concatenate([piece, piece_two], axis=0)
         column = lax.all_to_all(jnp.broadcast_to(pieces, (lax.axis_size("z"),) + pieces.shape), "z", 0, 0)
 
-    column, own_all = lax.optimization_barrier((column, own_all))
+    def other_core(x):
+        return lax.ppermute(x, "core", [(0, 1), (1, 0)])
+
     with jax.named_scope("weight_one"):
-        mine = from_all(column[:, :TILE_ROWS], "group")
-        prior_all = earlier(own_all)
-        mine, prior_all = lax.optimization_barrier((mine, prior_all))
-        swapped = lax.ppermute(mine, "core", [(0, 1), (1, 0)])
-        one_mine, one_swapped = mine, swapped
+        mine = ring(column[:, :TILE_ROWS], "group")
+        swapped = [other_core(jnp.stack(mine[:3])), other_core(jnp.concatenate(mine[3:]))]
 
     with jax.named_scope("weight_two"):
         column, _ = lax.optimization_barrier((column, mine))
@@ -304,14 +335,14 @@
     valid = (slots[:, None] - before[None, :] >= begins[:, None]).astype(jnp.float32)
 
     with jax.named_scope("first"):
-        first = conv_one_call(valid, place, prior_all, own_all, one_mine, one_swapped)
+        first = conv_one_call(valid, place, own, halo, mine, swapped)
 
     with jax.named_scope("weight_two"):
         squares = jnp.sum(first * first, axis=-1)
         squares = squares + across(squares, 1)
         squares, later = lax.optimization_barrier((squares, later))
         mine = jnp.stack(later)
-        swapped = lax.ppermute(mine, "core", [(0, 1), (1, 0)])
+        swapped = other_core(mine)
         taps = shards * shard // channels
         weight_two = assemble_call(
             assemble_two_kernel, place, mine, swapped, (taps * LANE, channels),
@@ -325,9 +356,14 @@
         scale = lax.rsqrt(squares / channels + EPS)
         hidden_two = jax.nn.silu(first * scale[..., None] * gain_mine).astype(jnp.bfloat16)
         prior_two = earlier(hidden_two)
-        sums, *rest = conv_two_call(valid, place, prior_two, hidden_two, weight_two, parts)
-        arrived = [onward(r, d) for d, r in enumerate(rest, 1)]
-        second = sum((r.astype(jnp.float32) for r in arrived), sums.astype(jnp.float32))
+        own_sum, up, down, up_last, down_last = conv_two_call(
+            valid, place, prior_two, hidden_two, weight_two, parts
+        )
+        up, down = onward(up, 1), onward(down, -1)
+        up_last = onward(up_last + up[:1], 1)
+        down_last = onward(down_last + down[1:], -1)
+        arrived = [jnp.concatenate([down[:1], up[1:]]), jnp.concatenate([up_last, down_last])]
+        second = sum((r.astype(jnp.float32) for r in arrived), own_sum.astype(jnp.float32))
 
     block = (source + second).astype(jnp.bfloat16)
     result = jnp.broadcast_to(

time: 114 us -> 121 us (1.061)
  starting transfers between devices: 29.4 us -> 42.9 us
  waiting for transfers between devices: 54.9 us -> 46.6 us
  local copies, waits for them, and re-layouts: 3.29 us -> 4.98 us
    ppermute x12 -> x15, waiting for transfers between devices: 44.3 us -> 16.7 us  [onward(): return lax.ppermute(x, axis, [(i, (i + by) % n) for i in range(n)])]
    all_to_all x1, waiting for transfers between devices: 0.01 us -> 13.5 us  [body(): lax.all_to_all(jnp.broadcast_to(pieces, (lax.axis_size('z'),) + pieces.sh...]
    ppermute x12 -> x15, starting transfers between devices: 15.2 us -> 24.5 us  [onward(): return lax.ppermute(x, axis, [(i, (i + by) % n) for i in range(n)])]
    ppermute x2 -> x4, waiting for transfers between devices: 3.01 us -> 8.5 us  [earlier(): return lax.ppermute(x, SLOT, [(i, i + 1) for i in range(n - 1)])]
    ppermute x2 -> x4, starting transfers between devices: 4.07 us -> 8.08 us  [earlier(): return lax.ppermute(x, SLOT, [(i, i + 1) for i in range(n - 1)])]
    unnamed x12 -> x26, local copies, waits for them, and re-layouts: 0.03 us -> 1.66 us
    another operation x3, other arithmetic: 1.58 us -> 0.37 us  [the longest x2 1.41 us: from_all(): jnp.stack([x] + [onward(x, d, axis) for d in range(1, lax.axis_size(axis))])]
  transfers between devices with their start and end apart: 19 -> 25, of which waited for: 12 -> 12; matrix products, arithmetic and copies ran while one was open for 3% -> 3% of each run, Pallas kernels for 12% -> 11%
where the time goes in v7:
time: 121 us; the launch traced here: 120 us
  waiting for transfers between devices  46.6 us (39%)
  starting transfers between devices  42.9 us (35%)
  Pallas kernels  20.8 us (17%)
  local copies, waits for them, and re-layouts  4.98 us (4%)
  other arithmetic  3.4 us (3%)
  matrix products  1.35 us (1%)
    ppermute x15, starting transfers between devices, onward(): return lax.ppermute(x, axis, [(i, (i + by) % n) for i in range(n)])  24.5 us
    ppermute x15, waiting for transfers between devices, onward(): return lax.ppermute(x, axis, [(i, (i + by) % n) for i in range(n)])  16.7 us
    all_to_all x1, waiting for transfers between devices, body(): lax.all_to_all(jnp.broadcast_to(pieces, (lax.axis_size('z'),) + pieces.sh...  13.5 us
    pallas_call x1, Pallas kernels, conv_one_call(): pl.pallas_call(functools.partial(conv_one_kernel, channels * each // rows...  9.49 us
    all_to_all x1, starting transfers between devices, body(): lax.all_to_all(jnp.broadcast_to(pieces, (lax.axis_size('z'),) + pieces.sh...  8.7 us
    ppermute x4, waiting for transfers between devices, earlier(): return lax.ppermute(x, SLOT, [(i, i + 1) for i in range(n - 1)])  8.5 us
    ppermute x4, starting transfers between devices, earlier(): return lax.ppermute(x, SLOT, [(i, i + 1) for i in range(n - 1)])  8.08 us
    ppermute x2, waiting for transfers between devices, across(): lax.ppermute(x, 'tile', [(i, i ^ bit) for i in range(lax.axis_size('tile'...  7.86 us
  transfers between devices with their start and end apart: 25, of which 12 were waited for; matrix products, arithmetic and copies ran while one was open for 3% of the time, Pallas kernels for 11%

profile of v7, /device:TPU:32, one launch (start us, length us, event | category | flops | bytes accessed | tf_op | source)
XLA Modules:
  0.0 120.4 jit_solution(5473130840743996315)
XLA Ops:
  0.0 1.2 fusion
  1.2 0.2 convolution_convert_fusion.1
  1.4 0.1 fusion.17
  1.6 0.9 broadcast_in_dim.15
  2.4 8.7 %all-to-all-start = ((bf16[8,96,384]{2,1,0:T(8,128)(2,1)}), bf16[8,96,384]{2,1,0:T(8,128)(2,1)S(1)}, u32[]{:S(2)}, u32[]{:S(2)}) async-start(bf16[8,96,384]{2,1,0:T(8,128)(2,1)} %broadcast_in_dim.15), calls=%async_computation | async-start | bytes 1179648 | tf_op jit(solution)/shard_map/pieces/all_to_all | solution.py:317
  11.1 0.1 fusion.1
  11.3 0.3 fusion.8.refs_0_
  11.5 1.6 %collective-permute-start = (bf16[2,3,64,384]{3,2,1,0:T(8,128)(2,1)S(1)}, bf16[2,3,64,384]{3,2,1,0:T(8,128)(2,1)S(1)}, u32[]{:S(2)}, u32[]{:S(2)}) collective-permute-start(bf16[2,3,64,384]{3,2,1,0:T(8,128)(2,1)S(1)} %fusion.8.refs_0_), channel_id=1, source_target_pairs={{0,4},{4,8},{8,12},{12,0},{1,5},{5,9},{9,13},{13,1},{2,6},{6,10},{... | collective-permute-start | bytes 884744 | tf_op jit(solution)/shard_map/pixels/ppermute | solution.py:28
  13.1 1.7 %collective-permute-start.1 = (bf16[2,3,64,384]{3,2,1,0:T(8,128)(2,1)S(1)}, bf16[2,3,64,384]{3,2,1,0:T(8,128)(2,1)S(1)}, u32[]{:S(2)}, u32[]{:S(2)}) collective-permute-start(bf16[2,3,64,384]{3,2,1,0:T(8,128)(2,1)S(1)} %fusion.8.refs_0_), channel_id=1, source_target_pairs={{0,12},{4,0},{8,4},{12,8},{1,13},{5,1},{9,5},{13,9},{2,14},{6,2},{... | collective-permute-start | bytes 884744 | tf_op jit(solution)/shard_map/pixels/ppermute | solution.py:28
  14.9 0.2 reduce-window_clone.1
  15.0 13.5 %all-to-all-done = bf16[8,96,384]{2,1,0:T(8,128)(2,1)S(1)} async-done(((bf16[8,96,384]{2,1,0:T(8,128)(2,1)}), bf16[8,96,384]{2,1,0:T(8,128)(2,1)S(1)}, u32[]{:S(2)}, u32[]{:S(2)}) %all-to-all-start) | async-done | bytes 589856 | tf_op jit(solution)/shard_map/pieces/all_to_all | solution.py:317
  28.6 0.1 slice_bitcast_fusion
  28.6 1.7 %collective-permute-start.7 = (bf16[8,48,384]{2,1,0:T(8,128)(2,1)S(1)}, bf16[8,48,384]{2,1,0:T(8,128)(2,1)S(1)}, u32[]{:S(2)}, u32[]{:S(2)}) collective-permute-start(bf16[8,48,384]{2,1,0:T(8,128)(2,1)S(1)} %get-tuple-element.28.refs_8_), channel_id=1, source_target_pairs={{0,1},{1,2},{2,3},{3,0},{4,5},{5,6},{6,7},{7,4},{8,9},{9,10},{10,1... | collective-permute-start | bytes 884744 | tf_op jit(solution)/shard_map/weight_one/ppermute | solution.py:28
  30.3 1.7 %collective-permute-start.8 = (bf16[8,48,384]{2,1,0:T(8,128)(2,1)S(1)}, bf16[8,48,384]{2,1,0:T(8,128)(2,1)S(1)}, u32[]{:S(2)}, u32[]{:S(2)}) collective-permute-start(bf16[8,48,384]{2,1,0:T(8,128)(2,1)S(1)} %get-tuple-element.28.refs_8_), channel_id=1, source_target_pairs={{0,3},{1,0},{2,1},{3,2},{4,7},{5,4},{6,5},{7,6},{8,11},{9,8},{10,9... | collective-permute-start | bytes 884744 | tf_op jit(solution)/shard_map/weight_one/ppermute | solution.py:28
  32.0 1.6 %collective-permute-start.2 = (bf16[1,3,64,384]{3,2,1,0:T(8,128)(2,1)S(1)}, bf16[1,3,64,384]{3,2,1,0:T(8,128)(2,1)S(1)}, u32[]{:S(2)}, u32[]{:S(2)}) collective-permute-start(bf16[1,3,64,384]{3,2,1,0:T(8,128)(2,1)S(1)} %slice.59), channel_id=1, source_target_pairs={{0,4},{4,8},{8,12},{12,0},{1,5},{5,9},{9,13},{13,1},{2,6},{6,10},{... | collective-permute-start | bytes 442376 | tf_op jit(solution)/shard_map/pixels/ppermute | solution.py:28
  33.6 3.1 %collective-permute-done.7.refs_9_ = bf16[8,48,384]{2,1,0:T(8,128)(2,1)S(1)} collective-permute-done((bf16[8,48,384]{2,1,0:T(8,128)(2,1)S(1)}, bf16[8,48,384]{2,1,0:T(8,128)(2,1)S(1)}, u32[]{:S(2)}, u32[]{:S(2)}) %collective-permute-start.7) | collective-permute-done | bytes 294944 | tf_op jit(solution)/shard_map/weight_one/ppermute | solution.py:28
  36.6 0.4 collective-permute-done.8.refs_10_
  37.0 0.1 pad_maximum_fusion.1
  37.1 0.1 collective-permute-start.11
  37.2 0.2 fusion.19
  37.5 2.8 %collective-permute-start.3 = (bf16[1,3,64,384]{3,2,1,0:T(8,128)(2,1)S(1)}, bf16[1,3,64,384]{3,2,1,0:T(8,128)(2,1)S(1)}, u32[]{:S(2)}, u32[]{:S(2)}) collective-permute-start(bf16[1,3,64,384]{3,2,1,0:T(8,128)(2,1)S(1)} %slice.60), channel_id=1, source_target_pairs={{0,12},{4,0},{8,4},{12,8},{1,13},{5,1},{9,5},{13,9},{2,14},{6,2},{... | collective-permute-start | bytes 442376 | tf_op jit(solution)/shard_map/pixels/ppermute | solution.py:28
  40.3 0.1 pad_maximum_fusion.2
  40.4 2.1 %collective-permute-start.5 = (bf16[2,2,3,64,384]{4,3,2,1,0:T(8,128)(2,1)S(1)}, bf16[2,2,3,64,384]{4,3,2,1,0:T(8,128)(2,1)S(1)}, u32[]{:S(2)}, u32[]{:S(2)}) collective-permute-start(bf16[2,2,3,64,384]{4,3,2,1,0:T(8,128)(2,1)S(1)} %pad_maximum_fusion.2), channel_id=1, source_target_pairs={{0,16},{16,32},{32,48},{48,64},{64,80},{80,96},{96,112},{112,128},... | collective-permute-start | bytes 1769480 | tf_op jit(solution)/shard_map/pixels/ppermute | solution.py:23
  42.5 1.7 %collective-permute-start.9 = (bf16[4,48,384]{2,1,0:T(8,128)(2,1)S(1)}, bf16[4,48,384]{2,1,0:T(8,128)(2,1)S(1)}, u32[]{:S(2)}, u32[]{:S(2)}) collective-permute-start(bf16[4,48,384]{2,1,0:T(8,128)(2,1)S(1)} %slice.65), channel_id=1, source_target_pairs={{0,1},{1,2},{2,3},{3,0},{4,5},{5,6},{6,7},{7,4},{8,9},{9,10},{10,1... | collective-permute-start | bytes 442376 | tf_op jit(solution)/shard_map/weight_one/ppermute | solution.py:28
  44.2 1.7 %collective-permute-start.10 = (bf16[4,48,384]{2,1,0:T(8,128)(2,1)S(1)}, bf16[4,48,384]{2,1,0:T(8,128)(2,1)S(1)}, u32[]{:S(2)}, u32[]{:S(2)}) collective-permute-start(bf16[4,48,384]{2,1,0:T(8,128)(2,1)S(1)} %slice.66), channel_id=1, source_target_pairs={{0,3},{1,0},{2,1},{3,2},{4,7},{5,4},{6,5},{7,6},{8,11},{9,8},{10,9... | collective-permute-start | bytes 442376 | tf_op jit(solution)/shard_map/weight_one/ppermute | solution.py:28
  46.0 1.9 %collective-permute-start.4 = (bf16[2,3,64,384]{3,2,1,0:T(8,128)(2,1)S(1)}, bf16[2,3,64,384]{3,2,1,0:T(8,128)(2,1)S(1)}, u32[]{:S(2)}, u32[]{:S(2)}) collective-permute-start(bf16[2,3,64,384]{3,2,1,0:T(8,128)(2,1)S(1)} %fusion.8.refs_0_), channel_id=1, source_target_pairs={{0,16},{16,32},{32,48},{48,64},{64,80},{80,96},{96,112},{112,128},... | collective-permute-start | bytes 884744 | tf_op jit(solution)/shard_map/pixels/ppermute | solution.py:23
  47.9 1.7 %collective-permute-done.9.refs_11_ = bf16[4,48,384]{2,1,0:T(8,128)(2,1)S(1)} collective-permute-done((bf16[4,48,384]{2,1,0:T(8,128)(2,1)S(1)}, bf16[4,48,384]{2,1,0:T(8,128)(2,1)S(1)}, u32[]{:S(2)}, u32[]{:S(2)}) %collective-permute-start.9) | collective-permute-done | bytes 147488 | tf_op jit(solution)/shard_map/weight_one/ppermute | solution.py:28
  49.6 1.9 %collective-permute-start.6 = (bf16[2,3,64,384]{3,2,1,0:T(8,128)(2,1)S(1)}, bf16[2,3,64,384]{3,2,1,0:T(8,128)(2,1)S(1)}, u32[]{:S(2)}, u32[]{:S(2)}) collective-permute-start(bf16[2,3,64,384]{3,2,1,0:T(8,128)(2,1)S(1)} %pad_maximum_fusion.3), channel_id=1, source_target_pairs={{0,16},{16,32},{32,48},{48,64},{64,80},{80,96},{96,112},{112,128},... | collective-permute-start | bytes 884744 | tf_op jit(solution)/shard_map/pixels/ppermute | solution.py:23
  51.6 0.5 collective-permute-start.12
  52.0 0.1 pad_add_fusion.place
  52.1 0.1 compare_convert_fusion.valid
  52.2 4.0 %collective-permute-done.4.refs_5_ = bf16[2,3,64,384]{3,2,1,0:T(8,128)(2,1)S(1)} collective-permute-done((bf16[2,3,64,384]{3,2,1,0:T(8,128)(2,1)S(1)}, bf16[2,3,64,384]{3,2,1,0:T(8,128)(2,1)S(1)}, u32[]{:S(2)}, u32[]{:S(2)}) %collective-permute-start.4) | collective-permute-done | bytes 294944 | tf_op jit(solution)/shard_map/pixels/ppermute | solution.py:23
  56.2 1.6 %collective-permute-start.14 = (bf16[8,48,384]{2,1,0:T(8,128)(2,1)S(1)}, bf16[8,48,384]{2,1,0:T(8,128)(2,1)S(1)}, u32[]{:S(2)}, u32[]{:S(2)}) collective-permute-start(bf16[8,48,384]{2,1,0:T(8,128)(2,1)S(1)} %slice.54), channel_id=1, source_target_pairs={{0,1},{1,2},{2,3},{3,0},{4,5},{5,6},{6,7},{7,4},{8,9},{9,10},{10,1... | collective-permute-start | bytes 884744 | tf_op jit(solution)/shard_map/weight_two/ppermute | solution.py:28
  57.8 1.6 %collective-permute-done.6.refs_7_ = bf16[2,3,64,384]{3,2,1,0:T(8,128)(2,1)S(1)} collective-permute-done((bf16[2,3,64,384]{3,2,1,0:T(8,128)(2,1)S(1)}, bf16[2,3,64,384]{3,2,1,0:T(8,128)(2,1)S(1)}, u32[]{:S(2)}, u32[]{:S(2)}) %collective-permute-start.6) | collective-permute-done | bytes 294944 | tf_op jit(solution)/shard_map/pixels/ppermute | solution.py:23
  59.4 2.9 %collective-permute-start.15 = (bf16[8,48,384]{2,1,0:T(8,128)(2,1)S(1)}, bf16[8,48,384]{2,1,0:T(8,128)(2,1)S(1)}, u32[]{:S(2)}, u32[]{:S(2)}) collective-permute-start(bf16[8,48,384]{2,1,0:T(8,128)(2,1)S(1)} %slice.54), channel_id=1, source_target_pairs={{0,2},{1,3},{2,0},{3,1},{4,6},{5,7},{6,4},{7,5},{8,10},{9,11},{10,... | collective-permute-start | bytes 884744 | tf_op jit(solution)/shard_map/weight_two/ppermute | solution.py:28
  62.3 1.3 %collective-permute-start.16 = (bf16[8,48,384]{2,1,0:T(8,128)(2,1)S(1)}, bf16[8,48,384]{2,1,0:T(8,128)(2,1)S(1)}, u32[]{:S(2)}, u32[]{:S(2)}) collective-permute-start(bf16[8,48,384]{2,1,0:T(8,128)(2,1)S(1)} %slice.54), channel_id=1, source_target_pairs={{0,3},{1,0},{2,1},{3,2},{4,7},{5,4},{6,5},{7,6},{8,11},{9,8},{10,9... | collective-permute-start | bytes 884744 | tf_op jit(solution)/shard_map/weight_two/ppermute | solution.py:28
  63.7 0.7 copy-done.11
  64.4 0.9 copy-done.8
  65.3 9.5 %conv_one.1 = f32[2,12,64,128]{3,2,1,0:T(8,128)} custom-call(f32[2,3]{1,0:T(2,128)S(1)} %compare_convert_fusion.valid, s32[3]{0:T(128)S(1)} %pad_add_fusion.place, bf16[2,3,64,384]{3,2,1,0:T(8,128)(2,1)S(1)} %fusion.8.refs_0_, bf16[2,3,64,384]{3,2,1,0:T(8,128)(2,1)S(1)} %collective-permute-done.refs_1_, ...), custom_call_target="tpu_custom_call" | custom-call | flops 4076863488 | bytes 6000000 | tf_op jit(solution)/shard_map/first/conv_one/pallas_call | solution.py:198
  74.8 1.4 %multiply_reduce_fusion = f32[2,12,64]{2,1,0:T(8,128)S(1)} fusion(f32[2,12,64,128]{3,2,1,0:T(8,128)} %conv_one.1), kind=kLoop, calls=%fused_computation.9 | loop fusion | flops 391680 | bytes 792576 | tf_op jit(solution)/shard_map/weight_two/reduce_sum | solution.py:341
  76.2 0.1 collective-permute-start.13
  76.3 3.7 %collective-permute-done.13 = f32[2,12,64]{2,1,0:T(8,128)S(1)} collective-permute-done((f32[2,12,64]{2,1,0:T(8,128)S(1)}, f32[2,12,64]{2,1,0:T(8,128)S(1)}, u32[]{:S(2)}, u32[]{:S(2)}) %collective-permute-start.13) | collective-permute-done | bytes 6176 | tf_op jit(solution)/shard_map/weight_two/ppermute | solution.py:32
  80.0 0.2 pad_maximum_fusion.mine
  80.2 0.1 collective-permute-start.19
  80.3 0.9 collective-permute-start.17
  81.2 0.1 reshape.33
  81.3 0.2 dynamic-slice_reduce_fusion
  81.5 4.1 %collective-permute-done.17 = f32[2,12,64]{2,1,0:T(8,128)S(1)} collective-permute-done((f32[2,12,64]{2,1,0:T(8,128)S(1)}, f32[2,12,64]{2,1,0:T(8,128)S(1)}, u32[]{:S(2)}, u32[]{:S(2)}) %collective-permute-start.17) | collective-permute-done | bytes 6176 | tf_op jit(solution)/shard_map/second/ppermute | solution.py:32
  85.7 0.3 multiply_convert_fusion.own
  86.0 2.1 %collective-permute-start.18 = (bf16[2,12,64,128]{3,2,1,0:T(8,128)(2,1)S(1)}, bf16[2,12,64,128]{3,2,1,0:T(8,128)(2,1)S(1)}, u32[]{:S(2)}, u32[]{:S(2)}) collective-permute-start(bf16[2,12,64,128]{3,2,1,0:T(8,128)(2,1)S(1)} %multiply_convert_fusion.own), channel_id=1, source_target_pairs={{0,16},{16,32},{32,48},{48,64},{64,80},{80,96},{96,112},{112,128},... | collective-permute-start | bytes 1179656 | tf_op jit(solution)/shard_map/second/ppermute | solution.py:23
  88.1 4.0 %assemble_two.1.weight = bf16[3456,384]{1,0:T(8,128)(2,1)} custom-call(s32[3]{0:T(128)S(1)} %pad_add_fusion.place, bf16[4,8,48,384]{3,2,1,0:T(8,128)(2,1)S(1)} %pad_maximum_fusion.mine, bf16[4,8,48,384]{3,2,1,0:T(8,128)(2,1)} %collective-permute-done.19.other), custom_call_target="tpu_custom_call" | custom-call | flops 4000000 | bytes 5000000 | tf_op jit(solution)/shard_map/weight_two/assemble_two/pallas_call | solution.py:270
  92.1 2.9 %collective-permute-done.18.halo = bf16[2,12,64,128]{3,2,1,0:T(8,128)(2,1)S(1)} collective-permute-done((bf16[2,12,64,128]{3,2,1,0:T(8,128)(2,1)S(1)}, bf16[2,12,64,128]{3,2,1,0:T(8,128)(2,1)S(1)}, u32[]{:S(2)}, u32[]{:S(2)}) %collective-permute-start.18) | collective-permute-done | bytes 393248 | tf_op jit(solution)/shard_map/second/ppermute | solution.py:23
  95.1 7.3 %conv_two.1 = (bf16[2,3,64,384]{3,2,1,0:T(8,128)(2,1)S(1)}, bf16[2,3,64,384]{3,2,1,0:T(8,128)(2,1)S(1)}, bf16[2,3,64,384]{3,2,1,0:T(8,128)(2,1)S(1)}, bf16[1,3,6...) custom-call(f32[2,3]{1,0:T(2,128)S(1)} %compare_convert_fusion.valid, s32[3]{0:T(128)S(1)} %pad_add_fusion.place, ...), custom_call_target="tpu_custom_call" | custom-call | flops 4076863488 | bytes 6000000 | tf_op jit(solution)/shard_map/second/conv_two/pallas_call | solution.py:221
  102.4 0.9 collective-permute-start.20
  103.3 1.2 collective-permute-start.21
  104.5 6.3 %collective-permute-done.20 = bf16[2,3,64,384]{3,2,1,0:T(8,128)(2,1)S(1)} collective-permute-done((bf16[2,3,64,384]{3,2,1,0:T(8,128)(2,1)S(1)}, bf16[2,3,64,384]{3,2,1,0:T(8,128)(2,1)S(1)}, u32[]{:S(2)}, u32[]{:S(2)}) %collective-permute-start.20) | collective-permute-done | bytes 294944 | tf_op jit(solution)/shard_map/second/ppermute | solution.py:28
  110.8 0.9 collective-permute-start.23
  111.8 0.0 collective-permute-done.21
  111.8 1.2 collective-permute-start.22
  113.0 3.0 %collective-permute-done.23 = bf16[1,3,64,384]{3,2,1,0:T(8,128)(2,1)S(1)} collective-permute-done((bf16[1,3,64,384]{3,2,1,0:T(8,128)(2,1)S(1)}, bf16[1,3,64,384]{3,2,1,0:T(8,128)(2,1)S(1)}, u32[]{:S(2)}, u32[]{:S(2)}) %collective-permute-start.23) | collective-permute-done | bytes 147488 | tf_op jit(solution)/shard_map/second/ppermute | solution.py:28
  116.0 2.2 %collective-permute-done.22 = bf16[1,3,64,384]{3,2,1,0:T(8,128)(2,1)S(1)} collective-permute-done((bf16[1,3,64,384]{3,2,1,0:T(8,128)(2,1)S(1)}, bf16[1,3,64,384]{3,2,1,0:T(8,128)(2,1)S(1)}, u32[]{:S(2)}, u32[]{:S(2)}) %collective-permute-start.22) | collective-permute-done | bytes 147488 | tf_op jit(solution)/shard_map/second/ppermute | solution.py:28
  118.3 0.2 fusion.9
  118.4 0.7 broadcast_in_dim.16
  119.1 1.3 %broadcast_in_dim_reshape.3 = bf16[1,2,6,128,384]{4,3,2,1,0:T(8,128)(2,1)} reshape(bf16[2,3,2,64,2,384]{5,4,3,2,1,0:T(2,128)(2,1)S(1)} %broadcast_in_dim.16) | data formatting | bytes 2359296 | tf_op jit(solution)/shard_map/broadcast_in_dim;reshape | solution.py:372
  (56 shorter events, 0.4 us)
Async XLA Ops:
  0.0 1.2 %copy-start = (bf16[162,384]{1,0:T(8,128)(2,1)S(1)}, bf16[162,384]{1,0:T(8,128)(2,1)}, u32[]{:S(2)}) copy-start(bf16[162,384]{1,0:T(8,128)(2,1)} %param.11) | copy-start | bytes 373252
  1.2 9.9 %copy-start.2 = (bf16[1,2,3,64,384]{4,3,2,1,0:T(8,128)(2,1)S(1)}, bf16[1,2,3,64,384]{4,3,2,1,0:T(8,128)(2,1)}, u32[]{:S(2)}) copy-start(bf16[1,2,3,64,384]{4,3,2,1,0:T(8,128)(2,1)} %param.6) | copy-start | bytes 884740
  1.4 9.9 %copy-start.6 = (f32[384]{0:T(512)S(1)}, f32[384]{0:T(512)}, u32[]{:S(2)}) copy-start(f32[384]{0:T(512)} %param.8) | copy-start | bytes 4612
  2.4 12.4 %copy-start.12 = (s32[1,4]{1,0:T(1,128)S(1)}, s32[1,4]{1,0:T(1,128)}, u32[]{:S(2)}) copy-start(s32[1,4]{1,0:T(1,128)} %param.7) | copy-start | bytes 52
  2.4 26.1 %all-to-all-start = ((bf16[8,96,384]{2,1,0:T(8,128)(2,1)}), bf16[8,96,384]{2,1,0:T(8,128)(2,1)S(1)}, u32[]{:S(2)}, u32[]{:S(2)}) async-start(bf16[8,96,384]{2,1,0:T(8,128)(2,1)} %broadcast_in_dim.15), calls=%async_computation | async-start | bytes 1179648 | tf_op jit(solution)/shard_map/pieces/all_to_all | solution.py:317
  11.5 20.4 %collective-permute-start = (bf16[2,3,64,384]{3,2,1,0:T(8,128)(2,1)S(1)}, bf16[2,3,64,384]{3,2,1,0:T(8,128)(2,1)S(1)}, u32[]{:S(2)}, u32[]{:S(2)}) collective-permute-start(bf16[2,3,64,384]{3,2,1,0:T(8,128)(2,1)S(1)} %fusion.8.refs_0_), channel_id=1, source_target_pairs={{0,4},{4,8},{8,12},{12,0},{1,5},{5,9},{9,13},{13,1},{2,6},{6,10},{... | collective-permute-start | bytes 884744 | tf_op jit(solution)/shard_map/pixels/ppermute | solution.py:28
  13.1 24.3 %collective-permute-start.1 = (bf16[2,3,64,384]{3,2,1,0:T(8,128)(2,1)S(1)}, bf16[2,3,64,384]{3,2,1,0:T(8,128)(2,1)S(1)}, u32[]{:S(2)}, u32[]{:S(2)}) collective-permute-start(bf16[2,3,64,384]{3,2,1,0:T(8,128)(2,1)S(1)} %fusion.8.refs_0_), channel_id=1, source_target_pairs={{0,12},{4,0},{8,4},{12,8},{1,13},{5,1},{9,5},{13,9},{2,14},{6,2},{... | collective-permute-start | bytes 884744 | tf_op jit(solution)/shard_map/pixels/ppermute | solution.py:28
  28.6 8.8 %copy-start.5 = (bf16[8,48,384]{2,1,0:T(8,128)(2,1)}, bf16[8,48,384]{2,1,0:T(8,128)(2,1)S(1)}, u32[]{:S(2)}) copy-start(bf16[8,48,384]{2,1,0:T(8,128)(2,1)S(1)} %get-tuple-element.28.refs_8_) | copy-start | bytes 884740
  28.6 8.0 %collective-permute-start.7 = (bf16[8,48,384]{2,1,0:T(8,128)(2,1)S(1)}, bf16[8,48,384]{2,1,0:T(8,128)(2,1)S(1)}, u32[]{:S(2)}, u32[]{:S(2)}) collective-permute-start(bf16[8,48,384]{2,1,0:T(8,128)(2,1)S(1)} %get-tuple-element.28.refs_8_), channel_id=1, source_target_pairs={{0,1},{1,2},{2,3},{3,0},{4,5},{5,6},{6,7},{7,4},{8,9},{9,10},{10,1... | collective-permute-start | bytes 884744 | tf_op jit(solution)/shard_map/weight_one/ppermute | solution.py:28
  30.3 6.7 %collective-permute-start.8 = (bf16[8,48,384]{2,1,0:T(8,128)(2,1)S(1)}, bf16[8,48,384]{2,1,0:T(8,128)(2,1)S(1)}, u32[]{:S(2)}, u32[]{:S(2)}) collective-permute-start(bf16[8,48,384]{2,1,0:T(8,128)(2,1)S(1)} %get-tuple-element.28.refs_8_), channel_id=1, source_target_pairs={{0,3},{1,0},{2,1},{3,2},{4,7},{5,4},{6,5},{7,6},{8,11},{9,8},{10,9... | collective-permute-start | bytes 884744 | tf_op jit(solution)/shard_map/weight_one/ppermute | solution.py:28
  32.0 12.2 %collective-permute-start.2 = (bf16[1,3,64,384]{3,2,1,0:T(8,128)(2,1)S(1)}, bf16[1,3,64,384]{3,2,1,0:T(8,128)(2,1)S(1)}, u32[]{:S(2)}, u32[]{:S(2)}) collective-permute-start(bf16[1,3,64,384]{3,2,1,0:T(8,128)(2,1)S(1)} %slice.59), channel_id=1, source_target_pairs={{0,4},{4,8},{8,12},{12,0},{1,5},{5,9},{9,13},{13,1},{2,6},{6,10},{... | collective-permute-start | bytes 442376 | tf_op jit(solution)/shard_map/pixels/ppermute | solution.py:28
  36.6 5.9 %copy-start.3 = (bf16[8,48,384]{2,1,0:T(8,128)(2,1)}, bf16[8,48,384]{2,1,0:T(8,128)(2,1)S(1)}, u32[]{:S(2)}) copy-start(bf16[8,48,384]{2,1,0:T(8,128)(2,1)S(1)} %collective-permute-done.7.refs_9_) | copy-start | bytes 884740
  37.0 7.2 %copy-start.4 = (bf16[8,48,384]{2,1,0:T(8,128)(2,1)}, bf16[8,48,384]{2,1,0:T(8,128)(2,1)S(1)}, u32[]{:S(2)}) copy-start(bf16[8,48,384]{2,1,0:T(8,128)(2,1)S(1)} %collective-permute-done.8.refs_10_) | copy-start | bytes 884740
  37.1 26.5 %collective-permute-start.11 = (bf16[3,8,48,384]{3,2,1,0:T(8,128)(2,1)S(1)}, bf16[3,8,48,384]{3,2,1,0:T(8,128)(2,1)S(1)}, u32[]{:S(2)}, u32[]{:S(2)}) collective-permute-start(bf16[3,8,48,384]{3,2,1,0:T(8,128)(2,1)S(1)} %pad_maximum_fusion.1), channel_id=1, source_target_pairs={{0,16},{16,0},{1,17},{17,1},{2,18},{18,2},{3,19},{19,3},{4,20},{20... | collective-permute-start | bytes 2654216 | tf_op jit(solution)/shard_map/weight_one/ppermute | solution.py:320
  37.5 8.5 %collective-permute-start.3 = (bf16[1,3,64,384]{3,2,1,0:T(8,128)(2,1)S(1)}, bf16[1,3,64,384]{3,2,1,0:T(8,128)(2,1)S(1)}, u32[]{:S(2)}, u32[]{:S(2)}) collective-permute-start(bf16[1,3,64,384]{3,2,1,0:T(8,128)(2,1)S(1)} %slice.60), channel_id=1, source_target_pairs={{0,12},{4,0},{8,4},{12,8},{1,13},{5,1},{9,5},{13,9},{2,14},{6,2},{... | collective-permute-start | bytes 442376 | tf_op jit(solution)/shard_map/pixels/ppermute | solution.py:28
  40.4 21.9 %collective-permute-start.5 = (bf16[2,2,3,64,384]{4,3,2,1,0:T(8,128)(2,1)S(1)}, bf16[2,2,3,64,384]{4,3,2,1,0:T(8,128)(2,1)S(1)}, u32[]{:S(2)}, u32[]{:S(2)}) collective-permute-start(bf16[2,2,3,64,384]{4,3,2,1,0:T(8,128)(2,1)S(1)} %pad_maximum_fusion.2), channel_id=1, source_target_pairs={{0,16},{16,32},{32,48},{48,64},{64,80},{80,96},{96,112},{112,128},... | collective-permute-start | bytes 1769480 | tf_op jit(solution)/shard_map/pixels/ppermute | solution.py:23
  42.5 7.1 %collective-permute-start.9 = (bf16[4,48,384]{2,1,0:T(8,128)(2,1)S(1)}, bf16[4,48,384]{2,1,0:T(8,128)(2,1)S(1)}, u32[]{:S(2)}, u32[]{:S(2)}) collective-permute-start(bf16[4,48,384]{2,1,0:T(8,128)(2,1)S(1)} %slice.65), channel_id=1, source_target_pairs={{0,1},{1,2},{2,3},{3,0},{4,5},{5,6},{6,7},{7,4},{8,9},{9,10},{10,1... | collective-permute-start | bytes 442376 | tf_op jit(solution)/shard_map/weight_one/ppermute | solution.py:28
  44.2 7.3 %collective-permute-start.10 = (bf16[4,48,384]{2,1,0:T(8,128)(2,1)S(1)}, bf16[4,48,384]{2,1,0:T(8,128)(2,1)S(1)}, u32[]{:S(2)}, u32[]{:S(2)}) collective-permute-start(bf16[4,48,384]{2,1,0:T(8,128)(2,1)S(1)} %slice.66), channel_id=1, source_target_pairs={{0,3},{1,0},{2,1},{3,2},{4,7},{5,4},{6,5},{7,6},{8,11},{9,8},{10,9... | collective-permute-start | bytes 442376 | tf_op jit(solution)/shard_map/weight_one/ppermute | solution.py:28
  46.0 10.2 %collective-permute-start.4 = (bf16[2,3,64,384]{3,2,1,0:T(8,128)(2,1)S(1)}, bf16[2,3,64,384]{3,2,1,0:T(8,128)(2,1)S(1)}, u32[]{:S(2)}, u32[]{:S(2)}) collective-permute-start(bf16[2,3,64,384]{3,2,1,0:T(8,128)(2,1)S(1)} %fusion.8.refs_0_), channel_id=1, source_target_pairs={{0,16},{16,32},{32,48},{48,64},{64,80},{80,96},{96,112},{112,128},... | collective-permute-start | bytes 884744 | tf_op jit(solution)/shard_map/pixels/ppermute | solution.py:23
  49.6 9.8 %collective-permute-start.6 = (bf16[2,3,64,384]{3,2,1,0:T(8,128)(2,1)S(1)}, bf16[2,3,64,384]{3,2,1,0:T(8,128)(2,1)S(1)}, u32[]{:S(2)}, u32[]{:S(2)}) collective-permute-start(bf16[2,3,64,384]{3,2,1,0:T(8,128)(2,1)S(1)} %pad_maximum_fusion.3), channel_id=1, source_target_pairs={{0,16},{16,32},{32,48},{48,64},{64,80},{80,96},{96,112},{112,128},... | collective-permute-start | bytes 884744 | tf_op jit(solution)/shard_map/pixels/ppermute | solution.py:23
  51.6 12.1 %collective-permute-start.12 = (bf16[8,48,384]{2,1,0:T(8,128)(2,1)S(1)}, bf16[8,48,384]{2,1,0:T(8,128)(2,1)S(1)}, u32[]{:S(2)}, u32[]{:S(2)}) collective-permute-start(bf16[8,48,384]{2,1,0:T(8,128)(2,1)S(1)} %pad_maximum_fusion.4), channel_id=1, source_target_pairs={{0,16},{16,0},{1,17},{17,1},{2,18},{18,2},{3,19},{19,3},{4,20},{20... | collective-permute-start | bytes 884744 | tf_op jit(solution)/shard_map/weight_one/ppermute | solution.py:320
  56.2 23.8 %collective-permute-start.14 = (bf16[8,48,384]{2,1,0:T(8,128)(2,1)S(1)}, bf16[8,48,384]{2,1,0:T(8,128)(2,1)S(1)}, u32[]{:S(2)}, u32[]{:S(2)}) collective-permute-start(bf16[8,48,384]{2,1,0:T(8,128)(2,1)S(1)} %slice.54), channel_id=1, source_target_pairs={{0,1},{1,2},{2,3},{3,0},{4,5},{5,6},{6,7},{7,4},{8,9},{9,10},{10,1... | collective-permute-start | bytes 884744 | tf_op jit(solution)/shard_map/weight_two/ppermute | solution.py:28
  59.4 4.3 %copy-start.10 = (bf16[2,3,64,384]{3,2,1,0:T(8,128)(2,1)}, bf16[2,3,64,384]{3,2,1,0:T(8,128)(2,1)S(1)}, u32[]{:S(2)}) copy-start(bf16[2,3,64,384]{3,2,1,0:T(8,128)(2,1)S(1)} %collective-permute-done.6.refs_7_) | copy-start | bytes 884740
  59.4 20.6 %collective-permute-start.15 = (bf16[8,48,384]{2,1,0:T(8,128)(2,1)S(1)}, bf16[8,48,384]{2,1,0:T(8,128)(2,1)S(1)}, u32[]{:S(2)}, u32[]{:S(2)}) collective-permute-start(bf16[8,48,384]{2,1,0:T(8,128)(2,1)S(1)} %slice.54), channel_id=1, source_target_pairs={{0,2},{1,3},{2,0},{3,1},{4,6},{5,7},{6,4},{7,5},{8,10},{9,11},{10,... | collective-permute-start | bytes 884744 | tf_op jit(solution)/shard_map/weight_two/ppermute | solution.py:28
  62.3 1.4 %copy-start.9 = (bf16[2,2,3,64,384]{4,3,2,1,0:T(8,128)(2,1)}, bf16[2,2,3,64,384]{4,3,2,1,0:T(8,128)(2,1)S(1)}, u32[]{:S(2)}) copy-start(bf16[2,2,3,64,384]{4,3,2,1,0:T(8,128)(2,1)S(1)} %collective-permute-done.5.refs_6_) | copy-start | bytes 1769476
  62.3 17.7 %collective-permute-start.16 = (bf16[8,48,384]{2,1,0:T(8,128)(2,1)S(1)}, bf16[8,48,384]{2,1,0:T(8,128)(2,1)S(1)}, u32[]{:S(2)}, u32[]{:S(2)}) collective-permute-start(bf16[8,48,384]{2,1,0:T(8,128)(2,1)S(1)} %slice.54), channel_id=1, source_target_pairs={{0,3},{1,0},{2,1},{3,2},{4,7},{5,4},{6,5},{7,6},{8,11},{9,8},{10,9... | collective-permute-start | bytes 884744 | tf_op jit(solution)/shard_map/weight_two/ppermute | solution.py:28
  63.6 0.7 copy-start.11
  64.4 0.9 copy-start.8
  76.2 3.8 %collective-permute-start.13 = (f32[2,12,64]{2,1,0:T(8,128)S(1)}, f32[2,12,64]{2,1,0:T(8,128)S(1)}, u32[]{:S(2)}, u32[]{:S(2)}) collective-permute-start(f32[2,12,64]{2,1,0:T(8,128)S(1)} %multiply_reduce_fusion), channel_id=1, source_target_pairs={{0,4},{4,0},{8,12},{12,8},{1,5},{5,1},{9,13},{13,9},{2,6},{6,2},{1... | collective-permute-start | bytes 18440 | tf_op jit(solution)/shard_map/weight_two/ppermute | solution.py:32
  80.0 1.2 %copy-start.7 = (f32[384]{0:T(512)S(1)}, f32[384]{0:T(512)}, u32[]{:S(2)}) copy-start(f32[384]{0:T(512)} %param.9) | copy-start | bytes 4612
  80.0 5.6 %copy-start.1 = (f32[2,12,64,128]{3,2,1,0:T(8,128)S(1)}, f32[2,12,64,128]{3,2,1,0:T(8,128)}, u32[]{:S(2)}) copy-start(f32[2,12,64,128]{3,2,1,0:T(8,128)} %conv_one.1) | copy-start | bytes 2359300
  80.2 7.9 %collective-permute-start.19 = (bf16[4,8,48,384]{3,2,1,0:T(8,128)(2,1)S(1)}, bf16[4,8,48,384]{3,2,1,0:T(8,128)(2,1)}, u32[]{:S(2)}, u32[]{:S(2)}) collective-permute-start(bf16[4,8,48,384]{3,2,1,0:T(8,128)(2,1)S(1)} %pad_maximum_fusion.mine), channel_id=1, source_target_pairs={{0,16},{16,0},{1,17},{17,1},{2,18},{18,2},{3,19},{19,3},{4,20},{20... | collective-permute-start | bytes 3538952 | tf_op jit(solution)/shard_map/weight_two/ppermute | solution.py:320
  80.3 5.3 %collective-permute-start.17 = (f32[2,12,64]{2,1,0:T(8,128)S(1)}, f32[2,12,64]{2,1,0:T(8,128)S(1)}, u32[]{:S(2)}, u32[]{:S(2)}) collective-permute-start(f32[2,12,64]{2,1,0:T(8,128)S(1)} %add.98), channel_id=1, source_target_pairs={{0,8},{4,12},{8,0},{12,4},{1,9},{5,13},{9,1},{13,5},{2,10},{6,14},... | collective-permute-start | bytes 18440 | tf_op jit(solution)/shard_map/second/ppermute | solution.py:32
  86.0 9.1 %collective-permute-start.18 = (bf16[2,12,64,128]{3,2,1,0:T(8,128)(2,1)S(1)}, bf16[2,12,64,128]{3,2,1,0:T(8,128)(2,1)S(1)}, u32[]{:S(2)}, u32[]{:S(2)}) collective-permute-start(bf16[2,12,64,128]{3,2,1,0:T(8,128)(2,1)S(1)} %multiply_convert_fusion.own), channel_id=1, source_target_pairs={{0,16},{16,32},{32,48},{48,64},{64,80},{80,96},{96,112},{112,128},... | collective-permute-start | bytes 1179656 | tf_op jit(solution)/shard_map/second/ppermute | solution.py:23
  102.4 8.4 %collective-permute-start.20 = (bf16[2,3,64,384]{3,2,1,0:T(8,128)(2,1)S(1)}, bf16[2,3,64,384]{3,2,1,0:T(8,128)(2,1)S(1)}, u32[]{:S(2)}, u32[]{:S(2)}) collective-permute-start(bf16[2,3,64,384]{3,2,1,0:T(8,128)(2,1)S(1)} %get-tuple-element.23), channel_id=1, source_target_pairs={{0,12},{4,0},{8,4},{12,8},{1,13},{5,1},{9,5},{13,9},{2,14},{6,2},{... | collective-permute-start | bytes 884744 | tf_op jit(solution)/shard_map/second/ppermute | solution.py:28
  103.3 8.5 %collective-permute-start.21 = (bf16[2,3,64,384]{3,2,1,0:T(8,128)(2,1)S(1)}, bf16[2,3,64,384]{3,2,1,0:T(8,128)(2,1)S(1)}, u32[]{:S(2)}, u32[]{:S(2)}) collective-permute-start(bf16[2,3,64,384]{3,2,1,0:T(8,128)(2,1)S(1)} %get-tuple-element.24), channel_id=1, source_target_pairs={{0,4},{4,8},{8,12},{12,0},{1,5},{5,9},{9,13},{13,1},{2,6},{6,10},{... | collective-permute-start | bytes 884744 | tf_op jit(solution)/shard_map/second/ppermute | solution.py:28
  110.8 5.2 %collective-permute-start.23 = (bf16[1,3,64,384]{3,2,1,0:T(8,128)(2,1)S(1)}, bf16[1,3,64,384]{3,2,1,0:T(8,128)(2,1)S(1)}, u32[]{:S(2)}, u32[]{:S(2)}) collective-permute-start(bf16[1,3,64,384]{3,2,1,0:T(8,128)(2,1)S(1)} %get-tuple-element.31), channel_id=1, source_target_pairs={{0,12},{4,0},{8,4},{12,8},{1,13},{5,1},{9,5},{13,9},{2,14},{6,2},{... | collective-permute-start | bytes 442376 | tf_op jit(solution)/shard_map/second/ppermute | solution.py:28
  111.8 6.4 %collective-permute-start.22 = (bf16[1,3,64,384]{3,2,1,0:T(8,128)(2,1)S(1)}, bf16[1,3,64,384]{3,2,1,0:T(8,128)(2,1)S(1)}, u32[]{:S(2)}, u32[]{:S(2)}) collective-permute-start(bf16[1,3,64,384]{3,2,1,0:T(8,128)(2,1)S(1)} %get-tuple-element.29), channel_id=1, source_target_pairs={{0,4},{4,8},{8,12},{12,0},{1,5},{5,9},{9,13},{13,1},{2,6},{6,10},{... | collective-permute-start | bytes 442376 | tf_op jit(solution)/shard_map/second/ppermute | solution.py:28

commit v8 on v7

--- a/solution.py
+++ b/solution.py
@@ -30,12 +30,6 @@
 
 def across(x, bit):
     return lax.ppermute(x, "tile", [(i, i ^ bit) for i in range(lax.axis_size("tile"))])
-
-
-def ring(x, axis):
-    low, high = onward(x, 1, axis), onward(x, -1, axis)
-    half = x.shape[0] // 2
-    return [x, low, high, onward(low[:half], 1, axis), onward(high[half:], -1, axis)]
 
 
 def from_all(x, axis):
@@ -84,8 +78,8 @@
 
 
 def conv_one_kernel(share, valid, place, *refs):
-    own_refs, halo_refs, mine_refs, other_refs = refs[:5], refs[5:8], refs[8:13], refs[13:15]
-    out, frame_buf, acc, weight, wide, pieces = refs[15:]
+    own_refs, halo_refs, mine_refs, other_ref = refs[:5], refs[5:7], refs[7:12], refs[12]
+    out, squares, frame_buf, acc, weight, wide, pieces = refs[13:]
     frames, each, width, channels = own_refs[0].shape
     rows = out.shape[1]
     parts = rows // each
@@ -104,21 +98,15 @@
         for back, ref in zip((0, 1, 3), own_refs):
             put(frames + s, back, ref[s])
         put(frames + s, 2, own_refs[3 + s][0])
-        put(s, 0, halo_refs[0][s])
-        put(s, 1, halo_refs[1][0, s])
-        put(s, 3, halo_refs[1][1, s])
-        put(s, 2, halo_refs[2][s])
-    half = zs // 2
-    for c, third in ((place[0], lambda i: mine_refs[i]), (1 - place[0], lambda i: other_refs[0].at[i])):
         for i, back in enumerate((0, 1, 3)):
-            source = third(i)
-            y = lax.rem(place[1] + ys - back, ys)
-            for z in range(zs):
-                pieces[c, y, z] = source[z]
-    y = lax.rem(place[1] + ys - 2, ys)
-    for z in range(zs):
-        pieces[place[0], y, z] = mine_refs[3 + z // half][z % half]
-        pieces[1 - place[0], y, z] = other_refs[1][z]
+            put(s, back, halo_refs[0][i, s])
+        put(s, 2, halo_refs[1][s])
+    for i, back in enumerate((0, 1, 3, 2)):
+        y = lax.rem(place[1] + ys - back, ys)
+        for z in range(zs):
+            ref, at = (mine_refs[i], z) if i < 3 else (mine_refs[3 + 2 * z // zs], z % (zs // 2))
+            pieces[place[0], y, z] = ref[at]
+            pieces[1 - place[0], y, z] = other_ref[i, z]
     assemble_one(pieces, weight, wide)
     for slot in range(2 * frames):
         pairs = [(s, slot - s) for s in range(frames) if 0 <= slot - s < 3]
@@ -145,7 +133,9 @@
         left = jnp.where(col == 0, 0.0, pltpu.roll(acc[s, 0], 1, 0))
         right = jnp.where(col == width - 1, 0.0, pltpu.roll(acc[s, 2], pixels - 1, 0))
         done = jnp.where(lane < share, acc[s, 1] + left + right, 0.0)
-        out[s] = done.reshape(rows, width, LANE)
+        done = done.reshape(rows, width, LANE)
+        out[s] = done
+        squares[s] = jnp.sum(done * done, axis=-1)
 
 
 def conv_two_kernel(valid, place, halo, own, weight, own_sum, up, down, up_last, down_last, taps, acc):
@@ -194,12 +184,15 @@
     rows = each * lax.axis_size("tile")
     zs, piece_rows, lanes = mine[0].shape
     flops = 2 * 6 * rows * width * 9 * channels * LANE
-    arrays = [*own, *halo, *mine, *other]
+    arrays = [*own, *halo, *mine, other]
     return pl.pallas_call(
         functools.partial(conv_one_kernel, channels * each // rows),
-        out_shape=jax.ShapeDtypeStruct((frames, rows, width, LANE), jnp.float32),
+        out_shape=[
+            jax.ShapeDtypeStruct((frames, rows, width, LANE), jnp.float32),
+            jax.ShapeDtypeStruct((frames, rows, width), jnp.float32),
+        ],
         in_specs=[SMEM, SMEM] + [VMEM] * len(arrays),
-        out_specs=VMEM,
+        out_specs=[VMEM, VMEM],
         scratch_shapes=[
             pltpu.VMEM((2 * frames, rows + 2, width, channels), jnp.bfloat16),
             pltpu.VMEM((frames, 3, rows * width, LANE), jnp.float32),
@@ -302,8 +295,11 @@
     with jax.named_scope("pixels"):
         mean_sq = jnp.mean(source * source, axis=-1, keepdims=True)
         hidden_one = jax.nn.silu(source * lax.rsqrt(mean_sq + EPS) * gain_one).astype(jnp.bfloat16)
-        own = ring(hidden_one, "tile")
-        halo = [earlier(own[0]), earlier(jnp.stack(own[1:3])), earlier(jnp.concatenate(own[3:]))]
+        own = [hidden_one, onward(hidden_one, 1), onward(hidden_one, -1)]
+
+    def column_of(piece):
+        n = lax.axis_size("z")
+        return lax.all_to_all(jnp.broadcast_to(piece, (n,) + piece.shape), "z", 0, 0)
 
     with jax.named_scope("pieces"):
         take = pick(channels, share, False, part, parts)
@@ -311,21 +307,28 @@
         piece = jnp.pad(piece, ((0, 4 * piece_rows - shard), (0, 0)))
         piece = jnp.concatenate([piece[j * piece_rows : (j + 1) * piece_rows] for j in range(4)], axis=1)
         piece = jnp.pad(piece, ((0, TILE_ROWS - piece_rows), (0, 0)))
-        rows_take = pick(TILE_ROWS, shard, True, part - 2 * side, parts)
-        piece_two = jnp.dot(rows_take, conv_two, preferred_element_type=jnp.float32).astype(jnp.bfloat16)
-        pieces = jnp.concatenate([piece, piece_two], axis=0)
-        column = lax.all_to_all(jnp.broadcast_to(pieces, (lax.axis_size("z"),) + pieces.shape), "z", 0, 0)
+        column = column_of(piece)
+
+    with jax.named_scope("pixels"):
+        own, column = lax.optimization_barrier((own, column))
+        own = own + [onward(own[1][:1], 1), onward(own[2][1:], -1)]
+        halo = [earlier(jnp.stack(own[:3])), earlier(jnp.concatenate(own[3:]))]
 
     def other_core(x):
         return lax.ppermute(x, "core", [(0, 1), (1, 0)])
 
     with jax.named_scope("weight_one"):
-        mine = ring(column[:, :TILE_ROWS], "group")
-        swapped = [other_core(jnp.stack(mine[:3])), other_core(jnp.concatenate(mine[3:]))]
+        mine = [column, onward(column, 1, "group"), onward(column, -1, "group")]
+        conv_two, mine = lax.optimization_barrier((conv_two, mine))
+        half = column.shape[0] // 2
+        mine = mine + [onward(mine[1][:half], 1, "group"), onward(mine[2][half:], -1, "group")]
+        rows_take = pick(TILE_ROWS, shard, True, part - 2 * side, parts)
+        piece = jnp.dot(rows_take, conv_two, preferred_element_type=jnp.float32).astype(jnp.bfloat16)
+        later = column_of(piece)
+        mine, halo, later = lax.optimization_barrier((mine, halo, later))
+        swapped = other_core(jnp.stack(mine[:3] + [jnp.concatenate(mine[3:])]))
 
     with jax.named_scope("weight_two"):
-        column, _ = lax.optimization_barrier((column, mine))
-        later = column[:, TILE_ROWS:]
         later = [later] + [onward(later, d, "group") for d in range(1, lax.axis_size("group"))]
 
     base = lax.axis_index(SLOT) * frames
@@ -335,10 +338,9 @@
     valid = (slots[:, None] - before[None, :] >= begins[:, None]).astype(jnp.float32)
 
     with jax.named_scope("first"):
-        first = conv_one_call(valid, place, own, halo, mine, swapped)
+        first, squares = conv_one_call(valid, place, own, halo, mine, swapped)
 
     with jax.named_scope("weight_two"):
-        squares = jnp.sum(first * first, axis=-1)
         squares = squares + across(squares, 1)
         squares, later = lax.optimization_barrier((squares, later))
         mine = jnp.stack(later)

time: 121 us -> 116 us (0.959); the launches traced: 120 us -> 114 us
  waiting for transfers between devices: 46.6 us -> 31.4 us
  starting transfers between devices: 42.9 us -> 49.7 us
  other arithmetic: 3.4 us -> 5.16 us
    all_to_all x1 -> x2, waiting for transfers between devices: 13.5 us -> 1.22 us  [column_of(): lax.all_to_all(jnp.broadcast_to(piece, (n,) + piece.shape), 'z', 0, 0)]
    all_to_all x1 -> x2, starting transfers between devices: 8.7 us -> 14.6 us  [column_of(): lax.all_to_all(jnp.broadcast_to(piece, (n,) + piece.shape), 'z', 0, 0)]
    ppermute x15, waiting for transfers between devices: 16.7 us -> 21.8 us  [onward(): return lax.ppermute(x, axis, [(i, (i + by) % n) for i in range(n)])]
    ppermute x4 -> x3, waiting for transfers between devices: 8.5 us -> 4.2 us  [earlier(): return lax.ppermute(x, SLOT, [(i, i + 1) for i in range(n - 1)])]
    ppermute x2, waiting for transfers between devices: 7.86 us -> 4.22 us  [across(): lax.ppermute(x, 'tile', [(i, i ^ bit) for i in range(lax.axis_size('tile'...]
    ppermute x2, starting transfers between devices: 0.98 us -> 4.54 us  [across(): lax.ppermute(x, 'tile', [(i, i ^ bit) for i in range(lax.axis_size('tile'...]
    ppermute x4 -> x3, starting transfers between devices: 8.08 us -> 5.97 us  [earlier(): return lax.ppermute(x, SLOT, [(i, i + 1) for i in range(n - 1)])]
    another operation x3 -> x4, other arithmetic: 0.37 us -> 2.44 us  [the longest x2 1.24 us: body(): swapped = other_core(jnp.stack(mine[:3] + [jnp.concatenate(mine[3:])]))]
  transfers between devices with their start and end apart: 25 -> 24, of which waited for: 12 -> 10; matrix products, arithmetic and copies ran while one was open for 3% -> 4% of each run, Pallas kernels for 11% -> 12%
where the time goes in v8:
time: 116 us; the launch traced here: 114 us
  starting transfers between devices  49.7 us (43%)
  waiting for transfers between devices  31.4 us (27%)
  Pallas kernels  20.8 us (18%)
  other arithmetic  5.16 us (4%)
  local copies, waits for them, and re-layouts  4.9 us (4%)
  matrix products  1.36 us (1%)
    ppermute x15, starting transfers between devices, onward(): return lax.ppermute(x, axis, [(i, (i + by) % n) for i in range(n)])  24.4 us
    ppermute x15, waiting for transfers between devices, onward(): return lax.ppermute(x, axis, [(i, (i + by) % n) for i in range(n)])  21.8 us
    all_to_all x2, starting transfers between devices, column_of(): lax.all_to_all(jnp.broadcast_to(piece, (n,) + piece.shape), 'z', 0, 0)  14.6 us
    pallas_call x1, Pallas kernels, conv_one_call(): pl.pallas_call(functools.partial(conv_one_kernel, channels * each // rows...  9.52 us
    pallas_call x1, Pallas kernels, conv_two_call(): pl.pallas_call(conv_two_kernel, out_shape=[jax.ShapeDtypeStruct(shape, jn...  7.33 us
    ppermute x3, starting transfers between devices, earlier(): return lax.ppermute(x, SLOT, [(i, i + 1) for i in range(n - 1)])  5.97 us
    ppermute x2, starting transfers between devices, across(): lax.ppermute(x, 'tile', [(i, i ^ bit) for i in range(lax.axis_size('tile'...  4.54 us
    ppermute x2, waiting for transfers between devices, across(): lax.ppermute(x, 'tile', [(i, i ^ bit) for i in range(lax.axis_size('tile'...  4.22 us
  transfers between devices with their start and end apart: 24, of which 10 were waited for; matrix products, arithmetic and copies ran while one was open for 4% of the time, Pallas kernels for 12%

profile of v8, /device:TPU:32, one launch (start us, length us, event | category | flops | bytes accessed | tf_op | source)
XLA Modules:
  0.0 113.7 jit_solution(9903639147480348087)
XLA Ops:
  0.0 1.2 %fusion = bf16[162,96]{1,0:T(8,128)(2,1)S(1)} fusion(bf16[162,384]{1,0:T(8,128)(2,1)} %param.10, s32[96]{0:T(128)S(1)} %multiply_add_fusion.1), kind=kOutput, calls=%fused_computation.4 | convolution fusion | flops 11996352 | bytes 155904 | tf_op jit(solution)/shard_map/pieces/dot_general | solution.py:306
  1.2 0.1 fusion.17
  1.3 0.7 broadcast_in_dim.17
  2.1 8.6 %all-to-all-start = ((bf16[8,48,384]{2,1,0:T(8,128)(2,1)}), bf16[8,48,384]{2,1,0:T(8,128)(2,1)S(1)}, u32[]{:S(2)}, u32[]{:S(2)}) async-start(bf16[8,48,384]{2,1,0:T(8,128)(2,1)} %broadcast_in_dim.17), calls=%async_computation | async-start | bytes 589824 | tf_op jit(solution)/shard_map/pieces/all_to_all | solution.py:302
  10.6 0.1 fusion.1
  10.8 0.3 fusion.8.refs_0_
  11.1 1.6 %collective-permute-start = (bf16[2,3,64,384]{3,2,1,0:T(8,128)(2,1)S(1)}, bf16[2,3,64,384]{3,2,1,0:T(8,128)(2,1)S(1)}, u32[]{:S(2)}, u32[]{:S(2)}) collective-permute-start(bf16[2,3,64,384]{3,2,1,0:T(8,128)(2,1)S(1)} %fusion.8.refs_0_), channel_id=1, source_target_pairs={{0,4},{4,8},{8,12},{12,0},{1,5},{5,9},{9,13},{13,1},{2,6},{6,10},{... | collective-permute-start | bytes 884744 | tf_op jit(solution)/shard_map/pixels/ppermute | solution.py:28
  12.6 1.7 %collective-permute-start.1 = (bf16[2,3,64,384]{3,2,1,0:T(8,128)(2,1)S(1)}, bf16[2,3,64,384]{3,2,1,0:T(8,128)(2,1)S(1)}, u32[]{:S(2)}, u32[]{:S(2)}) collective-permute-start(bf16[2,3,64,384]{3,2,1,0:T(8,128)(2,1)S(1)} %fusion.8.refs_0_), channel_id=1, source_target_pairs={{0,12},{4,0},{8,4},{12,8},{1,13},{5,1},{9,5},{13,9},{2,14},{6,2},{... | collective-permute-start | bytes 884744 | tf_op jit(solution)/shard_map/pixels/ppermute | solution.py:28
  14.4 6.2 %collective-permute-done.refs_1_ = bf16[2,3,64,384]{3,2,1,0:T(8,128)(2,1)S(1)} collective-permute-done((bf16[2,3,64,384]{3,2,1,0:T(8,128)(2,1)S(1)}, bf16[2,3,64,384]{3,2,1,0:T(8,128)(2,1)S(1)}, u32[]{:S(2)}, u32[]{:S(2)}) %collective-permute-start) | collective-permute-done | bytes 294944 | tf_op jit(solution)/shard_map/pixels/ppermute | solution.py:28
  20.5 1.2 %all-to-all-done.refs_7_ = bf16[8,48,384]{2,1,0:T(8,128)(2,1)S(1)} async-done(((bf16[8,48,384]{2,1,0:T(8,128)(2,1)}), bf16[8,48,384]{2,1,0:T(8,128)(2,1)S(1)}, u32[]{:S(2)}, u32[]{:S(2)}) %all-to-all-start) | async-done | bytes 294944 | tf_op jit(solution)/shard_map/pieces/all_to_all | solution.py:302
  21.8 1.6 %collective-permute-start.4 = (bf16[8,48,384]{2,1,0:T(8,128)(2,1)S(1)}, bf16[8,48,384]{2,1,0:T(8,128)(2,1)S(1)}, u32[]{:S(2)}, u32[]{:S(2)}) collective-permute-start(bf16[8,48,384]{2,1,0:T(8,128)(2,1)S(1)} %all-to-all-done.refs_7_), channel_id=1, source_target_pairs={{0,1},{1,2},{2,3},{3,0},{4,5},{5,6},{6,7},{7,4},{8,9},{9,10},{10,1... | collective-permute-start | bytes 884744 | tf_op jit(solution)/shard_map/weight_one/ppermute | solution.py:28
  23.3 1.7 %collective-permute-start.5 = (bf16[8,48,384]{2,1,0:T(8,128)(2,1)S(1)}, bf16[8,48,384]{2,1,0:T(8,128)(2,1)S(1)}, u32[]{:S(2)}, u32[]{:S(2)}) collective-permute-start(bf16[8,48,384]{2,1,0:T(8,128)(2,1)S(1)} %all-to-all-done.refs_7_), channel_id=1, source_target_pairs={{0,3},{1,0},{2,1},{3,2},{4,7},{5,4},{6,5},{7,6},{8,11},{9,8},{10,9... | collective-permute-start | bytes 884744 | tf_op jit(solution)/shard_map/weight_one/ppermute | solution.py:28
  25.0 1.0 pad_maximum_fusion.2
  26.0 1.9 %collective-permute-start.8 = (bf16[3,2,3,64,384]{4,3,2,1,0:T(8,128)(2,1)}, bf16[3,2,3,64,384]{4,3,2,1,0:T(8,128)(2,1)}, u32[]{:S(2)}, u32[]{:S(2)}) collective-permute-start(bf16[3,2,3,64,384]{4,3,2,1,0:T(8,128)(2,1)} %pad_maximum_fusion.2), channel_id=1, source_target_pairs={{0,16},{16,32},{32,48},{48,64},{64,80},{80,96},{96,112},{112,128},... | collective-permute-start | bytes 2654216 | tf_op jit(solution)/shard_map/pixels/ppermute | solution.py:23
  28.0 1.6 %collective-permute-start.2 = (bf16[1,3,64,384]{3,2,1,0:T(8,128)(2,1)S(1)}, bf16[1,3,64,384]{3,2,1,0:T(8,128)(2,1)S(1)}, u32[]{:S(2)}, u32[]{:S(2)}) collective-permute-start(bf16[1,3,64,384]{3,2,1,0:T(8,128)(2,1)S(1)} %slice.43), channel_id=1, source_target_pairs={{0,4},{4,8},{8,12},{12,0},{1,5},{5,9},{9,13},{13,1},{2,6},{6,10},{... | collective-permute-start | bytes 442376 | tf_op jit(solution)/shard_map/pixels/ppermute | solution.py:28
  29.6 1.7 %collective-permute-start.3 = (bf16[1,3,64,384]{3,2,1,0:T(8,128)(2,1)S(1)}, bf16[1,3,64,384]{3,2,1,0:T(8,128)(2,1)S(1)}, u32[]{:S(2)}, u32[]{:S(2)}) collective-permute-start(bf16[1,3,64,384]{3,2,1,0:T(8,128)(2,1)S(1)} %slice.44), channel_id=1, source_target_pairs={{0,12},{4,0},{8,4},{12,8},{1,13},{5,1},{9,5},{13,9},{2,14},{6,2},{... | collective-permute-start | bytes 442376 | tf_op jit(solution)/shard_map/pixels/ppermute | solution.py:28
  31.3 0.0 collective-permute-done.5.refs_9_
  31.4 0.2 convolution_convert_fusion.1
  31.6 0.7 broadcast_in_dim.18
  32.3 6.1 %all-to-all-start.1 = ((bf16[8,48,384]{2,1,0:T(8,128)(2,1)}), bf16[8,48,384]{2,1,0:T(8,128)(2,1)S(1)}, u32[]{:S(2)}, u32[]{:S(2)}) async-start(bf16[8,48,384]{2,1,0:T(8,128)(2,1)} %broadcast_in_dim.18), calls=%async_computation.1 | async-start | bytes 589824 | tf_op jit(solution)/shard_map/weight_one/all_to_all | solution.py:302
  38.4 0.0 collective-permute-done.2.refs_3_
  38.4 0.0 collective-permute-done.3.refs_4_
  38.4 1.9 %collective-permute-start.9 = (bf16[2,3,64,384]{3,2,1,0:T(8,128)(2,1)S(1)}, bf16[2,3,64,384]{3,2,1,0:T(8,128)(2,1)S(1)}, u32[]{:S(2)}, u32[]{:S(2)}) collective-permute-start(bf16[2,3,64,384]{3,2,1,0:T(8,128)(2,1)S(1)} %pad_maximum_fusion.3), channel_id=1, source_target_pairs={{0,16},{16,32},{32,48},{48,64},{64,80},{80,96},{96,112},{112,128},... | collective-permute-start | bytes 884744 | tf_op jit(solution)/shard_map/pixels/ppermute | solution.py:23
  40.4 0.6 collective-permute-start.6
  41.0 2.8 %collective-permute-start.7 = (bf16[4,48,384]{2,1,0:T(8,128)(2,1)S(1)}, bf16[4,48,384]{2,1,0:T(8,128)(2,1)S(1)}, u32[]{:S(2)}, u32[]{:S(2)}) collective-permute-start(bf16[4,48,384]{2,1,0:T(8,128)(2,1)S(1)} %slice.46), channel_id=1, source_target_pairs={{0,3},{1,0},{2,1},{3,2},{4,7},{5,4},{6,5},{7,6},{8,11},{9,8},{10,9... | collective-permute-start | bytes 442376 | tf_op jit(solution)/shard_map/weight_one/ppermute | solution.py:28
  43.8 4.1 %collective-permute-done.6.refs_10_ = bf16[4,48,384]{2,1,0:T(8,128)(2,1)S(1)} collective-permute-done((bf16[4,48,384]{2,1,0:T(8,128)(2,1)S(1)}, bf16[4,48,384]{2,1,0:T(8,128)(2,1)S(1)}, u32[]{:S(2)}, u32[]{:S(2)}) %collective-permute-start.6) | collective-permute-done | bytes 147488 | tf_op jit(solution)/shard_map/weight_one/ppermute | solution.py:28
  47.9 2.2 %collective-permute-done.9.refs_6_ = bf16[2,3,64,384]{3,2,1,0:T(8,128)(2,1)S(1)} collective-permute-done((bf16[2,3,64,384]{3,2,1,0:T(8,128)(2,1)S(1)}, bf16[2,3,64,384]{3,2,1,0:T(8,128)(2,1)S(1)}, u32[]{:S(2)}, u32[]{:S(2)}) %collective-permute-start.9) | collective-permute-done | bytes 294944 | tf_op jit(solution)/shard_map/pixels/ppermute | solution.py:23
  50.2 0.0 copy-start.8
  50.2 1.2 %pad_maximum_fusion = bf16[4,8,48,384]{3,2,1,0:T(8,128)(2,1)} fusion(bf16[1,8,48,384]{3,2,1,0:T(8,128)(2,1)S(1)} %maximum_bitcast_fusion, bf16[1,8,48,384]{3,2,1,0:T(8,128)(2,1)S(1)} %bitcast.32, bf16[1,8,48,384]{3,2,1,0:T(8,128)(2,1)S(1)} %bitcast.31, bf16[1,8,48,384]{3,2,1,0:T(8,128)(2,1)S(1)} %bitcast.29), kind=kLoop, calls=%fused_computation | loop fusion | flops 1769472 | bytes 2359296 | tf_op jit(solution)/shard_map/weight_one/stack | solution.py:329
  51.4 0.0 collective-permute-start.10
  51.4 0.2 reduce-window_clone.1
  51.6 0.1 pad_add_fusion.place
  51.7 0.2 fusion.19
  51.8 0.1 compare_convert_fusion.valid
  51.9 0.4 collective-permute-start.12
  52.3 2.9 %collective-permute-start.13 = (bf16[8,48,384]{2,1,0:T(8,128)(2,1)S(1)}, bf16[8,48,384]{2,1,0:T(8,128)(2,1)S(1)}, u32[]{:S(2)}, u32[]{:S(2)}) collective-permute-start(bf16[8,48,384]{2,1,0:T(8,128)(2,1)S(1)} %all-to-all-done.1), channel_id=1, source_target_pairs={{0,2},{1,3},{2,0},{3,1},{4,6},{5,7},{6,4},{7,5},{8,10},{9,11},{10,... | collective-permute-start | bytes 884744 | tf_op jit(solution)/shard_map/weight_two/ppermute | solution.py:28
  55.2 1.3 %collective-permute-start.14 = (bf16[8,48,384]{2,1,0:T(8,128)(2,1)S(1)}, bf16[8,48,384]{2,1,0:T(8,128)(2,1)S(1)}, u32[]{:S(2)}, u32[]{:S(2)}) collective-permute-start(bf16[8,48,384]{2,1,0:T(8,128)(2,1)S(1)} %all-to-all-done.1), channel_id=1, source_target_pairs={{0,3},{1,0},{2,1},{3,2},{4,7},{5,4},{6,5},{7,6},{8,11},{9,8},{10,9... | collective-permute-start | bytes 884744 | tf_op jit(solution)/shard_map/weight_two/ppermute | solution.py:28
  56.6 0.0 collective-permute-done.10.refs_12_
  56.6 9.5 %conv_one.1 = (f32[2,12,64,128]{3,2,1,0:T(8,128)}, f32[2,12,64]{2,1,0:T(8,128)S(1)}) custom-call(f32[2,3]{1,0:T(2,128)S(1)} %compare_convert_fusion.valid, s32[3]{0:T(128)S(1)} %pad_add_fusion.place, bf16[2,3,64,384]{3,2,1,0:T(8,128)(2,1)S(1)} %fusion.8.refs_0_, bf16[2,3,64,384]{3,2,1,0:T(8,128)(2,1)S(1)} %collective-permute-done.refs_1_, ...), custom_call_target="tpu_custom_call" | custom-call | flops 4076863488 | bytes 6000000 | tf_op jit(solution)/shard_map/first/conv_one/pallas_call | solution.py:188
  66.1 1.5 %collective-permute-start.11 = (f32[2,12,64]{2,1,0:T(8,128)S(1)}, f32[2,12,64]{2,1,0:T(8,128)S(1)}, u32[]{:S(2)}, u32[]{:S(2)}) collective-permute-start(f32[2,12,64]{2,1,0:T(8,128)S(1)} %get-tuple-element.49), channel_id=1, source_target_pairs={{0,4},{4,0},{8,12},{12,8},{1,5},{5,1},{9,13},{13,9},{2,6},{6,2},{1... | collective-permute-start | bytes 18440 | tf_op jit(solution)/shard_map/weight_two/ppermute | solution.py:32
  67.5 2.3 %collective-permute-done.11 = f32[2,12,64]{2,1,0:T(8,128)S(1)} collective-permute-done((f32[2,12,64]{2,1,0:T(8,128)S(1)}, f32[2,12,64]{2,1,0:T(8,128)S(1)}, u32[]{:S(2)}, u32[]{:S(2)}) %collective-permute-start.11) | collective-permute-done | bytes 6176 | tf_op jit(solution)/shard_map/weight_two/ppermute | solution.py:32
  69.8 0.0 copy-start.7
  69.9 0.2 pad_maximum_fusion.1.mine
  70.0 0.1 collective-permute-start.17
  70.1 3.1 %collective-permute-start.15 = (f32[2,12,64]{2,1,0:T(8,128)S(1)}, f32[2,12,64]{2,1,0:T(8,128)S(1)}, u32[]{:S(2)}, u32[]{:S(2)}) collective-permute-start(f32[2,12,64]{2,1,0:T(8,128)S(1)} %add.98), channel_id=1, source_target_pairs={{0,8},{4,12},{8,0},{12,4},{1,9},{5,13},{9,1},{13,5},{2,10},{6,14},... | collective-permute-start | bytes 18440 | tf_op jit(solution)/shard_map/second/ppermute | solution.py:32
  73.2 0.1 reshape.33
  73.3 0.2 dynamic-slice_reduce_fusion
  73.5 1.9 %collective-permute-done.15 = f32[2,12,64]{2,1,0:T(8,128)S(1)} collective-permute-done((f32[2,12,64]{2,1,0:T(8,128)S(1)}, f32[2,12,64]{2,1,0:T(8,128)S(1)}, u32[]{:S(2)}, u32[]{:S(2)}) %collective-permute-start.15) | collective-permute-done | bytes 6176 | tf_op jit(solution)/shard_map/second/ppermute | solution.py:32
  75.5 1.4 %multiply_convert_fusion.own = bf16[2,12,64,128]{3,2,1,0:T(8,128)(2,1)S(1)} fusion(f32[2,12,64,128]{3,2,1,0:T(8,128)} %get-tuple-element.48, f32[128]{0:T(128)S(1)} %pad.14, f32[2,12,64]{2,1,0:T(8,128)S(1)} %add_rsqrt_fusion), kind=kLoop, calls=%fused_computation.9 | loop fusion | flops 1376256 | bytes 1186304 | tf_op jit(solution)/shard_map/second/convert_element_type | solution.py:359
  76.9 2.1 %collective-permute-start.16 = (bf16[2,12,64,128]{3,2,1,0:T(8,128)(2,1)S(1)}, bf16[2,12,64,128]{3,2,1,0:T(8,128)(2,1)S(1)}, u32[]{:S(2)}, u32[]{:S(2)}) collective-permute-start(bf16[2,12,64,128]{3,2,1,0:T(8,128)(2,1)S(1)} %multiply_convert_fusion.own), channel_id=1, source_target_pairs={{0,16},{16,32},{32,48},{48,64},{64,80},{80,96},{96,112},{112,128},... | collective-permute-start | bytes 1179656 | tf_op jit(solution)/shard_map/second/ppermute | solution.py:23
  79.1 0.0 copy-start.3
  79.1 1.0 copy-done.3
  80.1 3.9 %assemble_two.1.weight = bf16[3456,384]{1,0:T(8,128)(2,1)} custom-call(s32[3]{0:T(128)S(1)} %pad_add_fusion.place, bf16[4,8,48,384]{3,2,1,0:T(8,128)(2,1)S(1)} %pad_maximum_fusion.1.mine, bf16[4,8,48,384]{3,2,1,0:T(8,128)(2,1)} %copy-done.3), custom_call_target="tpu_custom_call" | custom-call | flops 4000000 | bytes 5000000 | tf_op jit(solution)/shard_map/weight_two/assemble_two/pallas_call | solution.py:263
  84.0 2.0 %collective-permute-done.16.halo = bf16[2,12,64,128]{3,2,1,0:T(8,128)(2,1)S(1)} collective-permute-done((bf16[2,12,64,128]{3,2,1,0:T(8,128)(2,1)S(1)}, bf16[2,12,64,128]{3,2,1,0:T(8,128)(2,1)S(1)}, u32[]{:S(2)}, u32[]{:S(2)}) %collective-permute-start.16) | collective-permute-done | bytes 393248 | tf_op jit(solution)/shard_map/second/ppermute | solution.py:23
  86.0 7.3 %conv_two.1 = (bf16[2,3,64,384]{3,2,1,0:T(8,128)(2,1)S(1)}, bf16[2,3,64,384]{3,2,1,0:T(8,128)(2,1)S(1)}, bf16[2,3,64,384]{3,2,1,0:T(8,128)(2,1)S(1)}, bf16[1,3,6...) custom-call(f32[2,3]{1,0:T(2,128)S(1)} %compare_convert_fusion.valid, s32[3]{0:T(128)S(1)} %pad_add_fusion.place, ...), custom_call_target="tpu_custom_call" | custom-call | flops 4076863488 | bytes 6000000 | tf_op jit(solution)/shard_map/second/conv_two/pallas_call | solution.py:214
  93.4 2.8 %collective-permute-start.18 = (bf16[2,3,64,384]{3,2,1,0:T(8,128)(2,1)S(1)}, bf16[2,3,64,384]{3,2,1,0:T(8,128)(2,1)S(1)}, u32[]{:S(2)}, u32[]{:S(2)}) collective-permute-start(bf16[2,3,64,384]{3,2,1,0:T(8,128)(2,1)S(1)} %get-tuple-element.57), channel_id=1, source_target_pairs={{0,12},{4,0},{8,4},{12,8},{1,13},{5,1},{9,5},{13,9},{2,14},{6,2},{... | collective-permute-start | bytes 884744 | tf_op jit(solution)/shard_map/second/ppermute | solution.py:28
  96.2 5.2 %collective-permute-done.18 = bf16[2,3,64,384]{3,2,1,0:T(8,128)(2,1)S(1)} collective-permute-done((bf16[2,3,64,384]{3,2,1,0:T(8,128)(2,1)S(1)}, bf16[2,3,64,384]{3,2,1,0:T(8,128)(2,1)S(1)}, u32[]{:S(2)}, u32[]{:S(2)}) %collective-permute-start.18) | collective-permute-done | bytes 294944 | tf_op jit(solution)/shard_map/second/ppermute | solution.py:28
  101.4 3.6 %collective-permute-start.21 = (bf16[1,3,64,384]{3,2,1,0:T(8,128)(2,1)S(1)}, bf16[1,3,64,384]{3,2,1,0:T(8,128)(2,1)S(1)}, u32[]{:S(2)}, u32[]{:S(2)}) collective-permute-start(bf16[1,3,64,384]{3,2,1,0:T(8,128)(2,1)S(1)} %get-tuple-element.63), channel_id=1, source_target_pairs={{0,12},{4,0},{8,4},{12,8},{1,13},{5,1},{9,5},{13,9},{2,14},{6,2},{... | collective-permute-start | bytes 442376 | tf_op jit(solution)/shard_map/second/ppermute | solution.py:28
  105.1 0.1 collective-permute-start.20
  105.2 2.5 %collective-permute-done.21 = bf16[1,3,64,384]{3,2,1,0:T(8,128)(2,1)S(1)} collective-permute-done((bf16[1,3,64,384]{3,2,1,0:T(8,128)(2,1)S(1)}, bf16[1,3,64,384]{3,2,1,0:T(8,128)(2,1)S(1)}, u32[]{:S(2)}, u32[]{:S(2)}) %collective-permute-start.21) | collective-permute-done | bytes 147488 | tf_op jit(solution)/shard_map/second/ppermute | solution.py:28
  107.7 3.8 %collective-permute-done.20 = bf16[1,3,64,384]{3,2,1,0:T(8,128)(2,1)S(1)} collective-permute-done((bf16[1,3,64,384]{3,2,1,0:T(8,128)(2,1)S(1)}, bf16[1,3,64,384]{3,2,1,0:T(8,128)(2,1)S(1)}, u32[]{:S(2)}, u32[]{:S(2)}) %collective-permute-start.20) | collective-permute-done | bytes 147488 | tf_op jit(solution)/shard_map/second/ppermute | solution.py:28
  111.5 0.2 fusion.9
  111.7 0.7 broadcast_in_dim.19
  112.4 1.3 %broadcast_in_dim_reshape.3 = bf16[1,2,6,128,384]{4,3,2,1,0:T(8,128)(2,1)} reshape(bf16[2,3,2,64,2,384]{5,4,3,2,1,0:T(2,128)(2,1)S(1)} %broadcast_in_dim.19) | data formatting | bytes 2359296 | tf_op jit(solution)/shard_map/broadcast_in_dim;reshape | solution.py:374
  (43 shorter events, 0.3 us)
Async XLA Ops:
  0.0 31.3 %copy-start = (bf16[162,384]{1,0:T(8,128)(2,1)S(1)}, bf16[162,384]{1,0:T(8,128)(2,1)}, u32[]{:S(2)}) copy-start(bf16[162,384]{1,0:T(8,128)(2,1)} %param.11) | copy-start | bytes 373252
  0.0 10.6 %copy-start.1 = (bf16[1,2,3,64,384]{4,3,2,1,0:T(8,128)(2,1)S(1)}, bf16[1,2,3,64,384]{4,3,2,1,0:T(8,128)(2,1)}, u32[]{:S(2)}) copy-start(bf16[1,2,3,64,384]{4,3,2,1,0:T(8,128)(2,1)} %param.6) | copy-start | bytes 884740
  0.0 10.8 %copy-start.6 = (f32[384]{0:T(512)S(1)}, f32[384]{0:T(512)}, u32[]{:S(2)}) copy-start(f32[384]{0:T(512)} %param.8) | copy-start | bytes 4612
  2.1 19.7 %all-to-all-start = ((bf16[8,48,384]{2,1,0:T(8,128)(2,1)}), bf16[8,48,384]{2,1,0:T(8,128)(2,1)S(1)}, u32[]{:S(2)}, u32[]{:S(2)}) async-start(bf16[8,48,384]{2,1,0:T(8,128)(2,1)} %broadcast_in_dim.17), calls=%async_computation | async-start | bytes 589824 | tf_op jit(solution)/shard_map/pieces/all_to_all | solution.py:302
  11.1 9.5 %collective-permute-start = (bf16[2,3,64,384]{3,2,1,0:T(8,128)(2,1)S(1)}, bf16[2,3,64,384]{3,2,1,0:T(8,128)(2,1)S(1)}, u32[]{:S(2)}, u32[]{:S(2)}) collective-permute-start(bf16[2,3,64,384]{3,2,1,0:T(8,128)(2,1)S(1)} %fusion.8.refs_0_), channel_id=1, source_target_pairs={{0,4},{4,8},{8,12},{12,0},{1,5},{5,9},{9,13},{13,1},{2,6},{6,10},{... | collective-permute-start | bytes 884744 | tf_op jit(solution)/shard_map/pixels/ppermute | solution.py:28
  12.6 7.9 %collective-permute-start.1 = (bf16[2,3,64,384]{3,2,1,0:T(8,128)(2,1)S(1)}, bf16[2,3,64,384]{3,2,1,0:T(8,128)(2,1)S(1)}, u32[]{:S(2)}, u32[]{:S(2)}) collective-permute-start(bf16[2,3,64,384]{3,2,1,0:T(8,128)(2,1)S(1)} %fusion.8.refs_0_), channel_id=1, source_target_pairs={{0,12},{4,0},{8,4},{12,8},{1,13},{5,1},{9,5},{13,9},{2,14},{6,2},{... | collective-permute-start | bytes 884744 | tf_op jit(solution)/shard_map/pixels/ppermute | solution.py:28
  21.8 28.4 %copy-start.2 = (bf16[8,48,384]{2,1,0:T(8,128)(2,1)}, bf16[8,48,384]{2,1,0:T(8,128)(2,1)S(1)}, u32[]{:S(2)}) copy-start(bf16[8,48,384]{2,1,0:T(8,128)(2,1)S(1)} %all-to-all-done.refs_7_) | copy-start | bytes 884740
  21.8 9.6 %collective-permute-start.4 = (bf16[8,48,384]{2,1,0:T(8,128)(2,1)S(1)}, bf16[8,48,384]{2,1,0:T(8,128)(2,1)S(1)}, u32[]{:S(2)}, u32[]{:S(2)}) collective-permute-start(bf16[8,48,384]{2,1,0:T(8,128)(2,1)S(1)} %all-to-all-done.refs_7_), channel_id=1, source_target_pairs={{0,1},{1,2},{2,3},{3,0},{4,5},{5,6},{6,7},{7,4},{8,9},{9,10},{10,1... | collective-permute-start | bytes 884744 | tf_op jit(solution)/shard_map/weight_one/ppermute | solution.py:28
  23.3 8.0 %collective-permute-start.5 = (bf16[8,48,384]{2,1,0:T(8,128)(2,1)S(1)}, bf16[8,48,384]{2,1,0:T(8,128)(2,1)S(1)}, u32[]{:S(2)}, u32[]{:S(2)}) collective-permute-start(bf16[8,48,384]{2,1,0:T(8,128)(2,1)S(1)} %all-to-all-done.refs_7_), channel_id=1, source_target_pairs={{0,3},{1,0},{2,1},{3,2},{4,7},{5,4},{6,5},{7,6},{8,11},{9,8},{10,9... | collective-permute-start | bytes 884744 | tf_op jit(solution)/shard_map/weight_one/ppermute | solution.py:28
  26.0 24.1 %collective-permute-start.8 = (bf16[3,2,3,64,384]{4,3,2,1,0:T(8,128)(2,1)}, bf16[3,2,3,64,384]{4,3,2,1,0:T(8,128)(2,1)}, u32[]{:S(2)}, u32[]{:S(2)}) collective-permute-start(bf16[3,2,3,64,384]{4,3,2,1,0:T(8,128)(2,1)} %pad_maximum_fusion.2), channel_id=1, source_target_pairs={{0,16},{16,32},{32,48},{48,64},{64,80},{80,96},{96,112},{112,128},... | collective-permute-start | bytes 2654216 | tf_op jit(solution)/shard_map/pixels/ppermute | solution.py:23
  28.0 10.4 %collective-permute-start.2 = (bf16[1,3,64,384]{3,2,1,0:T(8,128)(2,1)S(1)}, bf16[1,3,64,384]{3,2,1,0:T(8,128)(2,1)S(1)}, u32[]{:S(2)}, u32[]{:S(2)}) collective-permute-start(bf16[1,3,64,384]{3,2,1,0:T(8,128)(2,1)S(1)} %slice.43), channel_id=1, source_target_pairs={{0,4},{4,8},{8,12},{12,0},{1,5},{5,9},{9,13},{13,1},{2,6},{6,10},{... | collective-permute-start | bytes 442376 | tf_op jit(solution)/shard_map/pixels/ppermute | solution.py:28
  29.6 8.8 %collective-permute-start.3 = (bf16[1,3,64,384]{3,2,1,0:T(8,128)(2,1)S(1)}, bf16[1,3,64,384]{3,2,1,0:T(8,128)(2,1)S(1)}, u32[]{:S(2)}, u32[]{:S(2)}) collective-permute-start(bf16[1,3,64,384]{3,2,1,0:T(8,128)(2,1)S(1)} %slice.44), channel_id=1, source_target_pairs={{0,12},{4,0},{8,4},{12,8},{1,13},{5,1},{9,5},{13,9},{2,14},{6,2},{... | collective-permute-start | bytes 442376 | tf_op jit(solution)/shard_map/pixels/ppermute | solution.py:28
  31.3 18.8 %copy-start.4 = (bf16[8,48,384]{2,1,0:T(8,128)(2,1)}, bf16[8,48,384]{2,1,0:T(8,128)(2,1)S(1)}, u32[]{:S(2)}) copy-start(bf16[8,48,384]{2,1,0:T(8,128)(2,1)S(1)} %collective-permute-done.4.refs_8_) | copy-start | bytes 884740
  31.3 18.8 %copy-start.5 = (bf16[8,48,384]{2,1,0:T(8,128)(2,1)}, bf16[8,48,384]{2,1,0:T(8,128)(2,1)S(1)}, u32[]{:S(2)}) copy-start(bf16[8,48,384]{2,1,0:T(8,128)(2,1)S(1)} %collective-permute-done.5.refs_9_) | copy-start | bytes 884740
  32.3 17.8 %all-to-all-start.1 = ((bf16[8,48,384]{2,1,0:T(8,128)(2,1)}), bf16[8,48,384]{2,1,0:T(8,128)(2,1)S(1)}, u32[]{:S(2)}, u32[]{:S(2)}) async-start(bf16[8,48,384]{2,1,0:T(8,128)(2,1)} %broadcast_in_dim.18), calls=%async_computation.1 | async-start | bytes 589824 | tf_op jit(solution)/shard_map/weight_one/all_to_all | solution.py:302
  38.4 11.7 %collective-permute-start.9 = (bf16[2,3,64,384]{3,2,1,0:T(8,128)(2,1)S(1)}, bf16[2,3,64,384]{3,2,1,0:T(8,128)(2,1)S(1)}, u32[]{:S(2)}, u32[]{:S(2)}) collective-permute-start(bf16[2,3,64,384]{3,2,1,0:T(8,128)(2,1)S(1)} %pad_maximum_fusion.3), channel_id=1, source_target_pairs={{0,16},{16,32},{32,48},{48,64},{64,80},{80,96},{96,112},{112,128},... | collective-permute-start | bytes 884744 | tf_op jit(solution)/shard_map/pixels/ppermute | solution.py:23
  40.4 7.5 %collective-permute-start.6 = (bf16[4,48,384]{2,1,0:T(8,128)(2,1)S(1)}, bf16[4,48,384]{2,1,0:T(8,128)(2,1)S(1)}, u32[]{:S(2)}, u32[]{:S(2)}) collective-permute-start(bf16[4,48,384]{2,1,0:T(8,128)(2,1)S(1)} %slice.45), channel_id=1, source_target_pairs={{0,1},{1,2},{2,3},{3,0},{4,5},{5,6},{6,7},{7,4},{8,9},{9,10},{10,1... | collective-permute-start | bytes 442376 | tf_op jit(solution)/shard_map/weight_one/ppermute | solution.py:28
  41.0 6.8 %collective-permute-start.7 = (bf16[4,48,384]{2,1,0:T(8,128)(2,1)S(1)}, bf16[4,48,384]{2,1,0:T(8,128)(2,1)S(1)}, u32[]{:S(2)}, u32[]{:S(2)}) collective-permute-start(bf16[4,48,384]{2,1,0:T(8,128)(2,1)S(1)} %slice.46), channel_id=1, source_target_pairs={{0,3},{1,0},{2,1},{3,2},{4,7},{5,4},{6,5},{7,6},{8,11},{9,8},{10,9... | collective-permute-start | bytes 442376 | tf_op jit(solution)/shard_map/weight_one/ppermute | solution.py:28
  50.2 1.2 %copy-start.8 = (s32[1,4]{1,0:T(1,128)S(1)}, s32[1,4]{1,0:T(1,128)}, u32[]{:S(2)}) copy-start(s32[1,4]{1,0:T(1,128)} %param.7) | copy-start | bytes 52
  51.4 5.2 %collective-permute-start.10 = (bf16[4,8,48,384]{3,2,1,0:T(8,128)(2,1)}, bf16[4,8,48,384]{3,2,1,0:T(8,128)(2,1)}, u32[]{:S(2)}, u32[]{:S(2)}) collective-permute-start(bf16[4,8,48,384]{3,2,1,0:T(8,128)(2,1)} %pad_maximum_fusion), channel_id=1, source_target_pairs={{0,16},{16,0},{1,17},{17,1},{2,18},{18,2},{3,19},{19,3},{4,20},{20... | collective-permute-start | bytes 3538952 | tf_op jit(solution)/shard_map/weight_one/ppermute | solution.py:318
  51.9 17.9 %collective-permute-start.12 = (bf16[8,48,384]{2,1,0:T(8,128)(2,1)S(1)}, bf16[8,48,384]{2,1,0:T(8,128)(2,1)S(1)}, u32[]{:S(2)}, u32[]{:S(2)}) collective-permute-start(bf16[8,48,384]{2,1,0:T(8,128)(2,1)S(1)} %all-to-all-done.1), channel_id=1, source_target_pairs={{0,1},{1,2},{2,3},{3,0},{4,5},{5,6},{6,7},{7,4},{8,9},{9,10},{10,1... | collective-permute-start | bytes 884744 | tf_op jit(solution)/shard_map/weight_two/ppermute | solution.py:28
  52.3 17.5 %collective-permute-start.13 = (bf16[8,48,384]{2,1,0:T(8,128)(2,1)S(1)}, bf16[8,48,384]{2,1,0:T(8,128)(2,1)S(1)}, u32[]{:S(2)}, u32[]{:S(2)}) collective-permute-start(bf16[8,48,384]{2,1,0:T(8,128)(2,1)S(1)} %all-to-all-done.1), channel_id=1, source_target_pairs={{0,2},{1,3},{2,0},{3,1},{4,6},{5,7},{6,4},{7,5},{8,10},{9,11},{10,... | collective-permute-start | bytes 884744 | tf_op jit(solution)/shard_map/weight_two/ppermute | solution.py:28
  55.2 14.6 %collective-permute-start.14 = (bf16[8,48,384]{2,1,0:T(8,128)(2,1)S(1)}, bf16[8,48,384]{2,1,0:T(8,128)(2,1)S(1)}, u32[]{:S(2)}, u32[]{:S(2)}) collective-permute-start(bf16[8,48,384]{2,1,0:T(8,128)(2,1)S(1)} %all-to-all-done.1), channel_id=1, source_target_pairs={{0,3},{1,0},{2,1},{3,2},{4,7},{5,4},{6,5},{7,6},{8,11},{9,8},{10,9... | collective-permute-start | bytes 884744 | tf_op jit(solution)/shard_map/weight_two/ppermute | solution.py:28
  66.1 3.7 %collective-permute-start.11 = (f32[2,12,64]{2,1,0:T(8,128)S(1)}, f32[2,12,64]{2,1,0:T(8,128)S(1)}, u32[]{:S(2)}, u32[]{:S(2)}) collective-permute-start(f32[2,12,64]{2,1,0:T(8,128)S(1)} %get-tuple-element.49), channel_id=1, source_target_pairs={{0,4},{4,0},{8,12},{12,8},{1,5},{5,1},{9,13},{13,9},{2,6},{6,2},{1... | collective-permute-start | bytes 18440 | tf_op jit(solution)/shard_map/weight_two/ppermute | solution.py:32
  69.8 3.4 %copy-start.7 = (f32[384]{0:T(512)S(1)}, f32[384]{0:T(512)}, u32[]{:S(2)}) copy-start(f32[384]{0:T(512)} %param.9) | copy-start | bytes 4612
  70.0 9.0 %collective-permute-start.17 = (bf16[4,8,48,384]{3,2,1,0:T(8,128)(2,1)S(1)}, bf16[4,8,48,384]{3,2,1,0:T(8,128)(2,1)S(1)}, u32[]{:S(2)}, u32[]{:S(2)}) collective-permute-start(bf16[4,8,48,384]{3,2,1,0:T(8,128)(2,1)S(1)} %pad_maximum_fusion.1.mine), channel_id=1, source_target_pairs={{0,16},{16,0},{1,17},{17,1},{2,18},{18,2},{3,19},{19,3},{4,20},{20... | collective-permute-start | bytes 3538952 | tf_op jit(solution)/shard_map/weight_two/ppermute | solution.py:318
  70.1 5.3 %collective-permute-start.15 = (f32[2,12,64]{2,1,0:T(8,128)S(1)}, f32[2,12,64]{2,1,0:T(8,128)S(1)}, u32[]{:S(2)}, u32[]{:S(2)}) collective-permute-start(f32[2,12,64]{2,1,0:T(8,128)S(1)} %add.98), channel_id=1, source_target_pairs={{0,8},{4,12},{8,0},{12,4},{1,9},{5,13},{9,1},{13,5},{2,10},{6,14},... | collective-permute-start | bytes 18440 | tf_op jit(solution)/shard_map/second/ppermute | solution.py:32
  76.9 9.1 %collective-permute-start.16 = (bf16[2,12,64,128]{3,2,1,0:T(8,128)(2,1)S(1)}, bf16[2,12,64,128]{3,2,1,0:T(8,128)(2,1)S(1)}, u32[]{:S(2)}, u32[]{:S(2)}) collective-permute-start(bf16[2,12,64,128]{3,2,1,0:T(8,128)(2,1)S(1)} %multiply_convert_fusion.own), channel_id=1, source_target_pairs={{0,16},{16,32},{32,48},{48,64},{64,80},{80,96},{96,112},{112,128},... | collective-permute-start | bytes 1179656 | tf_op jit(solution)/shard_map/second/ppermute | solution.py:23
  79.1 1.0 copy-start.3
  93.4 8.0 %collective-permute-start.18 = (bf16[2,3,64,384]{3,2,1,0:T(8,128)(2,1)S(1)}, bf16[2,3,64,384]{3,2,1,0:T(8,128)(2,1)S(1)}, u32[]{:S(2)}, u32[]{:S(2)}) collective-permute-start(bf16[2,3,64,384]{3,2,1,0:T(8,128)(2,1)S(1)} %get-tuple-element.57), channel_id=1, source_target_pairs={{0,12},{4,0},{8,4},{12,8},{1,13},{5,1},{9,5},{13,9},{2,14},{6,2},{... | collective-permute-start | bytes 884744 | tf_op jit(solution)/shard_map/second/ppermute | solution.py:28
  96.2 8.9 %collective-permute-start.19 = (bf16[2,3,64,384]{3,2,1,0:T(8,128)(2,1)S(1)}, bf16[2,3,64,384]{3,2,1,0:T(8,128)(2,1)S(1)}, u32[]{:S(2)}, u32[]{:S(2)}) collective-permute-start(bf16[2,3,64,384]{3,2,1,0:T(8,128)(2,1)S(1)} %get-tuple-element.58), channel_id=1, source_target_pairs={{0,4},{4,8},{8,12},{12,0},{1,5},{5,9},{9,13},{13,1},{2,6},{6,10},{... | collective-permute-start | bytes 884744 | tf_op jit(solution)/shard_map/second/ppermute | solution.py:28
  101.4 6.3 %collective-permute-start.21 = (bf16[1,3,64,384]{3,2,1,0:T(8,128)(2,1)S(1)}, bf16[1,3,64,384]{3,2,1,0:T(8,128)(2,1)S(1)}, u32[]{:S(2)}, u32[]{:S(2)}) collective-permute-start(bf16[1,3,64,384]{3,2,1,0:T(8,128)(2,1)S(1)} %get-tuple-element.63), channel_id=1, source_target_pairs={{0,12},{4,0},{8,4},{12,8},{1,13},{5,1},{9,5},{13,9},{2,14},{6,2},{... | collective-permute-start | bytes 442376 | tf_op jit(solution)/shard_map/second/ppermute | solution.py:28
  105.1 6.4 %collective-permute-start.20 = (bf16[1,3,64,384]{3,2,1,0:T(8,128)(2,1)S(1)}, bf16[1,3,64,384]{3,2,1,0:T(8,128)(2,1)S(1)}, u32[]{:S(2)}, u32[]{:S(2)}) collective-permute-start(bf16[1,3,64,384]{3,2,1,0:T(8,128)(2,1)S(1)} %get-tuple-element.61), channel_id=1, source_target_pairs={{0,4},{4,8},{8,12},{12,0},{1,5},{5,9},{9,13},{13,1},{2,6},{6,10},{... | collective-permute-start | bytes 442376 | tf_op jit(solution)/shard_map/second/ppermute | solution.py:28

commit v9 on v8

--- a/solution.py
+++ b/solution.py
@@ -77,36 +77,24 @@
     out[...] = wide[...].astype(out.dtype)
 
 
-def conv_one_kernel(share, valid, place, *refs):
-    own_refs, halo_refs, mine_refs, other_ref = refs[:5], refs[5:7], refs[7:12], refs[12]
-    out, squares, frame_buf, acc, weight, wide, pieces = refs[13:]
-    frames, each, width, channels = own_refs[0].shape
-    rows = out.shape[1]
-    parts = rows // each
+def conv_one_kernel(share, valid, place, halo, own, *refs):
+    mine_refs, other_ref = refs[:4], refs[4]
+    out, squares, frame_buf, acc, weight, wide, pieces = refs[5:]
+    parts, frames, each, width, channels = own.shape
+    rows = parts * each
     cores, ys, zs = pieces.shape[:3]
     blank = jnp.zeros((width, channels), frame_buf.dtype)
     for slot in range(2 * frames):
         frame_buf[slot, 0] = blank
         frame_buf[slot, rows + 1] = blank
-
-    def put(slot, back, block):
-        top = lax.rem(place[2] + parts - back, parts) * each + 1
-        for j in range(each):
-            frame_buf[slot, top + j] = block[j]
-
-    for s in range(frames):
-        for back, ref in zip((0, 1, 3), own_refs):
-            put(frames + s, back, ref[s])
-        put(frames + s, 2, own_refs[3 + s][0])
-        for i, back in enumerate((0, 1, 3)):
-            put(s, back, halo_refs[0][i, s])
-        put(s, 2, halo_refs[1][s])
-    for i, back in enumerate((0, 1, 3, 2)):
+        source = halo if slot < frames else own
+        for row in range(rows):
+            frame_buf[slot, row + 1] = source[row // each, slot % frames, row % each]
+    for back in range(ys):
         y = lax.rem(place[1] + ys - back, ys)
         for z in range(zs):
-            ref, at = (mine_refs[i], z) if i < 3 else (mine_refs[3 + 2 * z // zs], z % (zs // 2))
-            pieces[place[0], y, z] = ref[at]
-            pieces[1 - place[0], y, z] = other_ref[i, z]
+            pieces[place[0], y, z] = mine_refs[back][z]
+            pieces[1 - place[0], y, z] = other_ref[back, z]
     assemble_one(pieces, weight, wide)
     for slot in range(2 * frames):
         pairs = [(s, slot - s) for s in range(frames) if 0 <= slot - s < 3]
@@ -180,13 +168,13 @@
 
 
 def conv_one_call(valid, place, own, halo, mine, other):
-    frames, each, width, channels = own[0].shape
-    rows = each * lax.axis_size("tile")
+    parts, frames, each, width, channels = own.shape
+    rows = parts * each
     zs, piece_rows, lanes = mine[0].shape
     flops = 2 * 6 * rows * width * 9 * channels * LANE
-    arrays = [*own, *halo, *mine, other]
+    arrays = [halo, own, *mine, other]
     return pl.pallas_call(
-        functools.partial(conv_one_kernel, channels * each // rows),
+        functools.partial(conv_one_kernel, channels // parts),
         out_shape=[
             jax.ShapeDtypeStruct((frames, rows, width, LANE), jnp.float32),
             jax.ShapeDtypeStruct((frames, rows, width), jnp.float32),
@@ -229,8 +217,7 @@
 def gathered(place, mine, other, i):
     ys, zs = mine.shape[:2]
     z, c, y = i // (2 * ys), i // ys % 2, i % ys
-    at = lax.rem(place[1] + ys - y, ys), z
-    return jnp.where(place[0] == c, mine[at].astype(jnp.float32), other[at].astype(jnp.float32))
+    return jnp.where(place[0] == c, mine[y, z].astype(jnp.float32), other[y, z].astype(jnp.float32))
 
 
 def assemble_two_kernel(place, mine, other, out, wide, piece_buf):
@@ -295,7 +282,7 @@
     with jax.named_scope("pixels"):
         mean_sq = jnp.mean(source * source, axis=-1, keepdims=True)
         hidden_one = jax.nn.silu(source * lax.rsqrt(mean_sq + EPS) * gain_one).astype(jnp.bfloat16)
-        own = [hidden_one, onward(hidden_one, 1), onward(hidden_one, -1)]
+        own = lax.all_gather(hidden_one, "tile")
 
     def column_of(piece):
         n = lax.axis_size("z")
@@ -307,29 +294,24 @@
         piece = jnp.pad(piece, ((0, 4 * piece_rows - shard), (0, 0)))
         piece = jnp.concatenate([piece[j * piece_rows : (j + 1) * piece_rows] for j in range(4)], axis=1)
         piece = jnp.pad(piece, ((0, TILE_ROWS - piece_rows), (0, 0)))
-        column = column_of(piece)
+        rows_take = pick(TILE_ROWS, shard, True, part - 2 * side, parts)
+        piece_two = jnp.dot(rows_take, conv_two, preferred_element_type=jnp.float32).astype(jnp.bfloat16)
+        column = column_of(jnp.concatenate([piece, piece_two], axis=0))
+        column, later = column[:, :TILE_ROWS], column[:, TILE_ROWS:]
 
     with jax.named_scope("pixels"):
-        own, column = lax.optimization_barrier((own, column))
-        own = own + [onward(own[1][:1], 1), onward(own[2][1:], -1)]
-        halo = [earlier(jnp.stack(own[:3])), earlier(jnp.concatenate(own[3:]))]
+        halo = earlier(own)
 
     def other_core(x):
         return lax.ppermute(x, "core", [(0, 1), (1, 0)])
 
     with jax.named_scope("weight_one"):
-        mine = [column, onward(column, 1, "group"), onward(column, -1, "group")]
-        conv_two, mine = lax.optimization_barrier((conv_two, mine))
-        half = column.shape[0] // 2
-        mine = mine + [onward(mine[1][:half], 1, "group"), onward(mine[2][half:], -1, "group")]
-        rows_take = pick(TILE_ROWS, shard, True, part - 2 * side, parts)
-        piece = jnp.dot(rows_take, conv_two, preferred_element_type=jnp.float32).astype(jnp.bfloat16)
-        later = column_of(piece)
-        mine, halo, later = lax.optimization_barrier((mine, halo, later))
-        swapped = other_core(jnp.stack(mine[:3] + [jnp.concatenate(mine[3:])]))
+        mine = [column] + [onward(column, d, "group") for d in range(1, lax.axis_size("group"))]
+        mine, halo = lax.optimization_barrier((mine, halo))
+        swapped = other_core(jnp.stack(mine))
 
     with jax.named_scope("weight_two"):
-        later = [later] + [onward(later, d, "group") for d in range(1, lax.axis_size("group"))]
+        later = lax.all_gather(later, "group")
 
     base = lax.axis_index(SLOT) * frames
     slots = base + jnp.arange(frames, dtype=jnp.int32)
@@ -343,11 +325,10 @@
     with jax.named_scope("weight_two"):
         squares = squares + across(squares, 1)
         squares, later = lax.optimization_barrier((squares, later))
-        mine = jnp.stack(later)
-        swapped = other_core(mine)
+        swapped = other_core(later)
         taps = shards * shard // channels
         weight_two = assemble_call(
-            assemble_two_kernel, place, mine, swapped, (taps * LANE, channels),
+            assemble_two_kernel, place, later, swapped, (taps * LANE, channels),
             [pltpu.VMEM((2 * TILE_ROWS, channels), jnp.float32)], "assemble_two"
         )
 

time: 116 us -> 129 us (1.11)
  waiting for transfers between devices: 31.4 us -> 54.8 us
  starting transfers between devices: 49.7 us -> 26.6 us
  between operations: 0.36 us -> 15.1 us
    all_gather x0 -> x2, waiting for transfers between devices: none -> 19.6 us  [the longest x1 19.6 us: body(): own = lax.all_gather(hidden_one, 'tile')]
    ppermute x15 -> x7, starting transfers between devices: 24.4 us -> 10.7 us  [onward(): return lax.ppermute(x, axis, [(i, (i + by) % n) for i in range(n)])]
    all_to_all x2 -> x1, starting transfers between devices: 14.6 us -> 8.57 us  [column_of(): lax.all_to_all(jnp.broadcast_to(piece, (n,) + piece.shape), 'z', 0, 0)]
    ppermute x15 -> x7, waiting for transfers between devices: 21.8 us -> 25 us  [onward(): return lax.ppermute(x, axis, [(i, (i + by) % n) for i in range(n)])]
    another operation x5 -> x2, other arithmetic: 2.63 us -> 0.36 us  [the longest x1 0.18 us: body(): swapped = other_core(jnp.stack(mine))]
    ppermute x3 -> x2, waiting for transfers between devices: 4.2 us -> 2.04 us  [earlier(): return lax.ppermute(x, SLOT, [(i, i + 1) for i in range(n - 1)])]
    ppermute x2, waiting for transfers between devices: 0.01 us -> 2.07 us  [other_core(): return lax.ppermute(x, 'core', [(0, 1), (1, 0)])]
    ppermute x3 -> x2, starting transfers between devices: 5.97 us -> 4.01 us  [earlier(): return lax.ppermute(x, SLOT, [(i, i + 1) for i in range(n - 1)])]
  transfers between devices with their start and end apart: 24 -> 16, of which waited for: 10 -> 11; matrix products, arithmetic and copies ran while one was open for 4% -> 3% of each run, Pallas kernels for 12% -> 10%
where the time goes in v9:
time: 129 us; the launch traced here: 127 us
  waiting for transfers between devices  54.8 us (42%)
  starting transfers between devices  26.6 us (21%)
  Pallas kernels  19.9 us (15%)
  between operations  15.1 us (12%)
  local copies, waits for them, and re-layouts  6.14 us (5%)
  other arithmetic  4.42 us (3%)
    ppermute x7, waiting for transfers between devices, onward(): return lax.ppermute(x, axis, [(i, (i + by) % n) for i in range(n)])  25 us
    all_gather x1, waiting for transfers between devices, body(): own = lax.all_gather(hidden_one, 'tile')  19.6 us
    ppermute x7, starting transfers between devices, onward(): return lax.ppermute(x, axis, [(i, (i + by) % n) for i in range(n)])  10.7 us
    pallas_call x1, Pallas kernels, conv_one_call(): pl.pallas_call(functools.partial(conv_one_kernel, channels // parts), out...  8.65 us
    all_to_all x1, starting transfers between devices, column_of(): lax.all_to_all(jnp.broadcast_to(piece, (n,) + piece.shape), 'z', 0, 0)  8.57 us
    pallas_call x1, Pallas kernels, conv_two_call(): pl.pallas_call(conv_two_kernel, out_shape=[jax.ShapeDtypeStruct(shape, jn...  7.33 us
    ppermute x2, waiting for transfers between devices, across(): lax.ppermute(x, 'tile', [(i, i ^ bit) for i in range(lax.axis_size('tile'...  5.98 us
    ppermute x2, starting transfers between devices, earlier(): return lax.ppermute(x, SLOT, [(i, i + 1) for i in range(n - 1)])  4.01 us
  transfers between devices with their start and end apart: 16, of which 11 were waited for; matrix products, arithmetic and copies ran while one was open for 3% of the time, Pallas kernels for 10%

profile of v9, /device:TPU:32, one launch (start us, length us, event | category | flops | bytes accessed | tf_op | source)
XLA Modules:
  0.0 127.3 jit_solution(1905279654001203361)
XLA Ops:
  7.4 0.0 copy-start
  7.4 0.0 all-gather.4.cloned.1.call-start
  7.4 1.1 fusion.3
  8.5 1.9 %fusion.11 = bf16[1,2,3,64,384]{4,3,2,1,0:T(8,128)(2,1)} fusion(bf16[1,2,3,64,384]{4,3,2,1,0:T(8,128)(2,1)} %param.6, f32[384]{0:T(512)} %param.8, f32[2,3,64]{2,1,0:T(4,128)S(1)} %add_rsqrt_fusion.1), kind=kLoop, calls=%fused_computation.17 | loop fusion | flops 1179648 | bytes 592896 | tf_op jit(solution)/shard_map/pixels/convert_element_type | solution.py:284
  10.5 0.0 all-gather.4.cloned.1.call-update
  10.5 0.0 copy-done.4
  10.5 0.2 fusion
  10.8 0.1 fusion.19
  10.9 0.0 copy-done
  10.9 0.2 convolution_convert_fusion.1
  11.1 0.9 broadcast_in_dim.15
  12.0 8.6 %all-to-all-start = ((bf16[8,96,384]{2,1,0:T(8,128)(2,1)}), bf16[8,96,384]{2,1,0:T(8,128)(2,1)S(1)}, u32[]{:S(2)}, u32[]{:S(2)}) async-start(bf16[8,96,384]{2,1,0:T(8,128)(2,1)} %broadcast_in_dim.15), calls=%async_computation | async-start | bytes 1179648 | tf_op jit(solution)/shard_map/pieces/all_to_all | solution.py:289
  20.5 0.0 all-gather.6.cloned.1.call-start
  20.5 19.6 %all-gather.4.cloned.1.call-done.own = bf16[4,2,3,64,384]{4,3,2,1,0:T(8,128)(2,1)} async-done(((bf16[1,2,3,64,384]{4,3,2,1,0:T(8,128)(2,1)}), bf16[4,2,3,64,384]{4,3,2,1,0:T(8,128)(2,1)}) %all-gather.4.cloned.1.call-update) | async-done | bytes 1179664 | tf_op jit(solution)/shard_map/pixels/all_gather | solution.py:285
  40.2 1.9 %collective-permute-start.3 = (bf16[4,2,3,64,384]{4,3,2,1,0:T(8,128)(2,1)}, bf16[4,2,3,64,384]{4,3,2,1,0:T(8,128)(2,1)S(1)}, u32[]{:S(2)}, u32[]{:S(2)}) collective-permute-start(bf16[4,2,3,64,384]{4,3,2,1,0:T(8,128)(2,1)} %all-gather.4.cloned.1.call-done.own), channel_id=1, source_target_pairs={{0,16},{16,32},{32,48},{48,64},{64,80},{80,96},{96,112},{112,128},... | collective-permute-start | bytes 3538952 | tf_op jit(solution)/shard_map/pixels/ppermute | solution.py:23
  42.1 0.0 all-to-all-done
  42.1 0.8 fusion.22
  42.9 1.5 %collective-permute-start = (bf16[8,48,384]{2,1,0:T(8,128)(2,1)S(1)}, bf16[8,48,384]{2,1,0:T(8,128)(2,1)S(1)}, u32[]{:S(2)}, u32[]{:S(2)}) collective-permute-start(bf16[8,48,384]{2,1,0:T(8,128)(2,1)S(1)} %get-tuple-element.20.refs_0_), channel_id=1, source_target_pairs={{0,1},{1,2},{2,3},{3,0},{4,5},{5,6},{6,7},{7,4},{8,9},{9,10},{10,1... | collective-permute-start | bytes 884744 | tf_op jit(solution)/shard_map/weight_one/ppermute | solution.py:28
  44.4 2.7 %collective-permute-start.1 = (bf16[8,48,384]{2,1,0:T(8,128)(2,1)S(1)}, bf16[8,48,384]{2,1,0:T(8,128)(2,1)S(1)}, u32[]{:S(2)}, u32[]{:S(2)}) collective-permute-start(bf16[8,48,384]{2,1,0:T(8,128)(2,1)S(1)} %get-tuple-element.20.refs_0_), channel_id=1, source_target_pairs={{0,2},{1,3},{2,0},{3,1},{4,6},{5,7},{6,4},{7,5},{8,10},{9,11},{10,... | collective-permute-start | bytes 884744 | tf_op jit(solution)/shard_map/weight_one/ppermute | solution.py:28
  47.1 1.4 %collective-permute-start.2 = (bf16[8,48,384]{2,1,0:T(8,128)(2,1)S(1)}, bf16[8,48,384]{2,1,0:T(8,128)(2,1)S(1)}, u32[]{:S(2)}, u32[]{:S(2)}) collective-permute-start(bf16[8,48,384]{2,1,0:T(8,128)(2,1)S(1)} %get-tuple-element.20.refs_0_), channel_id=1, source_target_pairs={{0,3},{1,0},{2,1},{3,2},{4,7},{5,4},{6,5},{7,6},{8,11},{9,8},{10,9... | collective-permute-start | bytes 884744 | tf_op jit(solution)/shard_map/weight_one/ppermute | solution.py:28
  48.5 0.0 all-gather.6.cloned.1.call-update
  48.5 4.8 %collective-permute-done.refs_1_ = bf16[8,48,384]{2,1,0:T(8,128)(2,1)S(1)} collective-permute-done((bf16[8,48,384]{2,1,0:T(8,128)(2,1)S(1)}, bf16[8,48,384]{2,1,0:T(8,128)(2,1)S(1)}, u32[]{:S(2)}, u32[]{:S(2)}) %collective-permute-start) | collective-permute-done | bytes 294944 | tf_op jit(solution)/shard_map/weight_one/ppermute | solution.py:28
  53.3 7.3 %collective-permute-done.1.refs_2_ = bf16[8,48,384]{2,1,0:T(8,128)(2,1)S(1)} collective-permute-done((bf16[8,48,384]{2,1,0:T(8,128)(2,1)S(1)}, bf16[8,48,384]{2,1,0:T(8,128)(2,1)S(1)}, u32[]{:S(2)}, u32[]{:S(2)}) %collective-permute-start.1) | collective-permute-done | bytes 294944 | tf_op jit(solution)/shard_map/weight_one/ppermute | solution.py:28
  60.6 0.3 collective-permute-done.2.refs_3_
  60.9 0.0 collective-permute-done.3.halo
  60.9 1.0 copy-done.6
  61.9 0.2 pad_maximum_fusion
  62.1 0.3 collective-permute-start.4
  62.4 0.2 copy-done.7
  62.5 0.2 reduce-window_clone.1
  62.7 0.1 pad_add_fusion.place
  62.8 0.2 fusion.21
  63.0 0.1 compare_convert_fusion.valid
  63.1 2.1 %collective-permute-done.4.refs_4_ = bf16[4,8,48,384]{3,2,1,0:T(8,128)(2,1)} collective-permute-done((bf16[4,8,48,384]{3,2,1,0:T(8,128)(2,1)S(1)}, bf16[4,8,48,384]{3,2,1,0:T(8,128)(2,1)}, u32[]{:S(2)}, u32[]{:S(2)}) %collective-permute-start.4) | collective-permute-done | bytes 1179680 | tf_op jit(solution)/shard_map/weight_one/ppermute | solution.py:306
  65.1 8.7 %conv_one.1 = (f32[2,12,64,128]{3,2,1,0:T(8,128)S(1)}, f32[2,12,64]{2,1,0:T(8,128)S(1)}) custom-call(f32[2,3]{1,0:T(2,128)S(1)} %compare_convert_fusion.valid, s32[3]{0:T(128)S(1)} %pad_add_fusion.place, bf16[4,2,3,64,384]{4,3,2,1,0:T(8,128)(2,1)} %copy-done.6, bf16[4,2,3,64,384]{4,3,2,1,0:T(8,128)(2,1)} %all-gather.4.cloned.1.call-done.own, ...), custom_call_target="tpu_custom_call" | custom-call | flops 4076863488 | bytes 6000000 | tf_op jit(solution)/shard_map/first/conv_one/pallas_call | solution.py:176
  73.8 0.5 collective-permute-start.5
  74.3 3.3 %collective-permute-done.5 = f32[2,12,64]{2,1,0:T(8,128)S(1)} collective-permute-done((f32[2,12,64]{2,1,0:T(8,128)S(1)}, f32[2,12,64]{2,1,0:T(8,128)S(1)}, u32[]{:S(2)}, u32[]{:S(2)}) %collective-permute-start.5) | collective-permute-done | bytes 6176 | tf_op jit(solution)/shard_map/weight_two/ppermute | solution.py:32
  77.6 0.1 collective-permute-start.8
  77.7 2.4 %collective-permute-start.6 = (f32[2,12,64]{2,1,0:T(8,128)S(1)}, f32[2,12,64]{2,1,0:T(8,128)S(1)}, u32[]{:S(2)}, u32[]{:S(2)}) collective-permute-start(f32[2,12,64]{2,1,0:T(8,128)S(1)} %add.99), channel_id=1, source_target_pairs={{0,8},{4,12},{8,0},{12,4},{1,9},{5,13},{9,1},{13,5},{2,10},{6,14},... | collective-permute-start | bytes 18440 | tf_op jit(solution)/shard_map/second/ppermute | solution.py:32
  80.1 0.0 copy-done.5
  80.1 0.1 reshape.33
  80.2 0.2 dynamic-slice_reduce_fusion
  80.4 2.6 %collective-permute-done.6 = f32[2,12,64]{2,1,0:T(8,128)S(1)} collective-permute-done((f32[2,12,64]{2,1,0:T(8,128)S(1)}, f32[2,12,64]{2,1,0:T(8,128)S(1)}, u32[]{:S(2)}, u32[]{:S(2)}) %collective-permute-start.6) | collective-permute-done | bytes 6176 | tf_op jit(solution)/shard_map/second/ppermute | solution.py:32
  83.1 0.3 multiply_convert_fusion.own
  83.4 2.1 %collective-permute-start.7 = (bf16[2,12,64,128]{3,2,1,0:T(8,128)(2,1)S(1)}, bf16[2,12,64,128]{3,2,1,0:T(8,128)(2,1)S(1)}, u32[]{:S(2)}, u32[]{:S(2)}) collective-permute-start(bf16[2,12,64,128]{3,2,1,0:T(8,128)(2,1)S(1)} %multiply_convert_fusion.own), channel_id=1, source_target_pairs={{0,16},{16,32},{32,48},{48,64},{64,80},{80,96},{96,112},{112,128},... | collective-permute-start | bytes 1179656 | tf_op jit(solution)/shard_map/second/ppermute | solution.py:23
  85.5 0.0 collective-permute-done.8.other
  85.5 0.0 copy-start.3
  85.5 1.0 copy-done.3
  86.5 0.0 copy-done.1
  86.5 3.9 %assemble_two.1.weight = bf16[3456,384]{1,0:T(8,128)(2,1)} custom-call(s32[3]{0:T(128)S(1)} %pad_add_fusion.place, bf16[4,8,48,384]{3,2,1,0:T(8,128)(2,1)S(1)} %bitcast.26, bf16[4,8,48,384]{3,2,1,0:T(8,128)(2,1)} %copy-done.3), custom_call_target="tpu_custom_call" | custom-call | flops 4000000 | bytes 5000000 | tf_op jit(solution)/shard_map/weight_two/assemble_two/pallas_call | solution.py:250
  90.4 2.0 %collective-permute-done.7.halo = bf16[2,12,64,128]{3,2,1,0:T(8,128)(2,1)S(1)} collective-permute-done((bf16[2,12,64,128]{3,2,1,0:T(8,128)(2,1)S(1)}, bf16[2,12,64,128]{3,2,1,0:T(8,128)(2,1)S(1)}, u32[]{:S(2)}, u32[]{:S(2)}) %collective-permute-start.7) | collective-permute-done | bytes 393248 | tf_op jit(solution)/shard_map/second/ppermute | solution.py:23
  92.5 7.3 %conv_two.1 = (bf16[2,3,64,384]{3,2,1,0:T(8,128)(2,1)S(1)}, bf16[2,3,64,384]{3,2,1,0:T(8,128)(2,1)S(1)}, bf16[2,3,64,384]{3,2,1,0:T(8,128)(2,1)S(1)}, bf16[1,3,6...) custom-call(f32[2,3]{1,0:T(2,128)S(1)} %compare_convert_fusion.valid, s32[3]{0:T(128)S(1)} %pad_add_fusion.place, ...), custom_call_target="tpu_custom_call" | custom-call | flops 4076863488 | bytes 6000000 | tf_op jit(solution)/shard_map/second/conv_two/pallas_call | solution.py:202
  99.8 0.0 copy-start.2
  99.8 1.7 %collective-permute-start.9 = (bf16[2,3,64,384]{3,2,1,0:T(8,128)(2,1)S(1)}, bf16[2,3,64,384]{3,2,1,0:T(8,128)(2,1)S(1)}, u32[]{:S(2)}, u32[]{:S(2)}) collective-permute-start(bf16[2,3,64,384]{3,2,1,0:T(8,128)(2,1)S(1)} %get-tuple-element.29), channel_id=1, source_target_pairs={{0,12},{4,0},{8,4},{12,8},{1,13},{5,1},{9,5},{13,9},{2,14},{6,2},{... | collective-permute-start | bytes 884744 | tf_op jit(solution)/shard_map/second/ppermute | solution.py:28
  101.5 0.4 collective-permute-start.10
  101.9 6.3 %collective-permute-done.9 = bf16[2,3,64,384]{3,2,1,0:T(8,128)(2,1)S(1)} collective-permute-done((bf16[2,3,64,384]{3,2,1,0:T(8,128)(2,1)S(1)}, bf16[2,3,64,384]{3,2,1,0:T(8,128)(2,1)S(1)}, u32[]{:S(2)}, u32[]{:S(2)}) %collective-permute-start.9) | collective-permute-done | bytes 294944 | tf_op jit(solution)/shard_map/second/ppermute | solution.py:28
  108.3 2.9 %collective-permute-start.12 = (bf16[1,3,64,384]{3,2,1,0:T(8,128)(2,1)S(1)}, bf16[1,3,64,384]{3,2,1,0:T(8,128)(2,1)S(1)}, u32[]{:S(2)}, u32[]{:S(2)}) collective-permute-start(bf16[1,3,64,384]{3,2,1,0:T(8,128)(2,1)S(1)} %get-tuple-element.37), channel_id=1, source_target_pairs={{0,12},{4,0},{8,4},{12,8},{1,13},{5,1},{9,5},{13,9},{2,14},{6,2},{... | collective-permute-start | bytes 442376 | tf_op jit(solution)/shard_map/second/ppermute | solution.py:28
  111.2 0.0 collective-permute-done.10
  111.2 0.1 collective-permute-start.11
  111.3 2.5 %collective-permute-done.12 = bf16[1,3,64,384]{3,2,1,0:T(8,128)(2,1)S(1)} collective-permute-done((bf16[1,3,64,384]{3,2,1,0:T(8,128)(2,1)S(1)}, bf16[1,3,64,384]{3,2,1,0:T(8,128)(2,1)S(1)}, u32[]{:S(2)}, u32[]{:S(2)}) %collective-permute-start.12) | collective-permute-done | bytes 147488 | tf_op jit(solution)/shard_map/second/ppermute | solution.py:28
  113.9 3.8 %collective-permute-done.11 = bf16[1,3,64,384]{3,2,1,0:T(8,128)(2,1)S(1)} collective-permute-done((bf16[1,3,64,384]{3,2,1,0:T(8,128)(2,1)S(1)}, bf16[1,3,64,384]{3,2,1,0:T(8,128)(2,1)S(1)}, u32[]{:S(2)}, u32[]{:S(2)}) %collective-permute-start.11) | collective-permute-done | bytes 147488 | tf_op jit(solution)/shard_map/second/ppermute | solution.py:28
  117.7 0.2 fusion.4
  117.8 0.7 broadcast_in_dim.16
  118.5 1.3 %broadcast_in_dim_reshape.3 = bf16[1,2,6,128,384]{4,3,2,1,0:T(8,128)(2,1)} reshape(bf16[2,3,2,64,2,384]{5,4,3,2,1,0:T(2,128)(2,1)S(1)} %broadcast_in_dim.16) | data formatting | bytes 2359296 | tf_op jit(solution)/shard_map/broadcast_in_dim;reshape | solution.py:355
  (20 shorter events, 0.2 us)
Async XLA Ops:
  7.4 3.5 %copy-start = (bf16[162,384]{1,0:T(8,128)(2,1)S(1)}, bf16[162,384]{1,0:T(8,128)(2,1)}, u32[]{:S(2)}) copy-start(bf16[162,384]{1,0:T(8,128)(2,1)} %param.11) | copy-start | bytes 373252
  7.4 3.2 %copy-start.4 = (bf16[162,384]{1,0:T(8,128)(2,1)S(1)}, bf16[162,384]{1,0:T(8,128)(2,1)}, u32[]{:S(2)}) copy-start(bf16[162,384]{1,0:T(8,128)(2,1)} %param.10) | copy-start | bytes 373252
  7.4 32.8 %all-gather.4.cloned.1.call-start = ((), (), s32[]{:S(2)}) async-start(), calls=%async_computation.1 | async-start | bytes 1474560 | tf_op jit(solution)/shard_map/pixels/all_gather | solution.py:285
  12.0 30.1 %all-to-all-start = ((bf16[8,96,384]{2,1,0:T(8,128)(2,1)}), bf16[8,96,384]{2,1,0:T(8,128)(2,1)S(1)}, u32[]{:S(2)}, u32[]{:S(2)}) async-start(bf16[8,96,384]{2,1,0:T(8,128)(2,1)} %broadcast_in_dim.15), calls=%async_computation | async-start | bytes 1179648 | tf_op jit(solution)/shard_map/pieces/all_to_all | solution.py:289
  20.5 57.1 %all-gather.6.cloned.1.call-start = ((), (), s32[]{:S(2)}) async-start(), calls=%async_computation.2 | async-start | bytes 1474560 | tf_op jit(solution)/shard_map/weight_two/all_gather | solution.py:314
  40.2 20.7 %collective-permute-start.3 = (bf16[4,2,3,64,384]{4,3,2,1,0:T(8,128)(2,1)}, bf16[4,2,3,64,384]{4,3,2,1,0:T(8,128)(2,1)S(1)}, u32[]{:S(2)}, u32[]{:S(2)}) collective-permute-start(bf16[4,2,3,64,384]{4,3,2,1,0:T(8,128)(2,1)} %all-gather.4.cloned.1.call-done.own), channel_id=1, source_target_pairs={{0,16},{16,32},{32,48},{48,64},{64,80},{80,96},{96,112},{112,128},... | collective-permute-start | bytes 3538952 | tf_op jit(solution)/shard_map/pixels/ppermute | solution.py:23
  42.9 10.4 %collective-permute-start = (bf16[8,48,384]{2,1,0:T(8,128)(2,1)S(1)}, bf16[8,48,384]{2,1,0:T(8,128)(2,1)S(1)}, u32[]{:S(2)}, u32[]{:S(2)}) collective-permute-start(bf16[8,48,384]{2,1,0:T(8,128)(2,1)S(1)} %get-tuple-element.20.refs_0_), channel_id=1, source_target_pairs={{0,1},{1,2},{2,3},{3,0},{4,5},{5,6},{6,7},{7,4},{8,9},{9,10},{10,1... | collective-permute-start | bytes 884744 | tf_op jit(solution)/shard_map/weight_one/ppermute | solution.py:28
  44.4 16.2 %collective-permute-start.1 = (bf16[8,48,384]{2,1,0:T(8,128)(2,1)S(1)}, bf16[8,48,384]{2,1,0:T(8,128)(2,1)S(1)}, u32[]{:S(2)}, u32[]{:S(2)}) collective-permute-start(bf16[8,48,384]{2,1,0:T(8,128)(2,1)S(1)} %get-tuple-element.20.refs_0_), channel_id=1, source_target_pairs={{0,2},{1,3},{2,0},{3,1},{4,6},{5,7},{6,4},{7,5},{8,10},{9,11},{10,... | collective-permute-start | bytes 884744 | tf_op jit(solution)/shard_map/weight_one/ppermute | solution.py:28
  47.1 13.8 %collective-permute-start.2 = (bf16[8,48,384]{2,1,0:T(8,128)(2,1)S(1)}, bf16[8,48,384]{2,1,0:T(8,128)(2,1)S(1)}, u32[]{:S(2)}, u32[]{:S(2)}) collective-permute-start(bf16[8,48,384]{2,1,0:T(8,128)(2,1)S(1)} %get-tuple-element.20.refs_0_), channel_id=1, source_target_pairs={{0,3},{1,0},{2,1},{3,2},{4,7},{5,4},{6,5},{7,6},{8,11},{9,8},{10,9... | collective-permute-start | bytes 884744 | tf_op jit(solution)/shard_map/weight_one/ppermute | solution.py:28
  60.9 1.0 copy-start.6
  61.9 0.7 copy-start.7
  62.1 3.1 %collective-permute-start.4 = (bf16[4,8,48,384]{3,2,1,0:T(8,128)(2,1)S(1)}, bf16[4,8,48,384]{3,2,1,0:T(8,128)(2,1)}, u32[]{:S(2)}, u32[]{:S(2)}) collective-permute-start(bf16[4,8,48,384]{3,2,1,0:T(8,128)(2,1)S(1)} %pad_maximum_fusion), channel_id=1, source_target_pairs={{0,16},{16,0},{1,17},{17,1},{2,18},{18,2},{3,19},{19,3},{4,20},{20... | collective-permute-start | bytes 3538952 | tf_op jit(solution)/shard_map/weight_one/ppermute | solution.py:306
  63.1 17.0 %copy-start.5 = (f32[384]{0:T(512)S(1)}, f32[384]{0:T(512)}, u32[]{:S(2)}) copy-start(f32[384]{0:T(512)} %param.9) | copy-start | bytes 4612
  73.8 3.8 %collective-permute-start.5 = (f32[2,12,64]{2,1,0:T(8,128)S(1)}, f32[2,12,64]{2,1,0:T(8,128)S(1)}, u32[]{:S(2)}, u32[]{:S(2)}) collective-permute-start(f32[2,12,64]{2,1,0:T(8,128)S(1)} %get-tuple-element.25), channel_id=1, source_target_pairs={{0,4},{4,0},{8,12},{12,8},{1,5},{5,1},{9,13},{13,9},{2,6},{6,2},{1... | collective-permute-start | bytes 18440 | tf_op jit(solution)/shard_map/weight_two/ppermute | solution.py:32
  77.6 8.9 %copy-start.1 = (bf16[32,48,384]{2,1,0:T(8,128)(2,1)S(1)}, bf16[32,48,384]{2,1,0:T(8,128)(2,1)}, u32[]{:S(2)}) copy-start(bf16[32,48,384]{2,1,0:T(8,128)(2,1)} %all-gather.6.cloned.1.call-done) | copy-start | bytes 3538948
  77.6 7.8 %collective-permute-start.8 = (bf16[4,8,48,384]{3,2,1,0:T(8,128)(2,1)}, bf16[4,8,48,384]{3,2,1,0:T(8,128)(2,1)S(1)}, u32[]{:S(2)}, u32[]{:S(2)}) collective-permute-start(bf16[4,8,48,384]{3,2,1,0:T(8,128)(2,1)} %bitcast.25), channel_id=1, source_target_pairs={{0,16},{16,0},{1,17},{17,1},{2,18},{18,2},{3,19},{19,3},{4,20},{20... | collective-permute-start | bytes 3538952 | tf_op jit(solution)/shard_map/weight_two/ppermute | solution.py:306
  77.7 5.3 %collective-permute-start.6 = (f32[2,12,64]{2,1,0:T(8,128)S(1)}, f32[2,12,64]{2,1,0:T(8,128)S(1)}, u32[]{:S(2)}, u32[]{:S(2)}) collective-permute-start(f32[2,12,64]{2,1,0:T(8,128)S(1)} %add.99), channel_id=1, source_target_pairs={{0,8},{4,12},{8,0},{12,4},{1,9},{5,13},{9,1},{13,5},{2,10},{6,14},... | collective-permute-start | bytes 18440 | tf_op jit(solution)/shard_map/second/ppermute | solution.py:32
  83.4 9.1 %collective-permute-start.7 = (bf16[2,12,64,128]{3,2,1,0:T(8,128)(2,1)S(1)}, bf16[2,12,64,128]{3,2,1,0:T(8,128)(2,1)S(1)}, u32[]{:S(2)}, u32[]{:S(2)}) collective-permute-start(bf16[2,12,64,128]{3,2,1,0:T(8,128)(2,1)S(1)} %multiply_convert_fusion.own), channel_id=1, source_target_pairs={{0,16},{16,32},{32,48},{48,64},{64,80},{80,96},{96,112},{112,128},... | collective-permute-start | bytes 1179656 | tf_op jit(solution)/shard_map/second/ppermute | solution.py:23
  85.5 1.0 copy-start.3
  99.8 17.9 %copy-start.2 = (bf16[1,2,3,64,384]{4,3,2,1,0:T(8,128)(2,1)S(1)}, bf16[1,2,3,64,384]{4,3,2,1,0:T(8,128)(2,1)}, u32[]{:S(2)}) copy-start(bf16[1,2,3,64,384]{4,3,2,1,0:T(8,128)(2,1)} %param.6) | copy-start | bytes 884740
  99.8 8.4 %collective-permute-start.9 = (bf16[2,3,64,384]{3,2,1,0:T(8,128)(2,1)S(1)}, bf16[2,3,64,384]{3,2,1,0:T(8,128)(2,1)S(1)}, u32[]{:S(2)}, u32[]{:S(2)}) collective-permute-start(bf16[2,3,64,384]{3,2,1,0:T(8,128)(2,1)S(1)} %get-tuple-element.29), channel_id=1, source_target_pairs={{0,12},{4,0},{8,4},{12,8},{1,13},{5,1},{9,5},{13,9},{2,14},{6,2},{... | collective-permute-start | bytes 884744 | tf_op jit(solution)/shard_map/second/ppermute | solution.py:28
  101.5 9.7 %collective-permute-start.10 = (bf16[2,3,64,384]{3,2,1,0:T(8,128)(2,1)S(1)}, bf16[2,3,64,384]{3,2,1,0:T(8,128)(2,1)S(1)}, u32[]{:S(2)}, u32[]{:S(2)}) collective-permute-start(bf16[2,3,64,384]{3,2,1,0:T(8,128)(2,1)S(1)} %get-tuple-element.30), channel_id=1, source_target_pairs={{0,4},{4,8},{8,12},{12,0},{1,5},{5,9},{9,13},{13,1},{2,6},{6,10},{... | collective-permute-start | bytes 884744 | tf_op jit(solution)/shard_map/second/ppermute | solution.py:28
  108.3 5.6 %collective-permute-start.12 = (bf16[1,3,64,384]{3,2,1,0:T(8,128)(2,1)S(1)}, bf16[1,3,64,384]{3,2,1,0:T(8,128)(2,1)S(1)}, u32[]{:S(2)}, u32[]{:S(2)}) collective-permute-start(bf16[1,3,64,384]{3,2,1,0:T(8,128)(2,1)S(1)} %get-tuple-element.37), channel_id=1, source_target_pairs={{0,12},{4,0},{8,4},{12,8},{1,13},{5,1},{9,5},{13,9},{2,14},{6,2},{... | collective-permute-start | bytes 442376 | tf_op jit(solution)/shard_map/second/ppermute | solution.py:28
  111.2 6.4 %collective-permute-start.11 = (bf16[1,3,64,384]{3,2,1,0:T(8,128)(2,1)S(1)}, bf16[1,3,64,384]{3,2,1,0:T(8,128)(2,1)S(1)}, u32[]{:S(2)}, u32[]{:S(2)}) collective-permute-start(bf16[1,3,64,384]{3,2,1,0:T(8,128)(2,1)S(1)} %get-tuple-element.35), channel_id=1, source_target_pairs={{0,4},{4,8},{8,12},{12,0},{1,5},{5,9},{9,13},{13,1},{2,6},{6,10},{... | collective-permute-start | bytes 442376 | tf_op jit(solution)/shard_map/second/ppermute | solution.py:28
Sparse Core Ops, SparseCore 0:
  10.6 29.5 all-gather.3
Sparse Core Ops, SparseCore 1:
  48.6 25.3 all-gather.5

commit v10 on v6

--- a/solution.py
+++ b/solution.py
@@ -79,7 +79,7 @@
     out[...] = wide[...].astype(out.dtype)
 
 
-def conv_one_kernel(share, valid, place, halo, own, mine, other, out, frame_buf, acc, weight, wide):
+def conv_one_kernel(share, valid, place, halo, own, mine, other, out, squares, frame_buf, acc, weight, wide):
     parts, frames, each, width, channels = own.shape
     rows = parts * each
     blank = jnp.zeros((width, channels), own.dtype)
@@ -117,25 +117,23 @@
         left = jnp.where(col == 0, 0.0, pltpu.roll(acc[s, 0], 1, 0))
         right = jnp.where(col == width - 1, 0.0, pltpu.roll(acc[s, 2], pixels - 1, 0))
         done = jnp.where(lane < share, acc[s, 1] + left + right, 0.0)
-        out[s] = done.reshape(rows, width, LANE)
-
-
-def conv_two_kernel(valid, place, halo, own, weight, *rest):
-    *outs, taps, acc = rest
-    frames, rows, width, lanes = own.shape
-    parts = len(outs)
-    each = rows // parts
+        done = done.reshape(rows, width, LANE)
+        out[s] = done
+        squares[s] = jnp.sum(done * done, axis=-1)
+
+
+def add_frames(valid, slots, source, weight, taps, add):
+    frames, rows, width, lanes = source.shape
     channels = weight.shape[1]
     clear_border(taps)
-    for slot in range(2 * frames):
-        source = halo if slot < frames else own
+    for slot in slots:
         for row in range(rows):
-            fill_shifted(taps, slot, row + 1, source[slot % frames, row])
-    for slot in range(2 * frames):
+            fill_shifted(taps, slot % frames, row + 1, source[slot % frames, row])
+    for slot in slots:
         pairs = [(s, slot - s) for s in range(frames) if 0 <= slot - s < 3]
         columns = jnp.concatenate(
             [
-                taps[e, slot, b : b + rows].reshape(rows * width, lanes)
+                taps[e, slot % frames, b : b + rows].reshape(rows * width, lanes)
                 for b in range(3)
                 for e in range(3)
             ],
@@ -145,16 +143,36 @@
         packed = blocks[0] if len(blocks) == 1 else jnp.concatenate(blocks, axis=1)
         term = jnp.dot(columns, packed, preferred_element_type=jnp.float32)
         for i, (s, a) in enumerate(pairs):
-            piece = valid[s, a] * term[:, i * channels : (i + 1) * channels]
-            if a == 0:
-                acc[s] = piece
-            else:
-                acc[s] = acc[s] + piece
-    for d in range(parts):
+            add(s, valid[s, a] * term[:, i * channels : (i + 1) * channels])
+
+
+def conv_two_own_kernel(valid, own, weight, acc, taps):
+    frames = own.shape[0]
+    seen = set()
+
+    def add(s, piece):
+        acc[s] = acc[s] + piece if s in seen else piece
+        seen.add(s)
+
+    add_frames(valid, range(frames, 2 * frames), own, weight, taps, add)
+
+
+def conv_two_halo_kernel(valid, place, halo, weight, started, own_sum, up, down, up_last, down_last, taps, acc):
+    frames, rows, width, _ = halo.shape
+    each = own_sum.shape[1]
+    parts = rows // each
+    seen = set()
+
+    def add(s, piece):
+        acc[s] = (acc if s in seen else started)[s] + piece
+        seen.add(s)
+
+    add_frames(valid, range(frames), halo, weight, taps, add)
+    for ref, d, s, at in ((own_sum, 0, 0, 0), (own_sum, 0, 1, 1), (up, 2, 0, 0), (up, 1, 1, 1),
+                          (down, 3, 0, 0), (down, 2, 1, 1), (up_last, 1, 0, 0), (down_last, 3, 1, 0)):
         top = pl.multiple_of(lax.rem(place[2] + d, parts) * (each * width), 64)
-        for s in range(frames):
-            done = acc[s, pl.ds(top, each * width), :].astype(outs[d].dtype)
-            outs[d][s] = done.reshape(each, width, channels)
+        done = acc[s, pl.ds(top, each * width), :].astype(ref.dtype)
+        ref[at] = done.reshape(each, width, done.shape[1])
 
 
 VMEM = pl.BlockSpec(memory_space=pltpu.VMEM)
@@ -168,9 +186,12 @@
     flops = 2 * 6 * rows * width * 9 * channels * LANE
     return pl.pallas_call(
         functools.partial(conv_one_kernel, channels // parts),
-        out_shape=jax.ShapeDtypeStruct((frames, rows, width, LANE), jnp.float32),
+        out_shape=[
+            jax.ShapeDtypeStruct((frames, rows, width, LANE), jnp.float32),
+            jax.ShapeDtypeStruct((frames, rows, width), jnp.float32),
+        ],
         in_specs=[SMEM, SMEM, VMEM, VMEM, VMEM, VMEM],
-        out_specs=VMEM,
+        out_specs=[VMEM, VMEM],
         scratch_shapes=[
             pltpu.VMEM((2 * frames, rows + 2, width, channels), jnp.bfloat16),
             pltpu.VMEM((frames, 3, rows * width, LANE), jnp.float32),
@@ -183,23 +204,38 @@
     )(valid, place, halo, own, mine, other)
 
 
-def conv_two_call(valid, place, halo, own, weight, parts):
+def conv_two_own_call(valid, own, weight):
     frames, rows, width, lanes = own.shape
     channels = weight.shape[1]
-    flops = 2 * 6 * rows * width * 9 * lanes * channels
     return pl.pallas_call(
-        conv_two_kernel,
-        out_shape=[jax.ShapeDtypeStruct((frames, rows // parts, width, channels), jnp.bfloat16)] * parts,
+        conv_two_own_kernel,
+        out_shape=jax.ShapeDtypeStruct((frames, rows * width, channels), jnp.float32),
+        in_specs=[SMEM, VMEM, VMEM],
+        out_specs=VMEM,
+        scratch_shapes=[pltpu.VMEM((3, frames, rows + 2, width, lanes), jnp.bfloat16)],
+        compiler_params=PARAMS,
+        cost_estimate=pl.CostEstimate(flops=3_000_000_000, bytes_accessed=5_000_000, transcendentals=0),
+        name="conv_two_own",
+    )(valid, own, weight)
+
+
+def conv_two_halo_call(valid, place, halo, weight, started, parts):
+    frames, rows, width, lanes = halo.shape
+    channels = weight.shape[1]
+    shapes = [(n, rows // parts, width, channels) for n in (frames, frames, frames, 1, 1)]
+    return pl.pallas_call(
+        conv_two_halo_kernel,
+        out_shape=[jax.ShapeDtypeStruct(shape, jnp.bfloat16) for shape in shapes],
         in_specs=[SMEM, SMEM, VMEM, VMEM, VMEM],
-        out_specs=[VMEM] * parts,
+        out_specs=[VMEM] * len(shapes),
         scratch_shapes=[
-            pltpu.VMEM((3, 2 * frames, rows + 2, width, lanes), jnp.bfloat16),
+            pltpu.VMEM((3, frames, rows + 2, width, lanes), jnp.bfloat16),
             pltpu.VMEM((frames, rows * width, channels), jnp.float32),
         ],
         compiler_params=PARAMS,
-        cost_estimate=pl.CostEstimate(flops=flops, bytes_accessed=6_000_000, transcendentals=0),
-        name="conv_two",
-    )(valid, place, halo, own, weight)
+        cost_estimate=pl.CostEstimate(flops=3_000_000_000, bytes_accessed=6_000_000, transcendentals=0),
+        name="conv_two_halo",
+    )(valid, place, halo, weight, started)
 
 
 def gathered(place, mine, other, i):
@@ -243,7 +279,7 @@
         out_specs=VMEM,
         scratch_shapes=[pltpu.VMEM(shape, jnp.float32)] + extra,
         compiler_params=PARAMS,
-        cost_estimate=pl.CostEstimate(flops=4_000_000, bytes_accessed=5_000_000, transcendentals=0),
+        cost_estimate=pl.CostEstimate(flops=4_000_000, bytes_accessed=12_000_000, transcendentals=0),
         name=name,
     )(place, mine, other)
 
@@ -286,16 +322,18 @@
 
     column, own_all = lax.optimization_barrier((column, own_all))
     with jax.named_scope("weight_one"):
-        mine = from_all(column[:, :TILE_ROWS], "group")
+        mine = [column[:, :TILE_ROWS]]
+        mine += [onward(mine[0], d, "group") for d in range(1, lax.axis_size("group"))]
         prior_all = earlier(own_all)
+
+    with jax.named_scope("weight_two"):
+        later, _ = lax.optimization_barrier((column[:, TILE_ROWS:], mine[1]))
+        later = [later] + [onward(later, d, "group") for d in range(1, lax.axis_size("group"))]
+
+    with jax.named_scope("weight_one"):
         mine, prior_all = lax.optimization_barrier((mine, prior_all))
-        swapped = lax.ppermute(mine, "core", [(0, 1), (1, 0)])
-        one_mine, one_swapped = mine, swapped
-
-    with jax.named_scope("weight_two"):
-        column, _ = lax.optimization_barrier((column, mine))
-        later = column[:, TILE_ROWS:]
-        later = [later] + [onward(later, d, "group") for d in range(1, lax.axis_size("group"))]
+        one_mine = jnp.stack(mine)
+        one_swapped = lax.ppermute(one_mine, "core", [(0, 1), (1, 0)])
 
     base = lax.axis_index(SLOT) * frames
     slots = base + jnp.arange(frames, dtype=jnp.int32)
@@ -304,10 +342,9 @@
     valid = (slots[:, None] - before[None, :] >= begins[:, None]).astype(jnp.float32)
 
     with jax.named_scope("first"):
-        first = conv_one_call(valid, place, prior_all, own_all, one_mine, one_swapped)
+        first, squares = conv_one_call(valid, place, prior_all, own_all, one_mine, one_swapped)
 
     with jax.named_scope("weight_two"):
-        squares = jnp.sum(first * first, axis=-1)
         squares = squares + across(squares, 1)
         squares, later = lax.optimization_barrier((squares, later))
         mine = jnp.stack(later)
@@ -319,15 +356,22 @@
         )
 
     with jax.named_scope("second"):
-        squares = squares + across(squares, 2)
+        other_squares, weight_two = lax.optimization_barrier((across(squares, 2), weight_two))
+        squares = squares + other_squares
         gain_mine = lax.dynamic_index_in_dim(gain_two.reshape(share, parts), part, 1, keepdims=False)
         gain_mine = jnp.pad(gain_mine, (0, LANE - share))
         scale = lax.rsqrt(squares / channels + EPS)
         hidden_two = jax.nn.silu(first * scale[..., None] * gain_mine).astype(jnp.bfloat16)
         prior_two = earlier(hidden_two)
-        sums, *rest = conv_two_call(valid, place, prior_two, hidden_two, weight_two, parts)
-        arrived = [onward(r, d) for d, r in enumerate(rest, 1)]
-        second = sum((r.astype(jnp.float32) for r in arrived), sums.astype(jnp.float32))
+        started = conv_two_own_call(valid, hidden_two, weight_two)
+        own_sum, up, down, up_last, down_last = conv_two_halo_call(
+            valid, place, prior_two, weight_two, started, parts
+        )
+        up, down = onward(up, 1), onward(down, -1)
+        up_last = onward(up_last + up[:1], 1)
+        down_last = onward(down_last + down[1:], -1)
+        arrived = [jnp.concatenate([down[:1], up[1:]]), jnp.concatenate([up_last, down_last])]
+        second = sum((r.astype(jnp.float32) for r in arrived), own_sum.astype(jnp.float32))
 
     block = (source + second).astype(jnp.bfloat16)
     result = jnp.broadcast_to(

time: 114 us -> 114 us (level)
  waiting for transfers between devices: 54.9 us -> 39.3 us
  starting transfers between devices: 29.4 us -> 40.5 us
  Pallas kernels: 20.4 us -> 24.6 us
    ppermute x12 -> x13, waiting for transfers between devices: 44.3 us -> 36.2 us  [onward(): return lax.ppermute(x, axis, [(i, (i + by) % n) for i in range(n)])]
    ppermute x12 -> x13, starting transfers between devices: 15.2 us -> 22.3 us  [onward(): return lax.ppermute(x, axis, [(i, (i + by) % n) for i in range(n)])]
    ppermute x2, waiting for transfers between devices: 7.53 us -> 2.09 us  [across(): lax.ppermute(x, 'tile', [(i, i ^ bit) for i in range(lax.axis_size('tile'...]
    pallas_call x1 -> x2, Pallas kernels: 7.31 us -> 11.4 us  [the longest x1 5.87 us: conv_two_own_call(): pl.pallas_call(conv_two_own_kernel, out_shape=jax.ShapeDtypeStruct((frame...]
    ppermute x2, starting transfers between devices: 1.31 us -> 4.98 us  [across(): lax.ppermute(x, 'tile', [(i, i ^ bit) for i in range(lax.axis_size('tile'...]
    ppermute x2, waiting for transfers between devices: 3.01 us -> 0.95 us  [earlier(): return lax.ppermute(x, SLOT, [(i, i + 1) for i in range(n - 1)])]
    another operation x2 -> x1, other arithmetic: 1.41 us -> 0.18 us  [from_all(): jnp.stack([x] + [onward(x, d, axis) for d in range(1, lax.axis_size(axis))])]
    another operation x1 -> x2, other arithmetic: 0.18 us -> 1.39 us  [the longest x1 1.21 us: body(): one_mine = jnp.stack(mine)]
  transfers between devices with their start and end apart: 19 -> 20, of which waited for: 12 -> 9; matrix products, arithmetic and copies ran while one was open for 3% -> 2% of each run, Pallas kernels for 12% -> 17%
where the time goes in v10:
time: 114 us; the launch traced here: 113 us
  starting transfers between devices  40.5 us (36%)
  waiting for transfers between devices  39.3 us (34%)
  Pallas kernels  24.6 us (22%)
  other arithmetic  3.39 us (3%)
  local copies, waits for them, and re-layouts  3.28 us (3%)
  matrix products  1.35 us (1%)
    ppermute x13, waiting for transfers between devices, onward(): return lax.ppermute(x, axis, [(i, (i + by) % n) for i in range(n)])  36.2 us
    ppermute x13, starting transfers between devices, onward(): return lax.ppermute(x, axis, [(i, (i + by) % n) for i in range(n)])  22.3 us
    pallas_call x1, Pallas kernels, conv_one_call(): pl.pallas_call(functools.partial(conv_one_kernel, channels // parts), out...  9.34 us
    all_to_all x1, starting transfers between devices, body(): lax.all_to_all(jnp.broadcast_to(pieces, (lax.axis_size('z'),) + pieces.sh...  8.57 us
    pallas_call x1, Pallas kernels, conv_two_own_call(): pl.pallas_call(conv_two_own_kernel, out_shape=jax.ShapeDtypeStruct((frame...  5.87 us
    pallas_call x1, Pallas kernels, conv_two_halo_call(): pl.pallas_call(conv_two_halo_kernel, out_shape=[jax.ShapeDtypeStruct(shap...  5.51 us
    ppermute x2, starting transfers between devices, across(): lax.ppermute(x, 'tile', [(i, i ^ bit) for i in range(lax.axis_size('tile'...  4.98 us
    ppermute x2, starting transfers between devices, earlier(): return lax.ppermute(x, SLOT, [(i, i + 1) for i in range(n - 1)])  4.19 us
  transfers between devices with their start and end apart: 20, of which 9 were waited for; matrix products, arithmetic and copies ran while one was open for 2% of the time, Pallas kernels for 17%

profile of v10, /device:TPU:32, one launch (start us, length us, event | category | flops | bytes accessed | tf_op | source)
XLA Modules:
  0.0 112.7 jit_solution(6245076197265634042)
XLA Ops:
  0.0 1.2 %fusion = bf16[162,96]{1,0:T(8,128)(2,1)S(1)} fusion(bf16[162,384]{1,0:T(8,128)(2,1)} %param.10, s32[96]{0:T(128)S(1)} %multiply_add_fusion.1), kind=kOutput, calls=%fused_computation.5 | convolution fusion | flops 11996352 | bytes 155904 | tf_op jit(solution)/shard_map/pieces/dot_general | solution.py:314
  1.2 0.0 copy-start.1
  1.2 0.2 convolution_convert_fusion.1
  1.4 0.0 copy-start.6
  1.4 0.1 fusion.27
  1.6 0.9 broadcast_in_dim.15
  2.4 8.6 %all-to-all-start = ((bf16[8,96,384]{2,1,0:T(8,128)(2,1)}), bf16[8,96,384]{2,1,0:T(8,128)(2,1)S(1)}, u32[]{:S(2)}, u32[]{:S(2)}) async-start(bf16[8,96,384]{2,1,0:T(8,128)(2,1)} %broadcast_in_dim.15), calls=%async_computation | async-start | bytes 1179648 | tf_op jit(solution)/shard_map/pieces/all_to_all | solution.py:321
  11.0 0.1 fusion.4
  11.2 0.3 fusion.11
  11.4 1.6 %collective-permute-start = (bf16[2,3,64,384]{3,2,1,0:T(8,128)(2,1)S(1)}, bf16[2,3,64,384]{3,2,1,0:T(8,128)(2,1)S(1)}, u32[]{:S(2)}, u32[]{:S(2)}) collective-permute-start(bf16[2,3,64,384]{3,2,1,0:T(8,128)(2,1)S(1)} %fusion.11), channel_id=1, source_target_pairs={{0,4},{4,8},{8,12},{12,0},{1,5},{5,9},{9,13},{13,1},{2,6},{6,10},{... | collective-permute-start | bytes 884744 | tf_op jit(solution)/shard_map/pixels/ppermute | solution.py:28
  13.0 2.7 %collective-permute-start.1 = (bf16[2,3,64,384]{3,2,1,0:T(8,128)(2,1)S(1)}, bf16[2,3,64,384]{3,2,1,0:T(8,128)(2,1)S(1)}, u32[]{:S(2)}, u32[]{:S(2)}) collective-permute-start(bf16[2,3,64,384]{3,2,1,0:T(8,128)(2,1)S(1)} %fusion.11), channel_id=1, source_target_pairs={{0,8},{4,12},{8,0},{12,4},{1,9},{5,13},{9,1},{13,5},{2,10},{6,14},... | collective-permute-start | bytes 884744 | tf_op jit(solution)/shard_map/pixels/ppermute | solution.py:28
  15.7 1.4 %collective-permute-start.2 = (bf16[2,3,64,384]{3,2,1,0:T(8,128)(2,1)S(1)}, bf16[2,3,64,384]{3,2,1,0:T(8,128)(2,1)S(1)}, u32[]{:S(2)}, u32[]{:S(2)}) collective-permute-start(bf16[2,3,64,384]{3,2,1,0:T(8,128)(2,1)S(1)} %fusion.11), channel_id=1, source_target_pairs={{0,12},{4,0},{8,4},{12,8},{1,13},{5,1},{9,5},{13,9},{2,14},{6,2},{... | collective-permute-start | bytes 884744 | tf_op jit(solution)/shard_map/pixels/ppermute | solution.py:28
  17.2 0.3 fusion.19
  17.4 4.3 %collective-permute-done = bf16[2,3,64,384]{3,2,1,0:T(8,128)(2,1)S(1)} collective-permute-done((bf16[2,3,64,384]{3,2,1,0:T(8,128)(2,1)S(1)}, bf16[2,3,64,384]{3,2,1,0:T(8,128)(2,1)S(1)}, u32[]{:S(2)}, u32[]{:S(2)}) %collective-permute-start) | collective-permute-done | bytes 294944 | tf_op jit(solution)/shard_map/pixels/ppermute | solution.py:28
  21.7 6.5 %collective-permute-done.1 = bf16[2,3,64,384]{3,2,1,0:T(8,128)(2,1)S(1)} collective-permute-done((bf16[2,3,64,384]{3,2,1,0:T(8,128)(2,1)S(1)}, bf16[2,3,64,384]{3,2,1,0:T(8,128)(2,1)S(1)}, u32[]{:S(2)}, u32[]{:S(2)}) %collective-permute-start.1) | collective-permute-done | bytes 294944 | tf_op jit(solution)/shard_map/pixels/ppermute | solution.py:28
  28.2 0.2 pad_maximum_fusion.own
  28.4 0.0 copy-start.5
  28.4 0.0 all-to-all-done
  28.4 1.9 %collective-permute-start.6 = (bf16[4,2,3,64,384]{4,3,2,1,0:T(8,128)(2,1)S(1)}, bf16[4,2,3,64,384]{4,3,2,1,0:T(8,128)(2,1)S(1)}, u32[]{:S(2)}, u32[]{:S(2)}) collective-permute-start(bf16[4,2,3,64,384]{4,3,2,1,0:T(8,128)(2,1)S(1)} %pad_maximum_fusion.own), channel_id=1, source_target_pairs={{0,16},{16,32},{32,48},{48,64},{64,80},{80,96},{96,112},{112,128},... | collective-permute-start | bytes 3538952 | tf_op jit(solution)/shard_map/weight_one/ppermute | solution.py:23
  30.4 0.1 fusion.30
  30.4 1.7 %collective-permute-start.3 = (bf16[8,48,384]{2,1,0:T(8,128)(2,1)S(1)}, bf16[8,48,384]{2,1,0:T(8,128)(2,1)S(1)}, u32[]{:S(2)}, u32[]{:S(2)}) collective-permute-start(bf16[8,48,384]{2,1,0:T(8,128)(2,1)S(1)} %get-tuple-element.30), channel_id=1, source_target_pairs={{0,1},{1,2},{2,3},{3,0},{4,5},{5,6},{6,7},{7,4},{8,9},{9,10},{10,1... | collective-permute-start | bytes 884744 | tf_op jit(solution)/shard_map/weight_one/ppermute | solution.py:28
  32.1 2.9 %collective-permute-start.4 = (bf16[8,48,384]{2,1,0:T(8,128)(2,1)S(1)}, bf16[8,48,384]{2,1,0:T(8,128)(2,1)S(1)}, u32[]{:S(2)}, u32[]{:S(2)}) collective-permute-start(bf16[8,48,384]{2,1,0:T(8,128)(2,1)S(1)} %get-tuple-element.30), channel_id=1, source_target_pairs={{0,2},{1,3},{2,0},{3,1},{4,6},{5,7},{6,4},{7,5},{8,10},{9,11},{10,... | collective-permute-start | bytes 884744 | tf_op jit(solution)/shard_map/weight_one/ppermute | solution.py:28
  35.0 1.3 %collective-permute-start.5 = (bf16[8,48,384]{2,1,0:T(8,128)(2,1)S(1)}, bf16[8,48,384]{2,1,0:T(8,128)(2,1)S(1)}, u32[]{:S(2)}, u32[]{:S(2)}) collective-permute-start(bf16[8,48,384]{2,1,0:T(8,128)(2,1)S(1)} %get-tuple-element.30), channel_id=1, source_target_pairs={{0,3},{1,0},{2,1},{3,2},{4,7},{5,4},{6,5},{7,6},{8,11},{9,8},{10,9... | collective-permute-start | bytes 884744 | tf_op jit(solution)/shard_map/weight_one/ppermute | solution.py:28
  36.3 4.7 %collective-permute-done.3 = bf16[8,48,384]{2,1,0:T(8,128)(2,1)S(1)} collective-permute-done((bf16[8,48,384]{2,1,0:T(8,128)(2,1)S(1)}, bf16[8,48,384]{2,1,0:T(8,128)(2,1)S(1)}, u32[]{:S(2)}, u32[]{:S(2)}) %collective-permute-start.3) | collective-permute-done | bytes 294944 | tf_op jit(solution)/shard_map/weight_one/ppermute | solution.py:28
  41.0 7.6 %collective-permute-done.4 = bf16[8,48,384]{2,1,0:T(8,128)(2,1)S(1)} collective-permute-done((bf16[8,48,384]{2,1,0:T(8,128)(2,1)S(1)}, bf16[8,48,384]{2,1,0:T(8,128)(2,1)S(1)}, u32[]{:S(2)}, u32[]{:S(2)}) %collective-permute-start.4) | collective-permute-done | bytes 294944 | tf_op jit(solution)/shard_map/weight_one/ppermute | solution.py:28
  48.7 0.0 collective-permute-done.5
  48.7 0.0 collective-permute-done.6.halo
  48.7 1.2 %pad_maximum_fusion.1.mine = bf16[4,8,48,384]{3,2,1,0:T(8,128)(2,1)} fusion(bf16[1,8,48,384]{3,2,1,0:T(8,128)(2,1)S(1)} %bitcast.57, bf16[1,8,48,384]{3,2,1,0:T(8,128)(2,1)S(1)} %bitcast.55, bf16[1,8,48,384]{3,2,1,0:T(8,128)(2,1)S(1)} %bitcast.53, bf16[1,8,48,384]{3,2,1,0:T(8,128)(2,1)S(1)} %bitcast.49), kind=kLoop, calls=%fused_computation.1 | loop fusion | flops 1769472 | bytes 2359296 | tf_op jit(solution)/shard_map/weight_one/stack | solution.py:335
  49.9 0.3 collective-permute-start.7
  50.2 0.2 reduce-window_clone.1
  50.4 0.1 pad_add_fusion.place
  50.5 0.2 fusion.29
  50.7 0.1 compare_convert_fusion.valid
  50.8 2.9 %collective-permute-start.10 = (bf16[8,48,384]{2,1,0:T(8,128)(2,1)S(1)}, bf16[8,48,384]{2,1,0:T(8,128)(2,1)S(1)}, u32[]{:S(2)}, u32[]{:S(2)}) collective-permute-start(bf16[8,48,384]{2,1,0:T(8,128)(2,1)S(1)} %get-tuple-element.38), channel_id=1, source_target_pairs={{0,2},{1,3},{2,0},{3,1},{4,6},{5,7},{6,4},{7,5},{8,10},{9,11},{10,... | collective-permute-start | bytes 884744 | tf_op jit(solution)/shard_map/weight_two/ppermute | solution.py:28
  53.7 1.6 %collective-permute-start.11 = (bf16[8,48,384]{2,1,0:T(8,128)(2,1)S(1)}, bf16[8,48,384]{2,1,0:T(8,128)(2,1)S(1)}, u32[]{:S(2)}, u32[]{:S(2)}) collective-permute-start(bf16[8,48,384]{2,1,0:T(8,128)(2,1)S(1)} %get-tuple-element.38), channel_id=1, source_target_pairs={{0,3},{1,0},{2,1},{3,2},{4,7},{5,4},{6,5},{7,6},{8,11},{9,8},{10,9... | collective-permute-start | bytes 884744 | tf_op jit(solution)/shard_map/weight_two/ppermute | solution.py:28
  55.2 0.4 collective-permute-start.9
  55.7 0.0 collective-permute-done.7.other
  55.7 9.3 %conv_one.1 = (f32[2,12,64,128]{3,2,1,0:T(8,128)S(1)}, f32[2,12,64]{2,1,0:T(8,128)S(1)}) custom-call(f32[2,3]{1,0:T(2,128)S(1)} %compare_convert_fusion.valid, s32[3]{0:T(128)S(1)} %pad_add_fusion.place, bf16[4,2,3,64,384]{4,3,2,1,0:T(8,128)(2,1)S(1)} %collective-permute-done.6.halo, bf16[4,2,3,64,384]{4,3,2,1,0:T(8,128)(2,1)} %copy-done.5, ...), custom_call_target="tpu_custom_call" | custom-call | flops 4076863488 | bytes 6000000 | tf_op jit(solution)/shard_map/first/conv_one/pallas_call | solution.py:187
  65.0 1.7 %collective-permute-start.8 = (f32[2,12,64]{2,1,0:T(8,128)S(1)}, f32[2,12,64]{2,1,0:T(8,128)S(1)}, u32[]{:S(2)}, u32[]{:S(2)}) collective-permute-start(f32[2,12,64]{2,1,0:T(8,128)S(1)} %get-tuple-element.35), channel_id=1, source_target_pairs={{0,4},{4,0},{8,12},{12,8},{1,5},{5,1},{9,13},{13,9},{2,6},{6,2},{1... | collective-permute-start | bytes 18440 | tf_op jit(solution)/shard_map/weight_two/ppermute | solution.py:32
  66.8 2.1 %collective-permute-done.8 = f32[2,12,64]{2,1,0:T(8,128)S(1)} collective-permute-done((f32[2,12,64]{2,1,0:T(8,128)S(1)}, f32[2,12,64]{2,1,0:T(8,128)S(1)}, u32[]{:S(2)}, u32[]{:S(2)}) %collective-permute-start.8) | collective-permute-done | bytes 6176 | tf_op jit(solution)/shard_map/weight_two/ppermute | solution.py:32
  68.9 0.0 collective-permute-done.11
  68.9 0.0 copy-start.7
  68.9 0.2 pad_maximum_fusion.2.mine
  69.1 0.1 collective-permute-start.13
  69.2 3.3 %collective-permute-start.12 = (f32[2,12,64]{2,1,0:T(8,128)S(1)}, f32[2,12,64]{2,1,0:T(8,128)S(1)}, u32[]{:S(2)}, u32[]{:S(2)}) collective-permute-start(f32[2,12,64]{2,1,0:T(8,128)S(1)} %add.102), channel_id=1, source_target_pairs={{0,8},{4,12},{8,0},{12,4},{1,9},{5,13},{9,1},{13,5},{2,10},{6,14},... | collective-permute-start | bytes 18440 | tf_op jit(solution)/shard_map/second/ppermute | solution.py:32
  72.5 0.1 reshape.33
  72.6 0.2 dynamic-slice_reduce_fusion
  72.8 0.0 collective-permute-done.13.other
  72.8 3.9 %assemble_two.1.weight = bf16[3456,384]{1,0:T(8,128)(2,1)} custom-call(s32[3]{0:T(128)S(1)} %pad_add_fusion.place, bf16[4,8,48,384]{3,2,1,0:T(8,128)(2,1)S(1)} %pad_maximum_fusion.2.mine, bf16[4,8,48,384]{3,2,1,0:T(8,128)(2,1)} %collective-permute-done.13.other), custom_call_target="tpu_custom_call" | custom-call | flops 4000000 | bytes 12000000 | tf_op jit(solution)/shard_map/weight_two/assemble_two/pallas_call | solution.py:275
  76.7 0.3 multiply_convert_fusion.own
  77.0 2.3 %collective-permute-start.14 = (bf16[2,12,64,128]{3,2,1,0:T(8,128)(2,1)S(1)}, bf16[2,12,64,128]{3,2,1,0:T(8,128)(2,1)S(1)}, u32[]{:S(2)}, u32[]{:S(2)}) collective-permute-start(bf16[2,12,64,128]{3,2,1,0:T(8,128)(2,1)S(1)} %multiply_convert_fusion.own), channel_id=1, source_target_pairs={{0,16},{16,32},{32,48},{48,64},{64,80},{80,96},{96,112},{112,128},... | collective-permute-start | bytes 1179656 | tf_op jit(solution)/shard_map/second/ppermute | solution.py:23
  79.3 5.9 %conv_two_own.1.started = f32[2,768,384]{2,1,0:T(8,128)} custom-call(f32[2,3]{1,0:T(2,128)S(1)} %compare_convert_fusion.valid, bf16[2,12,64,128]{3,2,1,0:T(8,128)(2,1)S(1)} %multiply_convert_fusion.own, bf16[3456,384]{1,0:T(8,128)(2,1)} %assemble_two.1.weight), custom_call_target="tpu_custom_call" | custom-call | flops 3000000000 | bytes 5000000 | tf_op jit(solution)/shard_map/second/conv_two_own/pallas_call | solution.py:210
  85.2 0.9 collective-permute-done.14.halo
  86.1 5.5 %conv_two_halo.1 = (bf16[2,3,64,384]{3,2,1,0:T(8,128)(2,1)S(1)}, bf16[2,3,64,384]{3,2,1,0:T(8,128)(2,1)S(1)}, bf16[2,3,64,384]{3,2,1,0:T(8,128)(2,1)S(1)}, bf16[...) custom-call(f32[2,3]{1,0:T(2,128)S(1)} %compare_convert_fusion.valid, s32[3]{0:T(128)S(1)} %pad_add_fusion.place, ...), custom_call_target="tpu_custom_call" | custom-call | flops 3000000000 | bytes 6000000 | tf_op jit(solution)/shard_map/second/conv_two_halo/pallas_call | solution.py:226
  91.6 0.0 copy-start.2
  91.6 2.2 %collective-permute-start.15 = (bf16[2,3,64,384]{3,2,1,0:T(8,128)(2,1)S(1)}, bf16[2,3,64,384]{3,2,1,0:T(8,128)(2,1)S(1)}, u32[]{:S(2)}, u32[]{:S(2)}) collective-permute-start(bf16[2,3,64,384]{3,2,1,0:T(8,128)(2,1)S(1)} %get-tuple-element.45), channel_id=1, source_target_pairs={{0,12},{4,0},{8,4},{12,8},{1,13},{5,1},{9,5},{13,9},{2,14},{6,2},{... | collective-permute-start | bytes 884744 | tf_op jit(solution)/shard_map/second/ppermute | solution.py:28
  93.8 6.8 %collective-permute-done.15 = bf16[2,3,64,384]{3,2,1,0:T(8,128)(2,1)S(1)} collective-permute-done((bf16[2,3,64,384]{3,2,1,0:T(8,128)(2,1)S(1)}, bf16[2,3,64,384]{3,2,1,0:T(8,128)(2,1)S(1)}, u32[]{:S(2)}, u32[]{:S(2)}) %collective-permute-start.15) | collective-permute-done | bytes 294944 | tf_op jit(solution)/shard_map/second/ppermute | solution.py:28
  100.6 3.5 %collective-permute-start.18 = (bf16[1,3,64,384]{3,2,1,0:T(8,128)(2,1)S(1)}, bf16[1,3,64,384]{3,2,1,0:T(8,128)(2,1)S(1)}, u32[]{:S(2)}, u32[]{:S(2)}) collective-permute-start(bf16[1,3,64,384]{3,2,1,0:T(8,128)(2,1)S(1)} %get-tuple-element.53), channel_id=1, source_target_pairs={{0,12},{4,0},{8,4},{12,8},{1,13},{5,1},{9,5},{13,9},{2,14},{6,2},{... | collective-permute-start | bytes 442376 | tf_op jit(solution)/shard_map/second/ppermute | solution.py:28
  104.1 0.1 collective-permute-start.17
  104.2 2.5 %collective-permute-done.18 = bf16[1,3,64,384]{3,2,1,0:T(8,128)(2,1)S(1)} collective-permute-done((bf16[1,3,64,384]{3,2,1,0:T(8,128)(2,1)S(1)}, bf16[1,3,64,384]{3,2,1,0:T(8,128)(2,1)S(1)}, u32[]{:S(2)}, u32[]{:S(2)}) %collective-permute-start.18) | collective-permute-done | bytes 147488 | tf_op jit(solution)/shard_map/second/ppermute | solution.py:28
  106.8 3.8 %collective-permute-done.17 = bf16[1,3,64,384]{3,2,1,0:T(8,128)(2,1)S(1)} collective-permute-done((bf16[1,3,64,384]{3,2,1,0:T(8,128)(2,1)S(1)}, bf16[1,3,64,384]{3,2,1,0:T(8,128)(2,1)S(1)}, u32[]{:S(2)}, u32[]{:S(2)}) %collective-permute-start.17) | collective-permute-done | bytes 147488 | tf_op jit(solution)/shard_map/second/ppermute | solution.py:28
  110.6 0.2 fusion.12
  110.7 0.7 broadcast_in_dim.16
  111.5 1.3 %broadcast_in_dim_reshape.3 = bf16[1,2,6,128,384]{4,3,2,1,0:T(8,128)(2,1)} reshape(bf16[2,3,2,64,2,384]{5,4,3,2,1,0:T(2,128)(2,1)S(1)} %broadcast_in_dim.16) | data formatting | bytes 2359296 | tf_op jit(solution)/shard_map/broadcast_in_dim;reshape | solution.py:380
  (32 shorter events, 0.2 us)
Async XLA Ops:
  0.0 1.2 %copy-start = (bf16[162,384]{1,0:T(8,128)(2,1)S(1)}, bf16[162,384]{1,0:T(8,128)(2,1)}, u32[]{:S(2)}) copy-start(bf16[162,384]{1,0:T(8,128)(2,1)} %param.11) | copy-start | bytes 373252
  1.2 9.8 %copy-start.1 = (bf16[1,2,3,64,384]{4,3,2,1,0:T(8,128)(2,1)S(1)}, bf16[1,2,3,64,384]{4,3,2,1,0:T(8,128)(2,1)}, u32[]{:S(2)}) copy-start(bf16[1,2,3,64,384]{4,3,2,1,0:T(8,128)(2,1)} %param.6) | copy-start | bytes 884740
  1.4 9.7 %copy-start.6 = (f32[384]{0:T(512)S(1)}, f32[384]{0:T(512)}, u32[]{:S(2)}) copy-start(f32[384]{0:T(512)} %param.8) | copy-start | bytes 4612
  2.4 26.0 %all-to-all-start = ((bf16[8,96,384]{2,1,0:T(8,128)(2,1)}), bf16[8,96,384]{2,1,0:T(8,128)(2,1)S(1)}, u32[]{:S(2)}, u32[]{:S(2)}) async-start(bf16[8,96,384]{2,1,0:T(8,128)(2,1)} %broadcast_in_dim.15), calls=%async_computation | async-start | bytes 1179648 | tf_op jit(solution)/shard_map/pieces/all_to_all | solution.py:321
  11.4 10.2 %collective-permute-start = (bf16[2,3,64,384]{3,2,1,0:T(8,128)(2,1)S(1)}, bf16[2,3,64,384]{3,2,1,0:T(8,128)(2,1)S(1)}, u32[]{:S(2)}, u32[]{:S(2)}) collective-permute-start(bf16[2,3,64,384]{3,2,1,0:T(8,128)(2,1)S(1)} %fusion.11), channel_id=1, source_target_pairs={{0,4},{4,8},{8,12},{12,0},{1,5},{5,9},{9,13},{13,1},{2,6},{6,10},{... | collective-permute-start | bytes 884744 | tf_op jit(solution)/shard_map/pixels/ppermute | solution.py:28
  13.0 15.2 %collective-permute-start.1 = (bf16[2,3,64,384]{3,2,1,0:T(8,128)(2,1)S(1)}, bf16[2,3,64,384]{3,2,1,0:T(8,128)(2,1)S(1)}, u32[]{:S(2)}, u32[]{:S(2)}) collective-permute-start(bf16[2,3,64,384]{3,2,1,0:T(8,128)(2,1)S(1)} %fusion.11), channel_id=1, source_target_pairs={{0,8},{4,12},{8,0},{12,4},{1,9},{5,13},{9,1},{13,5},{2,10},{6,14},... | collective-permute-start | bytes 884744 | tf_op jit(solution)/shard_map/pixels/ppermute | solution.py:28
  15.7 12.5 %collective-permute-start.2 = (bf16[2,3,64,384]{3,2,1,0:T(8,128)(2,1)S(1)}, bf16[2,3,64,384]{3,2,1,0:T(8,128)(2,1)S(1)}, u32[]{:S(2)}, u32[]{:S(2)}) collective-permute-start(bf16[2,3,64,384]{3,2,1,0:T(8,128)(2,1)S(1)} %fusion.11), channel_id=1, source_target_pairs={{0,12},{4,0},{8,4},{12,8},{1,13},{5,1},{9,5},{13,9},{2,14},{6,2},{... | collective-permute-start | bytes 884744 | tf_op jit(solution)/shard_map/pixels/ppermute | solution.py:28
  28.4 21.5 %copy-start.5 = (bf16[4,2,3,64,384]{4,3,2,1,0:T(8,128)(2,1)}, bf16[4,2,3,64,384]{4,3,2,1,0:T(8,128)(2,1)S(1)}, u32[]{:S(2)}) copy-start(bf16[4,2,3,64,384]{4,3,2,1,0:T(8,128)(2,1)S(1)} %pad_maximum_fusion.own) | copy-start | bytes 3538948
  28.4 20.2 %collective-permute-start.6 = (bf16[4,2,3,64,384]{4,3,2,1,0:T(8,128)(2,1)S(1)}, bf16[4,2,3,64,384]{4,3,2,1,0:T(8,128)(2,1)S(1)}, u32[]{:S(2)}, u32[]{:S(2)}) collective-permute-start(bf16[4,2,3,64,384]{4,3,2,1,0:T(8,128)(2,1)S(1)} %pad_maximum_fusion.own), channel_id=1, source_target_pairs={{0,16},{16,32},{32,48},{48,64},{64,80},{80,96},{96,112},{112,128},... | collective-permute-start | bytes 3538952 | tf_op jit(solution)/shard_map/weight_one/ppermute | solution.py:23
  30.4 24.8 %copy-start.3 = (bf16[8,48,384]{2,1,0:T(8,128)(2,1)}, bf16[8,48,384]{2,1,0:T(8,128)(2,1)S(1)}, u32[]{:S(2)}) copy-start(bf16[8,48,384]{2,1,0:T(8,128)(2,1)S(1)} %get-tuple-element.38) | copy-start | bytes 884740
  30.4 10.6 %collective-permute-start.3 = (bf16[8,48,384]{2,1,0:T(8,128)(2,1)S(1)}, bf16[8,48,384]{2,1,0:T(8,128)(2,1)S(1)}, u32[]{:S(2)}, u32[]{:S(2)}) collective-permute-start(bf16[8,48,384]{2,1,0:T(8,128)(2,1)S(1)} %get-tuple-element.30), channel_id=1, source_target_pairs={{0,1},{1,2},{2,3},{3,0},{4,5},{5,6},{6,7},{7,4},{8,9},{9,10},{10,1... | collective-permute-start | bytes 884744 | tf_op jit(solution)/shard_map/weight_one/ppermute | solution.py:28
  32.1 16.6 %collective-permute-start.4 = (bf16[8,48,384]{2,1,0:T(8,128)(2,1)S(1)}, bf16[8,48,384]{2,1,0:T(8,128)(2,1)S(1)}, u32[]{:S(2)}, u32[]{:S(2)}) collective-permute-start(bf16[8,48,384]{2,1,0:T(8,128)(2,1)S(1)} %get-tuple-element.30), channel_id=1, source_target_pairs={{0,2},{1,3},{2,0},{3,1},{4,6},{5,7},{6,4},{7,5},{8,10},{9,11},{10,... | collective-permute-start | bytes 884744 | tf_op jit(solution)/shard_map/weight_one/ppermute | solution.py:28
  35.0 13.7 %collective-permute-start.5 = (bf16[8,48,384]{2,1,0:T(8,128)(2,1)S(1)}, bf16[8,48,384]{2,1,0:T(8,128)(2,1)S(1)}, u32[]{:S(2)}, u32[]{:S(2)}) collective-permute-start(bf16[8,48,384]{2,1,0:T(8,128)(2,1)S(1)} %get-tuple-element.30), channel_id=1, source_target_pairs={{0,3},{1,0},{2,1},{3,2},{4,7},{5,4},{6,5},{7,6},{8,11},{9,8},{10,9... | collective-permute-start | bytes 884744 | tf_op jit(solution)/shard_map/weight_one/ppermute | solution.py:28
  48.7 1.6 %copy-start.8 = (s32[1,4]{1,0:T(1,128)S(1)}, s32[1,4]{1,0:T(1,128)}, u32[]{:S(2)}) copy-start(s32[1,4]{1,0:T(1,128)} %param.7) | copy-start | bytes 52
  49.9 5.8 %collective-permute-start.7 = (bf16[4,8,48,384]{3,2,1,0:T(8,128)(2,1)}, bf16[4,8,48,384]{3,2,1,0:T(8,128)(2,1)}, u32[]{:S(2)}, u32[]{:S(2)}) collective-permute-start(bf16[4,8,48,384]{3,2,1,0:T(8,128)(2,1)} %pad_maximum_fusion.1.mine), channel_id=1, source_target_pairs={{0,16},{16,0},{1,17},{17,1},{2,18},{18,2},{3,19},{19,3},{4,20},{20... | collective-permute-start | bytes 3538952 | tf_op jit(solution)/shard_map/weight_one/ppermute | solution.py:336
  50.8 18.1 %collective-permute-start.10 = (bf16[8,48,384]{2,1,0:T(8,128)(2,1)S(1)}, bf16[8,48,384]{2,1,0:T(8,128)(2,1)S(1)}, u32[]{:S(2)}, u32[]{:S(2)}) collective-permute-start(bf16[8,48,384]{2,1,0:T(8,128)(2,1)S(1)} %get-tuple-element.38), channel_id=1, source_target_pairs={{0,2},{1,3},{2,0},{3,1},{4,6},{5,7},{6,4},{7,5},{8,10},{9,11},{10,... | collective-permute-start | bytes 884744 | tf_op jit(solution)/shard_map/weight_two/ppermute | solution.py:28
  53.7 15.2 %collective-permute-start.11 = (bf16[8,48,384]{2,1,0:T(8,128)(2,1)S(1)}, bf16[8,48,384]{2,1,0:T(8,128)(2,1)S(1)}, u32[]{:S(2)}, u32[]{:S(2)}) collective-permute-start(bf16[8,48,384]{2,1,0:T(8,128)(2,1)S(1)} %get-tuple-element.38), channel_id=1, source_target_pairs={{0,3},{1,0},{2,1},{3,2},{4,7},{5,4},{6,5},{7,6},{8,11},{9,8},{10,9... | collective-permute-start | bytes 884744 | tf_op jit(solution)/shard_map/weight_two/ppermute | solution.py:28
  55.2 13.6 %collective-permute-start.9 = (bf16[8,48,384]{2,1,0:T(8,128)(2,1)S(1)}, bf16[8,48,384]{2,1,0:T(8,128)(2,1)S(1)}, u32[]{:S(2)}, u32[]{:S(2)}) collective-permute-start(bf16[8,48,384]{2,1,0:T(8,128)(2,1)S(1)} %get-tuple-element.38), channel_id=1, source_target_pairs={{0,1},{1,2},{2,3},{3,0},{4,5},{5,6},{6,7},{7,4},{8,9},{9,10},{10,1... | collective-permute-start | bytes 884744 | tf_op jit(solution)/shard_map/weight_two/ppermute | solution.py:28
  55.7 13.2 %copy-start.4 = (bf16[8,48,384]{2,1,0:T(8,128)(2,1)S(1)}, bf16[8,48,384]{2,1,0:T(8,128)(2,1)}, u32[]{:S(2)}) copy-start(bf16[8,48,384]{2,1,0:T(8,128)(2,1)} %copy-done.3) | copy-start | bytes 884740
  65.0 3.8 %collective-permute-start.8 = (f32[2,12,64]{2,1,0:T(8,128)S(1)}, f32[2,12,64]{2,1,0:T(8,128)S(1)}, u32[]{:S(2)}, u32[]{:S(2)}) collective-permute-start(f32[2,12,64]{2,1,0:T(8,128)S(1)} %get-tuple-element.35), channel_id=1, source_target_pairs={{0,4},{4,0},{8,12},{12,8},{1,5},{5,1},{9,13},{13,9},{2,6},{6,2},{1... | collective-permute-start | bytes 18440 | tf_op jit(solution)/shard_map/weight_two/ppermute | solution.py:32
  68.9 3.6 %copy-start.7 = (f32[384]{0:T(512)S(1)}, f32[384]{0:T(512)}, u32[]{:S(2)}) copy-start(f32[384]{0:T(512)} %param.9) | copy-start | bytes 4612
  69.1 3.7 %collective-permute-start.13 = (bf16[4,8,48,384]{3,2,1,0:T(8,128)(2,1)S(1)}, bf16[4,8,48,384]{3,2,1,0:T(8,128)(2,1)}, u32[]{:S(2)}, u32[]{:S(2)}) collective-permute-start(bf16[4,8,48,384]{3,2,1,0:T(8,128)(2,1)S(1)} %pad_maximum_fusion.2.mine), channel_id=1, source_target_pairs={{0,16},{16,0},{1,17},{17,1},{2,18},{18,2},{3,19},{19,3},{4,20},{20... | collective-permute-start | bytes 3538952 | tf_op jit(solution)/shard_map/weight_two/ppermute | solution.py:351
  69.2 7.5 %collective-permute-start.12 = (f32[2,12,64]{2,1,0:T(8,128)S(1)}, f32[2,12,64]{2,1,0:T(8,128)S(1)}, u32[]{:S(2)}, u32[]{:S(2)}) collective-permute-start(f32[2,12,64]{2,1,0:T(8,128)S(1)} %add.102), channel_id=1, source_target_pairs={{0,8},{4,12},{8,0},{12,4},{1,9},{5,13},{9,1},{13,5},{2,10},{6,14},... | collective-permute-start | bytes 18440 | tf_op jit(solution)/shard_map/second/ppermute | solution.py:32
  77.0 9.1 %collective-permute-start.14 = (bf16[2,12,64,128]{3,2,1,0:T(8,128)(2,1)S(1)}, bf16[2,12,64,128]{3,2,1,0:T(8,128)(2,1)S(1)}, u32[]{:S(2)}, u32[]{:S(2)}) collective-permute-start(bf16[2,12,64,128]{3,2,1,0:T(8,128)(2,1)S(1)} %multiply_convert_fusion.own), channel_id=1, source_target_pairs={{0,16},{16,32},{32,48},{48,64},{64,80},{80,96},{96,112},{112,128},... | collective-permute-start | bytes 1179656 | tf_op jit(solution)/shard_map/second/ppermute | solution.py:23
  91.6 18.9 %copy-start.2 = (bf16[1,2,3,64,384]{4,3,2,1,0:T(8,128)(2,1)S(1)}, bf16[1,2,3,64,384]{4,3,2,1,0:T(8,128)(2,1)}, u32[]{:S(2)}) copy-start(bf16[1,2,3,64,384]{4,3,2,1,0:T(8,128)(2,1)} %param.6) | copy-start | bytes 884740
  91.6 9.0 %collective-permute-start.15 = (bf16[2,3,64,384]{3,2,1,0:T(8,128)(2,1)S(1)}, bf16[2,3,64,384]{3,2,1,0:T(8,128)(2,1)S(1)}, u32[]{:S(2)}, u32[]{:S(2)}) collective-permute-start(bf16[2,3,64,384]{3,2,1,0:T(8,128)(2,1)S(1)} %get-tuple-element.45), channel_id=1, source_target_pairs={{0,12},{4,0},{8,4},{12,8},{1,13},{5,1},{9,5},{13,9},{2,14},{6,2},{... | collective-permute-start | bytes 884744 | tf_op jit(solution)/shard_map/second/ppermute | solution.py:28
  93.8 10.3 %collective-permute-start.16 = (bf16[2,3,64,384]{3,2,1,0:T(8,128)(2,1)S(1)}, bf16[2,3,64,384]{3,2,1,0:T(8,128)(2,1)S(1)}, u32[]{:S(2)}, u32[]{:S(2)}) collective-permute-start(bf16[2,3,64,384]{3,2,1,0:T(8,128)(2,1)S(1)} %get-tuple-element.46), channel_id=1, source_target_pairs={{0,4},{4,8},{8,12},{12,0},{1,5},{5,9},{9,13},{13,1},{2,6},{6,10},{... | collective-permute-start | bytes 884744 | tf_op jit(solution)/shard_map/second/ppermute | solution.py:28
  100.6 6.1 %collective-permute-start.18 = (bf16[1,3,64,384]{3,2,1,0:T(8,128)(2,1)S(1)}, bf16[1,3,64,384]{3,2,1,0:T(8,128)(2,1)S(1)}, u32[]{:S(2)}, u32[]{:S(2)}) collective-permute-start(bf16[1,3,64,384]{3,2,1,0:T(8,128)(2,1)S(1)} %get-tuple-element.53), channel_id=1, source_target_pairs={{0,12},{4,0},{8,4},{12,8},{1,13},{5,1},{9,5},{13,9},{2,14},{6,2},{... | collective-permute-start | bytes 442376 | tf_op jit(solution)/shard_map/second/ppermute | solution.py:28
  104.1 6.4 %collective-permute-start.17 = (bf16[1,3,64,384]{3,2,1,0:T(8,128)(2,1)S(1)}, bf16[1,3,64,384]{3,2,1,0:T(8,128)(2,1)S(1)}, u32[]{:S(2)}, u32[]{:S(2)}) collective-permute-start(bf16[1,3,64,384]{3,2,1,0:T(8,128)(2,1)S(1)} %get-tuple-element.51), channel_id=1, source_target_pairs={{0,4},{4,8},{8,12},{12,0},{1,5},{5,9},{9,13},{13,1},{2,6},{6,10},{... | collective-permute-start | bytes 442376 | tf_op jit(solution)/shard_map/second/ppermute | solution.py:28

commit v11 on v10

--- a/solution.py
+++ b/solution.py
@@ -122,57 +122,57 @@
         squares[s] = jnp.sum(done * done, axis=-1)
 
 
-def add_frames(valid, slots, source, weight, taps, add):
-    frames, rows, width, lanes = source.shape
+def conv_two_kernel(plan, valid, place, halo, own, weight, *rest):
+    *outs, taps = rest
+    frames, rows, width, lanes = own.shape
+    each = outs[0].shape[1]
+    parts = rows // each
     channels = weight.shape[1]
     clear_border(taps)
-    for slot in slots:
+    for slot in range(2 * frames):
+        source = halo if slot < frames else own
         for row in range(rows):
-            fill_shifted(taps, slot % frames, row + 1, source[slot % frames, row])
-    for slot in slots:
-        pairs = [(s, slot - s) for s in range(frames) if 0 <= slot - s < 3]
-        columns = jnp.concatenate(
-            [
-                taps[e, slot % frames, b : b + rows].reshape(rows * width, lanes)
-                for b in range(3)
-                for e in range(3)
-            ],
-            axis=1,
-        )
-        blocks = [weight[a * 9 * lanes : (a + 1) * 9 * lanes, :] for _, a in pairs]
-        packed = blocks[0] if len(blocks) == 1 else jnp.concatenate(blocks, axis=1)
-        term = jnp.dot(columns, packed, preferred_element_type=jnp.float32)
-        for i, (s, a) in enumerate(pairs):
-            add(s, valid[s, a] * term[:, i * channels : (i + 1) * channels])
-
-
-def conv_two_own_kernel(valid, own, weight, acc, taps):
-    frames = own.shape[0]
-    seen = set()
-
-    def add(s, piece):
-        acc[s] = acc[s] + piece if s in seen else piece
-        seen.add(s)
-
-    add_frames(valid, range(frames, 2 * frames), own, weight, taps, add)
-
-
-def conv_two_halo_kernel(valid, place, halo, weight, started, own_sum, up, down, up_last, down_last, taps, acc):
-    frames, rows, width, _ = halo.shape
-    each = own_sum.shape[1]
-    parts = rows // each
-    seen = set()
-
-    def add(s, piece):
-        acc[s] = (acc if s in seen else started)[s] + piece
-        seen.add(s)
-
-    add_frames(valid, range(frames), halo, weight, taps, add)
-    for ref, d, s, at in ((own_sum, 0, 0, 0), (own_sum, 0, 1, 1), (up, 2, 0, 0), (up, 1, 1, 1),
-                          (down, 3, 0, 0), (down, 2, 1, 1), (up_last, 1, 0, 0), (down_last, 3, 1, 0)):
-        top = pl.multiple_of(lax.rem(place[2] + d, parts) * (each * width), 64)
-        done = acc[s, pl.ds(top, each * width), :].astype(ref.dtype)
-        ref[at] = done.reshape(each, width, done.shape[1])
+            fill_shifted(taps, slot, row + 1, source[slot % frames, row])
+    for s, targets in enumerate(plan):
+        tops = [lax.rem(place[2] + d, parts) * each for d, _, _ in targets]
+        total = None
+        for a in range(3):
+            columns = jnp.concatenate(
+                [
+                    jnp.concatenate(
+                        [
+                            taps[e, s + a, pl.ds(top + b, each)].reshape(each * width, lanes)
+                            for b in range(3)
+                            for e in range(3)
+                        ],
+                        axis=1,
+                    )
+                    for top in tops
+                ],
+                axis=0,
+            )
+            block = weight[a * 9 * lanes : (a + 1) * 9 * lanes, :]
+            term = valid[s, a] * jnp.dot(columns, block, preferred_element_type=jnp.float32)
+            total = term if total is None else total + term
+        for i, (_, ref, at) in enumerate(targets):
+            done = total[i * each * width : (i + 1) * each * width]
+            outs[ref][at] = done.astype(outs[ref].dtype).reshape(each, width, channels)
+
+
+def finish_kernel(latents, own_sum, up, down, up_last, down_last, out, wide):
+    frames, each, width, _ = own_sum.shape
+    for s in range(frames):
+        for r in range(each):
+            terms = [own_sum[s, r], down[0, r], up_last[0, r]] if s == 0 else [own_sum[s, r], up[1, r], down_last[0, r]]
+            total = sum((t.astype(jnp.float32) for t in terms[1:]), terms[0].astype(jnp.float32))
+            block = (latents[s, r].astype(jnp.float32) + total).astype(out.dtype).astype(jnp.float32)
+            for k in range(wide.shape[0]):
+                lanes = slice(k * LANE, (k + 1) * LANE)
+                wide[k, pl.ds(0, width, stride=2), :] = block[:, lanes]
+                wide[k, pl.ds(1, width, stride=2), :] = block[:, lanes]
+                doubled = wide[k].astype(out.dtype)
+                out[s, 2 * r, :, lanes] = doubled
+                out[s, 2 * r + 1, :, lanes] = doubled
 
 
 VMEM = pl.BlockSpec(memory_space=pltpu.VMEM)
@@ -204,38 +204,34 @@
     )(valid, place, halo, own, mine, other)
 
 
-def conv_two_own_call(valid, own, weight):
+def conv_two_call(plan, leads, valid, place, halo, own, weight, parts):
     frames, rows, width, lanes = own.shape
     channels = weight.shape[1]
+    shapes = [(n, rows // parts, width, channels) for n in leads]
     return pl.pallas_call(
-        conv_two_own_kernel,
-        out_shape=jax.ShapeDtypeStruct((frames, rows * width, channels), jnp.float32),
-        in_specs=[SMEM, VMEM, VMEM],
-        out_specs=VMEM,
-        scratch_shapes=[pltpu.VMEM((3, frames, rows + 2, width, lanes), jnp.bfloat16)],
-        compiler_params=PARAMS,
-        cost_estimate=pl.CostEstimate(flops=3_000_000_000, bytes_accessed=5_000_000, transcendentals=0),
-        name="conv_two_own",
-    )(valid, own, weight)
-
-
-def conv_two_halo_call(valid, place, halo, weight, started, parts):
-    frames, rows, width, lanes = halo.shape
-    channels = weight.shape[1]
-    shapes = [(n, rows // parts, width, channels) for n in (frames, frames, frames, 1, 1)]
-    return pl.pallas_call(
-        conv_two_halo_kernel,
+        functools.partial(conv_two_kernel, plan),
         out_shape=[jax.ShapeDtypeStruct(shape, jnp.bfloat16) for shape in shapes],
         in_specs=[SMEM, SMEM, VMEM, VMEM, VMEM],
         out_specs=[VMEM] * len(shapes),
-        scratch_shapes=[
-            pltpu.VMEM((3, frames, rows + 2, width, lanes), jnp.bfloat16),
-            pltpu.VMEM((frames, rows * width, channels), jnp.float32),
-        ],
+        scratch_shapes=[pltpu.VMEM((3, 2 * frames, rows + 2, width, lanes), jnp.bfloat16)],
         compiler_params=PARAMS,
         cost_estimate=pl.CostEstimate(flops=3_000_000_000, bytes_accessed=6_000_000, transcendentals=0),
-        name="conv_two_halo",
-    )(valid, place, halo, weight, started)
+        name="conv_two",
+    )(valid, place, halo, own, weight)
+
+
+def finish_call(*arrays):
+    frames, each, width, channels = arrays[0].shape
+    return pl.pallas_call(
+        finish_kernel,
+        out_shape=jax.ShapeDtypeStruct((frames, 2 * each, 2 * width, channels), jnp.bfloat16),
+        in_specs=[VMEM] * len(arrays),
+        out_specs=VMEM,
+        scratch_shapes=[pltpu.VMEM((channels // LANE, 2 * width, LANE), jnp.float32)],
+        compiler_params=PARAMS,
+        cost_estimate=pl.CostEstimate(flops=2_000_000, bytes_accessed=3_000_000, transcendentals=0),
+        name="finish",
+    )(*arrays)
 
 
 def gathered(place, mine, other, i):
@@ -345,8 +341,8 @@
         first, squares = conv_one_call(valid, place, prior_all, own_all, one_mine, one_swapped)
 
     with jax.named_scope("weight_two"):
+        squares, later = lax.optimization_barrier((squares, later))
         squares = squares + across(squares, 1)
-        squares, later = lax.optimization_barrier((squares, later))
         mine = jnp.stack(later)
         swapped = lax.ppermute(mine, "core", [(0, 1), (1, 0)])
         taps = shards * shard // channels
@@ -363,21 +359,16 @@
         scale = lax.rsqrt(squares / channels + EPS)
         hidden_two = jax.nn.silu(first * scale[..., None] * gain_mine).astype(jnp.bfloat16)
         prior_two = earlier(hidden_two)
-        started = conv_two_own_call(valid, hidden_two, weight_two)
-        own_sum, up, down, up_last, down_last = conv_two_halo_call(
-            valid, place, prior_two, weight_two, started, parts
+        operands = (valid, place, prior_two, hidden_two, weight_two, parts)
+        up, down = conv_two_call((((2, 0, 0), (3, 1, 0)), ((1, 0, 1), (2, 1, 1))), (2, 2), *operands)
+        up, down = onward(up, 1), onward(down, -1)
+        own_sum, up_last, down_last = conv_two_call(
+            (((0, 0, 0), (1, 1, 0)), ((3, 2, 0), (0, 0, 1))), (2, 1, 1), *operands
         )
-        up, down = onward(up, 1), onward(down, -1)
         up_last = onward(up_last + up[:1], 1)
         down_last = onward(down_last + down[1:], -1)
-        arrived = [jnp.concatenate([down[:1], up[1:]]), jnp.concatenate([up_last, down_last])]
-        second = sum((r.astype(jnp.float32) for r in arrived), own_sum.astype(jnp.float32))
-
-    block = (source + second).astype(jnp.bfloat16)
-    result = jnp.broadcast_to(
-        block[:, :, None, :, None, :], (frames, each, 2, width, 2, channels)
-    ).reshape(frames, 2 * each, 2 * width, channels)
-    return result[None]
+
+    return finish_call(latents[0], own_sum, up, down, up_last, down_last)[None]
 
 
 def solution(mesh):

time: 114 us -> 115 us (level); the launches traced: 113 us -> 115 us
  waiting for transfers between devices: 39.3 us -> 44.5 us
  local copies, waits for them, and re-layouts: 3.28 us -> 1.26 us
  starting transfers between devices: 40.5 us -> 38.5 us
    ppermute x2, waiting for transfers between devices: 0.95 us -> 6.95 us  [earlier(): return lax.ppermute(x, SLOT, [(i, i + 1) for i in range(n - 1)])]
    another operation x1 -> x0, local copies, waits for them, and re-layouts: 1.29 us -> none  [body(): return result[None]]
    pallas_call x2 -> x3, Pallas kernels: 11.4 us -> 11.7 us  [the longest x2 10.3 us: conv_two_call(): pl.pallas_call(functools.partial(conv_two_kernel, plan), out_shape=[jax.S...]
  transfers between devices with their start and end apart: 20 -> 20, of which waited for: 9 -> 11; matrix products, arithmetic and copies ran while one was open for 2% -> 2% of each run, Pallas kernels for 17% -> 16%
where the time goes in v11:
time: 115 us
  waiting for transfers between devices  44.5 us (39%)
  starting transfers between devices  38.5 us (33%)
  Pallas kernels  24.9 us (22%)
  other arithmetic  4.25 us (4%)
  matrix products  1.35 us (1%)
  local copies, waits for them, and re-layouts  1.26 us (1%)
    ppermute x13, waiting for transfers between devices, onward(): return lax.ppermute(x, axis, [(i, (i + by) % n) for i in range(n)])  35.2 us
    ppermute x13, starting transfers between devices, onward(): return lax.ppermute(x, axis, [(i, (i + by) % n) for i in range(n)])  21.4 us
    pallas_call x2, Pallas kernels, conv_two_call(): pl.pallas_call(functools.partial(conv_two_kernel, plan), out_shape=[jax.S...  10.3 us
    pallas_call x1, Pallas kernels, conv_one_call(): pl.pallas_call(functools.partial(conv_one_kernel, channels // parts), out...  9.29 us
    all_to_all x1, starting transfers between devices, body(): lax.all_to_all(jnp.broadcast_to(pieces, (lax.axis_size('z'),) + pieces.sh...  8.57 us
    ppermute x2, waiting for transfers between devices, earlier(): return lax.ppermute(x, SLOT, [(i, i + 1) for i in range(n - 1)])  6.95 us
    ppermute x2, starting transfers between devices, across(): lax.ppermute(x, 'tile', [(i, i ^ bit) for i in range(lax.axis_size('tile'...  4.08 us
    ppermute x2, starting transfers between devices, earlier(): return lax.ppermute(x, SLOT, [(i, i + 1) for i in range(n - 1)])  4.05 us
  transfers between devices with their start and end apart: 20, of which 11 were waited for; matrix products, arithmetic and copies ran while one was open for 2% of the time, Pallas kernels for 16%

profile of v11, /device:TPU:32, one launch (start us, length us, event | category | flops | bytes accessed | tf_op | source)
XLA Modules:
  0.0 115.1 jit_solution(6441942910558945162)
XLA Ops:
  0.0 1.2 %fusion = bf16[162,96]{1,0:T(8,128)(2,1)S(1)} fusion(bf16[162,384]{1,0:T(8,128)(2,1)} %param.10, s32[96]{0:T(128)S(1)} %multiply_add_fusion.1), kind=kOutput, calls=%fused_computation.5 | convolution fusion | flops 11996352 | bytes 155904 | tf_op jit(solution)/shard_map/pieces/dot_general | solution.py:310
  1.2 0.0 copy-start.1
  1.2 0.2 convolution_convert_fusion.1
  1.4 0.0 copy-start.2
  1.4 0.1 fusion.16
  1.6 0.9 broadcast_in_dim.15
  2.4 8.6 %all-to-all-start = ((bf16[8,96,384]{2,1,0:T(8,128)(2,1)}), bf16[8,96,384]{2,1,0:T(8,128)(2,1)S(1)}, u32[]{:S(2)}, u32[]{:S(2)}) async-start(bf16[8,96,384]{2,1,0:T(8,128)(2,1)} %broadcast_in_dim.15), calls=%async_computation | async-start | bytes 1179648 | tf_op jit(solution)/shard_map/pieces/all_to_all | solution.py:317
  11.0 0.1 fusion.1
  11.2 0.3 fusion.8
  11.4 1.6 %collective-permute-start = (bf16[2,3,64,384]{3,2,1,0:T(8,128)(2,1)S(1)}, bf16[2,3,64,384]{3,2,1,0:T(8,128)(2,1)S(1)}, u32[]{:S(2)}, u32[]{:S(2)}) collective-permute-start(bf16[2,3,64,384]{3,2,1,0:T(8,128)(2,1)S(1)} %fusion.8), channel_id=1, source_target_pairs={{0,4},{4,8},{8,12},{12,0},{1,5},{5,9},{9,13},{13,1},{2,6},{6,10},{... | collective-permute-start | bytes 884744 | tf_op jit(solution)/shard_map/pixels/ppermute | solution.py:28
  13.0 2.7 %collective-permute-start.1 = (bf16[2,3,64,384]{3,2,1,0:T(8,128)(2,1)S(1)}, bf16[2,3,64,384]{3,2,1,0:T(8,128)(2,1)S(1)}, u32[]{:S(2)}, u32[]{:S(2)}) collective-permute-start(bf16[2,3,64,384]{3,2,1,0:T(8,128)(2,1)S(1)} %fusion.8), channel_id=1, source_target_pairs={{0,8},{4,12},{8,0},{12,4},{1,9},{5,13},{9,1},{13,5},{2,10},{6,14},... | collective-permute-start | bytes 884744 | tf_op jit(solution)/shard_map/pixels/ppermute | solution.py:28
  15.7 1.4 %collective-permute-start.2 = (bf16[2,3,64,384]{3,2,1,0:T(8,128)(2,1)S(1)}, bf16[2,3,64,384]{3,2,1,0:T(8,128)(2,1)S(1)}, u32[]{:S(2)}, u32[]{:S(2)}) collective-permute-start(bf16[2,3,64,384]{3,2,1,0:T(8,128)(2,1)S(1)} %fusion.8), channel_id=1, source_target_pairs={{0,12},{4,0},{8,4},{12,8},{1,13},{5,1},{9,5},{13,9},{2,14},{6,2},{... | collective-permute-start | bytes 884744 | tf_op jit(solution)/shard_map/pixels/ppermute | solution.py:28
  17.2 0.3 multiply_convert_fusion.1
  17.4 4.3 %collective-permute-done = bf16[2,3,64,384]{3,2,1,0:T(8,128)(2,1)S(1)} collective-permute-done((bf16[2,3,64,384]{3,2,1,0:T(8,128)(2,1)S(1)}, bf16[2,3,64,384]{3,2,1,0:T(8,128)(2,1)S(1)}, u32[]{:S(2)}, u32[]{:S(2)}) %collective-permute-start) | collective-permute-done | bytes 294944 | tf_op jit(solution)/shard_map/pixels/ppermute | solution.py:28
  21.7 6.5 %collective-permute-done.1 = bf16[2,3,64,384]{3,2,1,0:T(8,128)(2,1)S(1)} collective-permute-done((bf16[2,3,64,384]{3,2,1,0:T(8,128)(2,1)S(1)}, bf16[2,3,64,384]{3,2,1,0:T(8,128)(2,1)S(1)}, u32[]{:S(2)}, u32[]{:S(2)}) %collective-permute-start.1) | collective-permute-done | bytes 294944 | tf_op jit(solution)/shard_map/pixels/ppermute | solution.py:28
  28.2 0.0 collective-permute-done.2
  28.2 1.2 %pad_maximum_fusion.own = bf16[4,2,3,64,384]{4,3,2,1,0:T(8,128)(2,1)} fusion(bf16[1,2,3,64,384]{4,3,2,1,0:T(8,128)(2,1)S(1)} %bitcast.35, bf16[1,2,3,64,384]{4,3,2,1,0:T(8,128)(2,1)S(1)} %bitcast.33, bf16[1,2,3,64,384]{4,3,2,1,0:T(8,128)(2,1)S(1)} %bitcast.31, bf16[1,2,3,64,384]{4,3,2,1,0:T(8,128)(2,1)S(1)} %multiply_convert_fusion.1), kind=kLoop, calls=%fused_computation | loop fusion | flops 1769472 | bytes 2359296 | tf_op jit(solution)/shard_map/pixels/stack | solution.py:36
  29.4 0.0 all-to-all-done
  29.4 1.9 %collective-permute-start.6 = (bf16[4,2,3,64,384]{4,3,2,1,0:T(8,128)(2,1)}, bf16[4,2,3,64,384]{4,3,2,1,0:T(8,128)(2,1)S(1)}, u32[]{:S(2)}, u32[]{:S(2)}) collective-permute-start(bf16[4,2,3,64,384]{4,3,2,1,0:T(8,128)(2,1)} %pad_maximum_fusion.own), channel_id=1, source_target_pairs={{0,16},{16,32},{32,48},{48,64},{64,80},{80,96},{96,112},{112,128},... | collective-permute-start | bytes 3538952 | tf_op jit(solution)/shard_map/weight_one/ppermute | solution.py:23
  31.3 0.1 fusion.19
  31.4 1.7 %collective-permute-start.3 = (bf16[8,48,384]{2,1,0:T(8,128)(2,1)S(1)}, bf16[8,48,384]{2,1,0:T(8,128)(2,1)S(1)}, u32[]{:S(2)}, u32[]{:S(2)}) collective-permute-start(bf16[8,48,384]{2,1,0:T(8,128)(2,1)S(1)} %get-tuple-element.30), channel_id=1, source_target_pairs={{0,1},{1,2},{2,3},{3,0},{4,5},{5,6},{6,7},{7,4},{8,9},{9,10},{10,1... | collective-permute-start | bytes 884744 | tf_op jit(solution)/shard_map/weight_one/ppermute | solution.py:28
  33.0 2.9 %collective-permute-start.4 = (bf16[8,48,384]{2,1,0:T(8,128)(2,1)S(1)}, bf16[8,48,384]{2,1,0:T(8,128)(2,1)S(1)}, u32[]{:S(2)}, u32[]{:S(2)}) collective-permute-start(bf16[8,48,384]{2,1,0:T(8,128)(2,1)S(1)} %get-tuple-element.30), channel_id=1, source_target_pairs={{0,2},{1,3},{2,0},{3,1},{4,6},{5,7},{6,4},{7,5},{8,10},{9,11},{10,... | collective-permute-start | bytes 884744 | tf_op jit(solution)/shard_map/weight_one/ppermute | solution.py:28
  35.9 1.3 %collective-permute-start.5 = (bf16[8,48,384]{2,1,0:T(8,128)(2,1)S(1)}, bf16[8,48,384]{2,1,0:T(8,128)(2,1)S(1)}, u32[]{:S(2)}, u32[]{:S(2)}) collective-permute-start(bf16[8,48,384]{2,1,0:T(8,128)(2,1)S(1)} %get-tuple-element.30), channel_id=1, source_target_pairs={{0,3},{1,0},{2,1},{3,2},{4,7},{5,4},{6,5},{7,6},{8,11},{9,8},{10,9... | collective-permute-start | bytes 884744 | tf_op jit(solution)/shard_map/weight_one/ppermute | solution.py:28
  37.3 4.7 %collective-permute-done.3 = bf16[8,48,384]{2,1,0:T(8,128)(2,1)S(1)} collective-permute-done((bf16[8,48,384]{2,1,0:T(8,128)(2,1)S(1)}, bf16[8,48,384]{2,1,0:T(8,128)(2,1)S(1)}, u32[]{:S(2)}, u32[]{:S(2)}) %collective-permute-start.3) | collective-permute-done | bytes 294944 | tf_op jit(solution)/shard_map/weight_one/ppermute | solution.py:28
  42.0 7.6 %collective-permute-done.4 = bf16[8,48,384]{2,1,0:T(8,128)(2,1)S(1)} collective-permute-done((bf16[8,48,384]{2,1,0:T(8,128)(2,1)S(1)}, bf16[8,48,384]{2,1,0:T(8,128)(2,1)S(1)}, u32[]{:S(2)}, u32[]{:S(2)}) %collective-permute-start.4) | collective-permute-done | bytes 294944 | tf_op jit(solution)/shard_map/weight_one/ppermute | solution.py:28
  49.6 0.0 collective-permute-done.5
  49.6 0.0 collective-permute-done.6.halo
  49.6 1.2 %pad_maximum_fusion.1.mine = bf16[4,8,48,384]{3,2,1,0:T(8,128)(2,1)} fusion(bf16[1,8,48,384]{3,2,1,0:T(8,128)(2,1)S(1)} %bitcast.34, bf16[1,8,48,384]{3,2,1,0:T(8,128)(2,1)S(1)} %bitcast.32, bf16[1,8,48,384]{3,2,1,0:T(8,128)(2,1)S(1)} %bitcast.30, bf16[1,8,48,384]{3,2,1,0:T(8,128)(2,1)S(1)} %bitcast.26), kind=kLoop, calls=%fused_computation.1 | loop fusion | flops 1769472 | bytes 2359296 | tf_op jit(solution)/shard_map/weight_one/stack | solution.py:331
  50.8 0.4 collective-permute-start.7
  51.2 0.2 reduce-window_clone.1
  51.4 0.1 pad_add_fusion.place
  51.5 0.2 fusion.18
  51.7 0.1 compare_convert_fusion.valid
  51.7 2.6 %collective-permute-start.10 = (bf16[8,48,384]{2,1,0:T(8,128)(2,1)S(1)}, bf16[8,48,384]{2,1,0:T(8,128)(2,1)S(1)}, u32[]{:S(2)}, u32[]{:S(2)}) collective-permute-start(bf16[8,48,384]{2,1,0:T(8,128)(2,1)S(1)} %get-tuple-element.38), channel_id=1, source_target_pairs={{0,3},{1,0},{2,1},{3,2},{4,7},{5,4},{6,5},{7,6},{8,11},{9,8},{10,9... | collective-permute-start | bytes 884744 | tf_op jit(solution)/shard_map/weight_two/ppermute | solution.py:28
  54.3 0.0 collective-permute-start.8
  54.4 2.3 %collective-permute-start.9 = (bf16[8,48,384]{2,1,0:T(8,128)(2,1)S(1)}, bf16[8,48,384]{2,1,0:T(8,128)(2,1)S(1)}, u32[]{:S(2)}, u32[]{:S(2)}) collective-permute-start(bf16[8,48,384]{2,1,0:T(8,128)(2,1)S(1)} %get-tuple-element.38), channel_id=1, source_target_pairs={{0,2},{1,3},{2,0},{3,1},{4,6},{5,7},{6,4},{7,5},{8,10},{9,11},{10,... | collective-permute-start | bytes 884744 | tf_op jit(solution)/shard_map/weight_two/ppermute | solution.py:28
  56.6 0.0 collective-permute-done.7.other
  56.6 9.3 %conv_one.1 = (f32[2,12,64,128]{3,2,1,0:T(8,128)S(1)}, f32[2,12,64]{2,1,0:T(8,128)S(1)}) custom-call(f32[2,3]{1,0:T(2,128)S(1)} %compare_convert_fusion.valid, s32[3]{0:T(128)S(1)} %pad_add_fusion.place, bf16[4,2,3,64,384]{4,3,2,1,0:T(8,128)(2,1)S(1)} %collective-permute-done.6.halo, bf16[4,2,3,64,384]{4,3,2,1,0:T(8,128)(2,1)} %pad_maximum_fusion.own, ...), custom_call_target="tpu_custom_call" | custom-call | flops 4076863488 | bytes 6000000 | tf_op jit(solution)/shard_map/first/conv_one/pallas_call | solution.py:187
  65.9 1.6 %collective-permute-done.10 = bf16[8,48,384]{2,1,0:T(8,128)(2,1)S(1)} collective-permute-done((bf16[8,48,384]{2,1,0:T(8,128)(2,1)S(1)}, bf16[8,48,384]{2,1,0:T(8,128)(2,1)S(1)}, u32[]{:S(2)}, u32[]{:S(2)}) %collective-permute-start.10) | collective-permute-done | bytes 294944 | tf_op jit(solution)/shard_map/weight_two/ppermute | solution.py:28
  67.5 3.4 %collective-permute-done.8 = bf16[8,48,384]{2,1,0:T(8,128)(2,1)S(1)} collective-permute-done((bf16[8,48,384]{2,1,0:T(8,128)(2,1)S(1)}, bf16[8,48,384]{2,1,0:T(8,128)(2,1)S(1)}, u32[]{:S(2)}, u32[]{:S(2)}) %collective-permute-start.8) | collective-permute-done | bytes 294944 | tf_op jit(solution)/shard_map/weight_two/ppermute | solution.py:28
  70.9 0.0 collective-permute-done.9
  70.9 0.2 pad_maximum_fusion.2.mine
  71.1 0.1 collective-permute-start.13
  71.2 1.4 %collective-permute-start.11 = (f32[2,12,64]{2,1,0:T(8,128)S(1)}, f32[2,12,64]{2,1,0:T(8,128)S(1)}, u32[]{:S(2)}, u32[]{:S(2)}) collective-permute-start(f32[2,12,64]{2,1,0:T(8,128)S(1)} %get-tuple-element.37), channel_id=1, source_target_pairs={{0,4},{4,0},{8,12},{12,8},{1,5},{5,1},{9,13},{13,9},{2,6},{6,2},{1... | collective-permute-start | bytes 18440 | tf_op jit(solution)/shard_map/weight_two/ppermute | solution.py:32
  72.6 2.4 %collective-permute-done.11 = f32[2,12,64]{2,1,0:T(8,128)S(1)} collective-permute-done((f32[2,12,64]{2,1,0:T(8,128)S(1)}, f32[2,12,64]{2,1,0:T(8,128)S(1)}, u32[]{:S(2)}, u32[]{:S(2)}) %collective-permute-start.11) | collective-permute-done | bytes 6176 | tf_op jit(solution)/shard_map/weight_two/ppermute | solution.py:32
  75.0 2.7 %collective-permute-start.12 = (f32[2,12,64]{2,1,0:T(8,128)S(1)}, f32[2,12,64]{2,1,0:T(8,128)S(1)}, u32[]{:S(2)}, u32[]{:S(2)}) collective-permute-start(f32[2,12,64]{2,1,0:T(8,128)S(1)} %add.93), channel_id=1, source_target_pairs={{0,8},{4,12},{8,0},{12,4},{1,9},{5,13},{9,1},{13,5},{2,10},{6,14},... | collective-permute-start | bytes 18440 | tf_op jit(solution)/shard_map/second/ppermute | solution.py:32
  77.7 0.1 reshape.30
  77.8 0.2 dynamic-slice_reduce_fusion
  78.0 0.0 collective-permute-done.13.other
  78.0 3.9 %assemble_two.1.weight = bf16[3456,384]{1,0:T(8,128)(2,1)} custom-call(s32[3]{0:T(128)S(1)} %pad_add_fusion.place, bf16[4,8,48,384]{3,2,1,0:T(8,128)(2,1)S(1)} %pad_maximum_fusion.2.mine, bf16[4,8,48,384]{3,2,1,0:T(8,128)(2,1)} %collective-permute-done.13.other), custom_call_target="tpu_custom_call" | custom-call | flops 4000000 | bytes 12000000 | tf_op jit(solution)/shard_map/weight_two/assemble_two/pallas_call | solution.py:271
  81.9 0.3 multiply_convert_fusion.own
  82.2 2.1 %collective-permute-start.14 = (bf16[2,12,64,128]{3,2,1,0:T(8,128)(2,1)S(1)}, bf16[2,12,64,128]{3,2,1,0:T(8,128)(2,1)S(1)}, u32[]{:S(2)}, u32[]{:S(2)}) collective-permute-start(bf16[2,12,64,128]{3,2,1,0:T(8,128)(2,1)S(1)} %multiply_convert_fusion.own), channel_id=1, source_target_pairs={{0,16},{16,32},{32,48},{48,64},{64,80},{80,96},{96,112},{112,128},... | collective-permute-start | bytes 1179656 | tf_op jit(solution)/shard_map/second/ppermute | solution.py:23
  84.4 6.9 %collective-permute-done.14.halo = bf16[2,12,64,128]{3,2,1,0:T(8,128)(2,1)S(1)} collective-permute-done((bf16[2,12,64,128]{3,2,1,0:T(8,128)(2,1)S(1)}, bf16[2,12,64,128]{3,2,1,0:T(8,128)(2,1)S(1)}, u32[]{:S(2)}, u32[]{:S(2)}) %collective-permute-start.14) | collective-permute-done | bytes 393248 | tf_op jit(solution)/shard_map/second/ppermute | solution.py:23
  91.3 5.2 %conv_two.3 = (bf16[2,3,64,384]{3,2,1,0:T(8,128)(2,1)S(1)}, bf16[2,3,64,384]{3,2,1,0:T(8,128)(2,1)S(1)}) custom-call(f32[2,3]{1,0:T(2,128)S(1)} %compare_convert_fusion.valid, s32[3]{0:T(128)S(1)} %pad_add_fusion.place, bf16[2,12,64,128]{3,2,1,0:T(8,128)(2,1)S(1)} %collective-permute-done.14.halo, bf16[2,12,64,128]{3,2,1,0:T(8,128)(2,1)S(1)} %multiply_convert_fusion.own, ...), custom_call_target="tpu_custom_call" | custom-call | flops 3000000000 | bytes 6000000 | tf_op jit(solution)/shard_map/second/conv_two/pallas_call | solution.py:211
  96.5 1.4 %collective-permute-start.16 = (bf16[2,3,64,384]{3,2,1,0:T(8,128)(2,1)S(1)}, bf16[2,3,64,384]{3,2,1,0:T(8,128)(2,1)S(1)}, u32[]{:S(2)}, u32[]{:S(2)}) collective-permute-start(bf16[2,3,64,384]{3,2,1,0:T(8,128)(2,1)S(1)} %get-tuple-element.46), channel_id=1, source_target_pairs={{0,12},{4,0},{8,4},{12,8},{1,13},{5,1},{9,5},{13,9},{2,14},{6,2},{... | collective-permute-start | bytes 884744 | tf_op jit(solution)/shard_map/second/ppermute | solution.py:28
  97.9 0.7 collective-permute-start.15
  98.6 5.2 %conv_two.2 = (bf16[2,3,64,384]{3,2,1,0:T(8,128)(2,1)S(1)}, bf16[1,3,64,384]{3,2,1,0:T(8,128)(2,1)S(1)}, bf16[1,3,64,384]{3,2,1,0:T(8,128)(2,1)S(1)}) custom-call(f32[2,3]{1,0:T(2,128)S(1)} %compare_convert_fusion.valid, s32[3]{0:T(128)S(1)} %pad_add_fusion.place, bf16[2,12,64,128]{3,2,1,0:T(8,128)(2,1)S(1)} %collective-permute-done.14.halo, ...), custom_call_target="tpu_custom_call" | custom-call | flops 3000000000 | bytes 6000000 | tf_op jit(solution)/shard_map/second/conv_two/pallas_call | solution.py:211
  103.7 0.8 collective-permute-done.16.down
  104.6 2.6 %collective-permute-start.18 = (bf16[1,3,64,384]{3,2,1,0:T(8,128)(2,1)S(1)}, bf16[1,3,64,384]{3,2,1,0:T(8,128)(2,1)S(1)}, u32[]{:S(2)}, u32[]{:S(2)}) collective-permute-start(bf16[1,3,64,384]{3,2,1,0:T(8,128)(2,1)S(1)} %slice_add_fusion), channel_id=1, source_target_pairs={{0,12},{4,0},{8,4},{12,8},{1,13},{5,1},{9,5},{13,9},{2,14},{6,2},{... | collective-permute-start | bytes 442376 | tf_op jit(solution)/shard_map/second/ppermute | solution.py:28
  107.2 0.0 collective-permute-done.15.up
  107.3 0.1 collective-permute-start.17
  107.4 2.6 %collective-permute-done.18.down_last = bf16[1,3,64,384]{3,2,1,0:T(8,128)(2,1)S(1)} collective-permute-done((bf16[1,3,64,384]{3,2,1,0:T(8,128)(2,1)S(1)}, bf16[1,3,64,384]{3,2,1,0:T(8,128)(2,1)S(1)}, u32[]{:S(2)}, u32[]{:S(2)}) %collective-permute-start.18) | collective-permute-done | bytes 147488 | tf_op jit(solution)/shard_map/second/ppermute | solution.py:28
  109.9 3.8 %collective-permute-done.17.up_last = bf16[1,3,64,384]{3,2,1,0:T(8,128)(2,1)S(1)} collective-permute-done((bf16[1,3,64,384]{3,2,1,0:T(8,128)(2,1)S(1)}, bf16[1,3,64,384]{3,2,1,0:T(8,128)(2,1)S(1)}, u32[]{:S(2)}, u32[]{:S(2)}) %collective-permute-start.17) | collective-permute-done | bytes 147488 | tf_op jit(solution)/shard_map/second/ppermute | solution.py:28
  113.7 1.4 %finish.1 = bf16[2,6,128,384]{3,2,1,0:T(8,128)(2,1)} custom-call(bf16[2,3,64,384]{3,2,1,0:T(8,128)(2,1)S(1)} %bitcast.24, bf16[2,3,64,384]{3,2,1,0:T(8,128)(2,1)S(1)} %get-tuple-element.44.own_sum, bf16[2,3,64,384]{3,2,1,0:T(8,128)(2,1)S(1)} %collective-permute-done.15.up, bf16[2,3,64,384]{3,2,1,0:T(8,128)(2,1)S(1)} %collective-permute-done.16.down, ...), custom_call_target="tpu_custom_call" | custom-call | flops 2000000 | bytes 3000000 | tf_op jit(solution)/shard_map/finish/pallas_call | solution.py:225
  (22 shorter events, 0.1 us)
Async XLA Ops:
  0.0 1.2 %copy-start = (bf16[162,384]{1,0:T(8,128)(2,1)S(1)}, bf16[162,384]{1,0:T(8,128)(2,1)}, u32[]{:S(2)}) copy-start(bf16[162,384]{1,0:T(8,128)(2,1)} %param.11) | copy-start | bytes 373252
  1.2 9.8 %copy-start.1 = (bf16[1,2,3,64,384]{4,3,2,1,0:T(8,128)(2,1)S(1)}, bf16[1,2,3,64,384]{4,3,2,1,0:T(8,128)(2,1)}, u32[]{:S(2)}) copy-start(bf16[1,2,3,64,384]{4,3,2,1,0:T(8,128)(2,1)} %param.6) | copy-start | bytes 884740
  1.4 9.7 %copy-start.2 = (f32[384]{0:T(512)S(1)}, f32[384]{0:T(512)}, u32[]{:S(2)}) copy-start(f32[384]{0:T(512)} %param.8) | copy-start | bytes 4612
  2.4 27.0 %all-to-all-start = ((bf16[8,96,384]{2,1,0:T(8,128)(2,1)}), bf16[8,96,384]{2,1,0:T(8,128)(2,1)S(1)}, u32[]{:S(2)}, u32[]{:S(2)}) async-start(bf16[8,96,384]{2,1,0:T(8,128)(2,1)} %broadcast_in_dim.15), calls=%async_computation | async-start | bytes 1179648 | tf_op jit(solution)/shard_map/pieces/all_to_all | solution.py:317
  11.4 10.2 %collective-permute-start = (bf16[2,3,64,384]{3,2,1,0:T(8,128)(2,1)S(1)}, bf16[2,3,64,384]{3,2,1,0:T(8,128)(2,1)S(1)}, u32[]{:S(2)}, u32[]{:S(2)}) collective-permute-start(bf16[2,3,64,384]{3,2,1,0:T(8,128)(2,1)S(1)} %fusion.8), channel_id=1, source_target_pairs={{0,4},{4,8},{8,12},{12,0},{1,5},{5,9},{9,13},{13,1},{2,6},{6,10},{... | collective-permute-start | bytes 884744 | tf_op jit(solution)/shard_map/pixels/ppermute | solution.py:28
  13.0 15.2 %collective-permute-start.1 = (bf16[2,3,64,384]{3,2,1,0:T(8,128)(2,1)S(1)}, bf16[2,3,64,384]{3,2,1,0:T(8,128)(2,1)S(1)}, u32[]{:S(2)}, u32[]{:S(2)}) collective-permute-start(bf16[2,3,64,384]{3,2,1,0:T(8,128)(2,1)S(1)} %fusion.8), channel_id=1, source_target_pairs={{0,8},{4,12},{8,0},{12,4},{1,9},{5,13},{9,1},{13,5},{2,10},{6,14},... | collective-permute-start | bytes 884744 | tf_op jit(solution)/shard_map/pixels/ppermute | solution.py:28
  15.7 12.5 %collective-permute-start.2 = (bf16[2,3,64,384]{3,2,1,0:T(8,128)(2,1)S(1)}, bf16[2,3,64,384]{3,2,1,0:T(8,128)(2,1)S(1)}, u32[]{:S(2)}, u32[]{:S(2)}) collective-permute-start(bf16[2,3,64,384]{3,2,1,0:T(8,128)(2,1)S(1)} %fusion.8), channel_id=1, source_target_pairs={{0,12},{4,0},{8,4},{12,8},{1,13},{5,1},{9,5},{13,9},{2,14},{6,2},{... | collective-permute-start | bytes 884744 | tf_op jit(solution)/shard_map/pixels/ppermute | solution.py:28
  29.4 20.2 %collective-permute-start.6 = (bf16[4,2,3,64,384]{4,3,2,1,0:T(8,128)(2,1)}, bf16[4,2,3,64,384]{4,3,2,1,0:T(8,128)(2,1)S(1)}, u32[]{:S(2)}, u32[]{:S(2)}) collective-permute-start(bf16[4,2,3,64,384]{4,3,2,1,0:T(8,128)(2,1)} %pad_maximum_fusion.own), channel_id=1, source_target_pairs={{0,16},{16,32},{32,48},{48,64},{64,80},{80,96},{96,112},{112,128},... | collective-permute-start | bytes 3538952 | tf_op jit(solution)/shard_map/weight_one/ppermute | solution.py:23
  31.4 10.6 %collective-permute-start.3 = (bf16[8,48,384]{2,1,0:T(8,128)(2,1)S(1)}, bf16[8,48,384]{2,1,0:T(8,128)(2,1)S(1)}, u32[]{:S(2)}, u32[]{:S(2)}) collective-permute-start(bf16[8,48,384]{2,1,0:T(8,128)(2,1)S(1)} %get-tuple-element.30), channel_id=1, source_target_pairs={{0,1},{1,2},{2,3},{3,0},{4,5},{5,6},{6,7},{7,4},{8,9},{9,10},{10,1... | collective-permute-start | bytes 884744 | tf_op jit(solution)/shard_map/weight_one/ppermute | solution.py:28
  33.0 16.5 %collective-permute-start.4 = (bf16[8,48,384]{2,1,0:T(8,128)(2,1)S(1)}, bf16[8,48,384]{2,1,0:T(8,128)(2,1)S(1)}, u32[]{:S(2)}, u32[]{:S(2)}) collective-permute-start(bf16[8,48,384]{2,1,0:T(8,128)(2,1)S(1)} %get-tuple-element.30), channel_id=1, source_target_pairs={{0,2},{1,3},{2,0},{3,1},{4,6},{5,7},{6,4},{7,5},{8,10},{9,11},{10,... | collective-permute-start | bytes 884744 | tf_op jit(solution)/shard_map/weight_one/ppermute | solution.py:28
  35.9 13.6 %collective-permute-start.5 = (bf16[8,48,384]{2,1,0:T(8,128)(2,1)S(1)}, bf16[8,48,384]{2,1,0:T(8,128)(2,1)S(1)}, u32[]{:S(2)}, u32[]{:S(2)}) collective-permute-start(bf16[8,48,384]{2,1,0:T(8,128)(2,1)S(1)} %get-tuple-element.30), channel_id=1, source_target_pairs={{0,3},{1,0},{2,1},{3,2},{4,7},{5,4},{6,5},{7,6},{8,11},{9,8},{10,9... | collective-permute-start | bytes 884744 | tf_op jit(solution)/shard_map/weight_one/ppermute | solution.py:28
  49.6 1.6 %copy-start.4 = (s32[1,4]{1,0:T(1,128)S(1)}, s32[1,4]{1,0:T(1,128)}, u32[]{:S(2)}) copy-start(s32[1,4]{1,0:T(1,128)} %param.7) | copy-start | bytes 52
  50.8 5.8 %collective-permute-start.7 = (bf16[4,8,48,384]{3,2,1,0:T(8,128)(2,1)}, bf16[4,8,48,384]{3,2,1,0:T(8,128)(2,1)}, u32[]{:S(2)}, u32[]{:S(2)}) collective-permute-start(bf16[4,8,48,384]{3,2,1,0:T(8,128)(2,1)} %pad_maximum_fusion.1.mine), channel_id=1, source_target_pairs={{0,16},{16,0},{1,17},{17,1},{2,18},{18,2},{3,19},{19,3},{4,20},{20... | collective-permute-start | bytes 3538952 | tf_op jit(solution)/shard_map/weight_one/ppermute | solution.py:332
  51.7 15.8 %collective-permute-start.10 = (bf16[8,48,384]{2,1,0:T(8,128)(2,1)S(1)}, bf16[8,48,384]{2,1,0:T(8,128)(2,1)S(1)}, u32[]{:S(2)}, u32[]{:S(2)}) collective-permute-start(bf16[8,48,384]{2,1,0:T(8,128)(2,1)S(1)} %get-tuple-element.38), channel_id=1, source_target_pairs={{0,3},{1,0},{2,1},{3,2},{4,7},{5,4},{6,5},{7,6},{8,11},{9,8},{10,9... | collective-permute-start | bytes 884744 | tf_op jit(solution)/shard_map/weight_two/ppermute | solution.py:28
  54.3 16.5 %collective-permute-start.8 = (bf16[8,48,384]{2,1,0:T(8,128)(2,1)S(1)}, bf16[8,48,384]{2,1,0:T(8,128)(2,1)S(1)}, u32[]{:S(2)}, u32[]{:S(2)}) collective-permute-start(bf16[8,48,384]{2,1,0:T(8,128)(2,1)S(1)} %get-tuple-element.38), channel_id=1, source_target_pairs={{0,1},{1,2},{2,3},{3,0},{4,5},{5,6},{6,7},{7,4},{8,9},{9,10},{10,1... | collective-permute-start | bytes 884744 | tf_op jit(solution)/shard_map/weight_two/ppermute | solution.py:28
  54.4 16.5 %collective-permute-start.9 = (bf16[8,48,384]{2,1,0:T(8,128)(2,1)S(1)}, bf16[8,48,384]{2,1,0:T(8,128)(2,1)S(1)}, u32[]{:S(2)}, u32[]{:S(2)}) collective-permute-start(bf16[8,48,384]{2,1,0:T(8,128)(2,1)S(1)} %get-tuple-element.38), channel_id=1, source_target_pairs={{0,2},{1,3},{2,0},{3,1},{4,6},{5,7},{6,4},{7,5},{8,10},{9,11},{10,... | collective-permute-start | bytes 884744 | tf_op jit(solution)/shard_map/weight_two/ppermute | solution.py:28
  70.9 6.8 %copy-start.3 = (f32[384]{0:T(512)S(1)}, f32[384]{0:T(512)}, u32[]{:S(2)}) copy-start(f32[384]{0:T(512)} %param.9) | copy-start | bytes 4612
  71.1 6.9 %collective-permute-start.13 = (bf16[4,8,48,384]{3,2,1,0:T(8,128)(2,1)S(1)}, bf16[4,8,48,384]{3,2,1,0:T(8,128)(2,1)}, u32[]{:S(2)}, u32[]{:S(2)}) collective-permute-start(bf16[4,8,48,384]{3,2,1,0:T(8,128)(2,1)S(1)} %pad_maximum_fusion.2.mine), channel_id=1, source_target_pairs={{0,16},{16,0},{1,17},{17,1},{2,18},{18,2},{3,19},{19,3},{4,20},{20... | collective-permute-start | bytes 3538952 | tf_op jit(solution)/shard_map/weight_two/ppermute | solution.py:347
  71.2 3.8 %collective-permute-start.11 = (f32[2,12,64]{2,1,0:T(8,128)S(1)}, f32[2,12,64]{2,1,0:T(8,128)S(1)}, u32[]{:S(2)}, u32[]{:S(2)}) collective-permute-start(f32[2,12,64]{2,1,0:T(8,128)S(1)} %get-tuple-element.37), channel_id=1, source_target_pairs={{0,4},{4,0},{8,12},{12,8},{1,5},{5,1},{9,13},{13,9},{2,6},{6,2},{1... | collective-permute-start | bytes 18440 | tf_op jit(solution)/shard_map/weight_two/ppermute | solution.py:32
  75.0 6.9 %collective-permute-start.12 = (f32[2,12,64]{2,1,0:T(8,128)S(1)}, f32[2,12,64]{2,1,0:T(8,128)S(1)}, u32[]{:S(2)}, u32[]{:S(2)}) collective-permute-start(f32[2,12,64]{2,1,0:T(8,128)S(1)} %add.93), channel_id=1, source_target_pairs={{0,8},{4,12},{8,0},{12,4},{1,9},{5,13},{9,1},{13,5},{2,10},{6,14},... | collective-permute-start | bytes 18440 | tf_op jit(solution)/shard_map/second/ppermute | solution.py:32
  82.2 9.1 %collective-permute-start.14 = (bf16[2,12,64,128]{3,2,1,0:T(8,128)(2,1)S(1)}, bf16[2,12,64,128]{3,2,1,0:T(8,128)(2,1)S(1)}, u32[]{:S(2)}, u32[]{:S(2)}) collective-permute-start(bf16[2,12,64,128]{3,2,1,0:T(8,128)(2,1)S(1)} %multiply_convert_fusion.own), channel_id=1, source_target_pairs={{0,16},{16,32},{32,48},{48,64},{64,80},{80,96},{96,112},{112,128},... | collective-permute-start | bytes 1179656 | tf_op jit(solution)/shard_map/second/ppermute | solution.py:23
  96.5 8.1 %collective-permute-start.16 = (bf16[2,3,64,384]{3,2,1,0:T(8,128)(2,1)S(1)}, bf16[2,3,64,384]{3,2,1,0:T(8,128)(2,1)S(1)}, u32[]{:S(2)}, u32[]{:S(2)}) collective-permute-start(bf16[2,3,64,384]{3,2,1,0:T(8,128)(2,1)S(1)} %get-tuple-element.46), channel_id=1, source_target_pairs={{0,12},{4,0},{8,4},{12,8},{1,13},{5,1},{9,5},{13,9},{2,14},{6,2},{... | collective-permute-start | bytes 884744 | tf_op jit(solution)/shard_map/second/ppermute | solution.py:28
  97.9 9.3 %collective-permute-start.15 = (bf16[2,3,64,384]{3,2,1,0:T(8,128)(2,1)S(1)}, bf16[2,3,64,384]{3,2,1,0:T(8,128)(2,1)S(1)}, u32[]{:S(2)}, u32[]{:S(2)}) collective-permute-start(bf16[2,3,64,384]{3,2,1,0:T(8,128)(2,1)S(1)} %get-tuple-element.45), channel_id=1, source_target_pairs={{0,4},{4,8},{8,12},{12,0},{1,5},{5,9},{9,13},{13,1},{2,6},{6,10},{... | collective-permute-start | bytes 884744 | tf_op jit(solution)/shard_map/second/ppermute | solution.py:28
  104.6 5.3 %collective-permute-start.18 = (bf16[1,3,64,384]{3,2,1,0:T(8,128)(2,1)S(1)}, bf16[1,3,64,384]{3,2,1,0:T(8,128)(2,1)S(1)}, u32[]{:S(2)}, u32[]{:S(2)}) collective-permute-start(bf16[1,3,64,384]{3,2,1,0:T(8,128)(2,1)S(1)} %slice_add_fusion), channel_id=1, source_target_pairs={{0,12},{4,0},{8,4},{12,8},{1,13},{5,1},{9,5},{13,9},{2,14},{6,2},{... | collective-permute-start | bytes 442376 | tf_op jit(solution)/shard_map/second/ppermute | solution.py:28
  107.3 6.4 %collective-permute-start.17 = (bf16[1,3,64,384]{3,2,1,0:T(8,128)(2,1)S(1)}, bf16[1,3,64,384]{3,2,1,0:T(8,128)(2,1)S(1)}, u32[]{:S(2)}, u32[]{:S(2)}) collective-permute-start(bf16[1,3,64,384]{3,2,1,0:T(8,128)(2,1)S(1)} %slice_add_fusion.1), channel_id=1, source_target_pairs={{0,4},{4,8},{8,12},{12,0},{1,5},{5,9},{9,13},{13,1},{2,6},{6,10},{... | collective-permute-start | bytes 442376 | tf_op jit(solution)/shard_map/second/ppermute | solution.py:28

commit v12 on v11

--- a/solution.py
+++ b/solution.py
@@ -122,10 +122,9 @@
         squares[s] = jnp.sum(done * done, axis=-1)
 
 
-def conv_two_kernel(plan, valid, place, halo, own, weight, *rest):
-    *outs, taps = rest
+def conv_two_kernel(valid, place, halo, own, weight, own_sum, up, down, up_last, down_last, taps, acc):
     frames, rows, width, lanes = own.shape
-    each = outs[0].shape[1]
+    each = own_sum.shape[1]
     parts = rows // each
     channels = weight.shape[1]
     clear_border(taps)
@@ -133,30 +132,30 @@
         source = halo if slot < frames else own
         for row in range(rows):
             fill_shifted(taps, slot, row + 1, source[slot % frames, row])
-    for s, targets in enumerate(plan):
-        tops = [lax.rem(place[2] + d, parts) * each for d, _, _ in targets]
-        total = None
-        for a in range(3):
-            columns = jnp.concatenate(
-                [
-                    jnp.concatenate(
-                        [
-                            taps[e, s + a, pl.ds(top + b, each)].reshape(each * width, lanes)
-                            for b in range(3)
-                            for e in range(3)
-                        ],
-                        axis=1,
-                    )
-                    for top in tops
-                ],
-                axis=0,
-            )
-            block = weight[a * 9 * lanes : (a + 1) * 9 * lanes, :]
-            term = valid[s, a] * jnp.dot(columns, block, preferred_element_type=jnp.float32)
-            total = term if total is None else total + term
-        for i, (_, ref, at) in enumerate(targets):
-            done = total[i * each * width : (i + 1) * each * width]
-            outs[ref][at] = done.astype(outs[ref].dtype).reshape(each, width, channels)
+    for slot in range(2 * frames):
+        pairs = [(s, slot - s) for s in range(frames) if 0 <= slot - s < 3]
+        columns = jnp.concatenate(
+            [
+                taps[e, slot, b : b + rows].reshape(rows * width, lanes)
+                for b in range(3)
+                for e in range(3)
+            ],
+            axis=1,
+        )
+        blocks = [weight[a * 9 * lanes : (a + 1) * 9 * lanes, :] for _, a in pairs]
+        packed = blocks[0] if len(blocks) == 1 else jnp.concatenate(blocks, axis=1)
+        term = jnp.dot(columns, packed, preferred_element_type=jnp.float32)
+        for i, (s, a) in enumerate(pairs):
+            piece = valid[s, a] * term[:, i * channels : (i + 1) * channels]
+            if a == 0:
+                acc[s] = piece
+            else:
+                acc[s] = acc[s] + piece
+    for ref, d, s, at in ((own_sum, 0, 0, 0), (own_sum, 0, 1, 1), (up, 2, 0, 0), (up, 1, 1, 1),
+                          (down, 3, 0, 0), (down, 2, 1, 1), (up_last, 1, 0, 0), (down_last, 3, 1, 0)):
+        top = pl.multiple_of(lax.rem(place[2] + d, parts) * (each * width), 64)
+        done = acc[s, pl.ds(top, each * width), :].astype(ref.dtype)
+        ref[at] = done.reshape(each, width, channels)
 
 
 def finish_kernel(latents, own_sum, up, down, up_last, down_last, out, wide):
@@ -204,18 +203,22 @@
     )(valid, place, halo, own, mine, other)
 
 
-def conv_two_call(plan, leads, valid, place, halo, own, weight, parts):
+def conv_two_call(valid, place, halo, own, weight, parts):
     frames, rows, width, lanes = own.shape
     channels = weight.shape[1]
-    shapes = [(n, rows // parts, width, channels) for n in leads]
+    flops = 2 * 6 * rows * width * 9 * lanes * channels
+    shapes = [(n, rows // parts, width, channels) for n in (frames, frames, frames, 1, 1)]
     return pl.pallas_call(
-        functools.partial(conv_two_kernel, plan),
+        conv_two_kernel,
         out_shape=[jax.ShapeDtypeStruct(shape, jnp.bfloat16) for shape in shapes],
         in_specs=[SMEM, SMEM, VMEM, VMEM, VMEM],
         out_specs=[VMEM] * len(shapes),
-        scratch_shapes=[pltpu.VMEM((3, 2 * frames, rows + 2, width, lanes), jnp.bfloat16)],
+        scratch_shapes=[
+            pltpu.VMEM((3, 2 * frames, rows + 2, width, lanes), jnp.bfloat16),
+            pltpu.VMEM((frames, rows * width, channels), jnp.float32),
+        ],
         compiler_params=PARAMS,
-        cost_estimate=pl.CostEstimate(flops=3_000_000_000, bytes_accessed=6_000_000, transcendentals=0),
+        cost_estimate=pl.CostEstimate(flops=flops, bytes_accessed=6_000_000, transcendentals=0),
         name="conv_two",
     )(valid, place, halo, own, weight)
 
@@ -341,8 +344,8 @@
         first, squares = conv_one_call(valid, place, prior_all, own_all, one_mine, one_swapped)
 
     with jax.named_scope("weight_two"):
-        squares, later = lax.optimization_barrier((squares, later))
         squares = squares + across(squares, 1)
+        other_squares, later = lax.optimization_barrier((across(squares, 2), later))
         mine = jnp.stack(later)
         swapped = lax.ppermute(mine, "core", [(0, 1), (1, 0)])
         taps = shards * shard // channels
@@ -352,19 +355,16 @@
         )
 
     with jax.named_scope("second"):
-        other_squares, weight_two = lax.optimization_barrier((across(squares, 2), weight_two))
         squares = squares + other_squares
         gain_mine = lax.dynamic_index_in_dim(gain_two.reshape(share, parts), part, 1, keepdims=False)
         gain_mine = jnp.pad(gain_mine, (0, LANE - share))
         scale = lax.rsqrt(squares / channels + EPS)
         hidden_two = jax.nn.silu(first * scale[..., None] * gain_mine).astype(jnp.bfloat16)
         prior_two = earlier(hidden_two)
-        operands = (valid, place, prior_two, hidden_two, weight_two, parts)
-        up, down = conv_two_call((((2, 0, 0), (3, 1, 0)), ((1, 0, 1), (2, 1, 1))), (2, 2), *operands)
+        own_sum, up, down, up_last, down_last = conv_two_call(
+            valid, place, prior_two, hidden_two, weight_two, parts
+        )
         up, down = onward(up, 1), onward(down, -1)
-        own_sum, up_last, down_last = conv_two_call(
-            (((0, 0, 0), (1, 1, 0)), ((3, 2, 0), (0, 0, 1))), (2, 1, 1), *operands
-        )
         up_last = onward(up_last + up[:1], 1)
         down_last = onward(down_last + down[1:], -1)
 

time: 115 us -> 116 us (level)
  Pallas kernels: 24.9 us -> 21.9 us
  local copies, waits for them, and re-layouts: 1.26 us -> 3.97 us
  starting transfers between devices: 38.5 us -> 40.4 us
  waiting for transfers between devices: 44.5 us -> 43 us
    ppermute x2, waiting for transfers between devices: 6.95 us -> 2.91 us  [earlier(): return lax.ppermute(x, SLOT, [(i, i + 1) for i in range(n - 1)])]
    pallas_call x2 -> x1, Pallas kernels: 10.3 us -> 7.33 us  [conv_two_call(): pl.pallas_call(conv_two_kernel, out_shape=[jax.ShapeDtypeStruct(shape, jn...]
    unnamed x10 -> x14, local copies, waits for them, and re-layouts: 0.02 us -> 2.73 us
    ppermute x2, waiting for transfers between devices: 2.41 us -> 4.97 us  [across(): lax.ppermute(x, 'tile', [(i, i ^ bit) for i in range(lax.axis_size('tile'...]
    ppermute x13, starting transfers between devices: 21.4 us -> 23.1 us  [onward(): return lax.ppermute(x, axis, [(i, (i + by) % n) for i in range(n)])]
  transfers between devices with their start and end apart: 20 -> 20, of which waited for: 11 -> 10; matrix products, arithmetic and copies ran while one was open for 2% -> 3% of each run, Pallas kernels for 16% -> 11%
where the time goes in v12:
time: 116 us; the launch traced here: 115 us
  waiting for transfers between devices  43 us (37%)
  starting transfers between devices  40.4 us (35%)
  Pallas kernels  21.9 us (19%)
  other arithmetic  4.19 us (4%)
  local copies, waits for them, and re-layouts  3.97 us (3%)
  matrix products  1.35 us (1%)
    ppermute x13, waiting for transfers between devices, onward(): return lax.ppermute(x, axis, [(i, (i + by) % n) for i in range(n)])  35.2 us
    ppermute x13, starting transfers between devices, onward(): return lax.ppermute(x, axis, [(i, (i + by) % n) for i in range(n)])  23.1 us
    pallas_call x1, Pallas kernels, conv_one_call(): pl.pallas_call(functools.partial(conv_one_kernel, channels // parts), out...  9.29 us
    all_to_all x1, starting transfers between devices, body(): lax.all_to_all(jnp.broadcast_to(pieces, (lax.axis_size('z'),) + pieces.sh...  8.57 us
    pallas_call x1, Pallas kernels, conv_two_call(): pl.pallas_call(conv_two_kernel, out_shape=[jax.ShapeDtypeStruct(shape, jn...  7.33 us
    ppermute x2, waiting for transfers between devices, across(): lax.ppermute(x, 'tile', [(i, i ^ bit) for i in range(lax.axis_size('tile'...  4.97 us
    ppermute x2, starting transfers between devices, earlier(): return lax.ppermute(x, SLOT, [(i, i + 1) for i in range(n - 1)])  4.14 us
    ppermute x2, starting transfers between devices, across(): lax.ppermute(x, 'tile', [(i, i ^ bit) for i in range(lax.axis_size('tile'...  4.09 us
  transfers between devices with their start and end apart: 20, of which 10 were waited for; matrix products, arithmetic and copies ran while one was open for 3% of the time, Pallas kernels for 11%

profile of v12, /device:TPU:32, one launch (start us, length us, event | category | flops | bytes accessed | tf_op | source)
XLA Modules:
  0.0 115.1 jit_solution(5900415714631186355)
XLA Ops:
  0.0 1.2 %fusion = bf16[162,96]{1,0:T(8,128)(2,1)S(1)} fusion(bf16[162,384]{1,0:T(8,128)(2,1)} %param.10, s32[96]{0:T(128)S(1)} %multiply_add_fusion.1), kind=kOutput, calls=%fused_computation.5 | convolution fusion | flops 11996352 | bytes 155904 | tf_op jit(solution)/shard_map/pieces/dot_general | solution.py:313
  1.2 0.0 copy-start.1
  1.2 0.2 convolution_convert_fusion.1
  1.4 0.0 copy-start.4
  1.4 0.1 fusion.16
  1.6 0.9 broadcast_in_dim.15
  2.4 8.6 %all-to-all-start = ((bf16[8,96,384]{2,1,0:T(8,128)(2,1)}), bf16[8,96,384]{2,1,0:T(8,128)(2,1)S(1)}, u32[]{:S(2)}, u32[]{:S(2)}) async-start(bf16[8,96,384]{2,1,0:T(8,128)(2,1)} %broadcast_in_dim.15), calls=%async_computation | async-start | bytes 1179648 | tf_op jit(solution)/shard_map/pieces/all_to_all | solution.py:320
  11.0 0.1 fusion.1
  11.2 0.3 fusion.8
  11.4 1.6 %collective-permute-start = (bf16[2,3,64,384]{3,2,1,0:T(8,128)(2,1)S(1)}, bf16[2,3,64,384]{3,2,1,0:T(8,128)(2,1)S(1)}, u32[]{:S(2)}, u32[]{:S(2)}) collective-permute-start(bf16[2,3,64,384]{3,2,1,0:T(8,128)(2,1)S(1)} %fusion.8), channel_id=1, source_target_pairs={{0,4},{4,8},{8,12},{12,0},{1,5},{5,9},{9,13},{13,1},{2,6},{6,10},{... | collective-permute-start | bytes 884744 | tf_op jit(solution)/shard_map/pixels/ppermute | solution.py:28
  13.0 2.7 %collective-permute-start.1 = (bf16[2,3,64,384]{3,2,1,0:T(8,128)(2,1)S(1)}, bf16[2,3,64,384]{3,2,1,0:T(8,128)(2,1)S(1)}, u32[]{:S(2)}, u32[]{:S(2)}) collective-permute-start(bf16[2,3,64,384]{3,2,1,0:T(8,128)(2,1)S(1)} %fusion.8), channel_id=1, source_target_pairs={{0,8},{4,12},{8,0},{12,4},{1,9},{5,13},{9,1},{13,5},{2,10},{6,14},... | collective-permute-start | bytes 884744 | tf_op jit(solution)/shard_map/pixels/ppermute | solution.py:28
  15.7 1.4 %collective-permute-start.2 = (bf16[2,3,64,384]{3,2,1,0:T(8,128)(2,1)S(1)}, bf16[2,3,64,384]{3,2,1,0:T(8,128)(2,1)S(1)}, u32[]{:S(2)}, u32[]{:S(2)}) collective-permute-start(bf16[2,3,64,384]{3,2,1,0:T(8,128)(2,1)S(1)} %fusion.8), channel_id=1, source_target_pairs={{0,12},{4,0},{8,4},{12,8},{1,13},{5,1},{9,5},{13,9},{2,14},{6,2},{... | collective-permute-start | bytes 884744 | tf_op jit(solution)/shard_map/pixels/ppermute | solution.py:28
  17.2 0.3 multiply_convert_fusion.1
  17.4 4.3 %collective-permute-done = bf16[2,3,64,384]{3,2,1,0:T(8,128)(2,1)S(1)} collective-permute-done((bf16[2,3,64,384]{3,2,1,0:T(8,128)(2,1)S(1)}, bf16[2,3,64,384]{3,2,1,0:T(8,128)(2,1)S(1)}, u32[]{:S(2)}, u32[]{:S(2)}) %collective-permute-start) | collective-permute-done | bytes 294944 | tf_op jit(solution)/shard_map/pixels/ppermute | solution.py:28
  21.7 6.5 %collective-permute-done.1 = bf16[2,3,64,384]{3,2,1,0:T(8,128)(2,1)S(1)} collective-permute-done((bf16[2,3,64,384]{3,2,1,0:T(8,128)(2,1)S(1)}, bf16[2,3,64,384]{3,2,1,0:T(8,128)(2,1)S(1)}, u32[]{:S(2)}, u32[]{:S(2)}) %collective-permute-start.1) | collective-permute-done | bytes 294944 | tf_op jit(solution)/shard_map/pixels/ppermute | solution.py:28
  28.2 0.0 collective-permute-done.2
  28.2 1.2 %pad_maximum_fusion.own = bf16[4,2,3,64,384]{4,3,2,1,0:T(8,128)(2,1)} fusion(bf16[1,2,3,64,384]{4,3,2,1,0:T(8,128)(2,1)S(1)} %bitcast.35, bf16[1,2,3,64,384]{4,3,2,1,0:T(8,128)(2,1)S(1)} %bitcast.33, bf16[1,2,3,64,384]{4,3,2,1,0:T(8,128)(2,1)S(1)} %bitcast.31, bf16[1,2,3,64,384]{4,3,2,1,0:T(8,128)(2,1)S(1)} %multiply_convert_fusion.1), kind=kLoop, calls=%fused_computation | loop fusion | flops 1769472 | bytes 2359296 | tf_op jit(solution)/shard_map/pixels/stack | solution.py:36
  29.4 0.0 all-to-all-done
  29.4 1.9 %collective-permute-start.6 = (bf16[4,2,3,64,384]{4,3,2,1,0:T(8,128)(2,1)}, bf16[4,2,3,64,384]{4,3,2,1,0:T(8,128)(2,1)S(1)}, u32[]{:S(2)}, u32[]{:S(2)}) collective-permute-start(bf16[4,2,3,64,384]{4,3,2,1,0:T(8,128)(2,1)} %pad_maximum_fusion.own), channel_id=1, source_target_pairs={{0,16},{16,32},{32,48},{48,64},{64,80},{80,96},{96,112},{112,128},... | collective-permute-start | bytes 3538952 | tf_op jit(solution)/shard_map/weight_one/ppermute | solution.py:23
  31.3 0.1 fusion.19
  31.4 1.7 %collective-permute-start.3 = (bf16[8,48,384]{2,1,0:T(8,128)(2,1)S(1)}, bf16[8,48,384]{2,1,0:T(8,128)(2,1)S(1)}, u32[]{:S(2)}, u32[]{:S(2)}) collective-permute-start(bf16[8,48,384]{2,1,0:T(8,128)(2,1)S(1)} %get-tuple-element.28), channel_id=1, source_target_pairs={{0,1},{1,2},{2,3},{3,0},{4,5},{5,6},{6,7},{7,4},{8,9},{9,10},{10,1... | collective-permute-start | bytes 884744 | tf_op jit(solution)/shard_map/weight_one/ppermute | solution.py:28
  33.1 2.9 %collective-permute-start.4 = (bf16[8,48,384]{2,1,0:T(8,128)(2,1)S(1)}, bf16[8,48,384]{2,1,0:T(8,128)(2,1)S(1)}, u32[]{:S(2)}, u32[]{:S(2)}) collective-permute-start(bf16[8,48,384]{2,1,0:T(8,128)(2,1)S(1)} %get-tuple-element.28), channel_id=1, source_target_pairs={{0,2},{1,3},{2,0},{3,1},{4,6},{5,7},{6,4},{7,5},{8,10},{9,11},{10,... | collective-permute-start | bytes 884744 | tf_op jit(solution)/shard_map/weight_one/ppermute | solution.py:28
  36.0 1.3 %collective-permute-start.5 = (bf16[8,48,384]{2,1,0:T(8,128)(2,1)S(1)}, bf16[8,48,384]{2,1,0:T(8,128)(2,1)S(1)}, u32[]{:S(2)}, u32[]{:S(2)}) collective-permute-start(bf16[8,48,384]{2,1,0:T(8,128)(2,1)S(1)} %get-tuple-element.28), channel_id=1, source_target_pairs={{0,3},{1,0},{2,1},{3,2},{4,7},{5,4},{6,5},{7,6},{8,11},{9,8},{10,9... | collective-permute-start | bytes 884744 | tf_op jit(solution)/shard_map/weight_one/ppermute | solution.py:28
  37.3 4.7 %collective-permute-done.3 = bf16[8,48,384]{2,1,0:T(8,128)(2,1)S(1)} collective-permute-done((bf16[8,48,384]{2,1,0:T(8,128)(2,1)S(1)}, bf16[8,48,384]{2,1,0:T(8,128)(2,1)S(1)}, u32[]{:S(2)}, u32[]{:S(2)}) %collective-permute-start.3) | collective-permute-done | bytes 294944 | tf_op jit(solution)/shard_map/weight_one/ppermute | solution.py:28
  42.0 7.6 %collective-permute-done.4 = bf16[8,48,384]{2,1,0:T(8,128)(2,1)S(1)} collective-permute-done((bf16[8,48,384]{2,1,0:T(8,128)(2,1)S(1)}, bf16[8,48,384]{2,1,0:T(8,128)(2,1)S(1)}, u32[]{:S(2)}, u32[]{:S(2)}) %collective-permute-start.4) | collective-permute-done | bytes 294944 | tf_op jit(solution)/shard_map/weight_one/ppermute | solution.py:28
  49.6 0.0 collective-permute-done.5
  49.6 0.0 collective-permute-done.6.halo
  49.6 1.0 copy-done.2
  50.7 1.2 %pad_maximum_fusion.1.mine = bf16[4,8,48,384]{3,2,1,0:T(8,128)(2,1)} fusion(bf16[1,8,48,384]{3,2,1,0:T(8,128)(2,1)S(1)} %bitcast.34, bf16[1,8,48,384]{3,2,1,0:T(8,128)(2,1)S(1)} %bitcast.32, bf16[1,8,48,384]{3,2,1,0:T(8,128)(2,1)S(1)} %bitcast.30, bf16[1,8,48,384]{3,2,1,0:T(8,128)(2,1)S(1)} %bitcast.26), kind=kLoop, calls=%fused_computation.1 | loop fusion | flops 1769472 | bytes 2359296 | tf_op jit(solution)/shard_map/weight_one/stack | solution.py:334
  51.8 0.4 collective-permute-start.7
  52.2 0.2 reduce-window_clone.1
  52.4 0.1 pad_add_fusion.place
  52.5 0.2 fusion.18
  52.6 0.1 compare_convert_fusion.valid
  52.7 1.8 %collective-permute-start.10 = (bf16[8,48,384]{2,1,0:T(8,128)(2,1)S(1)}, bf16[8,48,384]{2,1,0:T(8,128)(2,1)S(1)}, u32[]{:S(2)}, u32[]{:S(2)}) collective-permute-start(bf16[8,48,384]{2,1,0:T(8,128)(2,1)S(1)} %get-tuple-element.36), channel_id=1, source_target_pairs={{0,1},{1,2},{2,3},{3,0},{4,5},{5,6},{6,7},{7,4},{8,9},{9,10},{10,1... | collective-permute-start | bytes 884744 | tf_op jit(solution)/shard_map/weight_two/ppermute | solution.py:28
  54.5 2.3 %collective-permute-start.11 = (bf16[8,48,384]{2,1,0:T(8,128)(2,1)S(1)}, bf16[8,48,384]{2,1,0:T(8,128)(2,1)S(1)}, u32[]{:S(2)}, u32[]{:S(2)}) collective-permute-start(bf16[8,48,384]{2,1,0:T(8,128)(2,1)S(1)} %get-tuple-element.36), channel_id=1, source_target_pairs={{0,2},{1,3},{2,0},{3,1},{4,6},{5,7},{6,4},{7,5},{8,10},{9,11},{10,... | collective-permute-start | bytes 884744 | tf_op jit(solution)/shard_map/weight_two/ppermute | solution.py:28
  56.8 1.4 %collective-permute-start.12 = (bf16[8,48,384]{2,1,0:T(8,128)(2,1)S(1)}, bf16[8,48,384]{2,1,0:T(8,128)(2,1)S(1)}, u32[]{:S(2)}, u32[]{:S(2)}) collective-permute-start(bf16[8,48,384]{2,1,0:T(8,128)(2,1)S(1)} %get-tuple-element.36), channel_id=1, source_target_pairs={{0,3},{1,0},{2,1},{3,2},{4,7},{5,4},{6,5},{7,6},{8,11},{9,8},{10,9... | collective-permute-start | bytes 884744 | tf_op jit(solution)/shard_map/weight_two/ppermute | solution.py:28
  58.2 1.3 %copy-done.3 = bf16[4,2,3,64,384]{4,3,2,1,0:T(8,128)(2,1)S(1)} copy-done((bf16[4,2,3,64,384]{4,3,2,1,0:T(8,128)(2,1)S(1)}, bf16[4,2,3,64,384]{4,3,2,1,0:T(8,128)(2,1)}, u32[]{:S(2)}) %copy-start.3) | copy-done | bytes 1179672
  59.5 9.3 %conv_one.1 = (f32[2,12,64,128]{3,2,1,0:T(8,128)S(1)}, f32[2,12,64]{2,1,0:T(8,128)S(1)}) custom-call(f32[2,3]{1,0:T(2,128)S(1)} %compare_convert_fusion.valid, s32[3]{0:T(128)S(1)} %pad_add_fusion.place, bf16[4,2,3,64,384]{4,3,2,1,0:T(8,128)(2,1)S(1)} %copy-done.3, bf16[4,2,3,64,384]{4,3,2,1,0:T(8,128)(2,1)} %pad_maximum_fusion.own, ...), custom_call_target="tpu_custom_call" | custom-call | flops 4076863488 | bytes 6000000 | tf_op jit(solution)/shard_map/first/conv_one/pallas_call | solution.py:186
  68.8 1.4 %collective-permute-start.8 = (f32[2,12,64]{2,1,0:T(8,128)S(1)}, f32[2,12,64]{2,1,0:T(8,128)S(1)}, u32[]{:S(2)}, u32[]{:S(2)}) collective-permute-start(f32[2,12,64]{2,1,0:T(8,128)S(1)} %get-tuple-element.33), channel_id=1, source_target_pairs={{0,4},{4,0},{8,12},{12,8},{1,5},{5,1},{9,13},{13,9},{2,6},{6,2},{1... | collective-permute-start | bytes 18440 | tf_op jit(solution)/shard_map/weight_two/ppermute | solution.py:32
  70.2 2.4 %collective-permute-done.8 = f32[2,12,64]{2,1,0:T(8,128)S(1)} collective-permute-done((f32[2,12,64]{2,1,0:T(8,128)S(1)}, f32[2,12,64]{2,1,0:T(8,128)S(1)}, u32[]{:S(2)}, u32[]{:S(2)}) %collective-permute-start.8) | collective-permute-done | bytes 6176 | tf_op jit(solution)/shard_map/weight_two/ppermute | solution.py:32
  72.6 2.7 %collective-permute-start.9 = (f32[2,12,64]{2,1,0:T(8,128)S(1)}, f32[2,12,64]{2,1,0:T(8,128)S(1)}, u32[]{:S(2)}, u32[]{:S(2)}) collective-permute-start(f32[2,12,64]{2,1,0:T(8,128)S(1)} %add.93), channel_id=1, source_target_pairs={{0,8},{4,12},{8,0},{12,4},{1,9},{5,13},{9,1},{13,5},{2,10},{6,14},... | collective-permute-start | bytes 18440 | tf_op jit(solution)/shard_map/weight_two/ppermute | solution.py:32
  75.3 0.0 collective-permute-done.12
  75.3 2.6 %collective-permute-done.9 = f32[2,12,64]{2,1,0:T(8,128)S(1)} collective-permute-done((f32[2,12,64]{2,1,0:T(8,128)S(1)}, f32[2,12,64]{2,1,0:T(8,128)S(1)}, u32[]{:S(2)}, u32[]{:S(2)}) %collective-permute-start.9) | collective-permute-done | bytes 6176 | tf_op jit(solution)/shard_map/weight_two/ppermute | solution.py:32
  77.9 0.2 pad_maximum_fusion.2.mine
  78.1 0.1 collective-permute-start.14
  78.2 0.4 copy-done.5
  78.6 0.1 reshape.30
  78.7 0.2 dynamic-slice_reduce_fusion
  78.9 0.3 multiply_convert_fusion.own
  79.2 2.2 %collective-permute-start.13 = (bf16[2,12,64,128]{3,2,1,0:T(8,128)(2,1)S(1)}, bf16[2,12,64,128]{3,2,1,0:T(8,128)(2,1)S(1)}, u32[]{:S(2)}, u32[]{:S(2)}) collective-permute-start(bf16[2,12,64,128]{3,2,1,0:T(8,128)(2,1)S(1)} %multiply_convert_fusion.own), channel_id=1, source_target_pairs={{0,16},{16,32},{32,48},{48,64},{64,80},{80,96},{96,112},{112,128},... | collective-permute-start | bytes 1179656 | tf_op jit(solution)/shard_map/second/ppermute | solution.py:23
  81.4 0.0 collective-permute-done.14.other
  81.4 3.9 %assemble_two.1.weight = bf16[3456,384]{1,0:T(8,128)(2,1)} custom-call(s32[3]{0:T(128)S(1)} %pad_add_fusion.place, bf16[4,8,48,384]{3,2,1,0:T(8,128)(2,1)S(1)} %pad_maximum_fusion.2.mine, bf16[4,8,48,384]{3,2,1,0:T(8,128)(2,1)} %collective-permute-done.14.other), custom_call_target="tpu_custom_call" | custom-call | flops 4000000 | bytes 12000000 | tf_op jit(solution)/shard_map/weight_two/assemble_two/pallas_call | solution.py:274
  85.4 2.9 %collective-permute-done.13.halo = bf16[2,12,64,128]{3,2,1,0:T(8,128)(2,1)S(1)} collective-permute-done((bf16[2,12,64,128]{3,2,1,0:T(8,128)(2,1)S(1)}, bf16[2,12,64,128]{3,2,1,0:T(8,128)(2,1)S(1)}, u32[]{:S(2)}, u32[]{:S(2)}) %collective-permute-start.13) | collective-permute-done | bytes 393248 | tf_op jit(solution)/shard_map/second/ppermute | solution.py:23
  88.3 7.3 %conv_two.1 = (bf16[2,3,64,384]{3,2,1,0:T(8,128)(2,1)S(1)}, bf16[2,3,64,384]{3,2,1,0:T(8,128)(2,1)S(1)}, bf16[2,3,64,384]{3,2,1,0:T(8,128)(2,1)S(1)}, bf16[1,3,6...) custom-call(f32[2,3]{1,0:T(2,128)S(1)} %compare_convert_fusion.valid, s32[3]{0:T(128)S(1)} %pad_add_fusion.place, ...), custom_call_target="tpu_custom_call" | custom-call | flops 4076863488 | bytes 6000000 | tf_op jit(solution)/shard_map/second/conv_two/pallas_call | solution.py:211
  95.6 2.3 %collective-permute-start.16 = (bf16[2,3,64,384]{3,2,1,0:T(8,128)(2,1)S(1)}, bf16[2,3,64,384]{3,2,1,0:T(8,128)(2,1)S(1)}, u32[]{:S(2)}, u32[]{:S(2)}) collective-permute-start(bf16[2,3,64,384]{3,2,1,0:T(8,128)(2,1)S(1)} %get-tuple-element.42), channel_id=1, source_target_pairs={{0,12},{4,0},{8,4},{12,8},{1,13},{5,1},{9,5},{13,9},{2,14},{6,2},{... | collective-permute-start | bytes 884744 | tf_op jit(solution)/shard_map/second/ppermute | solution.py:28
  98.0 0.0 collective-permute-start.15
  98.0 5.7 %collective-permute-done.16.down = bf16[2,3,64,384]{3,2,1,0:T(8,128)(2,1)S(1)} collective-permute-done((bf16[2,3,64,384]{3,2,1,0:T(8,128)(2,1)S(1)}, bf16[2,3,64,384]{3,2,1,0:T(8,128)(2,1)S(1)}, u32[]{:S(2)}, u32[]{:S(2)}) %collective-permute-start.16) | collective-permute-done | bytes 294944 | tf_op jit(solution)/shard_map/second/ppermute | solution.py:28
  103.7 3.6 %collective-permute-start.18 = (bf16[1,3,64,384]{3,2,1,0:T(8,128)(2,1)S(1)}, bf16[1,3,64,384]{3,2,1,0:T(8,128)(2,1)S(1)}, u32[]{:S(2)}, u32[]{:S(2)}) collective-permute-start(bf16[1,3,64,384]{3,2,1,0:T(8,128)(2,1)S(1)} %slice_add_fusion), channel_id=1, source_target_pairs={{0,12},{4,0},{8,4},{12,8},{1,13},{5,1},{9,5},{13,9},{2,14},{6,2},{... | collective-permute-start | bytes 442376 | tf_op jit(solution)/shard_map/second/ppermute | solution.py:28
  107.3 0.0 collective-permute-done.15.up
  107.3 0.1 collective-permute-start.17
  107.4 2.6 %collective-permute-done.18.down_last = bf16[1,3,64,384]{3,2,1,0:T(8,128)(2,1)S(1)} collective-permute-done((bf16[1,3,64,384]{3,2,1,0:T(8,128)(2,1)S(1)}, bf16[1,3,64,384]{3,2,1,0:T(8,128)(2,1)S(1)}, u32[]{:S(2)}, u32[]{:S(2)}) %collective-permute-start.18) | collective-permute-done | bytes 147488 | tf_op jit(solution)/shard_map/second/ppermute | solution.py:28
  110.0 3.8 %collective-permute-done.17.up_last = bf16[1,3,64,384]{3,2,1,0:T(8,128)(2,1)S(1)} collective-permute-done((bf16[1,3,64,384]{3,2,1,0:T(8,128)(2,1)S(1)}, bf16[1,3,64,384]{3,2,1,0:T(8,128)(2,1)S(1)}, u32[]{:S(2)}, u32[]{:S(2)}) %collective-permute-start.17) | collective-permute-done | bytes 147488 | tf_op jit(solution)/shard_map/second/ppermute | solution.py:28
  113.8 1.4 %finish.1 = bf16[2,6,128,384]{3,2,1,0:T(8,128)(2,1)} custom-call(bf16[2,3,64,384]{3,2,1,0:T(8,128)(2,1)S(1)} %bitcast.24, bf16[2,3,64,384]{3,2,1,0:T(8,128)(2,1)S(1)} %get-tuple-element.40.own_sum, bf16[2,3,64,384]{3,2,1,0:T(8,128)(2,1)S(1)} %collective-permute-done.15.up, bf16[2,3,64,384]{3,2,1,0:T(8,128)(2,1)S(1)} %collective-permute-done.16.down, ...), custom_call_target="tpu_custom_call" | custom-call | flops 2000000 | bytes 3000000 | tf_op jit(solution)/shard_map/finish/pallas_call | solution.py:228
  (25 shorter events, 0.1 us)
Async XLA Ops:
  0.0 1.2 %copy-start = (bf16[162,384]{1,0:T(8,128)(2,1)S(1)}, bf16[162,384]{1,0:T(8,128)(2,1)}, u32[]{:S(2)}) copy-start(bf16[162,384]{1,0:T(8,128)(2,1)} %param.11) | copy-start | bytes 373252
  1.2 9.8 %copy-start.1 = (bf16[1,2,3,64,384]{4,3,2,1,0:T(8,128)(2,1)S(1)}, bf16[1,2,3,64,384]{4,3,2,1,0:T(8,128)(2,1)}, u32[]{:S(2)}) copy-start(bf16[1,2,3,64,384]{4,3,2,1,0:T(8,128)(2,1)} %param.6) | copy-start | bytes 884740
  1.4 9.7 %copy-start.4 = (f32[384]{0:T(512)S(1)}, f32[384]{0:T(512)}, u32[]{:S(2)}) copy-start(f32[384]{0:T(512)} %param.8) | copy-start | bytes 4612
  2.4 27.0 %all-to-all-start = ((bf16[8,96,384]{2,1,0:T(8,128)(2,1)}), bf16[8,96,384]{2,1,0:T(8,128)(2,1)S(1)}, u32[]{:S(2)}, u32[]{:S(2)}) async-start(bf16[8,96,384]{2,1,0:T(8,128)(2,1)} %broadcast_in_dim.15), calls=%async_computation | async-start | bytes 1179648 | tf_op jit(solution)/shard_map/pieces/all_to_all | solution.py:320
  11.4 10.2 %collective-permute-start = (bf16[2,3,64,384]{3,2,1,0:T(8,128)(2,1)S(1)}, bf16[2,3,64,384]{3,2,1,0:T(8,128)(2,1)S(1)}, u32[]{:S(2)}, u32[]{:S(2)}) collective-permute-start(bf16[2,3,64,384]{3,2,1,0:T(8,128)(2,1)S(1)} %fusion.8), channel_id=1, source_target_pairs={{0,4},{4,8},{8,12},{12,0},{1,5},{5,9},{9,13},{13,1},{2,6},{6,10},{... | collective-permute-start | bytes 884744 | tf_op jit(solution)/shard_map/pixels/ppermute | solution.py:28
  13.0 15.2 %collective-permute-start.1 = (bf16[2,3,64,384]{3,2,1,0:T(8,128)(2,1)S(1)}, bf16[2,3,64,384]{3,2,1,0:T(8,128)(2,1)S(1)}, u32[]{:S(2)}, u32[]{:S(2)}) collective-permute-start(bf16[2,3,64,384]{3,2,1,0:T(8,128)(2,1)S(1)} %fusion.8), channel_id=1, source_target_pairs={{0,8},{4,12},{8,0},{12,4},{1,9},{5,13},{9,1},{13,5},{2,10},{6,14},... | collective-permute-start | bytes 884744 | tf_op jit(solution)/shard_map/pixels/ppermute | solution.py:28
  15.7 12.5 %collective-permute-start.2 = (bf16[2,3,64,384]{3,2,1,0:T(8,128)(2,1)S(1)}, bf16[2,3,64,384]{3,2,1,0:T(8,128)(2,1)S(1)}, u32[]{:S(2)}, u32[]{:S(2)}) collective-permute-start(bf16[2,3,64,384]{3,2,1,0:T(8,128)(2,1)S(1)} %fusion.8), channel_id=1, source_target_pairs={{0,12},{4,0},{8,4},{12,8},{1,13},{5,1},{9,5},{13,9},{2,14},{6,2},{... | collective-permute-start | bytes 884744 | tf_op jit(solution)/shard_map/pixels/ppermute | solution.py:28
  29.4 20.2 %collective-permute-start.6 = (bf16[4,2,3,64,384]{4,3,2,1,0:T(8,128)(2,1)}, bf16[4,2,3,64,384]{4,3,2,1,0:T(8,128)(2,1)S(1)}, u32[]{:S(2)}, u32[]{:S(2)}) collective-permute-start(bf16[4,2,3,64,384]{4,3,2,1,0:T(8,128)(2,1)} %pad_maximum_fusion.own), channel_id=1, source_target_pairs={{0,16},{16,32},{32,48},{48,64},{64,80},{80,96},{96,112},{112,128},... | collective-permute-start | bytes 3538952 | tf_op jit(solution)/shard_map/weight_one/ppermute | solution.py:23
  31.4 10.6 %collective-permute-start.3 = (bf16[8,48,384]{2,1,0:T(8,128)(2,1)S(1)}, bf16[8,48,384]{2,1,0:T(8,128)(2,1)S(1)}, u32[]{:S(2)}, u32[]{:S(2)}) collective-permute-start(bf16[8,48,384]{2,1,0:T(8,128)(2,1)S(1)} %get-tuple-element.28), channel_id=1, source_target_pairs={{0,1},{1,2},{2,3},{3,0},{4,5},{5,6},{6,7},{7,4},{8,9},{9,10},{10,1... | collective-permute-start | bytes 884744 | tf_op jit(solution)/shard_map/weight_one/ppermute | solution.py:28
  33.1 16.5 %collective-permute-start.4 = (bf16[8,48,384]{2,1,0:T(8,128)(2,1)S(1)}, bf16[8,48,384]{2,1,0:T(8,128)(2,1)S(1)}, u32[]{:S(2)}, u32[]{:S(2)}) collective-permute-start(bf16[8,48,384]{2,1,0:T(8,128)(2,1)S(1)} %get-tuple-element.28), channel_id=1, source_target_pairs={{0,2},{1,3},{2,0},{3,1},{4,6},{5,7},{6,4},{7,5},{8,10},{9,11},{10,... | collective-permute-start | bytes 884744 | tf_op jit(solution)/shard_map/weight_one/ppermute | solution.py:28
  36.0 13.6 %collective-permute-start.5 = (bf16[8,48,384]{2,1,0:T(8,128)(2,1)S(1)}, bf16[8,48,384]{2,1,0:T(8,128)(2,1)S(1)}, u32[]{:S(2)}, u32[]{:S(2)}) collective-permute-start(bf16[8,48,384]{2,1,0:T(8,128)(2,1)S(1)} %get-tuple-element.28), channel_id=1, source_target_pairs={{0,3},{1,0},{2,1},{3,2},{4,7},{5,4},{6,5},{7,6},{8,11},{9,8},{10,9... | collective-permute-start | bytes 884744 | tf_op jit(solution)/shard_map/weight_one/ppermute | solution.py:28
  49.6 1.0 copy-start.2
  50.6 1.5 %copy-start.6 = (s32[1,4]{1,0:T(1,128)S(1)}, s32[1,4]{1,0:T(1,128)}, u32[]{:S(2)}) copy-start(s32[1,4]{1,0:T(1,128)} %param.7) | copy-start | bytes 52
  51.8 6.4 %collective-permute-start.7 = (bf16[4,8,48,384]{3,2,1,0:T(8,128)(2,1)}, bf16[4,8,48,384]{3,2,1,0:T(8,128)(2,1)}, u32[]{:S(2)}, u32[]{:S(2)}) collective-permute-start(bf16[4,8,48,384]{3,2,1,0:T(8,128)(2,1)} %pad_maximum_fusion.1.mine), channel_id=1, source_target_pairs={{0,16},{16,0},{1,17},{17,1},{2,18},{18,2},{3,19},{19,3},{4,20},{20... | collective-permute-start | bytes 3538952 | tf_op jit(solution)/shard_map/weight_one/ppermute | solution.py:335
  52.7 22.6 %collective-permute-start.10 = (bf16[8,48,384]{2,1,0:T(8,128)(2,1)S(1)}, bf16[8,48,384]{2,1,0:T(8,128)(2,1)S(1)}, u32[]{:S(2)}, u32[]{:S(2)}) collective-permute-start(bf16[8,48,384]{2,1,0:T(8,128)(2,1)S(1)} %get-tuple-element.36), channel_id=1, source_target_pairs={{0,1},{1,2},{2,3},{3,0},{4,5},{5,6},{6,7},{7,4},{8,9},{9,10},{10,1... | collective-permute-start | bytes 884744 | tf_op jit(solution)/shard_map/weight_two/ppermute | solution.py:28
  54.5 20.8 %collective-permute-start.11 = (bf16[8,48,384]{2,1,0:T(8,128)(2,1)S(1)}, bf16[8,48,384]{2,1,0:T(8,128)(2,1)S(1)}, u32[]{:S(2)}, u32[]{:S(2)}) collective-permute-start(bf16[8,48,384]{2,1,0:T(8,128)(2,1)S(1)} %get-tuple-element.36), channel_id=1, source_target_pairs={{0,2},{1,3},{2,0},{3,1},{4,6},{5,7},{6,4},{7,5},{8,10},{9,11},{10,... | collective-permute-start | bytes 884744 | tf_op jit(solution)/shard_map/weight_two/ppermute | solution.py:28
  56.8 18.5 %collective-permute-start.12 = (bf16[8,48,384]{2,1,0:T(8,128)(2,1)S(1)}, bf16[8,48,384]{2,1,0:T(8,128)(2,1)S(1)}, u32[]{:S(2)}, u32[]{:S(2)}) collective-permute-start(bf16[8,48,384]{2,1,0:T(8,128)(2,1)S(1)} %get-tuple-element.36), channel_id=1, source_target_pairs={{0,3},{1,0},{2,1},{3,2},{4,7},{5,4},{6,5},{7,6},{8,11},{9,8},{10,9... | collective-permute-start | bytes 884744 | tf_op jit(solution)/shard_map/weight_two/ppermute | solution.py:28
  58.2 1.3 %copy-start.3 = (bf16[4,2,3,64,384]{4,3,2,1,0:T(8,128)(2,1)S(1)}, bf16[4,2,3,64,384]{4,3,2,1,0:T(8,128)(2,1)}, u32[]{:S(2)}) copy-start(bf16[4,2,3,64,384]{4,3,2,1,0:T(8,128)(2,1)} %copy-done.2) | copy-start | bytes 3538948
  68.8 3.8 %collective-permute-start.8 = (f32[2,12,64]{2,1,0:T(8,128)S(1)}, f32[2,12,64]{2,1,0:T(8,128)S(1)}, u32[]{:S(2)}, u32[]{:S(2)}) collective-permute-start(f32[2,12,64]{2,1,0:T(8,128)S(1)} %get-tuple-element.33), channel_id=1, source_target_pairs={{0,4},{4,0},{8,12},{12,8},{1,5},{5,1},{9,13},{13,9},{2,6},{6,2},{1... | collective-permute-start | bytes 18440 | tf_op jit(solution)/shard_map/weight_two/ppermute | solution.py:32
  72.6 5.2 %collective-permute-start.9 = (f32[2,12,64]{2,1,0:T(8,128)S(1)}, f32[2,12,64]{2,1,0:T(8,128)S(1)}, u32[]{:S(2)}, u32[]{:S(2)}) collective-permute-start(f32[2,12,64]{2,1,0:T(8,128)S(1)} %add.93), channel_id=1, source_target_pairs={{0,8},{4,12},{8,0},{12,4},{1,9},{5,13},{9,1},{13,5},{2,10},{6,14},... | collective-permute-start | bytes 18440 | tf_op jit(solution)/shard_map/weight_two/ppermute | solution.py:32
  77.9 0.7 copy-start.5
  78.1 3.4 %collective-permute-start.14 = (bf16[4,8,48,384]{3,2,1,0:T(8,128)(2,1)S(1)}, bf16[4,8,48,384]{3,2,1,0:T(8,128)(2,1)}, u32[]{:S(2)}, u32[]{:S(2)}) collective-permute-start(bf16[4,8,48,384]{3,2,1,0:T(8,128)(2,1)S(1)} %pad_maximum_fusion.2.mine), channel_id=1, source_target_pairs={{0,16},{16,0},{1,17},{17,1},{2,18},{18,2},{3,19},{19,3},{4,20},{20... | collective-permute-start | bytes 3538952 | tf_op jit(solution)/shard_map/weight_two/ppermute | solution.py:350
  79.2 9.1 %collective-permute-start.13 = (bf16[2,12,64,128]{3,2,1,0:T(8,128)(2,1)S(1)}, bf16[2,12,64,128]{3,2,1,0:T(8,128)(2,1)S(1)}, u32[]{:S(2)}, u32[]{:S(2)}) collective-permute-start(bf16[2,12,64,128]{3,2,1,0:T(8,128)(2,1)S(1)} %multiply_convert_fusion.own), channel_id=1, source_target_pairs={{0,16},{16,32},{32,48},{48,64},{64,80},{80,96},{96,112},{112,128},... | collective-permute-start | bytes 1179656 | tf_op jit(solution)/shard_map/second/ppermute | solution.py:23
  95.6 8.1 %collective-permute-start.16 = (bf16[2,3,64,384]{3,2,1,0:T(8,128)(2,1)S(1)}, bf16[2,3,64,384]{3,2,1,0:T(8,128)(2,1)S(1)}, u32[]{:S(2)}, u32[]{:S(2)}) collective-permute-start(bf16[2,3,64,384]{3,2,1,0:T(8,128)(2,1)S(1)} %get-tuple-element.42), channel_id=1, source_target_pairs={{0,12},{4,0},{8,4},{12,8},{1,13},{5,1},{9,5},{13,9},{2,14},{6,2},{... | collective-permute-start | bytes 884744 | tf_op jit(solution)/shard_map/second/ppermute | solution.py:28
  98.0 9.3 %collective-permute-start.15 = (bf16[2,3,64,384]{3,2,1,0:T(8,128)(2,1)S(1)}, bf16[2,3,64,384]{3,2,1,0:T(8,128)(2,1)S(1)}, u32[]{:S(2)}, u32[]{:S(2)}) collective-permute-start(bf16[2,3,64,384]{3,2,1,0:T(8,128)(2,1)S(1)} %get-tuple-element.41), channel_id=1, source_target_pairs={{0,4},{4,8},{8,12},{12,0},{1,5},{5,9},{9,13},{13,1},{2,6},{6,10},{... | collective-permute-start | bytes 884744 | tf_op jit(solution)/shard_map/second/ppermute | solution.py:28
  103.7 6.2 %collective-permute-start.18 = (bf16[1,3,64,384]{3,2,1,0:T(8,128)(2,1)S(1)}, bf16[1,3,64,384]{3,2,1,0:T(8,128)(2,1)S(1)}, u32[]{:S(2)}, u32[]{:S(2)}) collective-permute-start(bf16[1,3,64,384]{3,2,1,0:T(8,128)(2,1)S(1)} %slice_add_fusion), channel_id=1, source_target_pairs={{0,12},{4,0},{8,4},{12,8},{1,13},{5,1},{9,5},{13,9},{2,14},{6,2},{... | collective-permute-start | bytes 442376 | tf_op jit(solution)/shard_map/second/ppermute | solution.py:28
  107.3 6.4 %collective-permute-start.17 = (bf16[1,3,64,384]{3,2,1,0:T(8,128)(2,1)S(1)}, bf16[1,3,64,384]{3,2,1,0:T(8,128)(2,1)S(1)}, u32[]{:S(2)}, u32[]{:S(2)}) collective-permute-start(bf16[1,3,64,384]{3,2,1,0:T(8,128)(2,1)S(1)} %slice_add_fusion.1), channel_id=1, source_target_pairs={{0,4},{4,8},{8,12},{12,0},{1,5},{5,9},{9,13},{13,1},{2,6},{6,10},{... | collective-permute-start | bytes 442376 | tf_op jit(solution)/shard_map/second/ppermute | solution.py:28

commit v13 on v10

--- a/solution.py
+++ b/solution.py
@@ -175,6 +175,22 @@
         ref[at] = done.reshape(each, width, done.shape[1])
 
 
+def finish_kernel(latents, own_sum, up, down, up_last, down_last, out, wide):
+    frames, each, width, _ = own_sum.shape
+    for s in range(frames):
+        for r in range(each):
+            terms = [own_sum[s, r], down[0, r], up_last[0, r]] if s == 0 else [own_sum[s, r], up[1, r], down_last[0, r]]
+            total = sum((t.astype(jnp.float32) for t in terms[1:]), terms[0].astype(jnp.float32))
+            block = (latents[s, r].astype(jnp.float32) + total).astype(out.dtype).astype(jnp.float32)
+            for k in range(wide.shape[0]):
+                lanes = slice(k * LANE, (k + 1) * LANE)
+                wide[k, pl.ds(0, width, stride=2), :] = block[:, lanes]
+                wide[k, pl.ds(1, width, stride=2), :] = block[:, lanes]
+                doubled = wide[k].astype(out.dtype)
+                out[s, 2 * r, :, lanes] = doubled
+                out[s, 2 * r + 1, :, lanes] = doubled
+
+
 VMEM = pl.BlockSpec(memory_space=pltpu.VMEM)
 SMEM = pl.BlockSpec(memory_space=pltpu.SMEM)
 PARAMS = pltpu.CompilerParams(vmem_limit_bytes=52 * 1024 * 1024)
@@ -236,6 +252,20 @@
         cost_estimate=pl.CostEstimate(flops=3_000_000_000, bytes_accessed=6_000_000, transcendentals=0),
         name="conv_two_halo",
     )(valid, place, halo, weight, started)
+
+
+def finish_call(*arrays):
+    frames, each, width, channels = arrays[0].shape
+    return pl.pallas_call(
+        finish_kernel,
+        out_shape=jax.ShapeDtypeStruct((frames, 2 * each, 2 * width, channels), jnp.bfloat16),
+        in_specs=[VMEM] * len(arrays),
+        out_specs=VMEM,
+        scratch_shapes=[pltpu.VMEM((channels // LANE, 2 * width, LANE), jnp.float32)],
+        compiler_params=PARAMS,
+        cost_estimate=pl.CostEstimate(flops=2_000_000, bytes_accessed=3_000_000, transcendentals=0),
+        name="finish",
+    )(*arrays)
 
 
 def gathered(place, mine, other, i):
@@ -370,14 +400,8 @@
         up, down = onward(up, 1), onward(down, -1)
         up_last = onward(up_last + up[:1], 1)
         down_last = onward(down_last + down[1:], -1)
-        arrived = [jnp.concatenate([down[:1], up[1:]]), jnp.concatenate([up_last, down_last])]
-        second = sum((r.astype(jnp.float32) for r in arrived), own_sum.astype(jnp.float32))
-
-    block = (source + second).astype(jnp.bfloat16)
-    result = jnp.broadcast_to(
-        block[:, :, None, :, None, :], (frames, each, 2, width, 2, channels)
-    ).reshape(frames, 2 * each, 2 * width, channels)
-    return result[None]
+
+    return finish_call(latents[0], own_sum, up, down, up_last, down_last)[None]
 
 
 def solution(mesh):

time: 114 us -> 116 us (1.018)
  Pallas kernels: 24.6 us -> 26 us
    unnamed x18 -> x14, local copies, waits for them, and re-layouts: 0.05 us -> 2.34 us
    pallas_call x0 -> x1, Pallas kernels: none -> 1.38 us  [finish_call(): pl.pallas_call(finish_kernel, out_shape=jax.ShapeDtypeStruct((frames, 2 *...]
    another operation x1 -> x0, local copies, waits for them, and re-layouts: 1.29 us -> none  [body(): return result[None]]
where the time goes in v13:
time: 116 us; the launch traced here: 115 us
  waiting for transfers between devices  40.1 us (35%)
  starting transfers between devices  39.7 us (34%)
  Pallas kernels  26 us (22%)
  other arithmetic  4.19 us (4%)
  local copies, waits for them, and re-layouts  3.58 us (3%)
  matrix products  1.35 us (1%)
    ppermute x13, waiting for transfers between devices, onward(): return lax.ppermute(x, axis, [(i, (i + by) % n) for i in range(n)])  36.7 us
    ppermute x13, starting transfers between devices, onward(): return lax.ppermute(x, axis, [(i, (i + by) % n) for i in range(n)])  22.3 us
    pallas_call x1, Pallas kernels, conv_one_call(): pl.pallas_call(functools.partial(conv_one_kernel, channels // parts), out...  9.29 us
    all_to_all x1, starting transfers between devices, body(): lax.all_to_all(jnp.broadcast_to(pieces, (lax.axis_size('z'),) + pieces.sh...  8.57 us
    pallas_call x1, Pallas kernels, conv_two_own_call(): pl.pallas_call(conv_two_own_kernel, out_shape=jax.ShapeDtypeStruct((frame...  5.87 us
    pallas_call x1, Pallas kernels, conv_two_halo_call(): pl.pallas_call(conv_two_halo_kernel, out_shape=[jax.ShapeDtypeStruct(shap...  5.51 us
    ppermute x2, starting transfers between devices, earlier(): return lax.ppermute(x, SLOT, [(i, i + 1) for i in range(n - 1)])  4.19 us
    ppermute x2, starting transfers between devices, across(): lax.ppermute(x, 'tile', [(i, i ^ bit) for i in range(lax.axis_size('tile'...  4.17 us
  transfers between devices with their start and end apart: 20, of which 9 were waited for; matrix products, arithmetic and copies ran while one was open for 2% of the time, Pallas kernels for 17%

profile of v13, /device:TPU:32, one launch (start us, length us, event | category | flops | bytes accessed | tf_op | source)
XLA Modules:
  0.0 115.2 jit_solution(6905609535877899935)
XLA Ops:
  0.0 1.2 %fusion = bf16[162,96]{1,0:T(8,128)(2,1)S(1)} fusion(bf16[162,384]{1,0:T(8,128)(2,1)} %param.10, s32[96]{0:T(128)S(1)} %multiply_add_fusion.1), kind=kOutput, calls=%fused_computation.5 | convolution fusion | flops 11996352 | bytes 155904 | tf_op jit(solution)/shard_map/pieces/dot_general | solution.py:344
  1.2 0.0 copy-start.1
  1.2 0.2 convolution_convert_fusion.1
  1.4 0.0 copy-start.4
  1.4 0.1 fusion.16
  1.6 0.9 broadcast_in_dim.15
  2.4 8.6 %all-to-all-start = ((bf16[8,96,384]{2,1,0:T(8,128)(2,1)}), bf16[8,96,384]{2,1,0:T(8,128)(2,1)S(1)}, u32[]{:S(2)}, u32[]{:S(2)}) async-start(bf16[8,96,384]{2,1,0:T(8,128)(2,1)} %broadcast_in_dim.15), calls=%async_computation | async-start | bytes 1179648 | tf_op jit(solution)/shard_map/pieces/all_to_all | solution.py:351
  11.0 0.1 fusion.1
  11.2 0.3 fusion.8
  11.4 1.6 %collective-permute-start = (bf16[2,3,64,384]{3,2,1,0:T(8,128)(2,1)S(1)}, bf16[2,3,64,384]{3,2,1,0:T(8,128)(2,1)S(1)}, u32[]{:S(2)}, u32[]{:S(2)}) collective-permute-start(bf16[2,3,64,384]{3,2,1,0:T(8,128)(2,1)S(1)} %fusion.8), channel_id=1, source_target_pairs={{0,4},{4,8},{8,12},{12,0},{1,5},{5,9},{9,13},{13,1},{2,6},{6,10},{... | collective-permute-start | bytes 884744 | tf_op jit(solution)/shard_map/pixels/ppermute | solution.py:28
  13.0 2.7 %collective-permute-start.1 = (bf16[2,3,64,384]{3,2,1,0:T(8,128)(2,1)S(1)}, bf16[2,3,64,384]{3,2,1,0:T(8,128)(2,1)S(1)}, u32[]{:S(2)}, u32[]{:S(2)}) collective-permute-start(bf16[2,3,64,384]{3,2,1,0:T(8,128)(2,1)S(1)} %fusion.8), channel_id=1, source_target_pairs={{0,8},{4,12},{8,0},{12,4},{1,9},{5,13},{9,1},{13,5},{2,10},{6,14},... | collective-permute-start | bytes 884744 | tf_op jit(solution)/shard_map/pixels/ppermute | solution.py:28
  15.7 1.4 %collective-permute-start.2 = (bf16[2,3,64,384]{3,2,1,0:T(8,128)(2,1)S(1)}, bf16[2,3,64,384]{3,2,1,0:T(8,128)(2,1)S(1)}, u32[]{:S(2)}, u32[]{:S(2)}) collective-permute-start(bf16[2,3,64,384]{3,2,1,0:T(8,128)(2,1)S(1)} %fusion.8), channel_id=1, source_target_pairs={{0,12},{4,0},{8,4},{12,8},{1,13},{5,1},{9,5},{13,9},{2,14},{6,2},{... | collective-permute-start | bytes 884744 | tf_op jit(solution)/shard_map/pixels/ppermute | solution.py:28
  17.2 0.3 multiply_convert_fusion.1
  17.4 4.3 %collective-permute-done = bf16[2,3,64,384]{3,2,1,0:T(8,128)(2,1)S(1)} collective-permute-done((bf16[2,3,64,384]{3,2,1,0:T(8,128)(2,1)S(1)}, bf16[2,3,64,384]{3,2,1,0:T(8,128)(2,1)S(1)}, u32[]{:S(2)}, u32[]{:S(2)}) %collective-permute-start) | collective-permute-done | bytes 294944 | tf_op jit(solution)/shard_map/pixels/ppermute | solution.py:28
  21.7 6.5 %collective-permute-done.1 = bf16[2,3,64,384]{3,2,1,0:T(8,128)(2,1)S(1)} collective-permute-done((bf16[2,3,64,384]{3,2,1,0:T(8,128)(2,1)S(1)}, bf16[2,3,64,384]{3,2,1,0:T(8,128)(2,1)S(1)}, u32[]{:S(2)}, u32[]{:S(2)}) %collective-permute-start.1) | collective-permute-done | bytes 294944 | tf_op jit(solution)/shard_map/pixels/ppermute | solution.py:28
  28.2 1.2 %pad_maximum_fusion.own = bf16[4,2,3,64,384]{4,3,2,1,0:T(8,128)(2,1)} fusion(bf16[1,2,3,64,384]{4,3,2,1,0:T(8,128)(2,1)S(1)} %bitcast.35, bf16[1,2,3,64,384]{4,3,2,1,0:T(8,128)(2,1)S(1)} %bitcast.33, bf16[1,2,3,64,384]{4,3,2,1,0:T(8,128)(2,1)S(1)} %bitcast.31, bf16[1,2,3,64,384]{4,3,2,1,0:T(8,128)(2,1)S(1)} %multiply_convert_fusion.1), kind=kLoop, calls=%fused_computation | loop fusion | flops 1769472 | bytes 2359296 | tf_op jit(solution)/shard_map/pixels/stack | solution.py:36
  29.4 0.0 all-to-all-done
  29.4 1.9 %collective-permute-start.6 = (bf16[4,2,3,64,384]{4,3,2,1,0:T(8,128)(2,1)}, bf16[4,2,3,64,384]{4,3,2,1,0:T(8,128)(2,1)S(1)}, u32[]{:S(2)}, u32[]{:S(2)}) collective-permute-start(bf16[4,2,3,64,384]{4,3,2,1,0:T(8,128)(2,1)} %pad_maximum_fusion.own), channel_id=1, source_target_pairs={{0,16},{16,32},{32,48},{48,64},{64,80},{80,96},{96,112},{112,128},... | collective-permute-start | bytes 3538952 | tf_op jit(solution)/shard_map/weight_one/ppermute | solution.py:23
  31.3 0.1 fusion.19
  31.4 1.7 %collective-permute-start.3 = (bf16[8,48,384]{2,1,0:T(8,128)(2,1)S(1)}, bf16[8,48,384]{2,1,0:T(8,128)(2,1)S(1)}, u32[]{:S(2)}, u32[]{:S(2)}) collective-permute-start(bf16[8,48,384]{2,1,0:T(8,128)(2,1)S(1)} %get-tuple-element.30), channel_id=1, source_target_pairs={{0,1},{1,2},{2,3},{3,0},{4,5},{5,6},{6,7},{7,4},{8,9},{9,10},{10,1... | collective-permute-start | bytes 884744 | tf_op jit(solution)/shard_map/weight_one/ppermute | solution.py:28
  33.1 2.9 %collective-permute-start.4 = (bf16[8,48,384]{2,1,0:T(8,128)(2,1)S(1)}, bf16[8,48,384]{2,1,0:T(8,128)(2,1)S(1)}, u32[]{:S(2)}, u32[]{:S(2)}) collective-permute-start(bf16[8,48,384]{2,1,0:T(8,128)(2,1)S(1)} %get-tuple-element.30), channel_id=1, source_target_pairs={{0,2},{1,3},{2,0},{3,1},{4,6},{5,7},{6,4},{7,5},{8,10},{9,11},{10,... | collective-permute-start | bytes 884744 | tf_op jit(solution)/shard_map/weight_one/ppermute | solution.py:28
  36.0 1.3 %collective-permute-start.5 = (bf16[8,48,384]{2,1,0:T(8,128)(2,1)S(1)}, bf16[8,48,384]{2,1,0:T(8,128)(2,1)S(1)}, u32[]{:S(2)}, u32[]{:S(2)}) collective-permute-start(bf16[8,48,384]{2,1,0:T(8,128)(2,1)S(1)} %get-tuple-element.30), channel_id=1, source_target_pairs={{0,3},{1,0},{2,1},{3,2},{4,7},{5,4},{6,5},{7,6},{8,11},{9,8},{10,9... | collective-permute-start | bytes 884744 | tf_op jit(solution)/shard_map/weight_one/ppermute | solution.py:28
  37.3 4.7 %collective-permute-done.3 = bf16[8,48,384]{2,1,0:T(8,128)(2,1)S(1)} collective-permute-done((bf16[8,48,384]{2,1,0:T(8,128)(2,1)S(1)}, bf16[8,48,384]{2,1,0:T(8,128)(2,1)S(1)}, u32[]{:S(2)}, u32[]{:S(2)}) %collective-permute-start.3) | collective-permute-done | bytes 294944 | tf_op jit(solution)/shard_map/weight_one/ppermute | solution.py:28
  42.0 7.6 %collective-permute-done.4 = bf16[8,48,384]{2,1,0:T(8,128)(2,1)S(1)} collective-permute-done((bf16[8,48,384]{2,1,0:T(8,128)(2,1)S(1)}, bf16[8,48,384]{2,1,0:T(8,128)(2,1)S(1)}, u32[]{:S(2)}, u32[]{:S(2)}) %collective-permute-start.4) | collective-permute-done | bytes 294944 | tf_op jit(solution)/shard_map/weight_one/ppermute | solution.py:28
  49.6 0.0 collective-permute-done.5
  49.6 0.0 collective-permute-done.6.halo
  49.6 1.0 copy-done.2
  50.7 1.2 %pad_maximum_fusion.1.mine = bf16[4,8,48,384]{3,2,1,0:T(8,128)(2,1)} fusion(bf16[1,8,48,384]{3,2,1,0:T(8,128)(2,1)S(1)} %bitcast.34, bf16[1,8,48,384]{3,2,1,0:T(8,128)(2,1)S(1)} %bitcast.32, bf16[1,8,48,384]{3,2,1,0:T(8,128)(2,1)S(1)} %bitcast.30, bf16[1,8,48,384]{3,2,1,0:T(8,128)(2,1)S(1)} %bitcast.26), kind=kLoop, calls=%fused_computation.1 | loop fusion | flops 1769472 | bytes 2359296 | tf_op jit(solution)/shard_map/weight_one/stack | solution.py:365
  51.8 0.4 collective-permute-start.7
  52.2 0.2 reduce-window_clone.1
  52.4 0.1 pad_add_fusion.place
  52.5 0.2 fusion.18
  52.6 0.1 compare_convert_fusion.valid
  52.7 2.9 %collective-permute-start.10 = (bf16[8,48,384]{2,1,0:T(8,128)(2,1)S(1)}, bf16[8,48,384]{2,1,0:T(8,128)(2,1)S(1)}, u32[]{:S(2)}, u32[]{:S(2)}) collective-permute-start(bf16[8,48,384]{2,1,0:T(8,128)(2,1)S(1)} %get-tuple-element.38), channel_id=1, source_target_pairs={{0,2},{1,3},{2,0},{3,1},{4,6},{5,7},{6,4},{7,5},{8,10},{9,11},{10,... | collective-permute-start | bytes 884744 | tf_op jit(solution)/shard_map/weight_two/ppermute | solution.py:28
  55.6 1.6 %collective-permute-start.11 = (bf16[8,48,384]{2,1,0:T(8,128)(2,1)S(1)}, bf16[8,48,384]{2,1,0:T(8,128)(2,1)S(1)}, u32[]{:S(2)}, u32[]{:S(2)}) collective-permute-start(bf16[8,48,384]{2,1,0:T(8,128)(2,1)S(1)} %get-tuple-element.38), channel_id=1, source_target_pairs={{0,3},{1,0},{2,1},{3,2},{4,7},{5,4},{6,5},{7,6},{8,11},{9,8},{10,9... | collective-permute-start | bytes 884744 | tf_op jit(solution)/shard_map/weight_two/ppermute | solution.py:28
  57.2 0.5 collective-permute-start.9
  57.6 0.0 collective-permute-done.7.other
  57.6 1.3 %copy-done.3 = bf16[4,2,3,64,384]{4,3,2,1,0:T(8,128)(2,1)S(1)} copy-done((bf16[4,2,3,64,384]{4,3,2,1,0:T(8,128)(2,1)S(1)}, bf16[4,2,3,64,384]{4,3,2,1,0:T(8,128)(2,1)}, u32[]{:S(2)}) %copy-start.3) | copy-done | bytes 1179672
  58.9 9.3 %conv_one.1 = (f32[2,12,64,128]{3,2,1,0:T(8,128)S(1)}, f32[2,12,64]{2,1,0:T(8,128)S(1)}) custom-call(f32[2,3]{1,0:T(2,128)S(1)} %compare_convert_fusion.valid, s32[3]{0:T(128)S(1)} %pad_add_fusion.place, bf16[4,2,3,64,384]{4,3,2,1,0:T(8,128)(2,1)S(1)} %copy-done.3, bf16[4,2,3,64,384]{4,3,2,1,0:T(8,128)(2,1)} %pad_maximum_fusion.own, ...), custom_call_target="tpu_custom_call" | custom-call | flops 4076863488 | bytes 6000000 | tf_op jit(solution)/shard_map/first/conv_one/pallas_call | solution.py:203
  68.2 1.4 %collective-permute-start.8 = (f32[2,12,64]{2,1,0:T(8,128)S(1)}, f32[2,12,64]{2,1,0:T(8,128)S(1)}, u32[]{:S(2)}, u32[]{:S(2)}) collective-permute-start(f32[2,12,64]{2,1,0:T(8,128)S(1)} %get-tuple-element.35), channel_id=1, source_target_pairs={{0,4},{4,0},{8,12},{12,8},{1,5},{5,1},{9,13},{13,9},{2,6},{6,2},{1... | collective-permute-start | bytes 18440 | tf_op jit(solution)/shard_map/weight_two/ppermute | solution.py:32
  69.6 2.4 %collective-permute-done.8 = f32[2,12,64]{2,1,0:T(8,128)S(1)} collective-permute-done((f32[2,12,64]{2,1,0:T(8,128)S(1)}, f32[2,12,64]{2,1,0:T(8,128)S(1)}, u32[]{:S(2)}, u32[]{:S(2)}) %collective-permute-start.8) | collective-permute-done | bytes 6176 | tf_op jit(solution)/shard_map/weight_two/ppermute | solution.py:32
  72.0 0.0 collective-permute-done.10
  72.1 0.0 collective-permute-done.9
  72.1 0.0 copy-start.5
  72.1 0.2 pad_maximum_fusion.2.mine
  72.3 0.1 collective-permute-start.13
  72.4 2.7 %collective-permute-start.12 = (f32[2,12,64]{2,1,0:T(8,128)S(1)}, f32[2,12,64]{2,1,0:T(8,128)S(1)}, u32[]{:S(2)}, u32[]{:S(2)}) collective-permute-start(f32[2,12,64]{2,1,0:T(8,128)S(1)} %add.93), channel_id=1, source_target_pairs={{0,8},{4,12},{8,0},{12,4},{1,9},{5,13},{9,1},{13,5},{2,10},{6,14},... | collective-permute-start | bytes 18440 | tf_op jit(solution)/shard_map/second/ppermute | solution.py:32
  75.1 0.1 reshape.30
  75.2 0.2 dynamic-slice_reduce_fusion
  75.4 0.0 collective-permute-done.13.other
  75.4 3.9 %assemble_two.1.weight = bf16[3456,384]{1,0:T(8,128)(2,1)} custom-call(s32[3]{0:T(128)S(1)} %pad_add_fusion.place, bf16[4,8,48,384]{3,2,1,0:T(8,128)(2,1)S(1)} %pad_maximum_fusion.2.mine, bf16[4,8,48,384]{3,2,1,0:T(8,128)(2,1)} %collective-permute-done.13.other), custom_call_target="tpu_custom_call" | custom-call | flops 4000000 | bytes 12000000 | tf_op jit(solution)/shard_map/weight_two/assemble_two/pallas_call | solution.py:305
  79.4 0.0 collective-permute-done.12
  79.4 0.3 multiply_convert_fusion.own
  79.7 2.3 %collective-permute-start.14 = (bf16[2,12,64,128]{3,2,1,0:T(8,128)(2,1)S(1)}, bf16[2,12,64,128]{3,2,1,0:T(8,128)(2,1)S(1)}, u32[]{:S(2)}, u32[]{:S(2)}) collective-permute-start(bf16[2,12,64,128]{3,2,1,0:T(8,128)(2,1)S(1)} %multiply_convert_fusion.own), channel_id=1, source_target_pairs={{0,16},{16,32},{32,48},{48,64},{64,80},{80,96},{96,112},{112,128},... | collective-permute-start | bytes 1179656 | tf_op jit(solution)/shard_map/second/ppermute | solution.py:23
  82.0 5.9 %conv_two_own.1.started = f32[2,768,384]{2,1,0:T(8,128)} custom-call(f32[2,3]{1,0:T(2,128)S(1)} %compare_convert_fusion.valid, bf16[2,12,64,128]{3,2,1,0:T(8,128)(2,1)S(1)} %multiply_convert_fusion.own, bf16[3456,384]{1,0:T(8,128)(2,1)} %assemble_two.1.weight), custom_call_target="tpu_custom_call" | custom-call | flops 3000000000 | bytes 5000000 | tf_op jit(solution)/shard_map/second/conv_two_own/pallas_call | solution.py:226
  87.8 0.9 collective-permute-done.14.halo
  88.8 5.5 %conv_two_halo.1 = (bf16[2,3,64,384]{3,2,1,0:T(8,128)(2,1)S(1)}, bf16[2,3,64,384]{3,2,1,0:T(8,128)(2,1)S(1)}, bf16[2,3,64,384]{3,2,1,0:T(8,128)(2,1)S(1)}, bf16[...) custom-call(f32[2,3]{1,0:T(2,128)S(1)} %compare_convert_fusion.valid, s32[3]{0:T(128)S(1)} %pad_add_fusion.place, ...), custom_call_target="tpu_custom_call" | custom-call | flops 3000000000 | bytes 6000000 | tf_op jit(solution)/shard_map/second/conv_two_halo/pallas_call | solution.py:242
  94.3 2.2 %collective-permute-start.16 = (bf16[2,3,64,384]{3,2,1,0:T(8,128)(2,1)S(1)}, bf16[2,3,64,384]{3,2,1,0:T(8,128)(2,1)S(1)}, u32[]{:S(2)}, u32[]{:S(2)}) collective-permute-start(bf16[2,3,64,384]{3,2,1,0:T(8,128)(2,1)S(1)} %get-tuple-element.46), channel_id=1, source_target_pairs={{0,12},{4,0},{8,4},{12,8},{1,13},{5,1},{9,5},{13,9},{2,14},{6,2},{... | collective-permute-start | bytes 884744 | tf_op jit(solution)/shard_map/second/ppermute | solution.py:28
  96.6 7.2 %collective-permute-done.16.down = bf16[2,3,64,384]{3,2,1,0:T(8,128)(2,1)S(1)} collective-permute-done((bf16[2,3,64,384]{3,2,1,0:T(8,128)(2,1)S(1)}, bf16[2,3,64,384]{3,2,1,0:T(8,128)(2,1)S(1)}, u32[]{:S(2)}, u32[]{:S(2)}) %collective-permute-start.16) | collective-permute-done | bytes 294944 | tf_op jit(solution)/shard_map/second/ppermute | solution.py:28
  103.8 3.5 %collective-permute-start.18 = (bf16[1,3,64,384]{3,2,1,0:T(8,128)(2,1)S(1)}, bf16[1,3,64,384]{3,2,1,0:T(8,128)(2,1)S(1)}, u32[]{:S(2)}, u32[]{:S(2)}) collective-permute-start(bf16[1,3,64,384]{3,2,1,0:T(8,128)(2,1)S(1)} %slice_add_fusion), channel_id=1, source_target_pairs={{0,12},{4,0},{8,4},{12,8},{1,13},{5,1},{9,5},{13,9},{2,14},{6,2},{... | collective-permute-start | bytes 442376 | tf_op jit(solution)/shard_map/second/ppermute | solution.py:28
  107.3 0.1 collective-permute-start.17
  107.4 2.9 %collective-permute-done.18.down_last = bf16[1,3,64,384]{3,2,1,0:T(8,128)(2,1)S(1)} collective-permute-done((bf16[1,3,64,384]{3,2,1,0:T(8,128)(2,1)S(1)}, bf16[1,3,64,384]{3,2,1,0:T(8,128)(2,1)S(1)}, u32[]{:S(2)}, u32[]{:S(2)}) %collective-permute-start.18) | collective-permute-done | bytes 147488 | tf_op jit(solution)/shard_map/second/ppermute | solution.py:28
  110.3 3.5 %collective-permute-done.17.up_last = bf16[1,3,64,384]{3,2,1,0:T(8,128)(2,1)S(1)} collective-permute-done((bf16[1,3,64,384]{3,2,1,0:T(8,128)(2,1)S(1)}, bf16[1,3,64,384]{3,2,1,0:T(8,128)(2,1)S(1)}, u32[]{:S(2)}, u32[]{:S(2)}) %collective-permute-start.17) | collective-permute-done | bytes 147488 | tf_op jit(solution)/shard_map/second/ppermute | solution.py:28
  113.8 1.4 %finish.1 = bf16[2,6,128,384]{3,2,1,0:T(8,128)(2,1)} custom-call(bf16[2,3,64,384]{3,2,1,0:T(8,128)(2,1)S(1)} %bitcast.24, bf16[2,3,64,384]{3,2,1,0:T(8,128)(2,1)S(1)} %get-tuple-element.44.own_sum, bf16[2,3,64,384]{3,2,1,0:T(8,128)(2,1)S(1)} %collective-permute-done.15.up, bf16[2,3,64,384]{3,2,1,0:T(8,128)(2,1)S(1)} %collective-permute-done.16.down, ...), custom_call_target="tpu_custom_call" | custom-call | flops 2000000 | bytes 3000000 | tf_op jit(solution)/shard_map/finish/pallas_call | solution.py:259
  (26 shorter events, 0.1 us)
Async XLA Ops:
  0.0 1.2 %copy-start = (bf16[162,384]{1,0:T(8,128)(2,1)S(1)}, bf16[162,384]{1,0:T(8,128)(2,1)}, u32[]{:S(2)}) copy-start(bf16[162,384]{1,0:T(8,128)(2,1)} %param.11) | copy-start | bytes 373252
  1.2 9.8 %copy-start.1 = (bf16[1,2,3,64,384]{4,3,2,1,0:T(8,128)(2,1)S(1)}, bf16[1,2,3,64,384]{4,3,2,1,0:T(8,128)(2,1)}, u32[]{:S(2)}) copy-start(bf16[1,2,3,64,384]{4,3,2,1,0:T(8,128)(2,1)} %param.6) | copy-start | bytes 884740
  1.4 9.7 %copy-start.4 = (f32[384]{0:T(512)S(1)}, f32[384]{0:T(512)}, u32[]{:S(2)}) copy-start(f32[384]{0:T(512)} %param.8) | copy-start | bytes 4612
  2.4 27.0 %all-to-all-start = ((bf16[8,96,384]{2,1,0:T(8,128)(2,1)}), bf16[8,96,384]{2,1,0:T(8,128)(2,1)S(1)}, u32[]{:S(2)}, u32[]{:S(2)}) async-start(bf16[8,96,384]{2,1,0:T(8,128)(2,1)} %broadcast_in_dim.15), calls=%async_computation | async-start | bytes 1179648 | tf_op jit(solution)/shard_map/pieces/all_to_all | solution.py:351
  11.4 10.2 %collective-permute-start = (bf16[2,3,64,384]{3,2,1,0:T(8,128)(2,1)S(1)}, bf16[2,3,64,384]{3,2,1,0:T(8,128)(2,1)S(1)}, u32[]{:S(2)}, u32[]{:S(2)}) collective-permute-start(bf16[2,3,64,384]{3,2,1,0:T(8,128)(2,1)S(1)} %fusion.8), channel_id=1, source_target_pairs={{0,4},{4,8},{8,12},{12,0},{1,5},{5,9},{9,13},{13,1},{2,6},{6,10},{... | collective-permute-start | bytes 884744 | tf_op jit(solution)/shard_map/pixels/ppermute | solution.py:28
  13.0 15.2 %collective-permute-start.1 = (bf16[2,3,64,384]{3,2,1,0:T(8,128)(2,1)S(1)}, bf16[2,3,64,384]{3,2,1,0:T(8,128)(2,1)S(1)}, u32[]{:S(2)}, u32[]{:S(2)}) collective-permute-start(bf16[2,3,64,384]{3,2,1,0:T(8,128)(2,1)S(1)} %fusion.8), channel_id=1, source_target_pairs={{0,8},{4,12},{8,0},{12,4},{1,9},{5,13},{9,1},{13,5},{2,10},{6,14},... | collective-permute-start | bytes 884744 | tf_op jit(solution)/shard_map/pixels/ppermute | solution.py:28
  15.7 12.5 %collective-permute-start.2 = (bf16[2,3,64,384]{3,2,1,0:T(8,128)(2,1)S(1)}, bf16[2,3,64,384]{3,2,1,0:T(8,128)(2,1)S(1)}, u32[]{:S(2)}, u32[]{:S(2)}) collective-permute-start(bf16[2,3,64,384]{3,2,1,0:T(8,128)(2,1)S(1)} %fusion.8), channel_id=1, source_target_pairs={{0,12},{4,0},{8,4},{12,8},{1,13},{5,1},{9,5},{13,9},{2,14},{6,2},{... | collective-permute-start | bytes 884744 | tf_op jit(solution)/shard_map/pixels/ppermute | solution.py:28
  29.4 20.2 %collective-permute-start.6 = (bf16[4,2,3,64,384]{4,3,2,1,0:T(8,128)(2,1)}, bf16[4,2,3,64,384]{4,3,2,1,0:T(8,128)(2,1)S(1)}, u32[]{:S(2)}, u32[]{:S(2)}) collective-permute-start(bf16[4,2,3,64,384]{4,3,2,1,0:T(8,128)(2,1)} %pad_maximum_fusion.own), channel_id=1, source_target_pairs={{0,16},{16,32},{32,48},{48,64},{64,80},{80,96},{96,112},{112,128},... | collective-permute-start | bytes 3538952 | tf_op jit(solution)/shard_map/weight_one/ppermute | solution.py:23
  31.4 10.6 %collective-permute-start.3 = (bf16[8,48,384]{2,1,0:T(8,128)(2,1)S(1)}, bf16[8,48,384]{2,1,0:T(8,128)(2,1)S(1)}, u32[]{:S(2)}, u32[]{:S(2)}) collective-permute-start(bf16[8,48,384]{2,1,0:T(8,128)(2,1)S(1)} %get-tuple-element.30), channel_id=1, source_target_pairs={{0,1},{1,2},{2,3},{3,0},{4,5},{5,6},{6,7},{7,4},{8,9},{9,10},{10,1... | collective-permute-start | bytes 884744 | tf_op jit(solution)/shard_map/weight_one/ppermute | solution.py:28
  33.1 16.5 %collective-permute-start.4 = (bf16[8,48,384]{2,1,0:T(8,128)(2,1)S(1)}, bf16[8,48,384]{2,1,0:T(8,128)(2,1)S(1)}, u32[]{:S(2)}, u32[]{:S(2)}) collective-permute-start(bf16[8,48,384]{2,1,0:T(8,128)(2,1)S(1)} %get-tuple-element.30), channel_id=1, source_target_pairs={{0,2},{1,3},{2,0},{3,1},{4,6},{5,7},{6,4},{7,5},{8,10},{9,11},{10,... | collective-permute-start | bytes 884744 | tf_op jit(solution)/shard_map/weight_one/ppermute | solution.py:28
  36.0 13.6 %collective-permute-start.5 = (bf16[8,48,384]{2,1,0:T(8,128)(2,1)S(1)}, bf16[8,48,384]{2,1,0:T(8,128)(2,1)S(1)}, u32[]{:S(2)}, u32[]{:S(2)}) collective-permute-start(bf16[8,48,384]{2,1,0:T(8,128)(2,1)S(1)} %get-tuple-element.30), channel_id=1, source_target_pairs={{0,3},{1,0},{2,1},{3,2},{4,7},{5,4},{6,5},{7,6},{8,11},{9,8},{10,9... | collective-permute-start | bytes 884744 | tf_op jit(solution)/shard_map/weight_one/ppermute | solution.py:28
  49.6 1.0 copy-start.2
  50.6 1.5 %copy-start.6 = (s32[1,4]{1,0:T(1,128)S(1)}, s32[1,4]{1,0:T(1,128)}, u32[]{:S(2)}) copy-start(s32[1,4]{1,0:T(1,128)} %param.7) | copy-start | bytes 52
  51.8 5.8 %collective-permute-start.7 = (bf16[4,8,48,384]{3,2,1,0:T(8,128)(2,1)}, bf16[4,8,48,384]{3,2,1,0:T(8,128)(2,1)}, u32[]{:S(2)}, u32[]{:S(2)}) collective-permute-start(bf16[4,8,48,384]{3,2,1,0:T(8,128)(2,1)} %pad_maximum_fusion.1.mine), channel_id=1, source_target_pairs={{0,16},{16,0},{1,17},{17,1},{2,18},{18,2},{3,19},{19,3},{4,20},{20... | collective-permute-start | bytes 3538952 | tf_op jit(solution)/shard_map/weight_one/ppermute | solution.py:366
  52.7 19.3 %collective-permute-start.10 = (bf16[8,48,384]{2,1,0:T(8,128)(2,1)S(1)}, bf16[8,48,384]{2,1,0:T(8,128)(2,1)S(1)}, u32[]{:S(2)}, u32[]{:S(2)}) collective-permute-start(bf16[8,48,384]{2,1,0:T(8,128)(2,1)S(1)} %get-tuple-element.38), channel_id=1, source_target_pairs={{0,2},{1,3},{2,0},{3,1},{4,6},{5,7},{6,4},{7,5},{8,10},{9,11},{10,... | collective-permute-start | bytes 884744 | tf_op jit(solution)/shard_map/weight_two/ppermute | solution.py:28
  55.6 16.4 %collective-permute-start.11 = (bf16[8,48,384]{2,1,0:T(8,128)(2,1)S(1)}, bf16[8,48,384]{2,1,0:T(8,128)(2,1)S(1)}, u32[]{:S(2)}, u32[]{:S(2)}) collective-permute-start(bf16[8,48,384]{2,1,0:T(8,128)(2,1)S(1)} %get-tuple-element.38), channel_id=1, source_target_pairs={{0,3},{1,0},{2,1},{3,2},{4,7},{5,4},{6,5},{7,6},{8,11},{9,8},{10,9... | collective-permute-start | bytes 884744 | tf_op jit(solution)/shard_map/weight_two/ppermute | solution.py:28
  57.2 14.9 %collective-permute-start.9 = (bf16[8,48,384]{2,1,0:T(8,128)(2,1)S(1)}, bf16[8,48,384]{2,1,0:T(8,128)(2,1)S(1)}, u32[]{:S(2)}, u32[]{:S(2)}) collective-permute-start(bf16[8,48,384]{2,1,0:T(8,128)(2,1)S(1)} %get-tuple-element.38), channel_id=1, source_target_pairs={{0,1},{1,2},{2,3},{3,0},{4,5},{5,6},{6,7},{7,4},{8,9},{9,10},{10,1... | collective-permute-start | bytes 884744 | tf_op jit(solution)/shard_map/weight_two/ppermute | solution.py:28
  57.6 1.3 %copy-start.3 = (bf16[4,2,3,64,384]{4,3,2,1,0:T(8,128)(2,1)S(1)}, bf16[4,2,3,64,384]{4,3,2,1,0:T(8,128)(2,1)}, u32[]{:S(2)}) copy-start(bf16[4,2,3,64,384]{4,3,2,1,0:T(8,128)(2,1)} %copy-done.2) | copy-start | bytes 3538948
  68.2 3.8 %collective-permute-start.8 = (f32[2,12,64]{2,1,0:T(8,128)S(1)}, f32[2,12,64]{2,1,0:T(8,128)S(1)}, u32[]{:S(2)}, u32[]{:S(2)}) collective-permute-start(f32[2,12,64]{2,1,0:T(8,128)S(1)} %get-tuple-element.35), channel_id=1, source_target_pairs={{0,4},{4,0},{8,12},{12,8},{1,5},{5,1},{9,13},{13,9},{2,6},{6,2},{1... | collective-permute-start | bytes 18440 | tf_op jit(solution)/shard_map/weight_two/ppermute | solution.py:32
  72.1 3.1 %copy-start.5 = (f32[384]{0:T(512)S(1)}, f32[384]{0:T(512)}, u32[]{:S(2)}) copy-start(f32[384]{0:T(512)} %param.9) | copy-start | bytes 4612
  72.3 3.2 %collective-permute-start.13 = (bf16[4,8,48,384]{3,2,1,0:T(8,128)(2,1)S(1)}, bf16[4,8,48,384]{3,2,1,0:T(8,128)(2,1)}, u32[]{:S(2)}, u32[]{:S(2)}) collective-permute-start(bf16[4,8,48,384]{3,2,1,0:T(8,128)(2,1)S(1)} %pad_maximum_fusion.2.mine), channel_id=1, source_target_pairs={{0,16},{16,0},{1,17},{17,1},{2,18},{18,2},{3,19},{19,3},{4,20},{20... | collective-permute-start | bytes 3538952 | tf_op jit(solution)/shard_map/weight_two/ppermute | solution.py:381
  72.4 7.0 %collective-permute-start.12 = (f32[2,12,64]{2,1,0:T(8,128)S(1)}, f32[2,12,64]{2,1,0:T(8,128)S(1)}, u32[]{:S(2)}, u32[]{:S(2)}) collective-permute-start(f32[2,12,64]{2,1,0:T(8,128)S(1)} %add.93), channel_id=1, source_target_pairs={{0,8},{4,12},{8,0},{12,4},{1,9},{5,13},{9,1},{13,5},{2,10},{6,14},... | collective-permute-start | bytes 18440 | tf_op jit(solution)/shard_map/second/ppermute | solution.py:32
  79.7 9.1 %collective-permute-start.14 = (bf16[2,12,64,128]{3,2,1,0:T(8,128)(2,1)S(1)}, bf16[2,12,64,128]{3,2,1,0:T(8,128)(2,1)S(1)}, u32[]{:S(2)}, u32[]{:S(2)}) collective-permute-start(bf16[2,12,64,128]{3,2,1,0:T(8,128)(2,1)S(1)} %multiply_convert_fusion.own), channel_id=1, source_target_pairs={{0,16},{16,32},{32,48},{48,64},{64,80},{80,96},{96,112},{112,128},... | collective-permute-start | bytes 1179656 | tf_op jit(solution)/shard_map/second/ppermute | solution.py:23
  94.3 9.5 %collective-permute-start.16 = (bf16[2,3,64,384]{3,2,1,0:T(8,128)(2,1)S(1)}, bf16[2,3,64,384]{3,2,1,0:T(8,128)(2,1)S(1)}, u32[]{:S(2)}, u32[]{:S(2)}) collective-permute-start(bf16[2,3,64,384]{3,2,1,0:T(8,128)(2,1)S(1)} %get-tuple-element.46), channel_id=1, source_target_pairs={{0,12},{4,0},{8,4},{12,8},{1,13},{5,1},{9,5},{13,9},{2,14},{6,2},{... | collective-permute-start | bytes 884744 | tf_op jit(solution)/shard_map/second/ppermute | solution.py:28
  96.5 10.7 %collective-permute-start.15 = (bf16[2,3,64,384]{3,2,1,0:T(8,128)(2,1)S(1)}, bf16[2,3,64,384]{3,2,1,0:T(8,128)(2,1)S(1)}, u32[]{:S(2)}, u32[]{:S(2)}) collective-permute-start(bf16[2,3,64,384]{3,2,1,0:T(8,128)(2,1)S(1)} %get-tuple-element.45), channel_id=1, source_target_pairs={{0,4},{4,8},{8,12},{12,0},{1,5},{5,9},{9,13},{13,1},{2,6},{6,10},{... | collective-permute-start | bytes 884744 | tf_op jit(solution)/shard_map/second/ppermute | solution.py:28
  103.8 6.4 %collective-permute-start.18 = (bf16[1,3,64,384]{3,2,1,0:T(8,128)(2,1)S(1)}, bf16[1,3,64,384]{3,2,1,0:T(8,128)(2,1)S(1)}, u32[]{:S(2)}, u32[]{:S(2)}) collective-permute-start(bf16[1,3,64,384]{3,2,1,0:T(8,128)(2,1)S(1)} %slice_add_fusion), channel_id=1, source_target_pairs={{0,12},{4,0},{8,4},{12,8},{1,13},{5,1},{9,5},{13,9},{2,14},{6,2},{... | collective-permute-start | bytes 442376 | tf_op jit(solution)/shard_map/second/ppermute | solution.py:28
  107.3 6.5 %collective-permute-start.17 = (bf16[1,3,64,384]{3,2,1,0:T(8,128)(2,1)S(1)}, bf16[1,3,64,384]{3,2,1,0:T(8,128)(2,1)S(1)}, u32[]{:S(2)}, u32[]{:S(2)}) collective-permute-start(bf16[1,3,64,384]{3,2,1,0:T(8,128)(2,1)S(1)} %slice_add_fusion.1), channel_id=1, source_target_pairs={{0,4},{4,8},{8,12},{12,0},{1,5},{5,9},{9,13},{13,1},{2,6},{6,10},{... | collective-permute-start | bytes 442376 | tf_op jit(solution)/shard_map/second/ppermute | solution.py:28

commit v14 on v6

--- a/solution.py
+++ b/solution.py
@@ -64,7 +64,7 @@
     for pieces, core in ((mine, place[0]), (other, 1 - place[0])):
         for z in range(zs):
             top = pl.multiple_of((2 * z + core) * (ys * shard), 8)
-            view = wide.at[pl.ds(top, ys * shard), :]
+            view = wide.at[pl.ds(top, ys * shard + 8), :]
             for y in range(ys):
                 piece = pieces[lax.rem(place[1] + ys - y, ys), z].astype(jnp.float32)
                 for j in range(4):
@@ -76,7 +76,7 @@
                         window = pltpu.roll(window, window.shape[1] - shift, 1)
                     first = shard * y + j * piece_rows
                     view[first : first + rows, :] = window[:rows, :LANE]
-    out[...] = wide[...].astype(out.dtype)
+    out[...] = wide[: out.shape[0], :].astype(out.dtype)
 
 
 def conv_one_kernel(share, valid, place, halo, own, mine, other, out, frame_buf, acc, weight, wide):
@@ -175,7 +175,7 @@
             pltpu.VMEM((2 * frames, rows + 2, width, channels), jnp.bfloat16),
             pltpu.VMEM((frames, 3, rows * width, LANE), jnp.float32),
             pltpu.VMEM((27 * channels, LANE), jnp.bfloat16),
-            pltpu.VMEM((27 * channels, LANE), jnp.float32),
+            pltpu.VMEM((27 * channels + 8, LANE), jnp.float32),
         ],
         compiler_params=PARAMS,
         cost_estimate=pl.CostEstimate(flops=flops, bytes_accessed=6_000_000, transcendentals=0),

time: 114 us -> 114 us (level)
  no operation moved by 1% of the time
where the time goes in v14:
time: 114 us; the launch traced here: 113 us
  waiting for transfers between devices  54.9 us (48%)
  starting transfers between devices  29.4 us (26%)
  Pallas kernels  20.4 us (18%)
  other arithmetic  3.64 us (3%)
  local copies, waits for them, and re-layouts  3.29 us (3%)
  matrix products  1.35 us (1%)
    ppermute x12, waiting for transfers between devices, onward(): return lax.ppermute(x, axis, [(i, (i + by) % n) for i in range(n)])  44.3 us
    ppermute x12, starting transfers between devices, onward(): return lax.ppermute(x, axis, [(i, (i + by) % n) for i in range(n)])  15.2 us
    pallas_call x1, Pallas kernels, conv_one_call(): pl.pallas_call(functools.partial(conv_one_kernel, channels // parts), out...  9.19 us
    all_to_all x1, starting transfers between devices, body(): lax.all_to_all(jnp.broadcast_to(pieces, (lax.axis_size('z'),) + pieces.sh...  8.57 us
    ppermute x2, waiting for transfers between devices, across(): lax.ppermute(x, 'tile', [(i, i ^ bit) for i in range(lax.axis_size('tile'...  7.53 us
    pallas_call x1, Pallas kernels, conv_two_call(): pl.pallas_call(conv_two_kernel, out_shape=[jax.ShapeDtypeStruct((frames,...  7.31 us
    ppermute x2, starting transfers between devices, earlier(): return lax.ppermute(x, SLOT, [(i, i + 1) for i in range(n - 1)])  4.07 us
    pallas_call x1, Pallas kernels, assemble_call(): pl.pallas_call(kernel, out_shape=jax.ShapeDtypeStruct(shape, jnp.bfloat16...  3.93 us
  transfers between devices with their start and end apart: 19, of which 12 were waited for; matrix products, arithmetic and copies ran while one was open for 3% of the time, Pallas kernels for 12%

profile of v14, /device:TPU:32, one launch (start us, length us, event | category | flops | bytes accessed | tf_op | source)
XLA Modules:
  0.0 113.2 jit_solution(12778586331394964124)
XLA Ops:
  0.0 1.2 %fusion = bf16[162,96]{1,0:T(8,128)(2,1)S(1)} fusion(bf16[162,384]{1,0:T(8,128)(2,1)} %param.10, s32[96]{0:T(128)S(1)} %multiply_add_fusion.1), kind=kOutput, calls=%fused_computation.5 | convolution fusion | flops 11996352 | bytes 155904 | tf_op jit(solution)/shard_map/pieces/dot_general | solution.py:278
  1.2 0.0 copy-start.1
  1.2 0.2 convolution_convert_fusion.1
  1.4 0.0 copy-start.3
  1.4 0.1 fusion.27
  1.6 0.9 broadcast_in_dim.15
  2.4 8.6 %all-to-all-start = ((bf16[8,96,384]{2,1,0:T(8,128)(2,1)}), bf16[8,96,384]{2,1,0:T(8,128)(2,1)S(1)}, u32[]{:S(2)}, u32[]{:S(2)}) async-start(bf16[8,96,384]{2,1,0:T(8,128)(2,1)} %broadcast_in_dim.15), calls=%async_computation | async-start | bytes 1179648 | tf_op jit(solution)/shard_map/pieces/all_to_all | solution.py:285
  11.0 0.1 fusion.4
  11.2 0.3 fusion.11
  11.4 2.8 %collective-permute-start.2 = (bf16[2,3,64,384]{3,2,1,0:T(8,128)(2,1)S(1)}, bf16[2,3,64,384]{3,2,1,0:T(8,128)(2,1)S(1)}, u32[]{:S(2)}, u32[]{:S(2)}) collective-permute-start(bf16[2,3,64,384]{3,2,1,0:T(8,128)(2,1)S(1)} %fusion.11), channel_id=1, source_target_pairs={{0,12},{4,0},{8,4},{12,8},{1,13},{5,1},{9,5},{13,9},{2,14},{6,2},{... | collective-permute-start | bytes 884744 | tf_op jit(solution)/shard_map/pixels/ppermute | solution.py:28
  14.3 0.8 collective-permute-start.1
  15.1 0.9 collective-permute-start
  15.9 0.3 fusion.19
  16.2 10.1 %collective-permute-done.2 = bf16[2,3,64,384]{3,2,1,0:T(8,128)(2,1)S(1)} collective-permute-done((bf16[2,3,64,384]{3,2,1,0:T(8,128)(2,1)S(1)}, bf16[2,3,64,384]{3,2,1,0:T(8,128)(2,1)S(1)}, u32[]{:S(2)}, u32[]{:S(2)}) %collective-permute-start.2) | collective-permute-done | bytes 294944 | tf_op jit(solution)/shard_map/pixels/ppermute | solution.py:28
  26.3 0.0 collective-permute-done.1
  26.3 3.7 %collective-permute-done = bf16[2,3,64,384]{3,2,1,0:T(8,128)(2,1)S(1)} collective-permute-done((bf16[2,3,64,384]{3,2,1,0:T(8,128)(2,1)S(1)}, bf16[2,3,64,384]{3,2,1,0:T(8,128)(2,1)S(1)}, u32[]{:S(2)}, u32[]{:S(2)}) %collective-permute-start) | collective-permute-done | bytes 294944 | tf_op jit(solution)/shard_map/pixels/ppermute | solution.py:28
  30.0 0.2 pad_maximum_fusion.own
  30.2 0.0 copy-start.2
  30.2 0.0 all-to-all-done
  30.2 1.9 %collective-permute-start.6 = (bf16[4,2,3,64,384]{4,3,2,1,0:T(8,128)(2,1)S(1)}, bf16[4,2,3,64,384]{4,3,2,1,0:T(8,128)(2,1)S(1)}, u32[]{:S(2)}, u32[]{:S(2)}) collective-permute-start(bf16[4,2,3,64,384]{4,3,2,1,0:T(8,128)(2,1)S(1)} %pad_maximum_fusion.own), channel_id=1, source_target_pairs={{0,16},{16,32},{32,48},{48,64},{64,80},{80,96},{96,112},{112,128},... | collective-permute-start | bytes 3538952 | tf_op jit(solution)/shard_map/weight_one/ppermute | solution.py:23
  32.1 0.1 slice_bitcast_fusion
  32.2 3.1 %collective-permute-start.5 = (bf16[8,48,384]{2,1,0:T(8,128)(2,1)S(1)}, bf16[8,48,384]{2,1,0:T(8,128)(2,1)S(1)}, u32[]{:S(2)}, u32[]{:S(2)}) collective-permute-start(bf16[8,48,384]{2,1,0:T(8,128)(2,1)S(1)} %get-tuple-element.34), channel_id=1, source_target_pairs={{0,3},{1,0},{2,1},{3,2},{4,7},{5,4},{6,5},{7,6},{8,11},{9,8},{10,9... | collective-permute-start | bytes 884744 | tf_op jit(solution)/shard_map/weight_one/ppermute | solution.py:28
  35.3 0.6 collective-permute-start.4
  35.9 1.0 collective-permute-start.3
  36.9 11.4 %collective-permute-done.5 = bf16[8,48,384]{2,1,0:T(8,128)(2,1)S(1)} collective-permute-done((bf16[8,48,384]{2,1,0:T(8,128)(2,1)S(1)}, bf16[8,48,384]{2,1,0:T(8,128)(2,1)S(1)}, u32[]{:S(2)}, u32[]{:S(2)}) %collective-permute-start.5) | collective-permute-done | bytes 294944 | tf_op jit(solution)/shard_map/weight_one/ppermute | solution.py:28
  48.3 0.0 collective-permute-done.4
  48.3 4.7 %collective-permute-done.3 = bf16[8,48,384]{2,1,0:T(8,128)(2,1)S(1)} collective-permute-done((bf16[8,48,384]{2,1,0:T(8,128)(2,1)S(1)}, bf16[8,48,384]{2,1,0:T(8,128)(2,1)S(1)}, u32[]{:S(2)}, u32[]{:S(2)}) %collective-permute-start.3) | collective-permute-done | bytes 294944 | tf_op jit(solution)/shard_map/weight_one/ppermute | solution.py:28
  53.0 1.2 %pad_maximum_fusion.1.mine = bf16[4,8,48,384]{3,2,1,0:T(8,128)(2,1)} fusion(bf16[1,8,48,384]{3,2,1,0:T(8,128)(2,1)S(1)} %bitcast.54, bf16[1,8,48,384]{3,2,1,0:T(8,128)(2,1)S(1)} %bitcast.56, bf16[1,8,48,384]{3,2,1,0:T(8,128)(2,1)S(1)} %bitcast.58, bf16[1,8,48,384]{3,2,1,0:T(8,128)(2,1)S(1)} %get-tuple-element.33), kind=kLoop, calls=%fused_computation.1 | loop fusion | flops 1769472 | bytes 2359296 | tf_op jit(solution)/shard_map/weight_one/stack | solution.py:36
  54.2 0.1 collective-permute-start.7
  54.3 0.2 reduce-window_clone.1
  54.5 0.1 pad_add_fusion.place
  54.6 0.2 fusion.29
  54.8 0.1 compare_convert_fusion.valid
  54.9 0.1 collective-permute-start.9
  55.0 1.8 %collective-permute-start.10 = (bf16[8,48,384]{2,1,0:T(8,128)(2,1)S(1)}, bf16[8,48,384]{2,1,0:T(8,128)(2,1)S(1)}, u32[]{:S(2)}, u32[]{:S(2)}) collective-permute-start(bf16[8,48,384]{2,1,0:T(8,128)(2,1)S(1)} %slice.26), channel_id=1, source_target_pairs={{0,2},{1,3},{2,0},{3,1},{4,6},{5,7},{6,4},{7,5},{8,10},{9,11},{10,... | collective-permute-start | bytes 884744 | tf_op jit(solution)/shard_map/weight_two/ppermute | solution.py:28
  56.8 1.5 %collective-permute-start.11 = (bf16[8,48,384]{2,1,0:T(8,128)(2,1)S(1)}, bf16[8,48,384]{2,1,0:T(8,128)(2,1)S(1)}, u32[]{:S(2)}, u32[]{:S(2)}) collective-permute-start(bf16[8,48,384]{2,1,0:T(8,128)(2,1)S(1)} %slice.26), channel_id=1, source_target_pairs={{0,3},{1,0},{2,1},{3,2},{4,7},{5,4},{6,5},{7,6},{8,11},{9,8},{10,9... | collective-permute-start | bytes 884744 | tf_op jit(solution)/shard_map/weight_two/ppermute | solution.py:28
  58.3 0.0 collective-permute-done.7.other
  58.3 9.2 %conv_one.1 = f32[2,12,64,128]{3,2,1,0:T(8,128)S(1)} custom-call(f32[2,3]{1,0:T(2,128)S(1)} %compare_convert_fusion.valid, s32[3]{0:T(128)S(1)} %pad_add_fusion.place, bf16[4,2,3,64,384]{4,3,2,1,0:T(8,128)(2,1)S(1)} %collective-permute-done.6.halo, bf16[4,2,3,64,384]{4,3,2,1,0:T(8,128)(2,1)} %copy-done.2, bf16[4,8,48,384]{3,2,1,0:T(8,128)(2,1)} %pad_maximum_fusion.1.mine, ...), custom_call_target="tpu_custom_call" | custom-call | flops 4076863488 | bytes 6000000 | tf_op jit(solution)/shard_map/first/conv_one/pallas_call | solution.py:169
  67.5 0.3 multiply_reduce_fusion
  67.8 0.1 collective-permute-start.8
  67.9 3.7 %collective-permute-done.8 = f32[2,12,64]{2,1,0:T(8,128)S(1)} collective-permute-done((f32[2,12,64]{2,1,0:T(8,128)S(1)}, f32[2,12,64]{2,1,0:T(8,128)S(1)}, u32[]{:S(2)}, u32[]{:S(2)}) %collective-permute-start.8) | collective-permute-done | bytes 6176 | tf_op jit(solution)/shard_map/weight_two/ppermute | solution.py:32
  71.6 0.2 collective-permute-done.9
  71.8 0.0 collective-permute-done.10
  71.8 0.6 collective-permute-done.11
  72.4 0.2 pad_maximum_fusion.2.mine
  72.6 0.1 collective-permute-start.14
  72.7 1.2 %collective-permute-start.12 = (f32[2,12,64]{2,1,0:T(8,128)S(1)}, f32[2,12,64]{2,1,0:T(8,128)S(1)}, u32[]{:S(2)}, u32[]{:S(2)}) collective-permute-start(f32[2,12,64]{2,1,0:T(8,128)S(1)} %add.99), channel_id=1, source_target_pairs={{0,8},{4,12},{8,0},{12,4},{1,9},{5,13},{9,1},{13,5},{2,10},{6,14},... | collective-permute-start | bytes 18440 | tf_op jit(solution)/shard_map/second/ppermute | solution.py:32
  74.0 0.1 reshape.33
  74.1 0.2 dynamic-slice_reduce_fusion
  74.3 3.8 %collective-permute-done.12 = f32[2,12,64]{2,1,0:T(8,128)S(1)} collective-permute-done((f32[2,12,64]{2,1,0:T(8,128)S(1)}, f32[2,12,64]{2,1,0:T(8,128)S(1)}, u32[]{:S(2)}, u32[]{:S(2)}) %collective-permute-start.12) | collective-permute-done | bytes 6176 | tf_op jit(solution)/shard_map/second/ppermute | solution.py:32
  78.1 0.3 multiply_convert_fusion.own
  78.4 2.1 %collective-permute-start.13 = (bf16[2,12,64,128]{3,2,1,0:T(8,128)(2,1)S(1)}, bf16[2,12,64,128]{3,2,1,0:T(8,128)(2,1)S(1)}, u32[]{:S(2)}, u32[]{:S(2)}) collective-permute-start(bf16[2,12,64,128]{3,2,1,0:T(8,128)(2,1)S(1)} %multiply_convert_fusion.own), channel_id=1, source_target_pairs={{0,16},{16,32},{32,48},{48,64},{64,80},{80,96},{96,112},{112,128},... | collective-permute-start | bytes 1179656 | tf_op jit(solution)/shard_map/second/ppermute | solution.py:23
  80.5 3.9 %assemble_two.1.weight = bf16[3456,384]{1,0:T(8,128)(2,1)} custom-call(s32[3]{0:T(128)S(1)} %pad_add_fusion.place, bf16[4,8,48,384]{3,2,1,0:T(8,128)(2,1)S(1)} %pad_maximum_fusion.2.mine, bf16[4,8,48,384]{3,2,1,0:T(8,128)(2,1)} %collective-permute-done.14.other), custom_call_target="tpu_custom_call" | custom-call | flops 4000000 | bytes 5000000 | tf_op jit(solution)/shard_map/weight_two/assemble_two/pallas_call | solution.py:239
  84.5 3.0 %collective-permute-done.13.halo = bf16[2,12,64,128]{3,2,1,0:T(8,128)(2,1)S(1)} collective-permute-done((bf16[2,12,64,128]{3,2,1,0:T(8,128)(2,1)S(1)}, bf16[2,12,64,128]{3,2,1,0:T(8,128)(2,1)S(1)}, u32[]{:S(2)}, u32[]{:S(2)}) %collective-permute-start.13) | collective-permute-done | bytes 393248 | tf_op jit(solution)/shard_map/second/ppermute | solution.py:23
  87.5 7.3 %conv_two.1 = (bf16[2,3,64,384]{3,2,1,0:T(8,128)(2,1)S(1)}, bf16[2,3,64,384]{3,2,1,0:T(8,128)(2,1)S(1)}, bf16[2,3,64,384]{3,2,1,0:T(8,128)(2,1)S(1)}, bf16[2,3,64,384]{3,2,1,0:T(8,128)(2,1)S(1)}) custom-call(f32[2,3]{1,0:T(2,128)S(1)} %compare_convert_fusion.valid, s32[3]{0:T(128)S(1)} %pad_add_fusion.place, ...), custom_call_target="tpu_custom_call" | custom-call | flops 4076863488 | bytes 6000000 | tf_op jit(solution)/shard_map/second/conv_two/pallas_call | solution.py:190
  94.8 1.0 collective-permute-start.17
  95.8 0.8 collective-permute-start.16
  96.6 0.8 collective-permute-start.15
  97.4 7.4 %collective-permute-done.17 = bf16[2,3,64,384]{3,2,1,0:T(8,128)(2,1)S(1)} collective-permute-done((bf16[2,3,64,384]{3,2,1,0:T(8,128)(2,1)S(1)}, bf16[2,3,64,384]{3,2,1,0:T(8,128)(2,1)S(1)}, u32[]{:S(2)}, u32[]{:S(2)}) %collective-permute-start.17) | collective-permute-done | bytes 294944 | tf_op jit(solution)/shard_map/second/ppermute | solution.py:28
  104.8 2.5 %collective-permute-done.16 = bf16[2,3,64,384]{3,2,1,0:T(8,128)(2,1)S(1)} collective-permute-done((bf16[2,3,64,384]{3,2,1,0:T(8,128)(2,1)S(1)}, bf16[2,3,64,384]{3,2,1,0:T(8,128)(2,1)S(1)}, u32[]{:S(2)}, u32[]{:S(2)}) %collective-permute-start.16) | collective-permute-done | bytes 294944 | tf_op jit(solution)/shard_map/second/ppermute | solution.py:28
  107.3 3.8 %collective-permute-done.15 = bf16[2,3,64,384]{3,2,1,0:T(8,128)(2,1)S(1)} collective-permute-done((bf16[2,3,64,384]{3,2,1,0:T(8,128)(2,1)S(1)}, bf16[2,3,64,384]{3,2,1,0:T(8,128)(2,1)S(1)}, u32[]{:S(2)}, u32[]{:S(2)}) %collective-permute-start.15) | collective-permute-done | bytes 294944 | tf_op jit(solution)/shard_map/second/ppermute | solution.py:28
  111.0 0.2 fusion.12
  111.2 0.7 broadcast_in_dim.16
  111.9 1.3 %broadcast_in_dim_reshape.3 = bf16[1,2,6,128,384]{4,3,2,1,0:T(8,128)(2,1)} reshape(bf16[2,3,2,64,2,384]{5,4,3,2,1,0:T(2,128)(2,1)S(1)} %broadcast_in_dim.16) | data formatting | bytes 2359296 | tf_op jit(solution)/shard_map/broadcast_in_dim;reshape | solution.py:336
  (23 shorter events, 0.1 us)
Async XLA Ops:
  0.0 1.2 %copy-start = (bf16[162,384]{1,0:T(8,128)(2,1)S(1)}, bf16[162,384]{1,0:T(8,128)(2,1)}, u32[]{:S(2)}) copy-start(bf16[162,384]{1,0:T(8,128)(2,1)} %param.11) | copy-start | bytes 373252
  1.2 9.8 %copy-start.1 = (bf16[1,2,3,64,384]{4,3,2,1,0:T(8,128)(2,1)S(1)}, bf16[1,2,3,64,384]{4,3,2,1,0:T(8,128)(2,1)}, u32[]{:S(2)}) copy-start(bf16[1,2,3,64,384]{4,3,2,1,0:T(8,128)(2,1)} %param.6) | copy-start | bytes 884740
  1.4 9.7 %copy-start.3 = (f32[384]{0:T(512)S(1)}, f32[384]{0:T(512)}, u32[]{:S(2)}) copy-start(f32[384]{0:T(512)} %param.8) | copy-start | bytes 4612
  2.4 27.8 %all-to-all-start = ((bf16[8,96,384]{2,1,0:T(8,128)(2,1)}), bf16[8,96,384]{2,1,0:T(8,128)(2,1)S(1)}, u32[]{:S(2)}, u32[]{:S(2)}) async-start(bf16[8,96,384]{2,1,0:T(8,128)(2,1)} %broadcast_in_dim.15), calls=%async_computation | async-start | bytes 1179648 | tf_op jit(solution)/shard_map/pieces/all_to_all | solution.py:285
  11.4 14.9 %collective-permute-start.2 = (bf16[2,3,64,384]{3,2,1,0:T(8,128)(2,1)S(1)}, bf16[2,3,64,384]{3,2,1,0:T(8,128)(2,1)S(1)}, u32[]{:S(2)}, u32[]{:S(2)}) collective-permute-start(bf16[2,3,64,384]{3,2,1,0:T(8,128)(2,1)S(1)} %fusion.11), channel_id=1, source_target_pairs={{0,12},{4,0},{8,4},{12,8},{1,13},{5,1},{9,5},{13,9},{2,14},{6,2},{... | collective-permute-start | bytes 884744 | tf_op jit(solution)/shard_map/pixels/ppermute | solution.py:28
  14.3 12.1 %collective-permute-start.1 = (bf16[2,3,64,384]{3,2,1,0:T(8,128)(2,1)S(1)}, bf16[2,3,64,384]{3,2,1,0:T(8,128)(2,1)S(1)}, u32[]{:S(2)}, u32[]{:S(2)}) collective-permute-start(bf16[2,3,64,384]{3,2,1,0:T(8,128)(2,1)S(1)} %fusion.11), channel_id=1, source_target_pairs={{0,8},{4,12},{8,0},{12,4},{1,9},{5,13},{9,1},{13,5},{2,10},{6,14},... | collective-permute-start | bytes 884744 | tf_op jit(solution)/shard_map/pixels/ppermute | solution.py:28
  15.1 14.9 %collective-permute-start = (bf16[2,3,64,384]{3,2,1,0:T(8,128)(2,1)S(1)}, bf16[2,3,64,384]{3,2,1,0:T(8,128)(2,1)S(1)}, u32[]{:S(2)}, u32[]{:S(2)}) collective-permute-start(bf16[2,3,64,384]{3,2,1,0:T(8,128)(2,1)S(1)} %fusion.11), channel_id=1, source_target_pairs={{0,4},{4,8},{8,12},{12,0},{1,5},{5,9},{9,13},{13,1},{2,6},{6,10},{... | collective-permute-start | bytes 884744 | tf_op jit(solution)/shard_map/pixels/ppermute | solution.py:28
  30.2 24.0 %copy-start.2 = (bf16[4,2,3,64,384]{4,3,2,1,0:T(8,128)(2,1)}, bf16[4,2,3,64,384]{4,3,2,1,0:T(8,128)(2,1)S(1)}, u32[]{:S(2)}) copy-start(bf16[4,2,3,64,384]{4,3,2,1,0:T(8,128)(2,1)S(1)} %pad_maximum_fusion.own) | copy-start | bytes 3538948
  30.2 24.0 %collective-permute-start.6 = (bf16[4,2,3,64,384]{4,3,2,1,0:T(8,128)(2,1)S(1)}, bf16[4,2,3,64,384]{4,3,2,1,0:T(8,128)(2,1)S(1)}, u32[]{:S(2)}, u32[]{:S(2)}) collective-permute-start(bf16[4,2,3,64,384]{4,3,2,1,0:T(8,128)(2,1)S(1)} %pad_maximum_fusion.own), channel_id=1, source_target_pairs={{0,16},{16,32},{32,48},{48,64},{64,80},{80,96},{96,112},{112,128},... | collective-permute-start | bytes 3538952 | tf_op jit(solution)/shard_map/weight_one/ppermute | solution.py:23
  32.2 16.1 %collective-permute-start.5 = (bf16[8,48,384]{2,1,0:T(8,128)(2,1)S(1)}, bf16[8,48,384]{2,1,0:T(8,128)(2,1)S(1)}, u32[]{:S(2)}, u32[]{:S(2)}) collective-permute-start(bf16[8,48,384]{2,1,0:T(8,128)(2,1)S(1)} %get-tuple-element.34), channel_id=1, source_target_pairs={{0,3},{1,0},{2,1},{3,2},{4,7},{5,4},{6,5},{7,6},{8,11},{9,8},{10,9... | collective-permute-start | bytes 884744 | tf_op jit(solution)/shard_map/weight_one/ppermute | solution.py:28
  35.3 13.1 %collective-permute-start.4 = (bf16[8,48,384]{2,1,0:T(8,128)(2,1)S(1)}, bf16[8,48,384]{2,1,0:T(8,128)(2,1)S(1)}, u32[]{:S(2)}, u32[]{:S(2)}) collective-permute-start(bf16[8,48,384]{2,1,0:T(8,128)(2,1)S(1)} %get-tuple-element.34), channel_id=1, source_target_pairs={{0,2},{1,3},{2,0},{3,1},{4,6},{5,7},{6,4},{7,5},{8,10},{9,11},{10,... | collective-permute-start | bytes 884744 | tf_op jit(solution)/shard_map/weight_one/ppermute | solution.py:28
  35.9 17.1 %collective-permute-start.3 = (bf16[8,48,384]{2,1,0:T(8,128)(2,1)S(1)}, bf16[8,48,384]{2,1,0:T(8,128)(2,1)S(1)}, u32[]{:S(2)}, u32[]{:S(2)}) collective-permute-start(bf16[8,48,384]{2,1,0:T(8,128)(2,1)S(1)} %get-tuple-element.34), channel_id=1, source_target_pairs={{0,1},{1,2},{2,3},{3,0},{4,5},{5,6},{6,7},{7,4},{8,9},{9,10},{10,1... | collective-permute-start | bytes 884744 | tf_op jit(solution)/shard_map/weight_one/ppermute | solution.py:28
  53.0 1.4 %copy-start.5 = (s32[1,4]{1,0:T(1,128)S(1)}, s32[1,4]{1,0:T(1,128)}, u32[]{:S(2)}) copy-start(s32[1,4]{1,0:T(1,128)} %param.7) | copy-start | bytes 52
  54.2 4.1 %collective-permute-start.7 = (bf16[4,8,48,384]{3,2,1,0:T(8,128)(2,1)}, bf16[4,8,48,384]{3,2,1,0:T(8,128)(2,1)}, u32[]{:S(2)}, u32[]{:S(2)}) collective-permute-start(bf16[4,8,48,384]{3,2,1,0:T(8,128)(2,1)} %pad_maximum_fusion.1.mine), channel_id=1, source_target_pairs={{0,16},{16,0},{1,17},{17,1},{2,18},{18,2},{3,19},{19,3},{4,20},{20... | collective-permute-start | bytes 3538952 | tf_op jit(solution)/shard_map/weight_one/ppermute | solution.py:292
  54.9 16.9 %collective-permute-start.9 = (bf16[8,48,384]{2,1,0:T(8,128)(2,1)S(1)}, bf16[8,48,384]{2,1,0:T(8,128)(2,1)S(1)}, u32[]{:S(2)}, u32[]{:S(2)}) collective-permute-start(bf16[8,48,384]{2,1,0:T(8,128)(2,1)S(1)} %slice.26), channel_id=1, source_target_pairs={{0,1},{1,2},{2,3},{3,0},{4,5},{5,6},{6,7},{7,4},{8,9},{9,10},{10,1... | collective-permute-start | bytes 884744 | tf_op jit(solution)/shard_map/weight_two/ppermute | solution.py:28
  55.0 16.8 %collective-permute-start.10 = (bf16[8,48,384]{2,1,0:T(8,128)(2,1)S(1)}, bf16[8,48,384]{2,1,0:T(8,128)(2,1)S(1)}, u32[]{:S(2)}, u32[]{:S(2)}) collective-permute-start(bf16[8,48,384]{2,1,0:T(8,128)(2,1)S(1)} %slice.26), channel_id=1, source_target_pairs={{0,2},{1,3},{2,0},{3,1},{4,6},{5,7},{6,4},{7,5},{8,10},{9,11},{10,... | collective-permute-start | bytes 884744 | tf_op jit(solution)/shard_map/weight_two/ppermute | solution.py:28
  56.8 15.7 %collective-permute-start.11 = (bf16[8,48,384]{2,1,0:T(8,128)(2,1)S(1)}, bf16[8,48,384]{2,1,0:T(8,128)(2,1)S(1)}, u32[]{:S(2)}, u32[]{:S(2)}) collective-permute-start(bf16[8,48,384]{2,1,0:T(8,128)(2,1)S(1)} %slice.26), channel_id=1, source_target_pairs={{0,3},{1,0},{2,1},{3,2},{4,7},{5,4},{6,5},{7,6},{8,11},{9,8},{10,9... | collective-permute-start | bytes 884744 | tf_op jit(solution)/shard_map/weight_two/ppermute | solution.py:28
  67.8 3.8 %collective-permute-start.8 = (f32[2,12,64]{2,1,0:T(8,128)S(1)}, f32[2,12,64]{2,1,0:T(8,128)S(1)}, u32[]{:S(2)}, u32[]{:S(2)}) collective-permute-start(f32[2,12,64]{2,1,0:T(8,128)S(1)} %multiply_reduce_fusion), channel_id=1, source_target_pairs={{0,4},{4,0},{8,12},{12,8},{1,5},{5,1},{9,13},{13,9},{2,6},{6,2},{1... | collective-permute-start | bytes 18440 | tf_op jit(solution)/shard_map/weight_two/ppermute | solution.py:32
  72.4 1.5 %copy-start.4 = (f32[384]{0:T(512)S(1)}, f32[384]{0:T(512)}, u32[]{:S(2)}) copy-start(f32[384]{0:T(512)} %param.9) | copy-start | bytes 4612
  72.6 7.9 %collective-permute-start.14 = (bf16[4,8,48,384]{3,2,1,0:T(8,128)(2,1)S(1)}, bf16[4,8,48,384]{3,2,1,0:T(8,128)(2,1)}, u32[]{:S(2)}, u32[]{:S(2)}) collective-permute-start(bf16[4,8,48,384]{3,2,1,0:T(8,128)(2,1)S(1)} %pad_maximum_fusion.2.mine), channel_id=1, source_target_pairs={{0,16},{16,0},{1,17},{17,1},{2,18},{18,2},{3,19},{19,3},{4,20},{20... | collective-permute-start | bytes 3538952 | tf_op jit(solution)/shard_map/weight_two/ppermute | solution.py:314
  72.7 5.3 %collective-permute-start.12 = (f32[2,12,64]{2,1,0:T(8,128)S(1)}, f32[2,12,64]{2,1,0:T(8,128)S(1)}, u32[]{:S(2)}, u32[]{:S(2)}) collective-permute-start(f32[2,12,64]{2,1,0:T(8,128)S(1)} %add.99), channel_id=1, source_target_pairs={{0,8},{4,12},{8,0},{12,4},{1,9},{5,13},{9,1},{13,5},{2,10},{6,14},... | collective-permute-start | bytes 18440 | tf_op jit(solution)/shard_map/second/ppermute | solution.py:32
  78.4 9.1 %collective-permute-start.13 = (bf16[2,12,64,128]{3,2,1,0:T(8,128)(2,1)S(1)}, bf16[2,12,64,128]{3,2,1,0:T(8,128)(2,1)S(1)}, u32[]{:S(2)}, u32[]{:S(2)}) collective-permute-start(bf16[2,12,64,128]{3,2,1,0:T(8,128)(2,1)S(1)} %multiply_convert_fusion.own), channel_id=1, source_target_pairs={{0,16},{16,32},{32,48},{48,64},{64,80},{80,96},{96,112},{112,128},... | collective-permute-start | bytes 1179656 | tf_op jit(solution)/shard_map/second/ppermute | solution.py:23
  94.8 10.0 %collective-permute-start.17 = (bf16[2,3,64,384]{3,2,1,0:T(8,128)(2,1)S(1)}, bf16[2,3,64,384]{3,2,1,0:T(8,128)(2,1)S(1)}, u32[]{:S(2)}, u32[]{:S(2)}) collective-permute-start(bf16[2,3,64,384]{3,2,1,0:T(8,128)(2,1)S(1)} %get-tuple-element.32), channel_id=1, source_target_pairs={{0,12},{4,0},{8,4},{12,8},{1,13},{5,1},{9,5},{13,9},{2,14},{6,2},{... | collective-permute-start | bytes 884744 | tf_op jit(solution)/shard_map/second/ppermute | solution.py:28
  95.8 11.5 %collective-permute-start.16 = (bf16[2,3,64,384]{3,2,1,0:T(8,128)(2,1)S(1)}, bf16[2,3,64,384]{3,2,1,0:T(8,128)(2,1)S(1)}, u32[]{:S(2)}, u32[]{:S(2)}) collective-permute-start(bf16[2,3,64,384]{3,2,1,0:T(8,128)(2,1)S(1)} %get-tuple-element.31), channel_id=1, source_target_pairs={{0,8},{4,12},{8,0},{12,4},{1,9},{5,13},{9,1},{13,5},{2,10},{6,14},... | collective-permute-start | bytes 884744 | tf_op jit(solution)/shard_map/second/ppermute | solution.py:28
  96.6 14.4 %collective-permute-start.15 = (bf16[2,3,64,384]{3,2,1,0:T(8,128)(2,1)S(1)}, bf16[2,3,64,384]{3,2,1,0:T(8,128)(2,1)S(1)}, u32[]{:S(2)}, u32[]{:S(2)}) collective-permute-start(bf16[2,3,64,384]{3,2,1,0:T(8,128)(2,1)S(1)} %get-tuple-element.30), channel_id=1, source_target_pairs={{0,4},{4,8},{8,12},{12,0},{1,5},{5,9},{9,13},{13,1},{2,6},{6,10},{... | collective-permute-start | bytes 884744 | tf_op jit(solution)/shard_map/second/ppermute | solution.py:28
